TPU v7x, 512 devices: a whole 4x8x8 slice. The times are simulated.
512 devices in a mesh: dp: 8 (over z_lo, core), expert: 64 (over z_hi, y, x).
Axes of the slice: x: 4, y: 8, z: 8 (z_hi: 2, z_lo: 4; z = z_hi * 4 + z_lo), core: 2. Of those that a mesh axis runs over, the one named last changes fastest.
Arguments:
- tokens: bfloat16 [2, 2048, 4096], P(None, 'expert', 'dp'), may hold values from -6 to 6
- w_gate: bfloat16 [64, 1536, 4096], P('expert', 'dp'), may hold values from -0.09375 to 0.09375
- w_down: bfloat16 [64, 1536, 4096], P('expert', 'dp'), may hold values from -0.15625 to 0.15625
- expert_ids: int32 [2, 2048, 8], P(None, 'expert'), may hold values from 0 to 63, all different within a row
- route_weight: float32 [2, 2048, 8], P(None, 'expert'), may hold values from 0.1 to 1
- replica_pick: int32 [2, 2048, 8], P(None, 'expert'), may hold values from 0 to 63
- old_plan: int32 [64], replicated, may hold values from 0 to 63, each once
- new_plan: int32 [64], replicated, may hold values from 0 to 63, each once
Outputs:
- layer_out: bfloat16 [2, 2048, 4096], P(None, 'expert', 'dp')
Inputs may be any that keep to these rules, and one draw needn't show every extreme that they name: `expert_ids`: each token names 8 different experts, and every expert is named by some token. `old_plan`: each expert stands in exactly one host's second slot. `new_plan`: each expert stands in exactly one host's second slot.
All inputs are finite; a program needn't handle non-finite values.
Results may differ from a plain program's by a relative error of at most 0.02.
Values may be sent and summed in bfloat16 or wider, within the bound.
No kernel may reach another device: no remote copies, remote signals or barrier semaphores. Data moves between devices by JAX's collectives and lax.ppermute only.
A program may use at most 64 MiB of HBM per device.

v0:
```python
import jax
import jax.numpy as jnp
from jax import lax
from jax.sharding import PartitionSpec as P

TOPK = 8


def route_rows(placement, expert_ids, replica_pick):
    host_count = placement.shape[0]
    host_ids = jnp.arange(host_count, dtype=jnp.int32)
    same_plan = placement[:, None] == placement[None, :]
    before = host_ids[None, :] < host_ids[:, None]
    copy_rank = 1 + jnp.sum((same_plan & before).astype(jnp.int32), axis=1)
    copies = 1 + jnp.sum((placement[None, :] == host_ids[:, None]).astype(jnp.int32), axis=1)
    flat_ids = expert_ids.reshape(-1)
    flat_pick = replica_pick.reshape(-1)
    named_by = flat_ids[:, None] == host_ids[None, :]
    copy_count = jnp.sum(jnp.where(named_by, copies[None, :], 0), axis=1)
    replica = flat_pick % copy_count
    matched = (placement[None, :] == flat_ids[:, None]) & (copy_rank[None, :] == replica[:, None])
    second = jnp.sum(jnp.where(matched, host_ids[None, :], 0), axis=1)
    target = jnp.where(replica == 0, flat_ids, second)
    spare_slot = (replica > 0).astype(jnp.int32)
    landed = (target[:, None] == host_ids[None, :]).astype(jnp.int32)
    earlier = jnp.cumsum(landed, axis=0) - landed
    position = jnp.sum(earlier * landed, axis=1)
    return (target, spare_slot, position)


def project_rows(rows_in, gate_rows):
    return lax.dot_general(
        rows_in, gate_rows, (((1,), (1,)), ((), ())), preferred_element_type=jnp.float32
    )


def local(tokens, w_gate, w_down, expert_ids, route_weight, replica_pick, old_plan, new_plan):
    host_count = lax.axis_size("expert")
    gate_own = w_gate[0]
    down_own = w_down[0]
    outputs = []
    for batch_index, placement in ((0, old_plan), (1, new_plan)):
        activations = tokens[batch_index]
        group_tokens = activations.shape[0]
        capacity = group_tokens * TOPK // host_count
        row_count = group_tokens * TOPK
        target, spare_slot, position = route_rows(
            placement, expert_ids[batch_index], replica_pick[batch_index]
        )
        is_kept = position < capacity
        width_dest = 2 * capacity
        owner_host = jnp.where(spare_slot == 1, jnp.take(placement, target), target)
        destination = jnp.where(
            is_kept, owner_host * width_dest + spare_slot * capacity + position, -1
        )
        slot_count = host_count * width_dest
        slot_ids = jnp.arange(slot_count, dtype=jnp.int32)
        filled_map = destination[None, :] == slot_ids[:, None]
        filled = jnp.any(filled_map, axis=1)
        row_source = jnp.sum(
            jnp.where(filled_map, jnp.arange(row_count, dtype=jnp.int32)[None, :], 0), axis=1
        )
        token_source = row_source // TOPK

        def finish(hidden, item_count):
            expert_out = jnp.dot(hidden, down_own, preferred_element_type=jnp.float32)
            summed = lax.psum_scatter(
                expert_out.astype(jnp.bfloat16), "dp", scatter_dimension=1, tiled=True
            )
            result = summed.reshape(host_count, item_count, -1)
            return lax.all_to_all(result, "expert", split_axis=0, concat_axis=0, tiled=True)

        outgoing = jnp.where(
            filled[:, None], activations[token_source], jnp.zeros((), jnp.bfloat16)
        ).reshape(host_count, width_dest, -1)

        def on_slices(rows_in, finish=finish):
            item_count = rows_in.shape[1]
            flat_rows = rows_in.reshape(host_count * item_count, -1)
            gate_pre = project_rows(lax.all_gather(flat_rows, "dp", axis=1, tiled=True), gate_own)
            hidden = jax.nn.silu(gate_pre).astype(jnp.bfloat16)
            return finish(hidden, item_count)

        returned = on_slices(
            lax.all_to_all(outgoing, "expert", split_axis=0, concat_axis=0, tiled=True)
        )
        flat_back = returned.reshape(slot_count, -1)
        rows_back = flat_back[jnp.where(is_kept, destination, 0)]
        rows_back = jnp.where(is_kept[:, None], rows_back.astype(jnp.float32), 0.0)
        weights_row = route_weight[batch_index].reshape(-1)[:, None]
        combined = jnp.sum((weights_row * rows_back).reshape(group_tokens, TOPK, -1), axis=1)
        outputs.append(combined.astype(jnp.bfloat16))
    return jnp.stack(outputs)


def solution(mesh):
    placed = (
        P(None, "expert", "dp"),
        P("expert", "dp", None),
        P("expert", "dp", None),
        P(None, "expert", None),
        P(None, "expert", None),
        P(None, "expert", None),
        P(),
        P(),
    )
    return jax.shard_map(
        local, mesh=mesh, in_specs=placed, out_specs=P(None, "expert", "dp"), check_vma=False
    )
```

profile of v0, /device:TPU:8, one launch (start us, length us, event | category | flops | bytes accessed | tf_op | source)
XLA Modules:
  0.0 351.7 jit_solution(13884420601945435393)
XLA Ops:
  6.5 0.8 fusion.44
  7.6 0.7 fusion.45
  8.6 0.9 convert_reduce_fusion.2
  9.7 0.8 select_reduce_fusion.4
  10.7 0.6 reduce-window.14
  11.3 0.2 slice_reduce_fusion.1
  11.5 1.9 gather_fusion.4
  13.7 0.2 fusion.11
  13.9 0.8 slice_bitcast_fusion.1
  14.8 2.0 gather_fusion
  16.9 41.2 %all_to_all.20 = bf16[64,8,512]{2,1,0:T(8,128)(2,1)} all-to-all(bf16[64,8,512]{2,1,0:T(8,128)(2,1)S(1)} %bitcast_select_fusion.1), channel_id=1, replica_groups=mesh['dp'=8,'expert'=64] {'expert'}, dimensions={0} | all-to-all | bytes 1048576 | tf_op jit(solution)/shard_map/all_to_all | solution.py:85
  58.7 0.2 convert_reduce_fusion
  59.3 0.6 reduce-window.16
  59.9 0.2 slice_reduce_fusion
  60.2 1.9 gather_fusion.5
  62.2 0.2 fusion.10
  62.6 2.0 gather_fusion.2
  64.8 26.9 %all_to_all.21 = bf16[64,8,512]{2,1,0:T(8,128)(2,1)} all-to-all(bf16[64,8,512]{2,1,0:T(8,128)(2,1)S(1)} %bitcast_select_fusion), channel_id=1, replica_groups=mesh['dp'=8,'expert'=64] {'expert'}, dimensions={0} | all-to-all | bytes 1048576 | tf_op jit(solution)/shard_map/all_to_all | solution.py:85
  91.8 29.0 %all-gather.3.cloned.1.call-done = bf16[512,4096]{1,0:T(8,128)(2,1)} async-done(((bf16[512,512]{1,0:T(8,128)(2,1)}), bf16[512,4096]{1,0:T(8,128)(2,1)}) %all-gather.3.cloned.1.call-update) | async-done | bytes 4194320 | tf_op jit(solution)/shard_map/all_gather | solution.py:80
  120.8 7.5 %convolution_convert_fusion.1 = bf16[512,4096]{1,0:T(8,128)(2,1)} fusion(bf16[1,192,4096]{2,1,0:T(8,128)(2,1)S(1)} %copy-done, bf16[512,4096]{1,0:T(8,128)(2,1)} %all-gather.3.cloned.1.call-done, bf16[1,192,4096]{2,1,0:T(8,128)(2,1)} %param.11), kind=kOutput, calls=%fused_computation.7 | convolution fusion | flops 1613201408 | bytes 11534336 | tf_op jit(solution)/shard_map/dot_general | solution.py:66
  128.4 50.9 %all-gather.5.cloned.1.call-done = bf16[512,4096]{1,0:T(8,128)(2,1)} async-done(((bf16[512,512]{1,0:T(8,128)(2,1)}), bf16[512,4096]{1,0:T(8,128)(2,1)}) %all-gather.5.cloned.1.call-update) | async-done | bytes 4194320 | tf_op jit(solution)/shard_map/all_gather | solution.py:80
  179.3 7.0 %convolution_convert_fusion = bf16[512,4096]{1,0:T(8,128)(2,1)} fusion(bf16[1,192,4096]{2,1,0:T(8,128)(2,1)S(1)} %copy-done, bf16[512,4096]{1,0:T(8,128)(2,1)} %all-gather.5.cloned.1.call-done, bf16[1,192,4096]{2,1,0:T(8,128)(2,1)S(1)} %copy-done.3), kind=kOutput, calls=%fused_computation.6 | convolution fusion | flops 1613201408 | bytes 11534336 | tf_op jit(solution)/shard_map/dot_general | solution.py:66
  186.4 52.8 %reduce-scatter.3.cloned.1.call-done = bf16[512,512]{1,0:T(8,128)(2,1)} async-done(((bf16[512,4096]{1,0:T(8,128)(2,1)}), bf16[512,512]{1,0:T(8,128)(2,1)}) %reduce-scatter.3.cloned.1.call-update) | async-done | bytes 524304 | tf_op jit(solution)/shard_map/reduce_scatter | solution.py:67
  239.2 13.3 %all-to-all-start.1 = ((bf16[64,8,512]{2,1,0:T(8,128)(2,1)}), bf16[64,8,512]{2,1,0:T(8,128)(2,1)S(1)}, u32[]{:S(2)}, u32[]{:S(2)}) async-start(bf16[64,8,512]{2,1,0:T(8,128)(2,1)} %bitcast.105), calls=%async_computation.2 | async-start | bytes 1048576 | tf_op jit(solution)/shard_map/all_to_all | solution.py:71
  252.4 55.6 %reduce-scatter.5.cloned.1.call-done = bf16[512,512]{1,0:T(8,128)(2,1)} async-done(((bf16[512,4096]{1,0:T(8,128)(2,1)}), bf16[512,512]{1,0:T(8,128)(2,1)}) %reduce-scatter.5.cloned.1.call-update) | async-done | bytes 524304 | tf_op jit(solution)/shard_map/reduce_scatter | solution.py:67
  308.0 12.3 %all-to-all-start.3 = ((bf16[64,8,512]{2,1,0:T(8,128)(2,1)}), bf16[64,8,512]{2,1,0:T(8,128)(2,1)S(1)}, u32[]{:S(2)}, u32[]{:S(2)}) async-start(bf16[64,8,512]{2,1,0:T(8,128)(2,1)} %bitcast.104), calls=%async_computation.5 | async-start | bytes 1048576 | tf_op jit(solution)/shard_map/all_to_all | solution.py:71
  320.8 1.2 gather_fusion.1
  321.9 21.0 %all-to-all-done.3 = bf16[64,8,512]{2,1,0:T(8,128)(2,1)S(1)} async-done(((bf16[64,8,512]{2,1,0:T(8,128)(2,1)}), bf16[64,8,512]{2,1,0:T(8,128)(2,1)S(1)}, u32[]{:S(2)}, u32[]{:S(2)}) %all-to-all-start.3) | async-done | bytes 524320 | tf_op jit(solution)/shard_map/all_to_all | solution.py:71
  342.9 1.2 gather_fusion.3
  344.0 0.3 fusion.9
  344.3 0.3 fusion.7
  344.6 0.6 pad_maximum_fusion
  (71 shorter events, 3.6 us)
Async XLA Ops:
  6.5 114.2 %copy-start = (bf16[1,192,4096]{2,1,0:T(8,128)(2,1)S(1)}, bf16[1,192,4096]{2,1,0:T(8,128)(2,1)}, u32[]{:S(2)}) copy-start(bf16[1,192,4096]{2,1,0:T(8,128)(2,1)} %param.12) | copy-start | bytes 4718596
  6.5 114.2 %all-gather.3.cloned.1.call-start = ((), (), s32[]{:S(2)}) async-start(), calls=%async_computation.6 | async-start | bytes 4718592 | tf_op jit(solution)/shard_map/all_gather | solution.py:80
  11.5 47.1 %copy-start.1 = (s32[64]{0:T(128)S(1)}, s32[64]{0:T(128)}, u32[]{:S(2)}) copy-start(s32[64]{0:T(128)} %param.17) | copy-start | bytes 772
  58.1 121.2 %all-gather.5.cloned.1.call-start = ((), (), s32[]{:S(2)}) async-start(), calls=%async_computation.8 | async-start | bytes 4718592 | tf_op jit(solution)/shard_map/all_gather | solution.py:80
  91.7 147.4 %reduce-scatter.3.cloned.1.call-start = ((), (), s32[]{:S(2)}) async-start(), calls=%async_computation.7 | async-start | bytes 4718592 | tf_op jit(solution)/shard_map/reduce_scatter | solution.py:67
  128.3 51.0 %copy-start.3 = (bf16[1,192,4096]{2,1,0:T(8,128)(2,1)S(1)}, bf16[1,192,4096]{2,1,0:T(8,128)(2,1)}, u32[]{:S(2)}) copy-start(bf16[1,192,4096]{2,1,0:T(8,128)(2,1)} %param.11) | copy-start | bytes 4718596
  128.3 179.7 %reduce-scatter.5.cloned.1.call-start = ((), (), s32[]{:S(2)}) async-start(), calls=%async_computation.9 | async-start | bytes 4718592 | tf_op jit(solution)/shard_map/reduce_scatter | solution.py:67
  186.3 134.1 %copy-start.2 = (f32[2,32,8]{1,2,0:T(8,128)S(1)}, f32[2,32,8]{1,2,0:T(8,128)}, u32[]{:S(2)}) copy-start(f32[2,32,8]{1,2,0:T(8,128)} %param.14) | copy-start | bytes 6148
  239.2 68.9 %all-to-all-start.1 = ((bf16[64,8,512]{2,1,0:T(8,128)(2,1)}), bf16[64,8,512]{2,1,0:T(8,128)(2,1)S(1)}, u32[]{:S(2)}, u32[]{:S(2)}) async-start(bf16[64,8,512]{2,1,0:T(8,128)(2,1)} %bitcast.105), calls=%async_computation.2 | async-start | bytes 1048576 | tf_op jit(solution)/shard_map/all_to_all | solution.py:71
  308.0 34.8 %all-to-all-start.3 = ((bf16[64,8,512]{2,1,0:T(8,128)(2,1)}), bf16[64,8,512]{2,1,0:T(8,128)(2,1)S(1)}, u32[]{:S(2)}, u32[]{:S(2)}) async-start(bf16[64,8,512]{2,1,0:T(8,128)(2,1)} %bitcast.104), calls=%async_computation.5 | async-start | bytes 1048576 | tf_op jit(solution)/shard_map/all_to_all | solution.py:71
Sparse Core Ops, SparseCore 0:
  58.2 62.5 all-gather.2
  122.9 56.3 all-gather.4
  182.1 56.9 reduce-scatter.2
  241.9 66.1 reduce-scatter.4
where the time goes:
time: 352 us
  waiting for transfers between devices  209 us (59%)
  blocking collectives  68.1 us (19%)
  starting transfers between devices  25.7 us (7%)
  matrix products  14.6 us (4%)
  local copies, waits for them, and re-layouts  14.3 us (4%)
  between operations  13.4 us (4%)
  other arithmetic  6.36 us (2%)
    reduce_scatter x2, waiting for transfers between devices, finish(): lax.psum_scatter(expert_out.astype(jnp.bfloat16), 'dp', scatter_dimension...  108 us
    all_gather x2, waiting for transfers between devices, on_slices(): lax.all_gather(flat_rows, 'dp', axis=1, tiled=True)  79.9 us
    all_to_all x2, blocking collectives, local(): lax.all_to_all(outgoing, 'expert', split_axis=0, concat_axis=0, tiled=True)  68.1 us
    all_to_all x2, starting transfers between devices, finish(): lax.all_to_all(result, 'expert', split_axis=0, concat_axis=0, tiled=True)  25.6 us
    all_to_all x2, waiting for transfers between devices, finish(): lax.all_to_all(result, 'expert', split_axis=0, concat_axis=0, tiled=True)  21 us
    dot_general x2, matrix products, finish(): expert_out = jnp.dot(hidden, down_own, preferred_element_type=jnp.float32)  14.6 us
  transfers between devices with their start and end apart: 6, of which 5 were waited for; matrix products, arithmetic and copies ran while one was open for 6% of the time, Pallas kernels for 0%

commit v1 on v0

v1 whole, which is shorter than its diff:
```python
import jax
import jax.numpy as jnp
from jax import lax
from jax.sharding import Mesh
from jax.sharding import PartitionSpec as P

TOPK = 8
CAP = 4
BF = jnp.bfloat16
F32 = jnp.float32

SPLIT = (("p", 2), ("m", 2), ("k", 2), ("zh", 2), ("y", 8), ("x", 4))
MK = ("m", "k")


def dot(a, b, dims, out=F32):
    return lax.dot_general(a, b, (dims, ((), ())), preferred_element_type=out)


def swap(array, dm, dk):
    flip = 2 * dm + dk
    return lax.ppermute(array, MK, [(i, i ^ flip) for i in range(4)])


def recut(weight):
    m, k = lax.axis_index("m"), lax.axis_index("k")
    hidden, feats = weight.shape
    blocks = weight.reshape(hidden, 2, 2, 2, feats // 8)

    def part(dm, dk):
        taken = lax.dynamic_slice(
            blocks, (0, 0, m ^ dm, k ^ dk, 0), (hidden, 2, 1, 1, feats // 8)
        ).reshape(hidden, feats // 4)
        return swap(taken, dm, dk) if dm + dk else taken

    def both(dk):
        same, other = part(0, dk), part(1, dk)
        first = jnp.where(m == 0, same, other)
        second = jnp.where(m == 0, other, same)
        return jnp.concatenate([first, second], axis=0)

    return both(0), both(1)


def slots(codes, weights, plan):
    groups, rows = codes.shape
    hosts = plan.shape[0]
    nx = lax.axis_size("x")
    first = (lax.axis_index("zh") * lax.axis_size("y") + lax.axis_index("y")) * nx
    experts = first + jnp.arange(nx, dtype=jnp.int32)
    ids = jnp.arange(hosts, dtype=jnp.int32)
    spare_host = jnp.sum(jnp.where(plan[None, :] == experts[:, None], ids[None, :], 0), axis=1)
    here = jnp.sum(jnp.where(ids[None, :] == experts[:, None], plan[None, :], 0), axis=1)
    own_code = 2 * jnp.concatenate([experts, spare_host])
    spare_code = 2 * jnp.concatenate([here, experts]) + 1
    is_own = codes[:, None, :] == own_code[None, :, None]
    is_spare = codes[:, None, :] == spare_code[None, :, None]
    landed = is_own | is_spare
    at = jnp.arange(rows, dtype=jnp.int32)
    before = (at[:, None] < at[None, :]).astype(BF)
    position = dot(landed.astype(BF), before, ((2,), (0,)))
    fits = position < CAP
    kept = (is_own[:, :nx] & fits[:, :nx]) | (is_spare[:, nx:] & fits[:, nx:])
    rank = dot(kept.astype(BF), before, ((2,), (0,)))
    slot = jnp.arange(2 * CAP, dtype=F32)
    hit = kept[:, :, None, :] & (rank[:, :, None, :] == slot[None, None, :, None])
    token = at // TOPK + 1
    tokens_of = jnp.sum(jnp.where(hit, token[None, None, None, :], 0), axis=3)
    group = jnp.arange(groups, dtype=jnp.int32)[:, None, None]
    tokens_of = jnp.where(tokens_of > 0, tokens_of - 1 + group * (rows // TOPK), -1)
    weight_of = jnp.sum(jnp.where(hit, weights[:, None, None, :], 0.0), axis=3)
    order = lambda v: v.transpose(1, 0, 2).reshape(-1)
    return order(tokens_of), order(weight_of)


def local(tokens, w_gate, w_down, expert_ids, route_weight, replica_pick, old_plan, new_plan):
    batches, group, feats = tokens.shape
    nx = lax.axis_size("x")
    code = (2 * expert_ids + (replica_pick & 1)).astype(F32)
    info = jnp.stack([code, route_weight]).reshape(2, batches, group * TOPK)
    info = lax.all_gather(info, ("y", "zh"))

    cut = lax.all_gather(tokens, ("zh", "p"))
    cut = cut.reshape(2, 2, batches, group, feats).transpose(2, 0, 3, 1, 4)
    cut = cut.reshape(batches, 2 * group, 2 * feats)

    gate_own, gate_other = recut(w_gate[0])
    down_own, down_other = recut(w_down[0])

    outputs = []
    for index, plan in ((0, old_plan), (1, new_plan)):
        tok = lax.all_gather(cut[index], "y", axis=0, tiled=True)
        codes = info[:, 0, index].astype(jnp.int32)
        slot_token, slot_weight = slots(codes, info[:, 1, index], plan)
        pick = slot_token[:, None] == jnp.arange(tok.shape[0], dtype=jnp.int32)[None, :]
        rows = dot(pick.astype(BF), tok, ((1,), (0,)), BF)
        rows = rows.reshape(nx, -1, rows.shape[1])
        rows = lax.all_to_all(rows, "x", 0, 0, tiled=True).reshape(-1, rows.shape[2])

        send = dot(rows, gate_other, ((1,), (1,)), BF)
        part = dot(rows, gate_own, ((1,), (1,)))
        part = part + swap(send, 0, 1).astype(F32)
        gate = part + swap(part.astype(BF), 1, 0).astype(F32)
        hidden = jax.nn.silu(gate).astype(BF)
        hidden_other = swap(hidden, 0, 1)
        out = dot(hidden, down_own, ((1,), (0,))) + dot(hidden_other, down_other, ((1,), (0,)))
        out = out.astype(BF).reshape(nx, -1, out.shape[1])
        back = lax.all_to_all(out, "x", 0, 0, tiled=True).reshape(-1, out.shape[2])

        scale = jnp.where(pick, slot_weight[:, None], 0.0)
        high = scale.astype(BF)
        low = (scale - high.astype(F32)).astype(BF)
        mixed = dot(high, back, ((0,), (0,))) + dot(low, back, ((0,), (0,)))
        outputs.append(lax.psum_scatter(mixed.astype(BF), "y", scatter_dimension=0, tiled=True))

    mixed = jnp.stack(outputs).reshape(batches, 2, group, 2, feats)
    mixed = mixed.transpose(1, 3, 0, 2, 4).reshape(4, batches, group, feats)
    return lax.psum_scatter(mixed, ("zh", "p"), scatter_dimension=0, tiled=False)


def solution(mesh):
    names = tuple(name for name, _ in SPLIT)
    cut = Mesh(mesh.devices.reshape([size for _, size in SPLIT]), names)
    dp, expert = ("p", "m", "k"), ("zh", "y", "x")
    placed = (
        P(None, expert, dp),
        P(expert, dp, None),
        P(expert, dp, None),
        P(None, expert, None),
        P(None, expert, None),
        P(None, expert, None),
        P(),
        P(),
    )
    return jax.shard_map(
        local, mesh=cut, in_specs=placed, out_specs=P(None, expert, dp), check_vma=False
    )
```

time: 352 us -> 339 us (0.963)
  the two profiles are of different devices: /device:TPU:8 before, /device:TPU:2 now
where the time goes in v1:
time: 339 us; the launch traced here: 338 us
  waiting for transfers between devices  122 us (36%)
  blocking collectives  71.8 us (21%)
  starting transfers between devices  51.6 us (15%)
  local copies, waits for them, and re-layouts  36.3 us (11%)
  matrix products  31.9 us (9%)
  between operations  13.9 us (4%)
  other arithmetic  10 us (3%)
    reduce_scatter x2, waiting for transfers between devices, local(): lax.psum_scatter(mixed.astype(BF), 'y', scatter_dimension=0, tiled=True)  54.3 us
    all_gather x1, blocking collectives, local(): info = lax.all_gather(info, ('y', 'zh'))  51.5 us
    dot_general x18, matrix products, dot(): return lax.dot_general(a, b, (dims, ((), ())), preferred_element_type=out)  31.9 us
    ppermute x12, starting transfers between devices, swap(): return lax.ppermute(array, MK, [(i, i ^ flip) for i in range(4)])  31.6 us
    reduce_scatter x1, waiting for transfers between devices, local(): lax.psum_scatter(mixed, ('zh', 'p'), scatter_dimension=0, tiled=False)  28.6 us
    ppermute x12, waiting for transfers between devices, swap(): return lax.ppermute(array, MK, [(i, i ^ flip) for i in range(4)])  25.1 us
    dynamic_slice x1, local copies, waits for them, and re-layouts, part(): lax.dynamic_slice(blocks, (0, 0, m ^ dm, k ^ dk, 0), (hidden, 2, 1, 1, fe...  22.6 us
    all_gather x1, blocking collectives, local(): cut = lax.all_gather(tokens, ('zh', 'p'))  20.3 us
  transfers between devices with their start and end apart: 21, of which 7 were waited for; matrix products, arithmetic and copies ran while one was open for 22% of the time, Pallas kernels for 0%

profile of v1, /device:TPU:2, one launch (start us, length us, event | category | flops | bytes accessed | tf_op | source)
XLA Modules:
  0.0 337.6 jit_solution(14325850655694982789)
XLA Ops:
  6.6 20.3 %all-gather = bf16[8,32,512]{2,1,0:T(8,128)(2,1)S(1)} all-gather(bf16[2,32,512]{2,1,0:T(8,128)(2,1)} %param.8), channel_id=2, replica_groups=mesh['p'=2,'m'=2,'k'=2,'zh'=2,'y'=8,'x'=4] {'zh','p'}, dimensions={0}, use_global_device_ids=true | all-gather | bytes 327680 | tf_op jit(solution)/shard_map/all_gather | solution.py:83
  29.3 51.5 %all_gather.15 = f32[16,2,2,256]{3,2,1,0:T(2,128)S(1)} all-gather(f32[1,2,2,256]{3,2,1,0:T(2,128)S(1)} %pad_maximum_fusion.12), channel_id=1, replica_groups=mesh['p'=2,'m'=2,'k'=2,'zh'=2,'y'=8,'x'=4] {'y','zh'}, dimensions={0}, use_global_device_ids=true | all-gather | bytes 69632 | tf_op jit(solution)/shard_map/all_gather | solution.py:81
  83.3 2.3 select_reduce_fusion.3
  87.7 2.9 reshape_squeeze.7
  90.6 3.0 fusion.3
  93.6 4.8 %all-to-all-start = ((bf16[4,128,1024]{2,1,0:T(8,128)(2,1)}), bf16[4,128,1024]{2,1,0:T(8,128)(2,1)}, u32[]{:S(2)}, u32[]{:S(2)}) async-start(bf16[4,128,1024]{2,1,0:T(8,128)(2,1)} %bitcast.85), calls=%async_computation | async-start | bytes 2097152 | tf_op jit(solution)/shard_map/all_to_all | solution.py:98
  98.4 22.6 %dynamic-slice_reduce_fusion.3 = (bf16[192,2,512]{2,1,0:T(2,128)(2,1)S(1)}, bf16[192,2,512]{2,1,0:T(2,128)(2,1)}, bf16[192,2,512]{2,1,0:T(2,128)(2,1)}, bf16[192...) fusion(bf16[192,2,2,2,512]{4,3,2,1,0:T(2,128)(2,1)S(1)} %reshap, ...), kind=kLoop, calls=%fused_computation.26 | loop fusion | bytes 6291472 | tf_op jit(solution)/shard_map/dynamic_slice | solution.py:31
  125.0 4.1 %collective-permute-start.2 = (bf16[192,1024]{1,0:T(8,128)(2,1)S(1)}, bf16[192,1024]{1,0:T(8,128)(2,1)S(1)}, u32[]{:S(2)}, u32[]{:S(2)}) collective-permute-start(bf16[192,1024]{1,0:T(8,128)(2,1)S(1)} %bitcast.97), channel_id=1, source_target_pairs={{0,192},{64,128},{128,64},{192,0},{1,193},{65,129},{129,65},{193,1... | collective-permute-start | bytes 1179656 | tf_op jit(solution)/shard_map/ppermute | solution.py:22
  131.1 7.4 %collective-permute-done.2 = bf16[192,1024]{1,0:T(8,128)(2,1)S(1)} collective-permute-done((bf16[192,1024]{1,0:T(8,128)(2,1)S(1)}, bf16[192,1024]{1,0:T(8,128)(2,1)S(1)}, u32[]{:S(2)}, u32[]{:S(2)}) %collective-permute-start.2) | collective-permute-done | bytes 393248 | tf_op jit(solution)/shard_map/ppermute | solution.py:22
  138.7 3.0 fusion.27
  141.7 2.3 collective-permute-start.3
  144.1 2.2 collective-permute-start.7
  147.0 3.8 %collective-permute-start.8 = (bf16[192,1024]{1,0:T(8,128)(2,1)}, bf16[192,1024]{1,0:T(8,128)(2,1)}, u32[]{:S(2)}, u32[]{:S(2)}) collective-permute-start(bf16[192,1024]{1,0:T(8,128)(2,1)} %bitcast.40), channel_id=1, source_target_pairs={{0,192},{64,128},{128,64},{192,0},{1,193},{65,129},{129,65},{193,1... | collective-permute-start | bytes 1179656 | tf_op jit(solution)/shard_map/ppermute | solution.py:22
  153.9 3.0 fusion.59
  156.9 3.9 %collective-permute-start.4 = (bf16[512,384]{1,0:T(8,128)(2,1)}, bf16[512,384]{1,0:T(8,128)(2,1)}, u32[]{:S(2)}, u32[]{:S(2)}) collective-permute-start(bf16[512,384]{1,0:T(8,128)(2,1)} %get-tuple-element.47), channel_id=1, source_target_pairs={{0,128},{64,192},{128,0},{192,64},{1,129},{65,193},{129,1},{193,65... | collective-permute-start | bytes 1179656 | tf_op jit(solution)/shard_map/ppermute | solution.py:22
  160.9 3.0 fusion.2
  163.8 4.8 %all-to-all-start.2 = ((bf16[4,128,1024]{2,1,0:T(8,128)(2,1)}), bf16[4,128,1024]{2,1,0:T(8,128)(2,1)S(1)}, u32[]{:S(2)}, u32[]{:S(2)}) async-start(bf16[4,128,1024]{2,1,0:T(8,128)(2,1)} %bitcast.11), calls=%async_computation.3 | async-start | bytes 2097152 | tf_op jit(solution)/shard_map/all_to_all | solution.py:98
  169.8 7.9 %collective-permute-done.4 = bf16[512,384]{1,0:T(8,128)(2,1)} collective-permute-done((bf16[512,384]{1,0:T(8,128)(2,1)}, bf16[512,384]{1,0:T(8,128)(2,1)}, u32[]{:S(2)}, u32[]{:S(2)}) %collective-permute-start.4) | collective-permute-done | bytes 393248 | tf_op jit(solution)/shard_map/ppermute | solution.py:22
  178.9 1.9 collective-permute-start.6
  181.9 2.6 fusion.26
  184.5 2.4 collective-permute-start.9
  190.3 5.3 %all-to-all-start.1 = ((bf16[4,128,1024]{2,1,0:T(8,128)(2,1)}), bf16[4,128,1024]{2,1,0:T(8,128)(2,1)}, u32[]{:S(2)}, u32[]{:S(2)}) async-start(bf16[4,128,1024]{2,1,0:T(8,128)(2,1)} %bitcast.7), calls=%async_computation.1 | async-start | bytes 2097152 | tf_op jit(solution)/shard_map/all_to_all | solution.py:108
  195.7 2.9 fusion.58
  198.6 3.3 collective-permute-start.10
  202.3 9.8 %collective-permute-done.10 = bf16[512,384]{1,0:T(8,128)(2,1)S(1)} collective-permute-done((bf16[512,384]{1,0:T(8,128)(2,1)}, bf16[512,384]{1,0:T(8,128)(2,1)S(1)}, u32[]{:S(2)}, u32[]{:S(2)}) %collective-permute-start.10) | collective-permute-done | bytes 393248 | tf_op jit(solution)/shard_map/ppermute | solution.py:22
  215.4 2.1 fusion.4
  217.5 3.1 add_convert_fusion.2
  223.0 4.9 %all-to-all-start.3 = ((bf16[4,128,1024]{2,1,0:T(8,128)(2,1)}), bf16[4,128,1024]{2,1,0:T(8,128)(2,1)S(1)}, u32[]{:S(2)}, u32[]{:S(2)}) async-start(bf16[4,128,1024]{2,1,0:T(8,128)(2,1)} %bitcast.13), calls=%async_computation.4 | async-start | bytes 2097152 | tf_op jit(solution)/shard_map/all_to_all | solution.py:108
  228.2 14.0 %all-to-all-done.3 = bf16[4,128,1024]{2,1,0:T(8,128)(2,1)S(1)} async-done(((bf16[4,128,1024]{2,1,0:T(8,128)(2,1)}), bf16[4,128,1024]{2,1,0:T(8,128)(2,1)S(1)}, u32[]{:S(2)}, u32[]{:S(2)}) %all-to-all-start.3) | async-done | bytes 1048608 | tf_op jit(solution)/shard_map/all_to_all | solution.py:108
  245.0 12.6 %reduce-scatter.4.cloned.1.call-done = bf16[64,1024]{1,0:T(8,128)(2,1)} async-done(((bf16[512,1024]{1,0:T(8,128)(2,1)}), bf16[64,1024]{1,0:T(8,128)(2,1)}) %reduce-scatter.4.cloned.1.call-update) | async-done | bytes 131088 | tf_op jit(solution)/shard_map/reduce_scatter | solution.py:114
  258.6 41.7 %reduce-scatter.6.cloned.1.call-done = bf16[64,1024]{1,0:T(8,128)(2,1)} async-done(((bf16[512,1024]{1,0:T(8,128)(2,1)}), bf16[64,1024]{1,0:T(8,128)(2,1)}) %reduce-scatter.6.cloned.1.call-update) | async-done | bytes 131088 | tf_op jit(solution)/shard_map/reduce_scatter | solution.py:114
  302.4 28.6 %reduce-scatter.8.cloned.1.call-done = bf16[1,2,32,512]{3,2,1,0:T(8,128)(2,1)} async-done(((bf16[4,2,32,512]{3,2,1,0:T(8,128)(2,1)}), bf16[1,2,32,512]{3,2,1,0:T(8,128)(2,1)}) %reduce-scatter.8.cloned.1.call-update) | async-done | bytes 65552 | tf_op jit(solution)/shard_map/reduce_scatter | solution.py:118
  (146 shorter events, 35.9 us)
Async XLA Ops:
  6.5 22.3 %copy-start.21 = (s32[2,32,8]{1,2,0:T(8,128)S(1)}, s32[2,32,8]{1,2,0:T(8,128)}, u32[]{:S(2)}) copy-start(s32[2,32,8]{1,2,0:T(8,128)} %param.11) | copy-start | bytes 6148
  6.5 22.3 %copy-start.20 = (s32[2,32,8]{1,2,0:T(8,128)S(1)}, s32[2,32,8]{1,2,0:T(8,128)}, u32[]{:S(2)}) copy-start(s32[2,32,8]{1,2,0:T(8,128)} %param.13) | copy-start | bytes 6148
  6.5 22.5 %copy-start.22 = (f32[2,32,8]{1,2,0:T(8,128)S(1)}, f32[2,32,8]{1,2,0:T(8,128)}, u32[]{:S(2)}) copy-start(f32[2,32,8]{1,2,0:T(8,128)} %param.12) | copy-start | bytes 6148
  6.5 74.9 %copy-start.25 = (s32[64]{0:T(128)S(1)}, s32[64]{0:T(128)}, u32[]{:S(2)}) copy-start(s32[64]{0:T(128)} %param.14) | copy-start | bytes 772
  6.5 74.9 %copy-start.26 = (s32[64]{0:T(128)S(1)}, s32[64]{0:T(128)}, u32[]{:S(2)}) copy-start(s32[64]{0:T(128)} %param.15) | copy-start | bytes 772
  6.5 84.0 %all-gather.4.cloned.1.call-start = ((), (), s32[]{:S(2)}) async-start(), calls=%async_computation.7 | async-start | bytes 1179648 | tf_op jit(solution)/shard_map/all_gather | solution.py:92
  28.1 58.4 %copy-start.5 = (bf16[1,192,4096]{2,1,0:T(8,128)(2,1)S(1)}, bf16[1,192,4096]{2,1,0:T(8,128)(2,1)}, u32[]{:S(2)}) copy-start(bf16[1,192,4096]{2,1,0:T(8,128)(2,1)} %param.9) | copy-start | bytes 4718596
  28.1 132.8 %all-gather.6.cloned.1.call-start = ((), (), s32[]{:S(2)}) async-start(), calls=%async_computation.9 | async-start | bytes 1179648 | tf_op jit(solution)/shard_map/all_gather | solution.py:92
  93.6 45.1 %all-to-all-start = ((bf16[4,128,1024]{2,1,0:T(8,128)(2,1)}), bf16[4,128,1024]{2,1,0:T(8,128)(2,1)}, u32[]{:S(2)}, u32[]{:S(2)}) async-start(bf16[4,128,1024]{2,1,0:T(8,128)(2,1)} %bitcast.85), calls=%async_computation | async-start | bytes 2097152 | tf_op jit(solution)/shard_map/all_to_all | solution.py:98
  120.9 8.2 %copy-start.4 = (bf16[192,2,512]{2,1,0:T(2,128)(2,1)S(1)}, bf16[192,2,512]{2,1,0:T(2,128)(2,1)}, u32[]{:S(2)}) copy-start(bf16[192,2,512]{2,1,0:T(2,128)(2,1)} %get-tuple-element.54) | copy-start | bytes 1179652
  122.0 9.1 %collective-permute-start.1 = (bf16[192,1024]{1,0:T(8,128)(2,1)S(1)}, bf16[192,1024]{1,0:T(8,128)(2,1)S(1)}, u32[]{:S(2)}, u32[]{:S(2)}) collective-permute-start(bf16[192,1024]{1,0:T(8,128)(2,1)S(1)} %bitcast.96), channel_id=1, source_target_pairs={{0,64},{64,0},{128,192},{192,128},{1,65},{65,1},{129,193},{193,129... | collective-permute-start | bytes 1179656 | tf_op jit(solution)/shard_map/ppermute | solution.py:22
  125.0 13.5 %collective-permute-start.2 = (bf16[192,1024]{1,0:T(8,128)(2,1)S(1)}, bf16[192,1024]{1,0:T(8,128)(2,1)S(1)}, u32[]{:S(2)}, u32[]{:S(2)}) collective-permute-start(bf16[192,1024]{1,0:T(8,128)(2,1)S(1)} %bitcast.97), channel_id=1, source_target_pairs={{0,192},{64,128},{128,64},{192,0},{1,193},{65,129},{129,65},{193,1... | collective-permute-start | bytes 1179656 | tf_op jit(solution)/shard_map/ppermute | solution.py:22
  129.2 24.6 %collective-permute-start = (bf16[192,1024]{1,0:T(8,128)(2,1)S(1)}, bf16[192,1024]{1,0:T(8,128)(2,1)S(1)}, u32[]{:S(2)}, u32[]{:S(2)}) collective-permute-start(bf16[192,1024]{1,0:T(8,128)(2,1)S(1)} %bitcast.95), channel_id=1, source_target_pairs={{0,128},{64,192},{128,0},{192,64},{1,129},{65,193},{129,1},{193,65... | collective-permute-start | bytes 1179656 | tf_op jit(solution)/shard_map/ppermute | solution.py:22
  138.7 7.6 %copy-start.2 = (bf16[192,2,512]{2,1,0:T(2,128)(2,1)S(1)}, bf16[192,2,512]{2,1,0:T(2,128)(2,1)}, u32[]{:S(2)}) copy-start(bf16[192,2,512]{2,1,0:T(2,128)(2,1)} %get-tuple-element.8) | copy-start | bytes 1179652
  141.7 9.2 %copy-start.1 = (bf16[192,2,512]{2,1,0:T(2,128)(2,1)S(1)}, bf16[192,2,512]{2,1,0:T(2,128)(2,1)}, u32[]{:S(2)}) copy-start(bf16[192,2,512]{2,1,0:T(2,128)(2,1)} %get-tuple-element.7) | copy-start | bytes 1179652
  141.7 11.9 %copy-start = (bf16[192,2,512]{2,1,0:T(2,128)(2,1)S(1)}, bf16[192,2,512]{2,1,0:T(2,128)(2,1)}, u32[]{:S(2)}) copy-start(bf16[192,2,512]{2,1,0:T(2,128)(2,1)} %get-tuple-element.56) | copy-start | bytes 1179652
  141.7 12.2 %collective-permute-start.3 = (bf16[512,384]{1,0:T(8,128)(2,1)}, bf16[512,384]{1,0:T(8,128)(2,1)S(1)}, u32[]{:S(2)}, u32[]{:S(2)}) collective-permute-start(bf16[512,384]{1,0:T(8,128)(2,1)} %fusion.27), channel_id=1, source_target_pairs={{0,64},{64,0},{128,192},{192,128},{1,65},{65,1},{129,193},{193,129... | collective-permute-start | bytes 1179656 | tf_op jit(solution)/shard_map/ppermute | solution.py:22
  144.1 24.6 %collective-permute-start.7 = (bf16[192,1024]{1,0:T(8,128)(2,1)S(1)}, bf16[192,1024]{1,0:T(8,128)(2,1)}, u32[]{:S(2)}, u32[]{:S(2)}) collective-permute-start(bf16[192,1024]{1,0:T(8,128)(2,1)S(1)} %bitcast.94), channel_id=1, source_target_pairs={{0,64},{64,0},{128,192},{192,128},{1,65},{65,1},{129,193},{193,129... | collective-permute-start | bytes 1179656 | tf_op jit(solution)/shard_map/ppermute | solution.py:22
  147.0 21.6 %collective-permute-start.8 = (bf16[192,1024]{1,0:T(8,128)(2,1)}, bf16[192,1024]{1,0:T(8,128)(2,1)}, u32[]{:S(2)}, u32[]{:S(2)}) collective-permute-start(bf16[192,1024]{1,0:T(8,128)(2,1)} %bitcast.40), channel_id=1, source_target_pairs={{0,192},{64,128},{128,64},{192,0},{1,193},{65,129},{129,65},{193,1... | collective-permute-start | bytes 1179656 | tf_op jit(solution)/shard_map/ppermute | solution.py:22
  151.7 29.2 %collective-permute-start.5 = (bf16[192,1024]{1,0:T(8,128)(2,1)}, bf16[192,1024]{1,0:T(8,128)(2,1)}, u32[]{:S(2)}, u32[]{:S(2)}) collective-permute-start(bf16[192,1024]{1,0:T(8,128)(2,1)} %bitcast.36), channel_id=1, source_target_pairs={{0,128},{64,192},{128,0},{192,64},{1,129},{65,193},{129,1},{193,65... | collective-permute-start | bytes 1179656 | tf_op jit(solution)/shard_map/ppermute | solution.py:22
  156.9 20.8 %collective-permute-start.4 = (bf16[512,384]{1,0:T(8,128)(2,1)}, bf16[512,384]{1,0:T(8,128)(2,1)}, u32[]{:S(2)}, u32[]{:S(2)}) collective-permute-start(bf16[512,384]{1,0:T(8,128)(2,1)} %get-tuple-element.47), channel_id=1, source_target_pairs={{0,128},{64,192},{128,0},{192,64},{1,129},{65,193},{129,1},{193,65... | collective-permute-start | bytes 1179656 | tf_op jit(solution)/shard_map/ppermute | solution.py:22
  163.8 18.1 %all-to-all-start.2 = ((bf16[4,128,1024]{2,1,0:T(8,128)(2,1)}), bf16[4,128,1024]{2,1,0:T(8,128)(2,1)S(1)}, u32[]{:S(2)}, u32[]{:S(2)}) async-start(bf16[4,128,1024]{2,1,0:T(8,128)(2,1)} %bitcast.11), calls=%async_computation.3 | async-start | bytes 2097152 | tf_op jit(solution)/shard_map/all_to_all | solution.py:98
  178.9 8.0 %collective-permute-start.6 = (bf16[512,384]{1,0:T(8,128)(2,1)S(1)}, bf16[512,384]{1,0:T(8,128)(2,1)}, u32[]{:S(2)}, u32[]{:S(2)}) collective-permute-start(bf16[512,384]{1,0:T(8,128)(2,1)S(1)} %multiply_convert_fusion.1), channel_id=1, source_target_pairs={{0,64},{64,0},{128,192},{192,128},{1,65},{65,1},{129,193},{193,129... | collective-permute-start | bytes 1179656 | tf_op jit(solution)/shard_map/ppermute | solution.py:22
  184.5 11.2 %collective-permute-start.9 = (bf16[512,384]{1,0:T(8,128)(2,1)}, bf16[512,384]{1,0:T(8,128)(2,1)}, u32[]{:S(2)}, u32[]{:S(2)}) collective-permute-start(bf16[512,384]{1,0:T(8,128)(2,1)} %fusion.26), channel_id=1, source_target_pairs={{0,64},{64,0},{128,192},{192,128},{1,65},{65,1},{129,193},{193,129... | collective-permute-start | bytes 1179656 | tf_op jit(solution)/shard_map/ppermute | solution.py:22
  190.3 25.0 %all-to-all-start.1 = ((bf16[4,128,1024]{2,1,0:T(8,128)(2,1)}), bf16[4,128,1024]{2,1,0:T(8,128)(2,1)}, u32[]{:S(2)}, u32[]{:S(2)}) async-start(bf16[4,128,1024]{2,1,0:T(8,128)(2,1)} %bitcast.7), calls=%async_computation.1 | async-start | bytes 2097152 | tf_op jit(solution)/shard_map/all_to_all | solution.py:108
  195.6 62.0 %reduce-scatter.4.cloned.1.call-start = ((), (), s32[]{:S(2)}) async-start(), calls=%async_computation.8 | async-start | bytes 1179648 | tf_op jit(solution)/shard_map/reduce_scatter | solution.py:114
  198.6 16.8 %copy-start.24 = (s32[512]{0:T(512)S(1)}, s32[512]{0:T(512)}, u32[]{:S(2)}) copy-start(s32[512]{0:T(512)} %copy-done.23) | copy-start | bytes 6148
  198.6 13.5 %collective-permute-start.10 = (bf16[512,384]{1,0:T(8,128)(2,1)}, bf16[512,384]{1,0:T(8,128)(2,1)S(1)}, u32[]{:S(2)}, u32[]{:S(2)}) collective-permute-start(bf16[512,384]{1,0:T(8,128)(2,1)} %get-tuple-element.45), channel_id=1, source_target_pairs={{0,128},{64,192},{128,0},{192,64},{1,129},{65,193},{129,1},{193,65... | collective-permute-start | bytes 1179656 | tf_op jit(solution)/shard_map/ppermute | solution.py:22
  213.4 7.1 %collective-permute-start.11 = (bf16[512,384]{1,0:T(8,128)(2,1)S(1)}, bf16[512,384]{1,0:T(8,128)(2,1)S(1)}, u32[]{:S(2)}, u32[]{:S(2)}) collective-permute-start(bf16[512,384]{1,0:T(8,128)(2,1)S(1)} %multiply_convert_fusion), channel_id=1, source_target_pairs={{0,64},{64,0},{128,192},{192,128},{1,65},{65,1},{129,193},{193,129... | collective-permute-start | bytes 1179656 | tf_op jit(solution)/shard_map/ppermute | solution.py:22
  223.0 19.2 %all-to-all-start.3 = ((bf16[4,128,1024]{2,1,0:T(8,128)(2,1)}), bf16[4,128,1024]{2,1,0:T(8,128)(2,1)S(1)}, u32[]{:S(2)}, u32[]{:S(2)}) async-start(bf16[4,128,1024]{2,1,0:T(8,128)(2,1)} %bitcast.13), calls=%async_computation.4 | async-start | bytes 2097152 | tf_op jit(solution)/shard_map/all_to_all | solution.py:108
  227.9 72.4 %reduce-scatter.6.cloned.1.call-start = ((), (), s32[]{:S(2)}) async-start(), calls=%async_computation.10 | async-start | bytes 1179648 | tf_op jit(solution)/shard_map/reduce_scatter | solution.py:114
  245.0 86.1 %reduce-scatter.8.cloned.1.call-start = ((), (), s32[]{:S(2)}) async-start(), calls=%async_computation.11 | async-start | bytes 327680 | tf_op jit(solution)/shard_map/reduce_scatter | solution.py:118
  (16 other events, 70.4 us)
Sparse Core Ops, SparseCore 0:
  28.2 40.6 all-gather.3
  71.0 39.9 all-gather.5
  220.7 36.9 reduce-scatter.3
  260.3 39.9 reduce-scatter.5
  303.0 28.0 reduce-scatter.7

commit v2 on v1

v2 whole, which is shorter than its diff:
```python
import jax
import jax.numpy as jnp
from jax import lax
from jax.sharding import Mesh
from jax.sharding import PartitionSpec as P

TOPK = 8
CAP = 4
BF = jnp.bfloat16
F32 = jnp.float32

SPLIT = (("p", 2), ("m", 2), ("k", 2), ("zh", 2), ("y", 8), ("x", 4))


def dot(a, b, dims, out=F32):
    return lax.dot_general(a, b, (dims, ((), ())), preferred_element_type=out)


def swap(array, *axes):
    last = 2 ** len(axes) - 1
    return lax.ppermute(array, axes, [(i, last - i) for i in range(last + 1)])


def recut(weight):
    hidden, feats = weight.shape
    k = lax.axis_index("k")
    blocks = weight.reshape(hidden, 2, 2, 2, feats // 8).transpose(3, 2, 0, 1, 4)
    blocks = blocks.reshape(4, hidden, feats // 4)
    blocks = lax.all_to_all(blocks, ("k", "m"), 0, 0, tiled=True)
    blocks = blocks.reshape(2, 2 * hidden, feats // 4)
    own = lax.dynamic_index_in_dim(blocks, k, 0, keepdims=False)
    other = lax.dynamic_index_in_dim(blocks, 1 - k, 0, keepdims=False)
    return own, other


def slots(codes, weights, plan):
    groups, rows = codes.shape
    hosts = plan.shape[0]
    count = hosts // lax.axis_size("zh")
    experts = lax.axis_index("zh") * count + jnp.arange(count, dtype=jnp.int32)
    ids = jnp.arange(hosts, dtype=jnp.int32)
    spare_host = jnp.sum(jnp.where(plan[None, :] == experts[:, None], ids[None, :], 0), axis=1)
    here = jnp.sum(jnp.where(ids[None, :] == experts[:, None], plan[None, :], 0), axis=1)
    own_code = 2 * jnp.concatenate([experts, spare_host])
    spare_code = 2 * jnp.concatenate([here, experts]) + 1
    is_own = codes[:, None, :] == own_code[None, :, None]
    is_spare = codes[:, None, :] == spare_code[None, :, None]
    landed = is_own | is_spare
    at = jnp.arange(rows, dtype=jnp.int32)
    before = (at[:, None] < at[None, :]).astype(BF)
    position = dot(landed.astype(BF), before, ((2,), (0,)))
    fits = position < CAP
    kept = (is_own[:, :count] & fits[:, :count]) | (is_spare[:, count:] & fits[:, count:])
    rank = dot(kept.astype(BF), before, ((2,), (0,)))
    slot = jnp.arange(2 * CAP, dtype=F32)
    hit = kept[:, :, None, :] & (rank[:, :, None, :] == slot[None, None, :, None])
    token = at // TOPK + 1
    tokens_of = jnp.sum(jnp.where(hit, token[None, None, None, :], 0), axis=3)
    group = jnp.arange(groups, dtype=jnp.int32)[:, None, None]
    tokens_of = jnp.where(tokens_of > 0, tokens_of - 1 + group * (rows // TOPK), -1)
    weight_of = jnp.sum(jnp.where(hit, weights[:, None, None, :], 0.0), axis=3)
    order = lambda v: v.transpose(1, 0, 2).reshape(-1)
    return order(tokens_of), order(weight_of)


def both(first, second, axis_name, axis):
    at = lax.axis_index(axis_name)
    return jnp.stack([jnp.where(at == 0, first, second), jnp.where(at == 0, second, first)], axis)


def local(tokens, w_gate, w_down, expert_ids, route_weight, replica_pick, old_plan, new_plan):
    batches, group, feats = tokens.shape
    peers = lax.axis_size("y") * lax.axis_size("x")
    zh, p = lax.axis_index("zh"), lax.axis_index("p")
    code = (2 * expert_ids + (replica_pick & 1)).astype(F32)
    info = jnp.stack([code, route_weight]).reshape(2, batches, group * TOPK)
    info = both(info, swap(info, "zh"), "zh", 2)

    near = both(tokens, swap(tokens, "p"), "p", 2)
    far = both(swap(tokens, "zh"), swap(tokens, "p", "zh"), "p", 2)
    tok = both(near, far, "zh", 1).reshape(batches, 2 * group, 2 * feats)

    gate_own, gate_other = recut(w_gate[0])
    down_own, down_other = recut(w_down[0])

    outputs = []
    for index, plan in ((0, old_plan), (1, new_plan)):
        codes = info[0, index].astype(jnp.int32)
        slot_token, slot_weight = slots(codes, info[1, index], plan)
        pick = slot_token[:, None] == jnp.arange(2 * group, dtype=jnp.int32)[None, :]
        rows = dot(pick.astype(BF), tok[index], ((1,), (0,)), BF)
        rows = rows.reshape(peers, -1, rows.shape[1])
        rows = lax.all_to_all(rows, ("y", "x"), 0, 0, tiled=True).reshape(-1, rows.shape[2])

        send = dot(rows, gate_other, ((1,), (1,)), BF)
        part = dot(rows, gate_own, ((1,), (1,)))
        part = part + swap(send, "k").astype(F32)
        gate = part + swap(part.astype(BF), "m").astype(F32)
        hidden = jax.nn.silu(gate).astype(BF)
        hidden_other = swap(hidden, "k")
        out = dot(hidden, down_own, ((1,), (0,))) + dot(hidden_other, down_other, ((1,), (0,)))
        out = out.astype(BF).reshape(peers, -1, out.shape[1])
        back = lax.all_to_all(out, ("y", "x"), 0, 0, tiled=True).reshape(-1, out.shape[2])

        scale = jnp.where(pick, slot_weight[:, None], 0.0)
        high = scale.astype(BF)
        low = (scale - high.astype(F32)).astype(BF)
        mixed = dot(high, back, ((0,), (0,))) + dot(low, back, ((0,), (0,)))
        mixed = mixed.reshape(2, group, 2, feats)

        def block(other_zh, other_p):
            start = (zh ^ other_zh, 0, p ^ other_p, 0)
            return lax.dynamic_slice(mixed, start, (1, group, 1, feats)).reshape(group, feats)

        total = block(0, 0)
        total = total + swap(block(0, 1).astype(BF), "p").astype(F32)
        total = total + swap(block(1, 0).astype(BF), "zh").astype(F32)
        total = total + swap(block(1, 1).astype(BF), "p", "zh").astype(F32)
        outputs.append(total.astype(BF))
    return jnp.stack(outputs)


def solution(mesh):
    names = tuple(name for name, _ in SPLIT)
    cut = Mesh(mesh.devices.reshape([size for _, size in SPLIT]), names)
    dp, expert = ("p", "m", "k"), ("zh", "y", "x")
    placed = (
        P(None, expert, dp),
        P(expert, dp, None),
        P(expert, dp, None),
        P(None, expert, None),
        P(None, expert, None),
        P(None, expert, None),
        P(),
        P(),
    )
    return jax.shard_map(
        local, mesh=cut, in_specs=placed, out_specs=P(None, expert, dp), check_vma=False
    )
```

time: 339 us -> 255 us (0.75)
  blocking collectives: 71.8 us -> 0 us
  starting transfers between devices: 51.6 us -> 97.4 us
  local copies, waits for them, and re-layouts: 36.3 us -> 14.5 us
  between operations: 13.9 us -> 0.69 us
  matrix products: 31.9 us -> 20.5 us
  waiting for transfers between devices: 122 us -> 115 us
  other arithmetic: 10 us -> 5.99 us
    reduce_scatter x3 -> x0, waiting for transfers between devices: 82.9 us -> none  [the longest x2 54.3 us: local(): lax.psum_scatter(mixed.astype(BF), 'y', scatter_dimension=0, tiled=True)]
    all_gather x2 -> x0, blocking collectives: 71.8 us -> none  [the longest x1 51.5 us: local(): info = lax.all_gather(info, ('y', 'zh'))]
    all_to_all x4 -> x6, waiting for transfers between devices: 14 us -> 79.1 us  [the longest x2 44 us: local(): lax.all_to_all(rows, ('y', 'x'), 0, 0, tiled=True)]
    ppermute x12 -> x16, starting transfers between devices: 31.6 us -> 62.5 us  [swap(): return lax.ppermute(array, axes, [(i, last - i) for i in range(last + 1)])]
    dynamic_slice x1 -> x4, local copies, waits for them, and re-layouts: 22.6 us -> 0.51 us  [block(): lax.dynamic_slice(mixed, start, (1, group, 1, feats)).reshape(group, feats)]
    all_to_all x4 -> x6, starting transfers between devices: 19.8 us -> 34.9 us  [the longest x2 15.9 us: local(): lax.all_to_all(rows, ('y', 'x'), 0, 0, tiled=True)]
    dot_general x18, matrix products: 31.9 us -> 20.5 us  [dot(): return lax.dot_general(a, b, (dims, ((), ())), preferred_element_type=out)]
    ppermute x12 -> x16, waiting for transfers between devices: 25.1 us -> 35.6 us  [swap(): return lax.ppermute(array, axes, [(i, last - i) for i in range(last + 1)])]
  transfers between devices with their start and end apart: 21 -> 22, of which waited for: 7 -> 12; matrix products, arithmetic and copies ran while one was open for 22% -> 15% of each run, Pallas kernels for 0% -> 0%
where the time goes in v2:
time: 255 us; the launch traced here: 254 us
  waiting for transfers between devices  115 us (45%)
  starting transfers between devices  97.4 us (38%)
  matrix products  20.5 us (8%)
  local copies, waits for them, and re-layouts  14.5 us (6%)
  other arithmetic  5.99 us (2%)
    ppermute x16, starting transfers between devices, swap(): return lax.ppermute(array, axes, [(i, last - i) for i in range(last + 1)])  62.5 us
    all_to_all x2, waiting for transfers between devices, local(): lax.all_to_all(rows, ('y', 'x'), 0, 0, tiled=True)  44 us
    ppermute x16, waiting for transfers between devices, swap(): return lax.ppermute(array, axes, [(i, last - i) for i in range(last + 1)])  35.6 us
    dot_general x18, matrix products, dot(): return lax.dot_general(a, b, (dims, ((), ())), preferred_element_type=out)  20.5 us
    all_to_all x2, waiting for transfers between devices, local(): lax.all_to_all(out, ('y', 'x'), 0, 0, tiled=True).reshape(-1, out.shape[2])  19.7 us
    all_to_all x2, starting transfers between devices, local(): lax.all_to_all(rows, ('y', 'x'), 0, 0, tiled=True)  15.9 us
    all_to_all x2, waiting for transfers between devices, recut(): blocks = lax.all_to_all(blocks, ('k', 'm'), 0, 0, tiled=True)  15.4 us
    all_to_all x2, starting transfers between devices, local(): lax.all_to_all(out, ('y', 'x'), 0, 0, tiled=True).reshape(-1, out.shape[2])  11.1 us
  transfers between devices with their start and end apart: 22, of which 12 were waited for; matrix products, arithmetic and copies ran while one was open for 15% of the time, Pallas kernels for 0%

profile of v2, /device:TPU:2, one launch (start us, length us, event | category | flops | bytes accessed | tf_op | source)
XLA Modules:
  0.0 253.8 jit_solution(6285490738569533533)
XLA Ops:
  0.0 6.2 %collective-permute-start.1 = (bf16[2,32,512]{2,1,0:T(8,128)(2,1)}, bf16[2,32,512]{2,1,0:T(8,128)(2,1)S(1)}, u32[]{:S(2)}, u32[]{:S(2)}) collective-permute-start(bf16[2,32,512]{2,1,0:T(8,128)(2,1)} %param.8), channel_id=1, source_target_pairs={{0,256},{256,0},{1,257},{257,1},{2,258},{258,2},{3,259},{259,3},{4... | collective-permute-start | bytes 196616 | tf_op jit(solution)/shard_map/ppermute | solution.py:21
  6.2 7.3 %collective-permute-start.3 = (bf16[2,32,512]{2,1,0:T(8,128)(2,1)}, bf16[2,32,512]{2,1,0:T(8,128)(2,1)S(1)}, u32[]{:S(2)}, u32[]{:S(2)}) collective-permute-start(bf16[2,32,512]{2,1,0:T(8,128)(2,1)} %param.8), channel_id=1, source_target_pairs={{0,288},{32,256},{256,32},{288,0},{1,289},{33,257},{257,33},{289,1... | collective-permute-start | bytes 196616 | tf_op jit(solution)/shard_map/ppermute | solution.py:21
  13.5 3.7 %collective-permute-start.2 = (bf16[2,32,512]{2,1,0:T(8,128)(2,1)}, bf16[2,32,512]{2,1,0:T(8,128)(2,1)S(1)}, u32[]{:S(2)}, u32[]{:S(2)}) collective-permute-start(bf16[2,32,512]{2,1,0:T(8,128)(2,1)} %param.8), channel_id=1, source_target_pairs={{0,32},{32,0},{1,33},{33,1},{2,34},{34,2},{3,35},{35,3},{4,36},{36... | collective-permute-start | bytes 196616 | tf_op jit(solution)/shard_map/ppermute | solution.py:21
  19.1 6.0 %collective-permute-start = (f32[2,2,256]{2,1,0:T(2,128)S(1)}, f32[2,2,256]{2,1,0:T(2,128)S(1)}, u32[]{:S(2)}, u32[]{:S(2)}) collective-permute-start(f32[2,2,256]{2,1,0:T(2,128)S(1)} %constant_dynamic-update-slice_fusion), channel_id=1, source_target_pairs={{0,32},{32,0},{1,33},{33,1},{2,34},{34,2},{3,35},{35,3},{4,36},{36... | collective-permute-start | bytes 12296 | tf_op jit(solution)/shard_map/ppermute | solution.py:21
  26.1 2.4 collective-permute-done
  33.9 10.2 %all-to-all-start.4 = ((bf16[32,16,1024]{2,1,0:T(8,128)(2,1)}), bf16[32,16,1024]{2,1,0:T(8,128)(2,1)S(1)}, u32[]{:S(2)}, u32[]{:S(2)}) async-start(bf16[32,16,1024]{2,1,0:T(8,128)(2,1)} %fusion.41), calls=%async_computation.4 | async-start | bytes 2097152 | tf_op jit(solution)/shard_map/all_to_all | solution.py:93
  46.0 24.5 %all-to-all-done.4 = bf16[32,16,1024]{2,1,0:T(8,128)(2,1)S(1)} async-done(((bf16[32,16,1024]{2,1,0:T(8,128)(2,1)}), bf16[32,16,1024]{2,1,0:T(8,128)(2,1)S(1)}, u32[]{:S(2)}, u32[]{:S(2)}) %all-to-all-start.4) | async-done | bytes 1048608 | tf_op jit(solution)/shard_map/all_to_all | solution.py:93
  70.5 5.6 %all-to-all-start = ((bf16[32,16,1024]{2,1,0:T(8,128)(2,1)}), bf16[32,16,1024]{2,1,0:T(8,128)(2,1)}, u32[]{:S(2)}, u32[]{:S(2)}) async-start(bf16[32,16,1024]{2,1,0:T(8,128)(2,1)} %fusion.38), calls=%async_computation | async-start | bytes 2097152 | tf_op jit(solution)/shard_map/all_to_all | solution.py:93
  76.2 2.9 %reshape_squeeze.6 = bf16[192,2,2,2,512]{4,3,2,1,0:T(2,128)(2,1)S(1)} reshape(bf16[1,192,4096]{2,1,0:T(8,128)(2,1)} %param.9) | data formatting | bytes 3145728 | tf_op jit(solution)/shard_map/reshape;squeeze | solution.py:27
  80.3 2.4 reshape.333
  82.6 19.5 %all-to-all-done = bf16[32,16,1024]{2,1,0:T(8,128)(2,1)} async-done(((bf16[32,16,1024]{2,1,0:T(8,128)(2,1)}), bf16[32,16,1024]{2,1,0:T(8,128)(2,1)}, u32[]{:S(2)}, u32[]{:S(2)}) %all-to-all-start) | async-done | bytes 1048608 | tf_op jit(solution)/shard_map/all_to_all | solution.py:93
  102.1 4.3 %all-to-all-start.1 = ((bf16[4,192,1024]{2,1,0:T(8,128)(2,1)}), bf16[4,192,1024]{2,1,0:T(8,128)(2,1)}, u32[]{:S(2)}, u32[]{:S(2)}) async-start(bf16[4,192,1024]{2,1,0:T(8,128)(2,1)} %reshape.333), calls=%async_computation.1 | async-start | bytes 3145728 | tf_op jit(solution)/shard_map/all_to_all | solution.py:29
  111.3 15.4 %all-to-all-done.1 = bf16[4,192,1024]{2,1,0:T(8,128)(2,1)} async-done(((bf16[4,192,1024]{2,1,0:T(8,128)(2,1)}), bf16[4,192,1024]{2,1,0:T(8,128)(2,1)}, u32[]{:S(2)}, u32[]{:S(2)}) %all-to-all-start.1) | async-done | bytes 1572896 | tf_op jit(solution)/shard_map/all_to_all | solution.py:29
  126.6 3.6 %all-to-all-start.2 = ((bf16[4,192,1024]{2,1,0:T(8,128)(2,1)}), bf16[4,192,1024]{2,1,0:T(8,128)(2,1)S(1)}, u32[]{:S(2)}, u32[]{:S(2)}) async-start(bf16[4,192,1024]{2,1,0:T(8,128)(2,1)} %reshape.335), calls=%async_computation.2 | async-start | bytes 3145728 | tf_op jit(solution)/shard_map/all_to_all | solution.py:29
  130.2 2.6 %fusion.6 = bf16[512,384]{1,0:T(8,128)(2,1)} fusion(bf16[512,1024]{1,0:T(8,128)(2,1)S(1)} %bitcast.152, bf16[2,384,1024]{2,1,0:T(8,128)(2,1)} %bitcast.13, s32[]{:T(128)S(6)} %select_n.172), kind=kOutput, calls=%fused_computation.14 | convolution fusion | flops 402653184 | bytes 2228228 | tf_op jit(solution)/shard_map/dot_general | solution.py:16
  132.8 2.3 collective-permute-start.10
  138.6 3.8 %collective-permute-start.11 = (bf16[512,384]{1,0:T(8,128)(2,1)S(1)}, bf16[512,384]{1,0:T(8,128)(2,1)S(1)}, u32[]{:S(2)}, u32[]{:S(2)}) collective-permute-start(bf16[512,384]{1,0:T(8,128)(2,1)S(1)} %get-tuple-element.43), channel_id=1, source_target_pairs={{0,128},{128,0},{1,129},{129,1},{2,130},{130,2},{3,131},{131,3},{4... | collective-permute-start | bytes 1179656 | tf_op jit(solution)/shard_map/ppermute | solution.py:21
  142.4 16.3 %collective-permute-done.11 = bf16[512,384]{1,0:T(8,128)(2,1)S(1)} collective-permute-done((bf16[512,384]{1,0:T(8,128)(2,1)S(1)}, bf16[512,384]{1,0:T(8,128)(2,1)S(1)}, u32[]{:S(2)}, u32[]{:S(2)}) %collective-permute-start.11) | collective-permute-done | bytes 393248 | tf_op jit(solution)/shard_map/ppermute | solution.py:21
  160.8 2.9 %fusion.8 = bf16[512,384]{1,0:T(8,128)(2,1)} fusion(bf16[512,1024]{1,0:T(8,128)(2,1)} %bitcast.11, bf16[2,384,1024]{2,1,0:T(8,128)(2,1)} %bitcast.13, s32[]{:T(128)S(6)} %select_n.172), kind=kOutput, calls=%fused_computation.16 | convolution fusion | flops 402653184 | bytes 2228228 | tf_op jit(solution)/shard_map/dot_general | solution.py:16
  163.8 2.6 %collective-permute-start.4 = (bf16[512,384]{1,0:T(8,128)(2,1)}, bf16[512,384]{1,0:T(8,128)(2,1)S(1)}, u32[]{:S(2)}, u32[]{:S(2)}) collective-permute-start(bf16[512,384]{1,0:T(8,128)(2,1)} %fusion.8), channel_id=1, source_target_pairs={{0,64},{64,0},{1,65},{65,1},{2,66},{66,2},{3,67},{67,3},{4,68},{68... | collective-permute-start | bytes 1179656 | tf_op jit(solution)/shard_map/ppermute | solution.py:21
  168.8 5.6 %all-to-all-start.5 = ((bf16[32,16,1024]{2,1,0:T(8,128)(2,1)}), bf16[32,16,1024]{2,1,0:T(8,128)(2,1)S(1)}, u32[]{:S(2)}, u32[]{:S(2)}) async-start(bf16[32,16,1024]{2,1,0:T(8,128)(2,1)} %bitcast.151), calls=%async_computation.5 | async-start | bytes 2097152 | tf_op jit(solution)/shard_map/all_to_all | solution.py:103
  178.9 10.1 %collective-permute-done.5 = bf16[512,384]{1,0:T(8,128)(2,1)S(1)} collective-permute-done((bf16[512,384]{1,0:T(8,128)(2,1)S(1)}, bf16[512,384]{1,0:T(8,128)(2,1)S(1)}, u32[]{:S(2)}, u32[]{:S(2)}) %collective-permute-start.5) | collective-permute-done | bytes 393248 | tf_op jit(solution)/shard_map/ppermute | solution.py:21
  195.3 7.4 %all-to-all-done.5 = bf16[32,16,1024]{2,1,0:T(8,128)(2,1)S(1)} async-done(((bf16[32,16,1024]{2,1,0:T(8,128)(2,1)}), bf16[32,16,1024]{2,1,0:T(8,128)(2,1)S(1)}, u32[]{:S(2)}, u32[]{:S(2)}) %all-to-all-start.5) | async-done | bytes 1048608 | tf_op jit(solution)/shard_map/all_to_all | solution.py:103
  202.6 5.6 %all-to-all-start.3 = ((bf16[32,16,1024]{2,1,0:T(8,128)(2,1)}), bf16[32,16,1024]{2,1,0:T(8,128)(2,1)S(1)}, u32[]{:S(2)}, u32[]{:S(2)}) async-start(bf16[32,16,1024]{2,1,0:T(8,128)(2,1)} %bitcast.150), calls=%async_computation.3 | async-start | bytes 2097152 | tf_op jit(solution)/shard_map/all_to_all | solution.py:103
  210.8 5.4 %collective-permute-start.15 = (bf16[32,512]{1,0:T(8,128)(2,1)S(1)}, bf16[32,512]{1,0:T(8,128)(2,1)S(1)}, u32[]{:S(2)}, u32[]{:S(2)}) collective-permute-start(bf16[32,512]{1,0:T(8,128)(2,1)S(1)} %bitcast.158), channel_id=1, source_target_pairs={{0,288},{32,256},{256,32},{288,0},{1,289},{33,257},{257,33},{289,1... | collective-permute-start | bytes 98312 | tf_op jit(solution)/shard_map/ppermute | solution.py:21
  216.3 3.4 %collective-permute-start.14 = (bf16[32,512]{1,0:T(8,128)(2,1)S(1)}, bf16[32,512]{1,0:T(8,128)(2,1)S(1)}, u32[]{:S(2)}, u32[]{:S(2)}) collective-permute-start(bf16[32,512]{1,0:T(8,128)(2,1)S(1)} %bitcast.157), channel_id=1, source_target_pairs={{0,32},{32,0},{1,33},{33,1},{2,34},{34,2},{3,35},{35,3},{4,36},{36... | collective-permute-start | bytes 98312 | tf_op jit(solution)/shard_map/ppermute | solution.py:21
  219.7 3.4 %collective-permute-start.13 = (bf16[32,512]{1,0:T(8,128)(2,1)S(1)}, bf16[32,512]{1,0:T(8,128)(2,1)S(1)}, u32[]{:S(2)}, u32[]{:S(2)}) collective-permute-start(bf16[32,512]{1,0:T(8,128)(2,1)S(1)} %bitcast.156), channel_id=1, source_target_pairs={{0,256},{256,0},{1,257},{257,1},{2,258},{258,2},{3,259},{259,3},{4... | collective-permute-start | bytes 98312 | tf_op jit(solution)/shard_map/ppermute | solution.py:21
  223.2 12.4 %all-to-all-done.3 = bf16[32,16,1024]{2,1,0:T(8,128)(2,1)S(1)} async-done(((bf16[32,16,1024]{2,1,0:T(8,128)(2,1)}), bf16[32,16,1024]{2,1,0:T(8,128)(2,1)S(1)}, u32[]{:S(2)}, u32[]{:S(2)}) %all-to-all-start.3) | async-done | bytes 1048608 | tf_op jit(solution)/shard_map/all_to_all | solution.py:103
  237.2 5.4 %collective-permute-start.9 = (bf16[32,512]{1,0:T(8,128)(2,1)S(1)}, bf16[32,512]{1,0:T(8,128)(2,1)S(1)}, u32[]{:S(2)}, u32[]{:S(2)}) collective-permute-start(bf16[32,512]{1,0:T(8,128)(2,1)S(1)} %bitcast.161), channel_id=1, source_target_pairs={{0,288},{32,256},{256,32},{288,0},{1,289},{33,257},{257,33},{289,1... | collective-permute-start | bytes 98312 | tf_op jit(solution)/shard_map/ppermute | solution.py:21
  242.7 3.4 %collective-permute-start.8 = (bf16[32,512]{1,0:T(8,128)(2,1)S(1)}, bf16[32,512]{1,0:T(8,128)(2,1)S(1)}, u32[]{:S(2)}, u32[]{:S(2)}) collective-permute-start(bf16[32,512]{1,0:T(8,128)(2,1)S(1)} %bitcast.160), channel_id=1, source_target_pairs={{0,32},{32,0},{1,33},{33,1},{2,34},{34,2},{3,35},{35,3},{4,36},{36... | collective-permute-start | bytes 98312 | tf_op jit(solution)/shard_map/ppermute | solution.py:21
  246.1 3.4 %collective-permute-start.7 = (bf16[32,512]{1,0:T(8,128)(2,1)S(1)}, bf16[32,512]{1,0:T(8,128)(2,1)S(1)}, u32[]{:S(2)}, u32[]{:S(2)}) collective-permute-start(bf16[32,512]{1,0:T(8,128)(2,1)S(1)} %bitcast.159), channel_id=1, source_target_pairs={{0,256},{256,0},{1,257},{257,1},{2,258},{258,2},{3,259},{259,3},{4... | collective-permute-start | bytes 98312 | tf_op jit(solution)/shard_map/ppermute | solution.py:21
  249.6 3.2 %collective-permute-done.8 = bf16[32,512]{1,0:T(8,128)(2,1)S(1)} collective-permute-done((bf16[32,512]{1,0:T(8,128)(2,1)S(1)}, bf16[32,512]{1,0:T(8,128)(2,1)S(1)}, u32[]{:S(2)}, u32[]{:S(2)}) %collective-permute-start.8) | collective-permute-done | bytes 32800 | tf_op jit(solution)/shard_map/ppermute | solution.py:21
  (105 shorter events, 40.0 us)
Async XLA Ops:
  0.0 32.1 %copy-start.3 = (bf16[2,32,512]{2,1,0:T(8,128)(2,1)S(1)}, bf16[2,32,512]{2,1,0:T(8,128)(2,1)}, u32[]{:S(2)}) copy-start(bf16[2,32,512]{2,1,0:T(8,128)(2,1)} %param.8) | copy-start | bytes 196612
  0.0 32.1 %collective-permute-start.1 = (bf16[2,32,512]{2,1,0:T(8,128)(2,1)}, bf16[2,32,512]{2,1,0:T(8,128)(2,1)S(1)}, u32[]{:S(2)}, u32[]{:S(2)}) collective-permute-start(bf16[2,32,512]{2,1,0:T(8,128)(2,1)} %param.8), channel_id=1, source_target_pairs={{0,256},{256,0},{1,257},{257,1},{2,258},{258,2},{3,259},{259,3},{4... | collective-permute-start | bytes 196616 | tf_op jit(solution)/shard_map/ppermute | solution.py:21
  6.2 25.9 %collective-permute-start.3 = (bf16[2,32,512]{2,1,0:T(8,128)(2,1)}, bf16[2,32,512]{2,1,0:T(8,128)(2,1)S(1)}, u32[]{:S(2)}, u32[]{:S(2)}) collective-permute-start(bf16[2,32,512]{2,1,0:T(8,128)(2,1)} %param.8), channel_id=1, source_target_pairs={{0,288},{32,256},{256,32},{288,0},{1,289},{33,257},{257,33},{289,1... | collective-permute-start | bytes 196616 | tf_op jit(solution)/shard_map/ppermute | solution.py:21
  13.5 18.6 %collective-permute-start.2 = (bf16[2,32,512]{2,1,0:T(8,128)(2,1)}, bf16[2,32,512]{2,1,0:T(8,128)(2,1)S(1)}, u32[]{:S(2)}, u32[]{:S(2)}) collective-permute-start(bf16[2,32,512]{2,1,0:T(8,128)(2,1)} %param.8), channel_id=1, source_target_pairs={{0,32},{32,0},{1,33},{33,1},{2,34},{34,2},{3,35},{35,3},{4,36},{36... | collective-permute-start | bytes 196616 | tf_op jit(solution)/shard_map/ppermute | solution.py:21
  19.1 9.4 %collective-permute-start = (f32[2,2,256]{2,1,0:T(2,128)S(1)}, f32[2,2,256]{2,1,0:T(2,128)S(1)}, u32[]{:S(2)}, u32[]{:S(2)}) collective-permute-start(f32[2,2,256]{2,1,0:T(2,128)S(1)} %constant_dynamic-update-slice_fusion), channel_id=1, source_target_pairs={{0,32},{32,0},{1,33},{33,1},{2,34},{34,2},{3,35},{35,3},{4,36},{36... | collective-permute-start | bytes 12296 | tf_op jit(solution)/shard_map/ppermute | solution.py:21
  33.9 36.6 %all-to-all-start.4 = ((bf16[32,16,1024]{2,1,0:T(8,128)(2,1)}), bf16[32,16,1024]{2,1,0:T(8,128)(2,1)S(1)}, u32[]{:S(2)}, u32[]{:S(2)}) async-start(bf16[32,16,1024]{2,1,0:T(8,128)(2,1)} %fusion.41), calls=%async_computation.4 | async-start | bytes 2097152 | tf_op jit(solution)/shard_map/all_to_all | solution.py:93
  70.5 5.6 %copy-start = (bf16[32,16,1024]{2,1,0:T(8,128)(2,1)}, bf16[32,16,1024]{2,1,0:T(8,128)(2,1)S(1)}, u32[]{:S(2)}) copy-start(bf16[32,16,1024]{2,1,0:T(8,128)(2,1)S(1)} %all-to-all-done.4) | copy-start | bytes 3145732
  70.5 31.6 %all-to-all-start = ((bf16[32,16,1024]{2,1,0:T(8,128)(2,1)}), bf16[32,16,1024]{2,1,0:T(8,128)(2,1)}, u32[]{:S(2)}, u32[]{:S(2)}) async-start(bf16[32,16,1024]{2,1,0:T(8,128)(2,1)} %fusion.38), calls=%async_computation | async-start | bytes 2097152 | tf_op jit(solution)/shard_map/all_to_all | solution.py:93
  82.6 23.9 %copy-start.2 = (bf16[1,192,4096]{2,1,0:T(8,128)(2,1)S(1)}, bf16[1,192,4096]{2,1,0:T(8,128)(2,1)}, u32[]{:S(2)}) copy-start(bf16[1,192,4096]{2,1,0:T(8,128)(2,1)} %param.10) | copy-start | bytes 4718596
  102.1 24.5 %all-to-all-start.1 = ((bf16[4,192,1024]{2,1,0:T(8,128)(2,1)}), bf16[4,192,1024]{2,1,0:T(8,128)(2,1)}, u32[]{:S(2)}, u32[]{:S(2)}) async-start(bf16[4,192,1024]{2,1,0:T(8,128)(2,1)} %reshape.333), calls=%async_computation.1 | async-start | bytes 3145728 | tf_op jit(solution)/shard_map/all_to_all | solution.py:29
  111.3 19.0 %copy-start.1 = (bf16[32,16,1024]{2,1,0:T(8,128)(2,1)S(1)}, bf16[32,16,1024]{2,1,0:T(8,128)(2,1)}, u32[]{:S(2)}) copy-start(bf16[32,16,1024]{2,1,0:T(8,128)(2,1)} %copy-done) | copy-start | bytes 3145732
  126.6 39.7 %all-to-all-start.2 = ((bf16[4,192,1024]{2,1,0:T(8,128)(2,1)}), bf16[4,192,1024]{2,1,0:T(8,128)(2,1)S(1)}, u32[]{:S(2)}, u32[]{:S(2)}) async-start(bf16[4,192,1024]{2,1,0:T(8,128)(2,1)} %reshape.335), calls=%async_computation.2 | async-start | bytes 3145728 | tf_op jit(solution)/shard_map/all_to_all | solution.py:29
  132.8 3.9 %collective-permute-start.10 = (bf16[512,384]{1,0:T(8,128)(2,1)}, bf16[512,384]{1,0:T(8,128)(2,1)S(1)}, u32[]{:S(2)}, u32[]{:S(2)}) collective-permute-start(bf16[512,384]{1,0:T(8,128)(2,1)} %fusion.6), channel_id=1, source_target_pairs={{0,64},{64,0},{1,65},{65,1},{2,66},{66,2},{3,67},{67,3},{4,68},{68... | collective-permute-start | bytes 1179656 | tf_op jit(solution)/shard_map/ppermute | solution.py:21
  138.6 20.1 %collective-permute-start.11 = (bf16[512,384]{1,0:T(8,128)(2,1)S(1)}, bf16[512,384]{1,0:T(8,128)(2,1)S(1)}, u32[]{:S(2)}, u32[]{:S(2)}) collective-permute-start(bf16[512,384]{1,0:T(8,128)(2,1)S(1)} %get-tuple-element.43), channel_id=1, source_target_pairs={{0,128},{128,0},{1,129},{129,1},{2,130},{130,2},{3,131},{131,3},{4... | collective-permute-start | bytes 1179656 | tf_op jit(solution)/shard_map/ppermute | solution.py:21
  158.9 7.5 %collective-permute-start.12 = (bf16[512,384]{1,0:T(8,128)(2,1)S(1)}, bf16[512,384]{1,0:T(8,128)(2,1)S(1)}, u32[]{:S(2)}, u32[]{:S(2)}) collective-permute-start(bf16[512,384]{1,0:T(8,128)(2,1)S(1)} %multiply_convert_fusion), channel_id=1, source_target_pairs={{0,64},{64,0},{1,65},{65,1},{2,66},{66,2},{3,67},{67,3},{4,68},{68... | collective-permute-start | bytes 1179656 | tf_op jit(solution)/shard_map/ppermute | solution.py:21
  163.8 10.6 %collective-permute-start.4 = (bf16[512,384]{1,0:T(8,128)(2,1)}, bf16[512,384]{1,0:T(8,128)(2,1)S(1)}, u32[]{:S(2)}, u32[]{:S(2)}) collective-permute-start(bf16[512,384]{1,0:T(8,128)(2,1)} %fusion.8), channel_id=1, source_target_pairs={{0,64},{64,0},{1,65},{65,1},{2,66},{66,2},{3,67},{67,3},{4,68},{68... | collective-permute-start | bytes 1179656 | tf_op jit(solution)/shard_map/ppermute | solution.py:21
  168.8 33.8 %all-to-all-start.5 = ((bf16[32,16,1024]{2,1,0:T(8,128)(2,1)}), bf16[32,16,1024]{2,1,0:T(8,128)(2,1)S(1)}, u32[]{:S(2)}, u32[]{:S(2)}) async-start(bf16[32,16,1024]{2,1,0:T(8,128)(2,1)} %bitcast.151), calls=%async_computation.5 | async-start | bytes 2097152 | tf_op jit(solution)/shard_map/all_to_all | solution.py:103
  176.6 12.4 %collective-permute-start.5 = (bf16[512,384]{1,0:T(8,128)(2,1)S(1)}, bf16[512,384]{1,0:T(8,128)(2,1)S(1)}, u32[]{:S(2)}, u32[]{:S(2)}) collective-permute-start(bf16[512,384]{1,0:T(8,128)(2,1)S(1)} %get-tuple-element.45), channel_id=1, source_target_pairs={{0,128},{128,0},{1,129},{129,1},{2,130},{130,2},{3,131},{131,3},{4... | collective-permute-start | bytes 1179656 | tf_op jit(solution)/shard_map/ppermute | solution.py:21
  189.2 3.6 %collective-permute-start.6 = (bf16[512,384]{1,0:T(8,128)(2,1)S(1)}, bf16[512,384]{1,0:T(8,128)(2,1)S(1)}, u32[]{:S(2)}, u32[]{:S(2)}) collective-permute-start(bf16[512,384]{1,0:T(8,128)(2,1)S(1)} %multiply_convert_fusion.1), channel_id=1, source_target_pairs={{0,64},{64,0},{1,65},{65,1},{2,66},{66,2},{3,67},{67,3},{4,68},{68... | collective-permute-start | bytes 1179656 | tf_op jit(solution)/shard_map/ppermute | solution.py:21
  202.6 32.9 %all-to-all-start.3 = ((bf16[32,16,1024]{2,1,0:T(8,128)(2,1)}), bf16[32,16,1024]{2,1,0:T(8,128)(2,1)S(1)}, u32[]{:S(2)}, u32[]{:S(2)}) async-start(bf16[32,16,1024]{2,1,0:T(8,128)(2,1)} %bitcast.150), calls=%async_computation.3 | async-start | bytes 2097152 | tf_op jit(solution)/shard_map/all_to_all | solution.py:103
  210.8 35.2 %collective-permute-start.15 = (bf16[32,512]{1,0:T(8,128)(2,1)S(1)}, bf16[32,512]{1,0:T(8,128)(2,1)S(1)}, u32[]{:S(2)}, u32[]{:S(2)}) collective-permute-start(bf16[32,512]{1,0:T(8,128)(2,1)S(1)} %bitcast.158), channel_id=1, source_target_pairs={{0,288},{32,256},{256,32},{288,0},{1,289},{33,257},{257,33},{289,1... | collective-permute-start | bytes 98312 | tf_op jit(solution)/shard_map/ppermute | solution.py:21
  216.3 33.2 %collective-permute-start.14 = (bf16[32,512]{1,0:T(8,128)(2,1)S(1)}, bf16[32,512]{1,0:T(8,128)(2,1)S(1)}, u32[]{:S(2)}, u32[]{:S(2)}) collective-permute-start(bf16[32,512]{1,0:T(8,128)(2,1)S(1)} %bitcast.157), channel_id=1, source_target_pairs={{0,32},{32,0},{1,33},{33,1},{2,34},{34,2},{3,35},{35,3},{4,36},{36... | collective-permute-start | bytes 98312 | tf_op jit(solution)/shard_map/ppermute | solution.py:21
  219.7 29.9 %collective-permute-start.13 = (bf16[32,512]{1,0:T(8,128)(2,1)S(1)}, bf16[32,512]{1,0:T(8,128)(2,1)S(1)}, u32[]{:S(2)}, u32[]{:S(2)}) collective-permute-start(bf16[32,512]{1,0:T(8,128)(2,1)S(1)} %bitcast.156), channel_id=1, source_target_pairs={{0,256},{256,0},{1,257},{257,1},{2,258},{258,2},{3,259},{259,3},{4... | collective-permute-start | bytes 98312 | tf_op jit(solution)/shard_map/ppermute | solution.py:21
  237.2 12.3 %collective-permute-start.9 = (bf16[32,512]{1,0:T(8,128)(2,1)S(1)}, bf16[32,512]{1,0:T(8,128)(2,1)S(1)}, u32[]{:S(2)}, u32[]{:S(2)}) collective-permute-start(bf16[32,512]{1,0:T(8,128)(2,1)S(1)} %bitcast.161), channel_id=1, source_target_pairs={{0,288},{32,256},{256,32},{288,0},{1,289},{33,257},{257,33},{289,1... | collective-permute-start | bytes 98312 | tf_op jit(solution)/shard_map/ppermute | solution.py:21
  242.7 10.1 %collective-permute-start.8 = (bf16[32,512]{1,0:T(8,128)(2,1)S(1)}, bf16[32,512]{1,0:T(8,128)(2,1)S(1)}, u32[]{:S(2)}, u32[]{:S(2)}) collective-permute-start(bf16[32,512]{1,0:T(8,128)(2,1)S(1)} %bitcast.160), channel_id=1, source_target_pairs={{0,32},{32,0},{1,33},{33,1},{2,34},{34,2},{3,35},{35,3},{4,36},{36... | collective-permute-start | bytes 98312 | tf_op jit(solution)/shard_map/ppermute | solution.py:21
  246.1 7.1 %collective-permute-start.7 = (bf16[32,512]{1,0:T(8,128)(2,1)S(1)}, bf16[32,512]{1,0:T(8,128)(2,1)S(1)}, u32[]{:S(2)}, u32[]{:S(2)}) collective-permute-start(bf16[32,512]{1,0:T(8,128)(2,1)S(1)} %bitcast.159), channel_id=1, source_target_pairs={{0,256},{256,0},{1,257},{257,1},{2,258},{258,2},{3,259},{259,3},{4... | collective-permute-start | bytes 98312 | tf_op jit(solution)/shard_map/ppermute | solution.py:21

commit v3 on v2

--- a/solution.py
+++ b/solution.py
@@ -23,14 +23,23 @@
 
 def recut(weight):
     hidden, feats = weight.shape
-    k = lax.axis_index("k")
-    blocks = weight.reshape(hidden, 2, 2, 2, feats // 8).transpose(3, 2, 0, 1, 4)
-    blocks = blocks.reshape(4, hidden, feats // 4)
-    blocks = lax.all_to_all(blocks, ("k", "m"), 0, 0, tiled=True)
-    blocks = blocks.reshape(2, 2 * hidden, feats // 4)
-    own = lax.dynamic_index_in_dim(blocks, k, 0, keepdims=False)
-    other = lax.dynamic_index_in_dim(blocks, 1 - k, 0, keepdims=False)
-    return own, other
+    m, k = lax.axis_index("m"), lax.axis_index("k")
+    blocks = weight.reshape(hidden, 2, 2, 2, feats // 8)
+
+    def cut(at_m, at_k):
+        start = (0, 0, at_m, at_k, 0)
+        return lax.dynamic_slice(blocks, start, (hidden, 2, 1, 1, feats // 8)).reshape(hidden, feats // 4)
+
+    there = swap(jnp.stack([cut(m, 1 - k), cut(1 - m, 1 - k)]), "k")
+    near_own, near_other = cut(m, k), there[0]
+    far = swap(jnp.stack([cut(1 - m, k), there[1]]), "m")
+
+    def order(near, far):
+        first = jnp.where(m == 0, near, far)
+        second = jnp.where(m == 0, far, near)
+        return jnp.concatenate([first, second], axis=0)
+
+    return order(near_own, far[0]), order(near_other, far[1])
 
 
 def slots(codes, weights, plan):
@@ -63,6 +72,12 @@
     return order(tokens_of), order(weight_of)
 
 
+def thirds(value):
+    high = lax.reduce_precision(value, 8, 7)
+    mid = lax.reduce_precision(value - high, 8, 7)
+    return high.astype(BF), mid.astype(BF), (value - high - mid).astype(BF)
+
+
 def both(first, second, axis_name, axis):
     at = lax.axis_index(axis_name)
     return jnp.stack([jnp.where(at == 0, first, second), jnp.where(at == 0, second, first)], axis)
@@ -72,24 +87,29 @@
     batches, group, feats = tokens.shape
     peers = lax.axis_size("y") * lax.axis_size("x")
     zh, p = lax.axis_index("zh"), lax.axis_index("p")
-    code = (2 * expert_ids + (replica_pick & 1)).astype(F32)
-    info = jnp.stack([code, route_weight]).reshape(2, batches, group * TOPK)
-    info = both(info, swap(info, "zh"), "zh", 2)
-
-    near = both(tokens, swap(tokens, "p"), "p", 2)
-    far = both(swap(tokens, "zh"), swap(tokens, "p", "zh"), "p", 2)
-    tok = both(near, far, "zh", 1).reshape(batches, 2 * group, 2 * feats)
-
-    gate_own, gate_other = recut(w_gate[0])
-    down_own, down_other = recut(w_down[0])
+    code = (2 * expert_ids + (replica_pick & 1)).astype(BF)
+    parts = [code, *thirds(route_weight)]
+    info = jnp.stack(parts).reshape(-1, feats)
+    sent = jnp.concatenate([tokens.reshape(-1, feats), jnp.pad(info, ((0, 16 - info.shape[0]), (0, 0)))])
+    came = swap(sent, "zh")
+    tokens = both(tokens, came[: batches * group].reshape(tokens.shape), "zh", 1)
+    tokens = tokens.reshape(batches, 2 * group, feats)
+    far_info = came[batches * group :][: info.shape[0]]
+    info = both(info, far_info, "zh", 0).reshape(2, 4, batches, group * TOPK).astype(F32)
+    code = info[:, 0].astype(jnp.int32)
+    weight = info[:, 1] + info[:, 2] + info[:, 3]
+    tok = both(tokens, swap(tokens, "p"), "p", 2).reshape(batches, 2 * group, 2 * feats)
 
     outputs = []
     for index, plan in ((0, old_plan), (1, new_plan)):
-        codes = info[0, index].astype(jnp.int32)
-        slot_token, slot_weight = slots(codes, info[1, index], plan)
+        slot_token, slot_weight = slots(code[:, index], weight[:, index], plan)
         pick = slot_token[:, None] == jnp.arange(2 * group, dtype=jnp.int32)[None, :]
         rows = dot(pick.astype(BF), tok[index], ((1,), (0,)), BF)
         rows = rows.reshape(peers, -1, rows.shape[1])
+        if index == 0:
+            rows, w_gate, w_down = lax.optimization_barrier((rows, w_gate, w_down))
+            gate_own, gate_other = recut(w_gate[0])
+            down_own, down_other = recut(w_down[0])
         rows = lax.all_to_all(rows, ("y", "x"), 0, 0, tiled=True).reshape(-1, rows.shape[2])
 
         send = dot(rows, gate_other, ((1,), (1,)), BF)
@@ -103,8 +123,7 @@
         back = lax.all_to_all(out, ("y", "x"), 0, 0, tiled=True).reshape(-1, out.shape[2])
 
         scale = jnp.where(pick, slot_weight[:, None], 0.0)
-        high = scale.astype(BF)
-        low = (scale - high.astype(F32)).astype(BF)
+        high, low, _ = thirds(scale)
         mixed = dot(high, back, ((0,), (0,))) + dot(low, back, ((0,), (0,)))
         mixed = mixed.reshape(2, group, 2, feats)
 

time: 255 us -> 238 us (0.933)
  waiting for transfers between devices: 115 us -> 69 us
  local copies, waits for them, and re-layouts: 14.5 us -> 32.5 us
  other arithmetic: 5.99 us -> 13.7 us
  starting transfers between devices: 97.4 us -> 100 us
    all_to_all x2, waiting for transfers between devices: 44 us -> 0.01 us  [local(): lax.all_to_all(rows, ('y', 'x'), 0, 0, tiled=True)]
    dynamic_slice x0 -> x2, local copies, waits for them, and re-layouts: none -> 22.4 us  [cut(): lax.dynamic_slice(blocks, start, (hidden, 2, 1, 1, feats // 8))]
    ppermute x16 -> x18, waiting for transfers between devices: 35.6 us -> 51.1 us  [swap(): return lax.ppermute(array, axes, [(i, last - i) for i in range(last + 1)])]
    all_to_all x2 -> x0, waiting for transfers between devices: 15.4 us -> none  [recut(): blocks = lax.all_to_all(blocks, ('k', 'm'), 0, 0, tiled=True)]
    all_to_all x2 -> x0, starting transfers between devices: 7.91 us -> none  [recut(): blocks = lax.all_to_all(blocks, ('k', 'm'), 0, 0, tiled=True)]
    reshape x2 -> x0, local copies, waits for them, and re-layouts: 4.69 us -> none  [recut(): blocks = blocks.reshape(4, hidden, feats // 4)]
    all_to_all x2, starting transfers between devices: 15.9 us -> 20.3 us  [local(): lax.all_to_all(rows, ('y', 'x'), 0, 0, tiled=True)]
    all_to_all x2, starting transfers between devices: 11.1 us -> 15.3 us  [local(): lax.all_to_all(out, ('y', 'x'), 0, 0, tiled=True).reshape(-1, out.shape[2])]
  transfers between devices with their start and end apart: 22 -> 22, of which waited for: 12 -> 10; matrix products, arithmetic and copies ran while one was open for 15% -> 25% of each run, Pallas kernels for 0% -> 0%
where the time goes in v3:
time: 238 us; the launch traced here: 237 us
  starting transfers between devices  100 us (42%)
  waiting for transfers between devices  69 us (29%)
  local copies, waits for them, and re-layouts  32.5 us (14%)
  matrix products  20.1 us (8%)
  other arithmetic  13.7 us (6%)
    ppermute x18, starting transfers between devices, swap(): return lax.ppermute(array, axes, [(i, last - i) for i in range(last + 1)])  64.8 us
    ppermute x18, waiting for transfers between devices, swap(): return lax.ppermute(array, axes, [(i, last - i) for i in range(last + 1)])  51.1 us
    dynamic_slice x2, local copies, waits for them, and re-layouts, cut(): lax.dynamic_slice(blocks, start, (hidden, 2, 1, 1, feats // 8))  22.4 us
    all_to_all x2, starting transfers between devices, local(): lax.all_to_all(rows, ('y', 'x'), 0, 0, tiled=True)  20.3 us
    dot_general x18, matrix products, dot(): return lax.dot_general(a, b, (dims, ((), ())), preferred_element_type=out)  20.1 us
    all_to_all x2, waiting for transfers between devices, local(): lax.all_to_all(out, ('y', 'x'), 0, 0, tiled=True).reshape(-1, out.shape[2])  17.9 us
    all_to_all x2, starting transfers between devices, local(): lax.all_to_all(out, ('y', 'x'), 0, 0, tiled=True).reshape(-1, out.shape[2])  15.3 us
  transfers between devices with their start and end apart: 22, of which 10 were waited for; matrix products, arithmetic and copies ran while one was open for 25% of the time, Pallas kernels for 0%

profile of v3, /device:TPU:2, one launch (start us, length us, event | category | flops | bytes accessed | tf_op | source)
XLA Modules:
  0.0 236.6 jit_solution(8513629880444536940)
XLA Ops:
  3.1 10.9 %collective-permute-start = (bf16[80,512]{1,0:T(8,128)(2,1)S(1)}, bf16[80,512]{1,0:T(8,128)(2,1)S(1)}, u32[]{:S(2)}, u32[]{:S(2)}) collective-permute-start(bf16[80,512]{1,0:T(8,128)(2,1)S(1)} %fusion.49), channel_id=1, source_target_pairs={{0,32},{32,0},{1,33},{33,1},{2,34},{34,2},{3,35},{35,3},{4,36},{36... | collective-permute-start | bytes 245768 | tf_op jit(solution)/shard_map/ppermute | solution.py:21
  15.0 2.6 %collective-permute-done = bf16[80,512]{1,0:T(8,128)(2,1)S(1)} collective-permute-done((bf16[80,512]{1,0:T(8,128)(2,1)S(1)}, bf16[80,512]{1,0:T(8,128)(2,1)S(1)}, u32[]{:S(2)}, u32[]{:S(2)}) %collective-permute-start) | collective-permute-done | bytes 81952 | tf_op jit(solution)/shard_map/ppermute | solution.py:21
  19.5 4.9 %collective-permute-start.1 = (bf16[2,64,512]{2,1,0:T(8,128)(2,1)S(1)}, bf16[2,64,512]{2,1,0:T(8,128)(2,1)S(1)}, u32[]{:S(2)}, u32[]{:S(2)}) collective-permute-start(bf16[2,64,512]{2,1,0:T(8,128)(2,1)S(1)} %bitcast.143), channel_id=1, source_target_pairs={{0,256},{256,0},{1,257},{257,1},{2,258},{258,2},{3,259},{259,3},{4... | collective-permute-start | bytes 393224 | tf_op jit(solution)/shard_map/ppermute | solution.py:21
  24.5 2.2 select_reduce_fusion.3
  27.1 2.4 %collective-permute-done.1 = bf16[2,64,512]{2,1,0:T(8,128)(2,1)S(1)} collective-permute-done((bf16[2,64,512]{2,1,0:T(8,128)(2,1)S(1)}, bf16[2,64,512]{2,1,0:T(8,128)(2,1)S(1)}, u32[]{:S(2)}, u32[]{:S(2)}) %collective-permute-start.1) | collective-permute-done | bytes 131104 | tf_op jit(solution)/shard_map/ppermute | solution.py:21
  31.5 10.4 %all-to-all-start.2 = ((bf16[32,16,1024]{2,1,0:T(8,128)(2,1)}), bf16[32,16,1024]{2,1,0:T(8,128)(2,1)}, u32[]{:S(2)}, u32[]{:S(2)}) async-start(bf16[32,16,1024]{2,1,0:T(8,128)(2,1)} %fusion.25), calls=%async_computation.2 | async-start | bytes 2097152 | tf_op jit(solution)/shard_map/all_to_all | solution.py:113
  44.7 11.6 %dynamic-slice_reduce_fusion.6 = (bf16[192,2,512]{2,1,0:T(2,128)(2,1)}, bf16[192,2,512]{2,1,0:T(2,128)(2,1)S(1)}, bf16[192,2,512]{2,1,0:T(2,128)(2,1)S(1)}, bf16[192,2,512]{2,1,0:T(2,128)(2,1)}) fusion(bf16[192,2,2,2,512]{4,3,2,1,0:T(2,128)(2,1)S(1)} %reshape_squeeze.6, s32[]{:T(128)S(6)} %select_n.215, s32[]{:T(128)S(6)} %select_n.214, s32[]{:T(128)S(6)} %select_n.213, ...), kind=kLoop, calls=%fused_computation.24 | loop fusion | bytes 3145744 | tf_op jit(solution)/shard_map/dynamic_slice | solution.py:31
  58.8 2.1 collective-permute-start.2
  63.2 10.8 %dynamic-slice_reduce_fusion.3 = (bf16[192,2,512]{2,1,0:T(2,128)(2,1)S(1)}, bf16[192,2,512]{2,1,0:T(2,128)(2,1)S(1)}, bf16[192,2,512]{2,1,0:T(2,128)(2,1)S(1)}, bf16[192,2,512]{2,1,0:T(2,128)(2,1)S(1)}) fusion(bf16[192,2,2,2,512]{4,3,2,1,0:T(2,128)(2,1)S(1)} %reshape_squeeze.7, s32[]{:T(128)S(6)} %select_n.213, s32[]{:T(128)S(6)} %select_n.214, ...), kind=kLoop, calls=%fused_computation.19 | loop fusion | bytes 3145744 | tf_op jit(solution)/shard_map/dynamic_slice | solution.py:31
  75.6 2.4 %collective-permute-start.6 = (bf16[2,192,1024]{2,1,0:T(8,128)(2,1)}, bf16[2,192,1024]{2,1,0:T(8,128)(2,1)S(1)}, u32[]{:S(2)}, u32[]{:S(2)}) collective-permute-start(bf16[2,192,1024]{2,1,0:T(8,128)(2,1)} %pad_maximum_fusion.4), channel_id=1, source_target_pairs={{0,64},{64,0},{1,65},{65,1},{2,66},{66,2},{3,67},{67,3},{4,68},{68... | collective-permute-start | bytes 2359304 | tf_op jit(solution)/shard_map/ppermute | solution.py:21
  81.3 9.8 %all-to-all-start = ((bf16[32,16,1024]{2,1,0:T(8,128)(2,1)}), bf16[32,16,1024]{2,1,0:T(8,128)(2,1)}, u32[]{:S(2)}, u32[]{:S(2)}) async-start(bf16[32,16,1024]{2,1,0:T(8,128)(2,1)} %fusion.22), calls=%async_computation | async-start | bytes 2097152 | tf_op jit(solution)/shard_map/all_to_all | solution.py:113
  91.2 9.4 %collective-permute-done.3 = bf16[2,192,1024]{2,1,0:T(8,128)(2,1)} collective-permute-done((bf16[2,192,1024]{2,1,0:T(8,128)(2,1)S(1)}, bf16[2,192,1024]{2,1,0:T(8,128)(2,1)}, u32[]{:S(2)}, u32[]{:S(2)}) %collective-permute-start.3) | collective-permute-done | bytes 786464 | tf_op jit(solution)/shard_map/ppermute | solution.py:21
  101.8 2.2 fusion.6
  106.1 2.2 collective-permute-start.7
  111.4 3.6 %collective-permute-start.13 = (bf16[512,384]{1,0:T(8,128)(2,1)S(1)}, bf16[512,384]{1,0:T(8,128)(2,1)S(1)}, u32[]{:S(2)}, u32[]{:S(2)}) collective-permute-start(bf16[512,384]{1,0:T(8,128)(2,1)S(1)} %get-tuple-element.68), channel_id=1, source_target_pairs={{0,128},{128,0},{1,129},{129,1},{2,130},{130,2},{3,131},{131,3},{4... | collective-permute-start | bytes 1179656 | tf_op jit(solution)/shard_map/ppermute | solution.py:21
  115.1 13.2 %collective-permute-done.7 = bf16[2,192,1024]{2,1,0:T(8,128)(2,1)S(1)} collective-permute-done((bf16[2,192,1024]{2,1,0:T(8,128)(2,1)S(1)}, bf16[2,192,1024]{2,1,0:T(8,128)(2,1)S(1)}, u32[]{:S(2)}, u32[]{:S(2)}) %collective-permute-start.7) | collective-permute-done | bytes 786464 | tf_op jit(solution)/shard_map/ppermute | solution.py:21
  128.4 8.0 %collective-permute-done.13 = bf16[512,384]{1,0:T(8,128)(2,1)S(1)} collective-permute-done((bf16[512,384]{1,0:T(8,128)(2,1)S(1)}, bf16[512,384]{1,0:T(8,128)(2,1)S(1)}, u32[]{:S(2)}, u32[]{:S(2)}) %collective-permute-start.13) | collective-permute-done | bytes 393248 | tf_op jit(solution)/shard_map/ppermute | solution.py:21
  138.6 2.9 %fusion.7 = bf16[512,384]{1,0:T(8,128)(2,1)} fusion(bf16[512,1024]{1,0:T(8,128)(2,1)} %bitcast.15, bf16[192,1024]{1,0:T(8,128)(2,1)} %copy-done.7, bf16[192,1024]{1,0:T(8,128)(2,1)} %copy-done.6), kind=kOutput, calls=%fused_computation.39 | convolution fusion | flops 404226048 | bytes 2228224 | tf_op jit(solution)/shard_map/dot_general | solution.py:16
  141.5 2.4 %collective-permute-start.4 = (bf16[512,384]{1,0:T(8,128)(2,1)}, bf16[512,384]{1,0:T(8,128)(2,1)}, u32[]{:S(2)}, u32[]{:S(2)}) collective-permute-start(bf16[512,384]{1,0:T(8,128)(2,1)} %fusion.7), channel_id=1, source_target_pairs={{0,64},{64,0},{1,65},{65,1},{2,66},{66,2},{3,67},{67,3},{4,68},{68... | collective-permute-start | bytes 1179656 | tf_op jit(solution)/shard_map/ppermute | solution.py:21
  146.3 9.8 %all-to-all-start.3 = ((bf16[32,16,1024]{2,1,0:T(8,128)(2,1)}), bf16[32,16,1024]{2,1,0:T(8,128)(2,1)S(1)}, u32[]{:S(2)}, u32[]{:S(2)}) async-start(bf16[32,16,1024]{2,1,0:T(8,128)(2,1)} %bitcast.33), calls=%async_computation.3 | async-start | bytes 2097152 | tf_op jit(solution)/shard_map/all_to_all | solution.py:123
  158.2 2.2 collective-permute-start.5
  160.4 10.4 %collective-permute-done.5 = bf16[512,384]{1,0:T(8,128)(2,1)S(1)} collective-permute-done((bf16[512,384]{1,0:T(8,128)(2,1)S(1)}, bf16[512,384]{1,0:T(8,128)(2,1)S(1)}, u32[]{:S(2)}, u32[]{:S(2)}) %collective-permute-start.5) | collective-permute-done | bytes 393248 | tf_op jit(solution)/shard_map/ppermute | solution.py:21
  178.1 6.5 %all-to-all-done.3 = bf16[32,16,1024]{2,1,0:T(8,128)(2,1)S(1)} async-done(((bf16[32,16,1024]{2,1,0:T(8,128)(2,1)}), bf16[32,16,1024]{2,1,0:T(8,128)(2,1)S(1)}, u32[]{:S(2)}, u32[]{:S(2)}) %all-to-all-start.3) | async-done | bytes 1048608 | tf_op jit(solution)/shard_map/all_to_all | solution.py:123
  184.6 5.6 %all-to-all-start.1 = ((bf16[32,16,1024]{2,1,0:T(8,128)(2,1)}), bf16[32,16,1024]{2,1,0:T(8,128)(2,1)S(1)}, u32[]{:S(2)}, u32[]{:S(2)}) async-start(bf16[32,16,1024]{2,1,0:T(8,128)(2,1)} %bitcast.22), calls=%async_computation.1 | async-start | bytes 2097152 | tf_op jit(solution)/shard_map/all_to_all | solution.py:123
  192.9 6.9 %collective-permute-start.17 = (bf16[32,512]{1,0:T(8,128)(2,1)S(1)}, bf16[32,512]{1,0:T(8,128)(2,1)S(1)}, u32[]{:S(2)}, u32[]{:S(2)}) collective-permute-start(bf16[32,512]{1,0:T(8,128)(2,1)S(1)} %bitcast.150), channel_id=1, source_target_pairs={{0,288},{32,256},{256,32},{288,0},{1,289},{33,257},{257,33},{289,1... | collective-permute-start | bytes 98312 | tf_op jit(solution)/shard_map/ppermute | solution.py:21
  199.8 2.4 %collective-permute-start.16 = (bf16[32,512]{1,0:T(8,128)(2,1)S(1)}, bf16[32,512]{1,0:T(8,128)(2,1)S(1)}, u32[]{:S(2)}, u32[]{:S(2)}) collective-permute-start(bf16[32,512]{1,0:T(8,128)(2,1)S(1)} %bitcast.149), channel_id=1, source_target_pairs={{0,32},{32,0},{1,33},{33,1},{2,34},{34,2},{3,35},{35,3},{4,36},{36... | collective-permute-start | bytes 98312 | tf_op jit(solution)/shard_map/ppermute | solution.py:21
  202.3 3.8 %collective-permute-start.15 = (bf16[32,512]{1,0:T(8,128)(2,1)S(1)}, bf16[32,512]{1,0:T(8,128)(2,1)S(1)}, u32[]{:S(2)}, u32[]{:S(2)}) collective-permute-start(bf16[32,512]{1,0:T(8,128)(2,1)S(1)} %bitcast.148), channel_id=1, source_target_pairs={{0,256},{256,0},{1,257},{257,1},{2,258},{258,2},{3,259},{259,3},{4... | collective-permute-start | bytes 98312 | tf_op jit(solution)/shard_map/ppermute | solution.py:21
  206.1 11.4 %all-to-all-done.1 = bf16[32,16,1024]{2,1,0:T(8,128)(2,1)S(1)} async-done(((bf16[32,16,1024]{2,1,0:T(8,128)(2,1)}), bf16[32,16,1024]{2,1,0:T(8,128)(2,1)S(1)}, u32[]{:S(2)}, u32[]{:S(2)}) %all-to-all-start.1) | async-done | bytes 1048608 | tf_op jit(solution)/shard_map/all_to_all | solution.py:123
  219.3 6.9 %collective-permute-start.11 = (bf16[32,512]{1,0:T(8,128)(2,1)S(1)}, bf16[32,512]{1,0:T(8,128)(2,1)S(1)}, u32[]{:S(2)}, u32[]{:S(2)}) collective-permute-start(bf16[32,512]{1,0:T(8,128)(2,1)S(1)} %bitcast.153), channel_id=1, source_target_pairs={{0,288},{32,256},{256,32},{288,0},{1,289},{33,257},{257,33},{289,1... | collective-permute-start | bytes 98312 | tf_op jit(solution)/shard_map/ppermute | solution.py:21
  226.2 2.4 %collective-permute-start.10 = (bf16[32,512]{1,0:T(8,128)(2,1)S(1)}, bf16[32,512]{1,0:T(8,128)(2,1)S(1)}, u32[]{:S(2)}, u32[]{:S(2)}) collective-permute-start(bf16[32,512]{1,0:T(8,128)(2,1)S(1)} %bitcast.152), channel_id=1, source_target_pairs={{0,32},{32,0},{1,33},{33,1},{2,34},{34,2},{3,35},{35,3},{4,36},{36... | collective-permute-start | bytes 98312 | tf_op jit(solution)/shard_map/ppermute | solution.py:21
  228.7 3.8 %collective-permute-start.9 = (bf16[32,512]{1,0:T(8,128)(2,1)S(1)}, bf16[32,512]{1,0:T(8,128)(2,1)S(1)}, u32[]{:S(2)}, u32[]{:S(2)}) collective-permute-start(bf16[32,512]{1,0:T(8,128)(2,1)S(1)} %bitcast.151), channel_id=1, source_target_pairs={{0,256},{256,0},{1,257},{257,1},{2,258},{258,2},{3,259},{259,3},{4... | collective-permute-start | bytes 98312 | tf_op jit(solution)/shard_map/ppermute | solution.py:21
  232.5 3.4 %collective-permute-done.10 = bf16[32,512]{1,0:T(8,128)(2,1)S(1)} collective-permute-done((bf16[32,512]{1,0:T(8,128)(2,1)S(1)}, bf16[32,512]{1,0:T(8,128)(2,1)S(1)}, u32[]{:S(2)}, u32[]{:S(2)}) %collective-permute-start.10) | collective-permute-done | bytes 32800 | tf_op jit(solution)/shard_map/ppermute | solution.py:21
  (165 shorter events, 45.9 us)
Async XLA Ops:
  0.0 19.0 %copy-start.16 = (bf16[2,32,512]{2,1,0:T(8,128)(2,1)S(1)}, bf16[2,32,512]{2,1,0:T(8,128)(2,1)}, u32[]{:S(2)}) copy-start(bf16[2,32,512]{2,1,0:T(8,128)(2,1)} %param.8) | copy-start | bytes 196612
  3.1 14.5 %collective-permute-start = (bf16[80,512]{1,0:T(8,128)(2,1)S(1)}, bf16[80,512]{1,0:T(8,128)(2,1)S(1)}, u32[]{:S(2)}, u32[]{:S(2)}) collective-permute-start(bf16[80,512]{1,0:T(8,128)(2,1)S(1)} %fusion.49), channel_id=1, source_target_pairs={{0,32},{32,0},{1,33},{33,1},{2,34},{34,2},{3,35},{35,3},{4,36},{36... | collective-permute-start | bytes 245768 | tf_op jit(solution)/shard_map/ppermute | solution.py:21
  19.5 10.0 %collective-permute-start.1 = (bf16[2,64,512]{2,1,0:T(8,128)(2,1)S(1)}, bf16[2,64,512]{2,1,0:T(8,128)(2,1)S(1)}, u32[]{:S(2)}, u32[]{:S(2)}) collective-permute-start(bf16[2,64,512]{2,1,0:T(8,128)(2,1)S(1)} %bitcast.143), channel_id=1, source_target_pairs={{0,256},{256,0},{1,257},{257,1},{2,258},{258,2},{3,259},{259,3},{4... | collective-permute-start | bytes 393224 | tf_op jit(solution)/shard_map/ppermute | solution.py:21
  31.5 12.0 %copy-start = (bf16[1,192,4096]{2,1,0:T(8,128)(2,1)S(1)}, bf16[1,192,4096]{2,1,0:T(8,128)(2,1)}, u32[]{:S(2)}) copy-start(bf16[1,192,4096]{2,1,0:T(8,128)(2,1)} %param.9) | copy-start | bytes 4718596
  31.5 49.8 %all-to-all-start.2 = ((bf16[32,16,1024]{2,1,0:T(8,128)(2,1)}), bf16[32,16,1024]{2,1,0:T(8,128)(2,1)}, u32[]{:S(2)}, u32[]{:S(2)}) async-start(bf16[32,16,1024]{2,1,0:T(8,128)(2,1)} %fusion.25), calls=%async_computation.2 | async-start | bytes 2097152 | tf_op jit(solution)/shard_map/all_to_all | solution.py:113
  58.8 19.1 %collective-permute-start.2 = (bf16[2,192,1024]{2,1,0:T(8,128)(2,1)}, bf16[2,192,1024]{2,1,0:T(8,128)(2,1)}, u32[]{:S(2)}, u32[]{:S(2)}) collective-permute-start(bf16[2,192,1024]{2,1,0:T(8,128)(2,1)} %pad_maximum_fusion), channel_id=1, source_target_pairs={{0,64},{64,0},{1,65},{65,1},{2,66},{66,2},{3,67},{67,3},{4,68},{68... | collective-permute-start | bytes 2359304 | tf_op jit(solution)/shard_map/ppermute | solution.py:21
  75.6 5.7 %collective-permute-start.6 = (bf16[2,192,1024]{2,1,0:T(8,128)(2,1)}, bf16[2,192,1024]{2,1,0:T(8,128)(2,1)S(1)}, u32[]{:S(2)}, u32[]{:S(2)}) collective-permute-start(bf16[2,192,1024]{2,1,0:T(8,128)(2,1)} %pad_maximum_fusion.4), channel_id=1, source_target_pairs={{0,64},{64,0},{1,65},{65,1},{2,66},{66,2},{3,67},{67,3},{4,68},{68... | collective-permute-start | bytes 2359304 | tf_op jit(solution)/shard_map/ppermute | solution.py:21
  79.1 21.5 %collective-permute-start.3 = (bf16[2,192,1024]{2,1,0:T(8,128)(2,1)S(1)}, bf16[2,192,1024]{2,1,0:T(8,128)(2,1)}, u32[]{:S(2)}, u32[]{:S(2)}) collective-permute-start(bf16[2,192,1024]{2,1,0:T(8,128)(2,1)S(1)} %pad_maximum_fusion.1), channel_id=1, source_target_pairs={{0,128},{128,0},{1,129},{129,1},{2,130},{130,2},{3,131},{131,3},{4... | collective-permute-start | bytes 2359304 | tf_op jit(solution)/shard_map/ppermute | solution.py:21
  81.3 20.4 %copy-start.4 = (bf16[2,192,1024]{2,1,0:T(8,128)(2,1)}, bf16[2,192,1024]{2,1,0:T(8,128)(2,1)S(1)}, u32[]{:S(2)}) copy-start(bf16[2,192,1024]{2,1,0:T(8,128)(2,1)S(1)} %collective-permute-done.6) | copy-start | bytes 2359300
  81.3 57.3 %all-to-all-start = ((bf16[32,16,1024]{2,1,0:T(8,128)(2,1)}), bf16[32,16,1024]{2,1,0:T(8,128)(2,1)}, u32[]{:S(2)}, u32[]{:S(2)}) async-start(bf16[32,16,1024]{2,1,0:T(8,128)(2,1)} %fusion.22), calls=%async_computation | async-start | bytes 2097152 | tf_op jit(solution)/shard_map/all_to_all | solution.py:113
  104.0 5.3 %collective-permute-start.12 = (bf16[512,384]{1,0:T(8,128)(2,1)S(1)}, bf16[512,384]{1,0:T(8,128)(2,1)S(1)}, u32[]{:S(2)}, u32[]{:S(2)}) collective-permute-start(bf16[512,384]{1,0:T(8,128)(2,1)S(1)} %fusion.6), channel_id=1, source_target_pairs={{0,64},{64,0},{1,65},{65,1},{2,66},{66,2},{3,67},{67,3},{4,68},{68... | collective-permute-start | bytes 1179656 | tf_op jit(solution)/shard_map/ppermute | solution.py:21
  106.1 22.2 %collective-permute-start.7 = (bf16[2,192,1024]{2,1,0:T(8,128)(2,1)S(1)}, bf16[2,192,1024]{2,1,0:T(8,128)(2,1)S(1)}, u32[]{:S(2)}, u32[]{:S(2)}) collective-permute-start(bf16[2,192,1024]{2,1,0:T(8,128)(2,1)S(1)} %pad_maximum_fusion.5), channel_id=1, source_target_pairs={{0,128},{128,0},{1,129},{129,1},{2,130},{130,2},{3,131},{131,3},{4... | collective-permute-start | bytes 2359304 | tf_op jit(solution)/shard_map/ppermute | solution.py:21
  109.4 18.9 %copy-start.5 = (bf16[2,192,1024]{2,1,0:T(8,128)(2,1)S(1)}, bf16[2,192,1024]{2,1,0:T(8,128)(2,1)}, u32[]{:S(2)}) copy-start(bf16[2,192,1024]{2,1,0:T(8,128)(2,1)} %copy-done.4) | copy-start | bytes 2359300
  111.4 24.9 %collective-permute-start.13 = (bf16[512,384]{1,0:T(8,128)(2,1)S(1)}, bf16[512,384]{1,0:T(8,128)(2,1)S(1)}, u32[]{:S(2)}, u32[]{:S(2)}) collective-permute-start(bf16[512,384]{1,0:T(8,128)(2,1)S(1)} %get-tuple-element.68), channel_id=1, source_target_pairs={{0,128},{128,0},{1,129},{129,1},{2,130},{130,2},{3,131},{131,3},{4... | collective-permute-start | bytes 1179656 | tf_op jit(solution)/shard_map/ppermute | solution.py:21
  136.6 7.3 %collective-permute-start.14 = (bf16[512,384]{1,0:T(8,128)(2,1)S(1)}, bf16[512,384]{1,0:T(8,128)(2,1)S(1)}, u32[]{:S(2)}, u32[]{:S(2)}) collective-permute-start(bf16[512,384]{1,0:T(8,128)(2,1)S(1)} %multiply_convert_fusion), channel_id=1, source_target_pairs={{0,64},{64,0},{1,65},{65,1},{2,66},{66,2},{3,67},{67,3},{4,68},{68... | collective-permute-start | bytes 1179656 | tf_op jit(solution)/shard_map/ppermute | solution.py:21
  141.5 14.6 %collective-permute-start.4 = (bf16[512,384]{1,0:T(8,128)(2,1)}, bf16[512,384]{1,0:T(8,128)(2,1)}, u32[]{:S(2)}, u32[]{:S(2)}) collective-permute-start(bf16[512,384]{1,0:T(8,128)(2,1)} %fusion.7), channel_id=1, source_target_pairs={{0,64},{64,0},{1,65},{65,1},{2,66},{66,2},{3,67},{67,3},{4,68},{68... | collective-permute-start | bytes 1179656 | tf_op jit(solution)/shard_map/ppermute | solution.py:21
  146.3 38.3 %all-to-all-start.3 = ((bf16[32,16,1024]{2,1,0:T(8,128)(2,1)}), bf16[32,16,1024]{2,1,0:T(8,128)(2,1)S(1)}, u32[]{:S(2)}, u32[]{:S(2)}) async-start(bf16[32,16,1024]{2,1,0:T(8,128)(2,1)} %bitcast.33), calls=%async_computation.3 | async-start | bytes 2097152 | tf_op jit(solution)/shard_map/all_to_all | solution.py:123
  158.2 12.6 %collective-permute-start.5 = (bf16[512,384]{1,0:T(8,128)(2,1)S(1)}, bf16[512,384]{1,0:T(8,128)(2,1)S(1)}, u32[]{:S(2)}, u32[]{:S(2)}) collective-permute-start(bf16[512,384]{1,0:T(8,128)(2,1)S(1)} %get-tuple-element.70), channel_id=1, source_target_pairs={{0,128},{128,0},{1,129},{129,1},{2,130},{130,2},{3,131},{131,3},{4... | collective-permute-start | bytes 1179656 | tf_op jit(solution)/shard_map/ppermute | solution.py:21
  172.0 3.6 %collective-permute-start.8 = (bf16[512,384]{1,0:T(8,128)(2,1)S(1)}, bf16[512,384]{1,0:T(8,128)(2,1)S(1)}, u32[]{:S(2)}, u32[]{:S(2)}) collective-permute-start(bf16[512,384]{1,0:T(8,128)(2,1)S(1)} %multiply_convert_fusion.1), channel_id=1, source_target_pairs={{0,64},{64,0},{1,65},{65,1},{2,66},{66,2},{3,67},{67,3},{4,68},{68... | collective-permute-start | bytes 1179656 | tf_op jit(solution)/shard_map/ppermute | solution.py:21
  178.1 12.1 %copy-start.11 = (s32[32,2,8]{2,0,1:T(8,128)S(1)}, s32[32,2,8]{2,0,1:T(8,128)}, u32[]{:S(2)}) copy-start(s32[32,2,8]{2,0,1:T(8,128)} %copy-done.10) | copy-start | bytes 6148
  178.1 12.1 %copy-start.9 = (s32[32,2,8]{2,0,1:T(8,128)S(1)}, s32[32,2,8]{2,0,1:T(8,128)}, u32[]{:S(2)}) copy-start(s32[32,2,8]{2,0,1:T(8,128)} %copy-done.8) | copy-start | bytes 6148
  178.1 12.2 %copy-start.19 = (f32[2,2,256]{2,1,0:T(2,128)S(1)}, f32[2,2,256]{2,1,0:T(2,128)}, u32[]{:S(2)}) copy-start(f32[2,2,256]{2,1,0:T(2,128)} %get-tuple-element.49) | copy-start | bytes 12292
  178.1 12.2 %copy-start.15 = (f32[2,32,256]{2,1,0:T(8,128)S(1)}, f32[2,32,256]{2,1,0:T(8,128)}, u32[]{:S(2)}) copy-start(f32[2,32,256]{2,1,0:T(8,128)} %copy-done.14) | copy-start | bytes 196612
  178.1 12.2 %copy-start.18 = (pred[2,32,256]{2,1,0:T(8,128)(4,1)S(1)}, pred[2,32,256]{2,1,0:T(8,128)(4,1)}, u32[]{:S(2)}) copy-start(pred[2,32,256]{2,1,0:T(8,128)(4,1)} %copy-done.17) | copy-start | bytes 49156
  178.1 12.6 %copy-start.13 = (f32[2,32,256]{2,1,0:T(8,128)S(1)}, f32[2,32,256]{2,1,0:T(8,128)}, u32[]{:S(2)}) copy-start(f32[2,32,256]{2,1,0:T(8,128)} %copy-done.12) | copy-start | bytes 196612
  184.6 33.0 %all-to-all-start.1 = ((bf16[32,16,1024]{2,1,0:T(8,128)(2,1)}), bf16[32,16,1024]{2,1,0:T(8,128)(2,1)S(1)}, u32[]{:S(2)}, u32[]{:S(2)}) async-start(bf16[32,16,1024]{2,1,0:T(8,128)(2,1)} %bitcast.22), calls=%async_computation.1 | async-start | bytes 2097152 | tf_op jit(solution)/shard_map/all_to_all | solution.py:123
  192.9 35.8 %collective-permute-start.17 = (bf16[32,512]{1,0:T(8,128)(2,1)S(1)}, bf16[32,512]{1,0:T(8,128)(2,1)S(1)}, u32[]{:S(2)}, u32[]{:S(2)}) collective-permute-start(bf16[32,512]{1,0:T(8,128)(2,1)S(1)} %bitcast.150), channel_id=1, source_target_pairs={{0,288},{32,256},{256,32},{288,0},{1,289},{33,257},{257,33},{289,1... | collective-permute-start | bytes 98312 | tf_op jit(solution)/shard_map/ppermute | solution.py:21
  199.8 32.6 %collective-permute-start.16 = (bf16[32,512]{1,0:T(8,128)(2,1)S(1)}, bf16[32,512]{1,0:T(8,128)(2,1)S(1)}, u32[]{:S(2)}, u32[]{:S(2)}) collective-permute-start(bf16[32,512]{1,0:T(8,128)(2,1)S(1)} %bitcast.149), channel_id=1, source_target_pairs={{0,32},{32,0},{1,33},{33,1},{2,34},{34,2},{3,35},{35,3},{4,36},{36... | collective-permute-start | bytes 98312 | tf_op jit(solution)/shard_map/ppermute | solution.py:21
  202.3 30.2 %collective-permute-start.15 = (bf16[32,512]{1,0:T(8,128)(2,1)S(1)}, bf16[32,512]{1,0:T(8,128)(2,1)S(1)}, u32[]{:S(2)}, u32[]{:S(2)}) collective-permute-start(bf16[32,512]{1,0:T(8,128)(2,1)S(1)} %bitcast.148), channel_id=1, source_target_pairs={{0,256},{256,0},{1,257},{257,1},{2,258},{258,2},{3,259},{259,3},{4... | collective-permute-start | bytes 98312 | tf_op jit(solution)/shard_map/ppermute | solution.py:21
  219.3 13.2 %collective-permute-start.11 = (bf16[32,512]{1,0:T(8,128)(2,1)S(1)}, bf16[32,512]{1,0:T(8,128)(2,1)S(1)}, u32[]{:S(2)}, u32[]{:S(2)}) collective-permute-start(bf16[32,512]{1,0:T(8,128)(2,1)S(1)} %bitcast.153), channel_id=1, source_target_pairs={{0,288},{32,256},{256,32},{288,0},{1,289},{33,257},{257,33},{289,1... | collective-permute-start | bytes 98312 | tf_op jit(solution)/shard_map/ppermute | solution.py:21
  226.2 9.7 %collective-permute-start.10 = (bf16[32,512]{1,0:T(8,128)(2,1)S(1)}, bf16[32,512]{1,0:T(8,128)(2,1)S(1)}, u32[]{:S(2)}, u32[]{:S(2)}) collective-permute-start(bf16[32,512]{1,0:T(8,128)(2,1)S(1)} %bitcast.152), channel_id=1, source_target_pairs={{0,32},{32,0},{1,33},{33,1},{2,34},{34,2},{3,35},{35,3},{4,36},{36... | collective-permute-start | bytes 98312 | tf_op jit(solution)/shard_map/ppermute | solution.py:21
  228.7 7.3 %collective-permute-start.9 = (bf16[32,512]{1,0:T(8,128)(2,1)S(1)}, bf16[32,512]{1,0:T(8,128)(2,1)S(1)}, u32[]{:S(2)}, u32[]{:S(2)}) collective-permute-start(bf16[32,512]{1,0:T(8,128)(2,1)S(1)} %bitcast.151), channel_id=1, source_target_pairs={{0,256},{256,0},{1,257},{257,1},{2,258},{258,2},{3,259},{259,3},{4... | collective-permute-start | bytes 98312 | tf_op jit(solution)/shard_map/ppermute | solution.py:21
  (11 other events, 51.6 us)

commit v4 on v3

--- a/solution.py
+++ b/solution.py
@@ -1,6 +1,8 @@
 import jax
 import jax.numpy as jnp
 from jax import lax
+from jax.experimental import pallas as pl
+from jax.experimental.pallas import tpu as pltpu
 from jax.sharding import Mesh
 from jax.sharding import PartitionSpec as P
 
@@ -21,25 +23,46 @@
     return lax.ppermute(array, axes, [(i, last - i) for i in range(last + 1)])
 
 
-def recut(weight):
-    hidden, feats = weight.shape
-    m, k = lax.axis_index("m"), lax.axis_index("k")
-    blocks = weight.reshape(hidden, 2, 2, 2, feats // 8)
+def cut_kernel(place, gate, down, *outs):
+    m, k = place[0], place[1]
+    width = gate.shape[2] // 8
+    for which, weight in enumerate((gate, down)):
+        for dm in range(2):
+            for dk in range(2):
+                out = outs[4 * which + 2 * dm + dk]
+                for p in range(2):
+                    at = (4 * p + 2 * (m ^ dm) + (k ^ dk)) * width
+                    out[:, p * width : (p + 1) * width] = weight[0, :, pl.ds(pl.multiple_of(at, width), width)]
 
-    def cut(at_m, at_k):
-        start = (0, 0, at_m, at_k, 0)
-        return lax.dynamic_slice(blocks, start, (hidden, 2, 1, 1, feats // 8)).reshape(hidden, feats // 4)
 
-    there = swap(jnp.stack([cut(m, 1 - k), cut(1 - m, 1 - k)]), "k")
-    near_own, near_other = cut(m, k), there[0]
-    far = swap(jnp.stack([cut(1 - m, k), there[1]]), "m")
+def cut_weights(gate, down):
+    _, hidden, feats = gate.shape
+    place = jnp.stack([lax.axis_index("m"), lax.axis_index("k")]).astype(jnp.int32)
+    vmem = pl.BlockSpec(memory_space=pltpu.VMEM)
+    parts = pl.pallas_call(
+        cut_kernel,
+        out_shape=[jax.ShapeDtypeStruct((hidden, feats // 4), BF)] * 8,
+        in_specs=[pl.BlockSpec(memory_space=pltpu.SMEM), vmem, vmem],
+        out_specs=[vmem] * 8,
+        compiler_params=pltpu.CompilerParams(vmem_limit_bytes=32 << 20),
+        cost_estimate=pl.CostEstimate(flops=0, bytes_accessed=4 * gate.size * 2, transcendentals=0),
+    )(place, gate, down)
+    return parts[:4], parts[4:]
+
+
+def recut(parts):
+    m = lax.axis_index("m")
+    mine, for_k, for_m, for_mk = parts
+    far_own = swap(for_m, "m")
+    near_other = swap(for_k, "k")
+    far_other = swap(for_mk, "m", "k")
 
     def order(near, far):
         first = jnp.where(m == 0, near, far)
         second = jnp.where(m == 0, far, near)
         return jnp.concatenate([first, second], axis=0)
 
-    return order(near_own, far[0]), order(near_other, far[1])
+    return order(mine, far_own), order(near_other, far_other)
 
 
 def slots(codes, weights, plan):
@@ -78,28 +101,24 @@
     return high.astype(BF), mid.astype(BF), (value - high - mid).astype(BF)
 
 
-def both(first, second, axis_name, axis):
-    at = lax.axis_index(axis_name)
-    return jnp.stack([jnp.where(at == 0, first, second), jnp.where(at == 0, second, first)], axis)
-
-
 def local(tokens, w_gate, w_down, expert_ids, route_weight, replica_pick, old_plan, new_plan):
     batches, group, feats = tokens.shape
     peers = lax.axis_size("y") * lax.axis_size("x")
-    zh, p = lax.axis_index("zh"), lax.axis_index("p")
     code = (2 * expert_ids + (replica_pick & 1)).astype(BF)
     parts = [code, *thirds(route_weight)]
     info = jnp.stack(parts).reshape(-1, feats)
-    sent = jnp.concatenate([tokens.reshape(-1, feats), jnp.pad(info, ((0, 16 - info.shape[0]), (0, 0)))])
-    came = swap(sent, "zh")
-    tokens = both(tokens, came[: batches * group].reshape(tokens.shape), "zh", 1)
-    tokens = tokens.reshape(batches, 2 * group, feats)
-    far_info = came[batches * group :][: info.shape[0]]
-    info = both(info, far_info, "zh", 0).reshape(2, 4, batches, group * TOPK).astype(F32)
+    count = info.shape[0]
+    sent = jnp.concatenate([tokens.reshape(-1, feats), jnp.pad(info, ((0, 16 - count), (0, 0)))])
+    sent = jnp.broadcast_to(sent[None], (4, *sent.shape))
+    came = lax.all_to_all(sent, ("p", "zh"), 0, 0, tiled=True).reshape(2, 2, -1, feats)
+    tok = came[:, :, : batches * group].reshape(2, 2, batches, group, feats)
+    tok = tok.transpose(2, 1, 3, 0, 4).reshape(batches, 2 * group, 2 * feats)
+    info = came[0, :, batches * group : batches * group + count]
+    info = info.reshape(2, 4, batches, group * TOPK).astype(F32)
     code = info[:, 0].astype(jnp.int32)
     weight = info[:, 1] + info[:, 2] + info[:, 3]
-    tok = both(tokens, swap(tokens, "p"), "p", 2).reshape(batches, 2 * group, 2 * feats)
 
+    gate_parts, down_parts = cut_weights(w_gate, w_down)
     outputs = []
     for index, plan in ((0, old_plan), (1, new_plan)):
         slot_token, slot_weight = slots(code[:, index], weight[:, index], plan)
@@ -107,9 +126,9 @@
         rows = dot(pick.astype(BF), tok[index], ((1,), (0,)), BF)
         rows = rows.reshape(peers, -1, rows.shape[1])
         if index == 0:
-            rows, w_gate, w_down = lax.optimization_barrier((rows, w_gate, w_down))
-            gate_own, gate_other = recut(w_gate[0])
-            down_own, down_other = recut(w_down[0])
+            rows, gate_parts, down_parts = lax.optimization_barrier((rows, gate_parts, down_parts))
+            gate_own, gate_other = recut(gate_parts)
+            down_own, down_other = recut(down_parts)
         rows = lax.all_to_all(rows, ("y", "x"), 0, 0, tiled=True).reshape(-1, rows.shape[2])
 
         send = dot(rows, gate_other, ((1,), (1,)), BF)
@@ -125,18 +144,10 @@
         scale = jnp.where(pick, slot_weight[:, None], 0.0)
         high, low, _ = thirds(scale)
         mixed = dot(high, back, ((0,), (0,))) + dot(low, back, ((0,), (0,)))
-        mixed = mixed.reshape(2, group, 2, feats)
-
-        def block(other_zh, other_p):
-            start = (zh ^ other_zh, 0, p ^ other_p, 0)
-            return lax.dynamic_slice(mixed, start, (1, group, 1, feats)).reshape(group, feats)
-
-        total = block(0, 0)
-        total = total + swap(block(0, 1).astype(BF), "p").astype(F32)
-        total = total + swap(block(1, 0).astype(BF), "zh").astype(F32)
-        total = total + swap(block(1, 1).astype(BF), "p", "zh").astype(F32)
-        outputs.append(total.astype(BF))
-    return jnp.stack(outputs)
+        outputs.append(mixed.astype(BF).reshape(2, group, 2, feats))
+    mixed = jnp.stack(outputs).transpose(3, 1, 0, 2, 4).reshape(4, batches * group, feats)
+    terms = lax.all_to_all(mixed, ("p", "zh"), 0, 0, tiled=True)
+    return jnp.sum(terms.astype(F32), axis=0).astype(BF).reshape(batches, group, feats)
 
 
 def solution(mesh):

time: 238 us -> 206 us (0.87)
  starting transfers between devices: 100 us -> 76.2 us
  local copies, waits for them, and re-layouts: 32.5 us -> 10.4 us
  blocking collectives: 0 us -> 12.5 us
  waiting for transfers between devices: 69 us -> 75.5 us
  other arithmetic: 13.7 us -> 9 us
    ppermute x18 -> x12, starting transfers between devices: 64.8 us -> 34.7 us  [swap(): return lax.ppermute(array, axes, [(i, last - i) for i in range(last + 1)])]
    ppermute x18 -> x12, waiting for transfers between devices: 51.1 us -> 24.8 us  [swap(): return lax.ppermute(array, axes, [(i, last - i) for i in range(last + 1)])]
    dynamic_slice x6 -> x0, local copies, waits for them, and re-layouts: 22.9 us -> none  [the longest x2 22.4 us: cut(): lax.dynamic_slice(blocks, start, (hidden, 2, 1, 1, feats // 8))]
    all_to_all x2, waiting for transfers between devices: 17.9 us -> 32.6 us  [local(): lax.all_to_all(out, ('y', 'x'), 0, 0, tiled=True).reshape(-1, out.shape[2])]
    all_to_all x0 -> x1, blocking collectives: none -> 12.5 us  [local(): terms = lax.all_to_all(mixed, ('p', 'zh'), 0, 0, tiled=True)]
    all_to_all x0 -> x1, waiting for transfers between devices: none -> 11.4 us  [local(): lax.all_to_all(sent, ('p', 'zh'), 0, 0, tiled=True).reshape(2, 2, -1, feats)]
    all_to_all x0 -> x1, starting transfers between devices: none -> 10.3 us  [local(): lax.all_to_all(sent, ('p', 'zh'), 0, 0, tiled=True).reshape(2, 2, -1, feats)]
    all_to_all x2, waiting for transfers between devices: 0.01 us -> 6.64 us  [local(): lax.all_to_all(rows, ('y', 'x'), 0, 0, tiled=True)]
  transfers between devices with their start and end apart: 22 -> 17, of which waited for: 10 -> 8; matrix products, arithmetic and copies ran while one was open for 25% -> 10% of each run, Pallas kernels for 0% -> 0%
where the time goes in v4:
time: 206 us; the launch traced here: 205 us
  starting transfers between devices  76.2 us (37%)
  waiting for transfers between devices  75.5 us (37%)
  matrix products  20.1 us (10%)
  blocking collectives  12.5 us (6%)
  local copies, waits for them, and re-layouts  10.4 us (5%)
  other arithmetic  9 us (4%)
    ppermute x12, starting transfers between devices, swap(): return lax.ppermute(array, axes, [(i, last - i) for i in range(last + 1)])  34.7 us
    all_to_all x2, waiting for transfers between devices, local(): lax.all_to_all(out, ('y', 'x'), 0, 0, tiled=True).reshape(-1, out.shape[2])  32.6 us
    ppermute x12, waiting for transfers between devices, swap(): return lax.ppermute(array, axes, [(i, last - i) for i in range(last + 1)])  24.8 us
    dot_general x18, matrix products, dot(): return lax.dot_general(a, b, (dims, ((), ())), preferred_element_type=out)  20.1 us
    all_to_all x2, starting transfers between devices, local(): lax.all_to_all(rows, ('y', 'x'), 0, 0, tiled=True)  15.9 us
    all_to_all x2, starting transfers between devices, local(): lax.all_to_all(out, ('y', 'x'), 0, 0, tiled=True).reshape(-1, out.shape[2])  15.3 us
    all_to_all x1, blocking collectives, local(): terms = lax.all_to_all(mixed, ('p', 'zh'), 0, 0, tiled=True)  12.5 us
    all_to_all x1, waiting for transfers between devices, local(): lax.all_to_all(sent, ('p', 'zh'), 0, 0, tiled=True).reshape(2, 2, -1, feats)  11.4 us
  transfers between devices with their start and end apart: 17, of which 8 were waited for; matrix products, arithmetic and copies ran while one was open for 10% of the time, Pallas kernels for 0%

profile of v4, /device:TPU:2, one launch (start us, length us, event | category | flops | bytes accessed | tf_op | source)
XLA Modules:
  0.0 205.2 jit_solution(2326931337684858758)
XLA Ops:
  3.8 10.3 %all-to-all-start = ((bf16[4,80,512]{2,1,0:T(8,128)(2,1)}), bf16[4,80,512]{2,1,0:T(8,128)(2,1)S(1)}, u32[]{:S(2)}, u32[]{:S(2)}) async-start(bf16[4,80,512]{2,1,0:T(8,128)(2,1)} %broadcast_in_dim.131), calls=%async_computation | async-start | bytes 655360 | tf_op jit(solution)/shard_map/all_to_all | solution.py:113
  15.1 11.4 %all-to-all-done = bf16[4,80,512]{2,1,0:T(8,128)(2,1)S(1)} async-done(((bf16[4,80,512]{2,1,0:T(8,128)(2,1)}), bf16[4,80,512]{2,1,0:T(8,128)(2,1)S(1)}, u32[]{:S(2)}, u32[]{:S(2)}) %all-to-all-start) | async-done | bytes 327712 | tf_op jit(solution)/shard_map/all_to_all | solution.py:113
  29.0 2.2 %select_reduce_fusion.3 = (s32[2,32,8]{2,1,0:T(8,128)S(1)}, s32[2,32,8]{2,1,0:T(8,128)S(1)}) fusion(s32[256]{0:T(256)S(1)} %fusion.57, f32[2,32,256]{2,1,0:T(8,128)S(1)} %fusion.16, pred[2,32,256]{2,1,0:T(8,128)(4,1)S(1)} %fusion.46, f32[2,32,256]{2,1,0:T(8,128)S(1)} %fusion.13, pred[2,32,256]{2,1,0:T(8,128)(4,1)S(1)} %fusion.45), kind=kLoop, calls=%fused_computation.20 | loop fusion | flops 1047552 | bytes 168960 | tf_op jit(solution)/shard_map/reduce_sum | solution.py:90
  34.3 10.3 %all-to-all-start.3 = ((bf16[32,16,1024]{2,1,0:T(8,128)(2,1)}), bf16[32,16,1024]{2,1,0:T(8,128)(2,1)}, u32[]{:S(2)}, u32[]{:S(2)}) async-start(bf16[32,16,1024]{2,1,0:T(8,128)(2,1)} %fusion.23), calls=%async_computation.3 | async-start | bytes 2097152 | tf_op jit(solution)/shard_map/all_to_all | solution.py:132
  53.5 1.9 collective-permute-start.1
  55.4 3.6 %collective-permute-start.2 = (bf16[192,1024]{1,0:T(8,128)(2,1)S(1)}, bf16[192,1024]{1,0:T(8,128)(2,1)S(1)}, u32[]{:S(2)}, u32[]{:S(2)}) collective-permute-start(bf16[192,1024]{1,0:T(8,128)(2,1)S(1)} %copy-done.13), channel_id=1, source_target_pairs={{0,192},{64,128},{128,64},{192,0},{1,193},{65,129},{129,65},{193,1... | collective-permute-start | bytes 1179656 | tf_op jit(solution)/shard_map/ppermute | solution.py:23
  59.1 2.3 %collective-permute-start = (bf16[192,1024]{1,0:T(8,128)(2,1)S(1)}, bf16[192,1024]{1,0:T(8,128)(2,1)S(1)}, u32[]{:S(2)}, u32[]{:S(2)}) collective-permute-start(bf16[192,1024]{1,0:T(8,128)(2,1)S(1)} %copy-done.11), channel_id=1, source_target_pairs={{0,128},{128,0},{1,129},{129,1},{2,130},{130,2},{3,131},{131,3},{4... | collective-permute-start | bytes 1179656 | tf_op jit(solution)/shard_map/ppermute | solution.py:23
  61.4 6.6 %all-to-all-done.3 = bf16[32,16,1024]{2,1,0:T(8,128)(2,1)} async-done(((bf16[32,16,1024]{2,1,0:T(8,128)(2,1)}), bf16[32,16,1024]{2,1,0:T(8,128)(2,1)}, u32[]{:S(2)}, u32[]{:S(2)}) %all-to-all-start.3) | async-done | bytes 1048608 | tf_op jit(solution)/shard_map/all_to_all | solution.py:132
  68.0 5.6 %all-to-all-start.1 = ((bf16[32,16,1024]{2,1,0:T(8,128)(2,1)}), bf16[32,16,1024]{2,1,0:T(8,128)(2,1)}, u32[]{:S(2)}, u32[]{:S(2)}) async-start(bf16[32,16,1024]{2,1,0:T(8,128)(2,1)} %fusion.20), calls=%async_computation.1 | async-start | bytes 2097152 | tf_op jit(solution)/shard_map/all_to_all | solution.py:132
  73.8 2.2 %fusion.6 = bf16[512,384]{1,0:T(8,128)(2,1)S(1)} fusion(bf16[512,1024]{1,0:T(8,128)(2,1)} %bitcast.21, bf16[192,1024]{1,0:T(8,128)(2,1)S(1)} %get-tuple-element.54, bf16[192,1024]{1,0:T(8,128)(2,1)S(1)} %get-tuple-element.53), kind=kOutput, calls=%fused_computation.26 | convolution fusion | flops 404226048 | bytes 2228224 | tf_op jit(solution)/shard_map/dot_general | solution.py:18
  76.0 1.9 collective-permute-start.9
  78.0 7.5 %collective-permute-start.5 = (bf16[192,1024]{1,0:T(8,128)(2,1)S(1)}, bf16[192,1024]{1,0:T(8,128)(2,1)S(1)}, u32[]{:S(2)}, u32[]{:S(2)}) collective-permute-start(bf16[192,1024]{1,0:T(8,128)(2,1)S(1)} %copy-done.9), channel_id=1, source_target_pairs={{0,128},{128,0},{1,129},{129,1},{2,130},{130,2},{3,131},{131,3},{4... | collective-permute-start | bytes 1179656 | tf_op jit(solution)/shard_map/ppermute | solution.py:23
  85.6 2.0 fusion.75
  87.6 1.9 collective-permute-start.10
  89.6 2.1 %collective-permute-start.7 = (bf16[192,1024]{1,0:T(8,128)(2,1)S(1)}, bf16[192,1024]{1,0:T(8,128)(2,1)S(1)}, u32[]{:S(2)}, u32[]{:S(2)}) collective-permute-start(bf16[192,1024]{1,0:T(8,128)(2,1)S(1)} %copy-done.7), channel_id=1, source_target_pairs={{0,64},{64,0},{1,65},{65,1},{2,66},{66,2},{3,67},{67,3},{4,68},{68... | collective-permute-start | bytes 1179656 | tf_op jit(solution)/shard_map/ppermute | solution.py:23
  91.7 3.8 %collective-permute-start.8 = (bf16[192,1024]{1,0:T(8,128)(2,1)S(1)}, bf16[192,1024]{1,0:T(8,128)(2,1)S(1)}, u32[]{:S(2)}, u32[]{:S(2)}) collective-permute-start(bf16[192,1024]{1,0:T(8,128)(2,1)S(1)} %copy-done.5), channel_id=1, source_target_pairs={{0,192},{64,128},{128,64},{192,0},{1,193},{65,129},{129,65},{193,1... | collective-permute-start | bytes 1179656 | tf_op jit(solution)/shard_map/ppermute | solution.py:23
  95.6 8.2 %collective-permute-done.10 = bf16[512,384]{1,0:T(8,128)(2,1)S(1)} collective-permute-done((bf16[512,384]{1,0:T(8,128)(2,1)S(1)}, bf16[512,384]{1,0:T(8,128)(2,1)S(1)}, u32[]{:S(2)}, u32[]{:S(2)}) %collective-permute-start.10) | collective-permute-done | bytes 393248 | tf_op jit(solution)/shard_map/ppermute | solution.py:23
  104.1 1.9 collective-permute-start.11
  106.0 5.9 %collective-permute-done.8 = bf16[192,1024]{1,0:T(8,128)(2,1)S(1)} collective-permute-done((bf16[192,1024]{1,0:T(8,128)(2,1)S(1)}, bf16[192,1024]{1,0:T(8,128)(2,1)S(1)}, u32[]{:S(2)}, u32[]{:S(2)}) %collective-permute-start.8) | collective-permute-done | bytes 393248 | tf_op jit(solution)/shard_map/ppermute | solution.py:23
  111.9 2.9 %fusion.7 = bf16[512,384]{1,0:T(8,128)(2,1)} fusion(bf16[512,1024]{1,0:T(8,128)(2,1)} %bitcast.13, bf16[192,1024]{1,0:T(8,128)(2,1)} %copy-done.18, bf16[192,1024]{1,0:T(8,128)(2,1)} %copy-done.17), kind=kOutput, calls=%fused_computation.27 | convolution fusion | flops 404226048 | bytes 2228224 | tf_op jit(solution)/shard_map/dot_general | solution.py:18
  114.8 2.0 collective-permute-start.3
  117.6 1.7 add_convert_fusion
  119.3 9.8 %all-to-all-start.4 = ((bf16[32,16,1024]{2,1,0:T(8,128)(2,1)}), bf16[32,16,1024]{2,1,0:T(8,128)(2,1)S(1)}, u32[]{:S(2)}, u32[]{:S(2)}) async-start(bf16[32,16,1024]{2,1,0:T(8,128)(2,1)} %bitcast.22), calls=%async_computation.4 | async-start | bytes 2097152 | tf_op jit(solution)/shard_map/all_to_all | solution.py:142
  129.1 2.0 fusion.76
  131.1 3.5 %collective-permute-start.4 = (bf16[512,384]{1,0:T(8,128)(2,1)S(1)}, bf16[512,384]{1,0:T(8,128)(2,1)S(1)}, u32[]{:S(2)}, u32[]{:S(2)}) collective-permute-start(bf16[512,384]{1,0:T(8,128)(2,1)S(1)} %get-tuple-element.78), channel_id=1, source_target_pairs={{0,128},{128,0},{1,129},{129,1},{2,130},{130,2},{3,131},{131,3},{4... | collective-permute-start | bytes 1179656 | tf_op jit(solution)/shard_map/ppermute | solution.py:23
  134.7 9.2 %collective-permute-done.4 = bf16[512,384]{1,0:T(8,128)(2,1)S(1)} collective-permute-done((bf16[512,384]{1,0:T(8,128)(2,1)S(1)}, bf16[512,384]{1,0:T(8,128)(2,1)S(1)}, u32[]{:S(2)}, u32[]{:S(2)}) %collective-permute-start.4) | collective-permute-done | bytes 393248 | tf_op jit(solution)/shard_map/ppermute | solution.py:23
  144.2 2.1 %collective-permute-start.6 = (bf16[512,384]{1,0:T(8,128)(2,1)S(1)}, bf16[512,384]{1,0:T(8,128)(2,1)S(1)}, u32[]{:S(2)}, u32[]{:S(2)}) collective-permute-start(bf16[512,384]{1,0:T(8,128)(2,1)S(1)} %multiply_convert_fusion.1), channel_id=1, source_target_pairs={{0,64},{64,0},{1,65},{65,1},{2,66},{66,2},{3,67},{67,3},{4,68},{68... | collective-permute-start | bytes 1179656 | tf_op jit(solution)/shard_map/ppermute | solution.py:23
  148.5 1.7 add_convert_fusion.1
  150.2 7.5 %all-to-all-done.4 = bf16[32,16,1024]{2,1,0:T(8,128)(2,1)S(1)} async-done(((bf16[32,16,1024]{2,1,0:T(8,128)(2,1)}), bf16[32,16,1024]{2,1,0:T(8,128)(2,1)S(1)}, u32[]{:S(2)}, u32[]{:S(2)}) %all-to-all-start.4) | async-done | bytes 1048608 | tf_op jit(solution)/shard_map/all_to_all | solution.py:142
  157.7 5.6 %all-to-all-start.2 = ((bf16[32,16,1024]{2,1,0:T(8,128)(2,1)}), bf16[32,16,1024]{2,1,0:T(8,128)(2,1)S(1)}, u32[]{:S(2)}, u32[]{:S(2)}) async-start(bf16[32,16,1024]{2,1,0:T(8,128)(2,1)} %bitcast.14), calls=%async_computation.2 | async-start | bytes 2097152 | tf_op jit(solution)/shard_map/all_to_all | solution.py:142
  165.6 25.1 %all-to-all-done.2 = bf16[32,16,1024]{2,1,0:T(8,128)(2,1)S(1)} async-done(((bf16[32,16,1024]{2,1,0:T(8,128)(2,1)}), bf16[32,16,1024]{2,1,0:T(8,128)(2,1)S(1)}, u32[]{:S(2)}, u32[]{:S(2)}) %all-to-all-start.2) | async-done | bytes 1048608 | tf_op jit(solution)/shard_map/all_to_all | solution.py:142
  192.0 12.5 %all_to_all.30 = bf16[4,64,512]{2,1,0:T(8,128)(2,1)S(1)} all-to-all(bf16[4,64,512]{2,1,0:T(8,128)(2,1)S(1)} %bitcast.72), channel_id=1, replica_groups=mesh['p'=2,'m'=2,'k'=2,'zh'=2,'y'=8,'x'=4] {'p','zh'}, dimensions={0} | all-to-all | bytes 524288 | tf_op jit(solution)/shard_map/all_to_all | solution.py:149
  (144 shorter events, 26.9 us)
Async XLA Ops:
  3.8 22.7 %all-to-all-start = ((bf16[4,80,512]{2,1,0:T(8,128)(2,1)}), bf16[4,80,512]{2,1,0:T(8,128)(2,1)S(1)}, u32[]{:S(2)}, u32[]{:S(2)}) async-start(bf16[4,80,512]{2,1,0:T(8,128)(2,1)} %broadcast_in_dim.131), calls=%async_computation | async-start | bytes 655360 | tf_op jit(solution)/shard_map/all_to_all | solution.py:113
  32.8 11.9 %copy-start = (bf16[1,192,4096]{2,1,0:T(8,128)(2,1)S(1)}, bf16[1,192,4096]{2,1,0:T(8,128)(2,1)}, u32[]{:S(2)}) copy-start(bf16[1,192,4096]{2,1,0:T(8,128)(2,1)} %gate.1) | copy-start | bytes 4718596
  32.8 11.9 %copy-start.1 = (bf16[1,192,4096]{2,1,0:T(8,128)(2,1)S(1)}, bf16[1,192,4096]{2,1,0:T(8,128)(2,1)}, u32[]{:S(2)}) copy-start(bf16[1,192,4096]{2,1,0:T(8,128)(2,1)} %down.1) | copy-start | bytes 4718596
  34.3 33.8 %all-to-all-start.3 = ((bf16[32,16,1024]{2,1,0:T(8,128)(2,1)}), bf16[32,16,1024]{2,1,0:T(8,128)(2,1)}, u32[]{:S(2)}, u32[]{:S(2)}) async-start(bf16[32,16,1024]{2,1,0:T(8,128)(2,1)} %fusion.23), calls=%async_computation.3 | async-start | bytes 2097152 | tf_op jit(solution)/shard_map/all_to_all | solution.py:132
  44.7 6.1 %copy-start.16 = (bf16[1,2,32,2,512]{4,2,0,1,3:T(8,128)(2,1)S(1)}, bf16[1,2,32,2,512]{4,2,0,1,3:T(8,128)(2,1)}, u32[]{:S(2)}) copy-start(bf16[1,2,32,2,512]{4,2,0,1,3:T(8,128)(2,1)} %get-tuple-element.55) | copy-start | bytes 393220
  50.8 4.6 %copy-start.13 = (bf16[192,1024]{1,0:T(8,128)(2,1)S(1)}, bf16[192,1024]{1,0:T(8,128)(2,1)}, u32[]{:S(2)}) copy-start(bf16[192,1024]{1,0:T(8,128)(2,1)} %copy-done.12) | copy-start | bytes 1179652
  50.8 8.3 %copy-start.11 = (bf16[192,1024]{1,0:T(8,128)(2,1)S(1)}, bf16[192,1024]{1,0:T(8,128)(2,1)}, u32[]{:S(2)}) copy-start(bf16[192,1024]{1,0:T(8,128)(2,1)} %copy-done.10) | copy-start | bytes 1179652
  53.5 20.2 %collective-permute-start.1 = (bf16[192,1024]{1,0:T(8,128)(2,1)S(1)}, bf16[192,1024]{1,0:T(8,128)(2,1)S(1)}, u32[]{:S(2)}, u32[]{:S(2)}) collective-permute-start(bf16[192,1024]{1,0:T(8,128)(2,1)S(1)} %copy-done.15), channel_id=1, source_target_pairs={{0,64},{64,0},{1,65},{65,1},{2,66},{66,2},{3,67},{67,3},{4,68},{68... | collective-permute-start | bytes 1179656 | tf_op jit(solution)/shard_map/ppermute | solution.py:23
  55.4 18.3 %collective-permute-start.2 = (bf16[192,1024]{1,0:T(8,128)(2,1)S(1)}, bf16[192,1024]{1,0:T(8,128)(2,1)S(1)}, u32[]{:S(2)}, u32[]{:S(2)}) collective-permute-start(bf16[192,1024]{1,0:T(8,128)(2,1)S(1)} %copy-done.13), channel_id=1, source_target_pairs={{0,192},{64,128},{128,64},{192,0},{1,193},{65,129},{129,65},{193,1... | collective-permute-start | bytes 1179656 | tf_op jit(solution)/shard_map/ppermute | solution.py:23
  59.1 26.4 %collective-permute-start = (bf16[192,1024]{1,0:T(8,128)(2,1)S(1)}, bf16[192,1024]{1,0:T(8,128)(2,1)S(1)}, u32[]{:S(2)}, u32[]{:S(2)}) collective-permute-start(bf16[192,1024]{1,0:T(8,128)(2,1)S(1)} %copy-done.11), channel_id=1, source_target_pairs={{0,128},{128,0},{1,129},{129,1},{2,130},{130,2},{3,131},{131,3},{4... | collective-permute-start | bytes 1179656 | tf_op jit(solution)/shard_map/ppermute | solution.py:23
  68.0 43.9 %all-to-all-start.1 = ((bf16[32,16,1024]{2,1,0:T(8,128)(2,1)}), bf16[32,16,1024]{2,1,0:T(8,128)(2,1)}, u32[]{:S(2)}, u32[]{:S(2)}) async-start(bf16[32,16,1024]{2,1,0:T(8,128)(2,1)} %fusion.20), calls=%async_computation.1 | async-start | bytes 2097152 | tf_op jit(solution)/shard_map/all_to_all | solution.py:132
  73.8 11.8 %copy-start.17 = (bf16[192,1024]{1,0:T(8,128)(2,1)}, bf16[192,1024]{1,0:T(8,128)(2,1)S(1)}, u32[]{:S(2)}) copy-start(bf16[192,1024]{1,0:T(8,128)(2,1)S(1)} %get-tuple-element.53) | copy-start | bytes 1179652
  73.8 11.8 %copy-start.18 = (bf16[192,1024]{1,0:T(8,128)(2,1)}, bf16[192,1024]{1,0:T(8,128)(2,1)S(1)}, u32[]{:S(2)}) copy-start(bf16[192,1024]{1,0:T(8,128)(2,1)S(1)} %get-tuple-element.54) | copy-start | bytes 1179652
  73.8 11.7 %copy-start.3 = (bf16[192,1024]{1,0:T(8,128)(2,1)S(1)}, bf16[192,1024]{1,0:T(8,128)(2,1)}, u32[]{:S(2)}) copy-start(bf16[192,1024]{1,0:T(8,128)(2,1)} %copy-done.2) | copy-start | bytes 1179652
  76.0 9.5 %collective-permute-start.9 = (bf16[512,384]{1,0:T(8,128)(2,1)S(1)}, bf16[512,384]{1,0:T(8,128)(2,1)S(1)}, u32[]{:S(2)}, u32[]{:S(2)}) collective-permute-start(bf16[512,384]{1,0:T(8,128)(2,1)S(1)} %fusion.6), channel_id=1, source_target_pairs={{0,64},{64,0},{1,65},{65,1},{2,66},{66,2},{3,67},{67,3},{4,68},{68... | collective-permute-start | bytes 1179656 | tf_op jit(solution)/shard_map/ppermute | solution.py:23
  78.0 17.6 %collective-permute-start.5 = (bf16[192,1024]{1,0:T(8,128)(2,1)S(1)}, bf16[192,1024]{1,0:T(8,128)(2,1)S(1)}, u32[]{:S(2)}, u32[]{:S(2)}) collective-permute-start(bf16[192,1024]{1,0:T(8,128)(2,1)S(1)} %copy-done.9), channel_id=1, source_target_pairs={{0,128},{128,0},{1,129},{129,1},{2,130},{130,2},{3,131},{131,3},{4... | collective-permute-start | bytes 1179656 | tf_op jit(solution)/shard_map/ppermute | solution.py:23
  85.6 6.1 %copy-start.5 = (bf16[192,1024]{1,0:T(8,128)(2,1)S(1)}, bf16[192,1024]{1,0:T(8,128)(2,1)}, u32[]{:S(2)}) copy-start(bf16[192,1024]{1,0:T(8,128)(2,1)} %copy-done.4) | copy-start | bytes 1179652
  87.6 16.2 %collective-permute-start.10 = (bf16[512,384]{1,0:T(8,128)(2,1)S(1)}, bf16[512,384]{1,0:T(8,128)(2,1)S(1)}, u32[]{:S(2)}, u32[]{:S(2)}) collective-permute-start(bf16[512,384]{1,0:T(8,128)(2,1)S(1)} %get-tuple-element.76), channel_id=1, source_target_pairs={{0,128},{128,0},{1,129},{129,1},{2,130},{130,2},{3,131},{131,3},{4... | collective-permute-start | bytes 1179656 | tf_op jit(solution)/shard_map/ppermute | solution.py:23
  89.6 16.4 %collective-permute-start.7 = (bf16[192,1024]{1,0:T(8,128)(2,1)S(1)}, bf16[192,1024]{1,0:T(8,128)(2,1)S(1)}, u32[]{:S(2)}, u32[]{:S(2)}) collective-permute-start(bf16[192,1024]{1,0:T(8,128)(2,1)S(1)} %copy-done.7), channel_id=1, source_target_pairs={{0,64},{64,0},{1,65},{65,1},{2,66},{66,2},{3,67},{67,3},{4,68},{68... | collective-permute-start | bytes 1179656 | tf_op jit(solution)/shard_map/ppermute | solution.py:23
  91.7 20.2 %collective-permute-start.8 = (bf16[192,1024]{1,0:T(8,128)(2,1)S(1)}, bf16[192,1024]{1,0:T(8,128)(2,1)S(1)}, u32[]{:S(2)}, u32[]{:S(2)}) collective-permute-start(bf16[192,1024]{1,0:T(8,128)(2,1)S(1)} %copy-done.5), channel_id=1, source_target_pairs={{0,192},{64,128},{128,64},{192,0},{1,193},{65,129},{129,65},{193,1... | collective-permute-start | bytes 1179656 | tf_op jit(solution)/shard_map/ppermute | solution.py:23
  104.1 12.8 %collective-permute-start.11 = (bf16[512,384]{1,0:T(8,128)(2,1)S(1)}, bf16[512,384]{1,0:T(8,128)(2,1)S(1)}, u32[]{:S(2)}, u32[]{:S(2)}) collective-permute-start(bf16[512,384]{1,0:T(8,128)(2,1)S(1)} %multiply_convert_fusion), channel_id=1, source_target_pairs={{0,64},{64,0},{1,65},{65,1},{2,66},{66,2},{3,67},{67,3},{4,68},{68... | collective-permute-start | bytes 1179656 | tf_op jit(solution)/shard_map/ppermute | solution.py:23
  114.8 14.2 %collective-permute-start.3 = (bf16[512,384]{1,0:T(8,128)(2,1)}, bf16[512,384]{1,0:T(8,128)(2,1)}, u32[]{:S(2)}, u32[]{:S(2)}) collective-permute-start(bf16[512,384]{1,0:T(8,128)(2,1)} %fusion.7), channel_id=1, source_target_pairs={{0,64},{64,0},{1,65},{65,1},{2,66},{66,2},{3,67},{67,3},{4,68},{68... | collective-permute-start | bytes 1179656 | tf_op jit(solution)/shard_map/ppermute | solution.py:23
  119.3 38.4 %all-to-all-start.4 = ((bf16[32,16,1024]{2,1,0:T(8,128)(2,1)}), bf16[32,16,1024]{2,1,0:T(8,128)(2,1)S(1)}, u32[]{:S(2)}, u32[]{:S(2)}) async-start(bf16[32,16,1024]{2,1,0:T(8,128)(2,1)} %bitcast.22), calls=%async_computation.4 | async-start | bytes 2097152 | tf_op jit(solution)/shard_map/all_to_all | solution.py:142
  131.1 12.8 %collective-permute-start.4 = (bf16[512,384]{1,0:T(8,128)(2,1)S(1)}, bf16[512,384]{1,0:T(8,128)(2,1)S(1)}, u32[]{:S(2)}, u32[]{:S(2)}) collective-permute-start(bf16[512,384]{1,0:T(8,128)(2,1)S(1)} %get-tuple-element.78), channel_id=1, source_target_pairs={{0,128},{128,0},{1,129},{129,1},{2,130},{130,2},{3,131},{131,3},{4... | collective-permute-start | bytes 1179656 | tf_op jit(solution)/shard_map/ppermute | solution.py:23
  144.2 3.6 %collective-permute-start.6 = (bf16[512,384]{1,0:T(8,128)(2,1)S(1)}, bf16[512,384]{1,0:T(8,128)(2,1)S(1)}, u32[]{:S(2)}, u32[]{:S(2)}) collective-permute-start(bf16[512,384]{1,0:T(8,128)(2,1)S(1)} %multiply_convert_fusion.1), channel_id=1, source_target_pairs={{0,64},{64,0},{1,65},{65,1},{2,66},{66,2},{3,67},{67,3},{4,68},{68... | collective-permute-start | bytes 1179656 | tf_op jit(solution)/shard_map/ppermute | solution.py:23
  150.2 13.1 %copy-start.21 = (s32[32,2,8]{2,0,1:T(8,128)S(1)}, s32[32,2,8]{2,0,1:T(8,128)}, u32[]{:S(2)}) copy-start(s32[32,2,8]{2,0,1:T(8,128)} %get-tuple-element.70) | copy-start | bytes 6148
  150.2 13.2 %copy-start.20 = (s32[32,2,8]{2,0,1:T(8,128)S(1)}, s32[32,2,8]{2,0,1:T(8,128)}, u32[]{:S(2)}) copy-start(s32[32,2,8]{2,0,1:T(8,128)} %copy-done.19) | copy-start | bytes 6148
  150.2 13.2 %copy-start.28 = (f32[2,2,256]{2,1,0:T(2,128)S(1)}, f32[2,2,256]{2,1,0:T(2,128)}, u32[]{:S(2)}) copy-start(f32[2,2,256]{2,1,0:T(2,128)} %get-tuple-element.57) | copy-start | bytes 12292
  150.2 13.2 %copy-start.25 = (f32[2,32,256]{2,1,0:T(8,128)S(1)}, f32[2,32,256]{2,1,0:T(8,128)}, u32[]{:S(2)}) copy-start(f32[2,32,256]{2,1,0:T(8,128)} %copy-done.24) | copy-start | bytes 196612
  150.2 13.2 %copy-start.27 = (pred[2,32,256]{2,1,0:T(8,128)(4,1)S(1)}, pred[2,32,256]{2,1,0:T(8,128)(4,1)}, u32[]{:S(2)}) copy-start(pred[2,32,256]{2,1,0:T(8,128)(4,1)} %copy-done.26) | copy-start | bytes 49156
  150.2 13.6 %copy-start.23 = (f32[2,32,256]{2,1,0:T(8,128)S(1)}, f32[2,32,256]{2,1,0:T(8,128)}, u32[]{:S(2)}) copy-start(f32[2,32,256]{2,1,0:T(8,128)} %copy-done.22) | copy-start | bytes 196612
  157.7 33.0 %all-to-all-start.2 = ((bf16[32,16,1024]{2,1,0:T(8,128)(2,1)}), bf16[32,16,1024]{2,1,0:T(8,128)(2,1)S(1)}, u32[]{:S(2)}, u32[]{:S(2)}) async-start(bf16[32,16,1024]{2,1,0:T(8,128)(2,1)} %bitcast.14), calls=%async_computation.2 | async-start | bytes 2097152 | tf_op jit(solution)/shard_map/all_to_all | solution.py:142
  (14 other events, 24.2 us)

commit v5 on v4

v5 whole, which is shorter than its diff:
```python
import jax
import jax.numpy as jnp
from jax import lax
from jax.experimental import pallas as pl
from jax.experimental.pallas import tpu as pltpu
from jax.sharding import Mesh
from jax.sharding import PartitionSpec as P

TOPK = 8
CAP = 4
BF = jnp.bfloat16
F32 = jnp.float32

SPLIT = (("p", 2), ("m", 2), ("k", 2), ("zh", 2), ("y", 8), ("x", 4))


def dot(a, b, dims, out=F32):
    return lax.dot_general(a, b, (dims, ((), ())), preferred_element_type=out)


def swap(array, *axes):
    last = 2 ** len(axes) - 1
    return lax.ppermute(array, axes, [(i, last - i) for i in range(last + 1)])


def cut_kernel(place, gate, down, *outs):
    m, k = place[0], place[1]
    width = gate.shape[2] // 8
    for which, weight in enumerate((gate, down)):
        for dm in range(2):
            for dk in range(2):
                out = outs[4 * which + 2 * dm + dk]
                for p in range(2):
                    at = (4 * p + 2 * (m ^ dm) + (k ^ dk)) * width
                    out[:, p * width : (p + 1) * width] = weight[0, :, pl.ds(pl.multiple_of(at, width), width)]


def cut_weights(gate, down):
    _, hidden, feats = gate.shape
    place = jnp.stack([lax.axis_index("m"), lax.axis_index("k")]).astype(jnp.int32)
    rows = hidden // 2
    whole = pl.BlockSpec((1, rows, feats), lambda i: (0, i, 0))
    parts = pl.pallas_call(
        cut_kernel,
        out_shape=[jax.ShapeDtypeStruct((hidden, feats // 4), BF)] * 8,
        grid=(2,),
        in_specs=[pl.BlockSpec(memory_space=pltpu.SMEM), whole, whole],
        out_specs=[pl.BlockSpec((rows, feats // 4), lambda i: (i, 0))] * 8,
        compiler_params=pltpu.CompilerParams(vmem_limit_bytes=32 << 20),
        cost_estimate=pl.CostEstimate(flops=0, bytes_accessed=4 * gate.size * 2, transcendentals=0),
    )(place, gate, down)
    return parts[:4], parts[4:]


def recut(parts):
    m = lax.axis_index("m")
    mine, for_k, for_m, for_mk = parts
    far_own = swap(for_m, "m")
    near_other = swap(for_k, "k")
    far_other = swap(for_mk, "m", "k")

    def order(near, far):
        first = jnp.where(m == 0, near, far)
        second = jnp.where(m == 0, far, near)
        return jnp.concatenate([first, second], axis=0)

    return order(mine, far_own), order(near_other, far_other)


def thirds(value):
    high = lax.reduce_precision(value, 8, 7)
    mid = lax.reduce_precision(value - high, 8, 7)
    return high.astype(BF), mid.astype(BF), (value - high - mid).astype(BF)


def slots(codes, weights, plan, experts):
    rows = codes.shape[1]
    count = experts.shape[0]
    ids = jnp.arange(plan.shape[0], dtype=jnp.int32)
    spare_host = jnp.sum(jnp.where(plan[None, :] == experts[:, None], ids[None, :], 0), axis=1)
    here = jnp.sum(jnp.where(ids[None, :] == experts[:, None], plan[None, :], 0), axis=1)
    own_code = 2 * jnp.concatenate([experts, spare_host])
    spare_code = 2 * jnp.concatenate([here, experts]) + 1
    is_own = codes[:, None, :] == own_code[None, :, None]
    is_spare = codes[:, None, :] == spare_code[None, :, None]
    landed = is_own | is_spare
    at = jnp.arange(rows, dtype=jnp.int32)
    before = (at[:, None] < at[None, :]).astype(BF)
    position = dot(landed.astype(BF), before, ((2,), (0,)))
    fits = position < CAP
    kept = (is_own[:, :count] & fits[:, :count]) | (is_spare[:, count:] & fits[:, count:])
    rank = dot(kept.astype(BF), before, ((2,), (0,)))
    slot = jnp.arange(2 * CAP, dtype=F32)
    hit = kept[:, :, None, :] & (rank[:, :, None, :] == slot[None, None, :, None])
    token = at // TOPK + 1
    token_of = jnp.sum(jnp.where(hit, token[None, None, None, :], 0), axis=3) - 1
    weight_of = jnp.sum(jnp.where(hit, weights[:, None, None, :], 0.0), axis=3)
    return token_of, weight_of


def placed(token_of, starts, total):
    at = jnp.where(token_of >= 0, token_of + starts[:, None, None], -1)
    at = at.transpose(1, 0, 2).reshape(-1)
    return at[:, None] == jnp.arange(total, dtype=jnp.int32)[None, :]


def combine(hot, weight_of, back):
    scale = jnp.where(hot, weight_of.transpose(1, 0, 2).reshape(-1)[:, None], 0.0)
    high, low, _ = thirds(scale)
    return (dot(high, back, ((0,), (0,))) + dot(low, back, ((0,), (0,)))).astype(BF)


def local(tokens, w_gate, w_down, expert_ids, route_weight, replica_pick, old_plan, new_plan):
    batches, group, feats = tokens.shape
    ny, nx, wide = lax.axis_size("y"), lax.axis_size("x"), 2 * feats
    zh, y = lax.axis_index("zh"), lax.axis_index("y")
    gate_parts, down_parts = cut_weights(w_gate, w_down)
    gate_own, gate_other = recut(gate_parts)
    down_own, down_other = recut(down_parts)

    code = (2 * expert_ids + (replica_pick & 1)).astype(BF)
    info = jnp.stack([code, *thirds(route_weight)]).reshape(-1, feats)
    count = info.shape[0]
    sent = jnp.concatenate([tokens.reshape(-1, feats), jnp.pad(info, ((0, 16 - count), (0, 0)))])
    sent = jnp.broadcast_to(sent[None], (4, *sent.shape))
    came = lax.all_to_all(sent, ("p", "zh"), 0, 0, tiled=True).reshape(2, 2, -1, feats)
    tok = came[:, :, : batches * group].reshape(2, 2, batches, group, feats)
    tok = tok.transpose(2, 1, 3, 0, 4).reshape(batches, 2 * group, wide)
    info = came[0, :, batches * group : batches * group + count]

    def unpack(info, groups):
        info = info.reshape(groups, 4, batches, group * TOPK).astype(F32)
        return info[:, 0].astype(jnp.int32), info[:, 1] + info[:, 2] + info[:, 3]

    lines = info.reshape(-1, wide)
    step = 2 * group + 8
    lines = jnp.pad(lines, ((0, 8 - lines.shape[0]), (0, 0)))
    spread = lax.all_gather(jnp.concatenate([tok[1], lines]), "y", axis=0, tiled=True)

    near_code, near_weight = unpack(info, 2)
    near_experts = zh * (ny * nx) + jnp.arange(ny * nx, dtype=jnp.int32)
    near_starts = jnp.arange(2, dtype=jnp.int32) * group

    def near_slots(index, plan):
        token_of, weight_of = slots(near_code[:, index], near_weight[:, index], plan, near_experts)
        return placed(token_of, near_starts, 2 * group), weight_of

    row_experts = (zh * ny + y) * nx + jnp.arange(nx, dtype=jnp.int32)
    at = jnp.arange(2 * ny, dtype=jnp.int32)
    starts = (at // 2) * step + (at % 2) * group
    flat_starts = at * group

    def experts_out(rows):
        send = dot(rows, gate_other, ((1,), (1,)), BF)
        part = dot(rows, gate_own, ((1,), (1,)))
        part = part + swap(send, "k").astype(F32)
        gate = part + swap(part.astype(BF), "m").astype(F32)
        hidden = jax.nn.silu(gate).astype(BF)
        hidden_other = swap(hidden, "k")
        out = dot(hidden, down_own, ((1,), (0,))) + dot(hidden_other, down_other, ((1,), (0,)))
        return out.astype(BF)

    hot, _ = near_slots(0, old_plan)
    rows = dot(hot.astype(BF), tok[0], ((1,), (0,)), BF).reshape(ny * nx, -1, wide)
    rows = lax.all_to_all(rows, ("y", "x"), 0, 0, tiled=True).reshape(-1, wide)
    out_0 = experts_out(rows)

    all_code, all_weight = unpack(spread.reshape(ny, step, wide)[:, 2 * group : step - 4], 2 * ny)
    token_of, _ = slots(all_code[:, 1], all_weight[:, 1], new_plan, row_experts)
    hot = placed(token_of, starts, ny * step)
    rows = dot(hot.astype(BF), spread, ((1,), (0,)), BF).reshape(nx, -1, wide)
    rows = lax.all_to_all(rows, "x", 0, 0, tiled=True).reshape(-1, wide)
    out_1 = experts_out(rows)

    back = out_0.reshape(ny, nx, -1, wide).transpose(1, 0, 2, 3).reshape(nx, -1, wide)
    back = lax.all_to_all(back, "x", 0, 0, tiled=True).reshape(-1, wide)
    token_of, weight_of = slots(all_code[:, 0], all_weight[:, 0], old_plan, row_experts)
    mixed_0 = combine(placed(token_of, flat_starts, 2 * ny * group), weight_of, back)
    mixed_0 = lax.psum_scatter(mixed_0, "y", scatter_dimension=0, tiled=True)

    back = out_1.reshape(nx, ny, -1, wide).transpose(1, 0, 2, 3).reshape(ny * nx, -1, wide)
    back = lax.all_to_all(back, ("y", "x"), 0, 0, tiled=True).reshape(-1, wide)
    hot, weight_of = near_slots(1, new_plan)
    mixed_1 = combine(hot, weight_of, back)

    mixed = jnp.stack([mixed_0, mixed_1]).reshape(batches, 2, group, 2, feats)
    mixed = mixed.transpose(3, 1, 0, 2, 4).reshape(4, batches * group, feats)
    terms = lax.all_to_all(mixed, ("p", "zh"), 0, 0, tiled=True)
    return jnp.sum(terms.astype(F32), axis=0).astype(BF).reshape(batches, group, feats)


def solution(mesh):
    names = tuple(name for name, _ in SPLIT)
    cut = Mesh(mesh.devices.reshape([size for _, size in SPLIT]), names)
    dp, expert = ("p", "m", "k"), ("zh", "y", "x")
    specs = (
        P(None, expert, dp),
        P(expert, dp, None),
        P(expert, dp, None),
        P(None, expert, None),
        P(None, expert, None),
        P(None, expert, None),
        P(),
        P(),
    )
    return jax.shard_map(
        local, mesh=cut, in_specs=specs, out_specs=P(None, expert, dp), check_vma=False
    )
```

time: 206 us -> 245 us (1.19)
  the two profiles are of different devices: /device:TPU:2 before, /device:TPU:4 now
where the time goes in v5:
time: 245 us; the launch traced here: 244 us
  waiting for transfers between devices  89.6 us (37%)
  starting transfers between devices  72.6 us (30%)
  matrix products  22.7 us (9%)
  other arithmetic  18.2 us (7%)
  blocking collectives  15.6 us (6%)
  between operations  14.2 us (6%)
  local copies, waits for them, and re-layouts  8.89 us (4%)
    ppermute x12, starting transfers between devices, swap(): return lax.ppermute(array, axes, [(i, last - i) for i in range(last + 1)])  33.6 us
    all_to_all x1, waiting for transfers between devices, local(): back = lax.all_to_all(back, ('y', 'x'), 0, 0, tiled=True).reshape(-1, wide)  27.8 us
    dot_general x22, matrix products, dot(): return lax.dot_general(a, b, (dims, ((), ())), preferred_element_type=out)  22.7 us
    ppermute x12, waiting for transfers between devices, swap(): return lax.ppermute(array, axes, [(i, last - i) for i in range(last + 1)])  16.3 us
    all_to_all x1, blocking collectives, local(): terms = lax.all_to_all(mixed, ('p', 'zh'), 0, 0, tiled=True)  15.6 us
    reduce_scatter x1, waiting for transfers between devices, local(): mixed_0 = lax.psum_scatter(mixed_0, 'y', scatter_dimension=0, tiled=True)  14 us
    all_to_all x1, waiting for transfers between devices, local(): lax.all_to_all(sent, ('p', 'zh'), 0, 0, tiled=True).reshape(2, 2, -1, feats)  11.4 us
    all_gather x1, waiting for transfers between devices, local(): lax.all_gather(jnp.concatenate([tok[1], lines]), 'y', axis=0, tiled=True)  10.7 us
  transfers between devices with their start and end apart: 19, of which 8 were waited for; matrix products, arithmetic and copies ran while one was open for 14% of the time, Pallas kernels for 1%

profile of v5, /device:TPU:4, one launch (start us, length us, event | category | flops | bytes accessed | tf_op | source)
XLA Modules:
  0.0 243.7 jit_solution(7540973940289497606)
XLA Ops:
  10.4 10.3 %all-to-all-start = ((bf16[4,80,512]{2,1,0:T(8,128)(2,1)}), bf16[4,80,512]{2,1,0:T(8,128)(2,1)S(1)}, u32[]{:S(2)}, u32[]{:S(2)}) async-start(bf16[4,80,512]{2,1,0:T(8,128)(2,1)} %broadcast_in_dim.224), calls=%async_computation | async-start | bytes 655360 | tf_op jit(solution)/shard_map/all_to_all | solution.py:126
  21.7 11.4 %all-to-all-done = bf16[4,80,512]{2,1,0:T(8,128)(2,1)S(1)} async-done(((bf16[4,80,512]{2,1,0:T(8,128)(2,1)}), bf16[4,80,512]{2,1,0:T(8,128)(2,1)S(1)}, u32[]{:S(2)}, u32[]{:S(2)}) %all-to-all-start) | async-done | bytes 327712 | tf_op jit(solution)/shard_map/all_to_all | solution.py:126
  36.7 2.2 select_reduce_fusion.3
  41.3 10.4 %all-to-all-start.1 = ((bf16[32,16,1024]{2,1,0:T(8,128)(2,1)}), bf16[32,16,1024]{2,1,0:T(8,128)(2,1)}, u32[]{:S(2)}, u32[]{:S(2)}) async-start(bf16[32,16,1024]{2,1,0:T(8,128)(2,1)} %fusion.38), calls=%async_computation.1 | async-start | bytes 2097152 | tf_op jit(solution)/shard_map/all_to_all | solution.py:165
  52.7 2.0 shard_map.82
  56.2 3.5 %collective-permute-start = (bf16[192,1024]{1,0:T(8,128)(2,1)}, bf16[192,1024]{1,0:T(8,128)(2,1)S(1)}, u32[]{:S(2)}, u32[]{:S(2)}) collective-permute-start(bf16[192,1024]{1,0:T(8,128)(2,1)} %get-tuple-element.14), channel_id=1, source_target_pairs={{0,128},{128,0},{1,129},{129,1},{2,130},{130,2},{3,131},{131,3},{4... | collective-permute-start | bytes 1179656 | tf_op jit(solution)/shard_map/ppermute | solution.py:23
  59.7 1.9 collective-permute-start.1
  61.6 2.4 collective-permute-start.2
  64.1 3.5 %collective-permute-start.5 = (bf16[192,1024]{1,0:T(8,128)(2,1)}, bf16[192,1024]{1,0:T(8,128)(2,1)S(1)}, u32[]{:S(2)}, u32[]{:S(2)}) collective-permute-start(bf16[192,1024]{1,0:T(8,128)(2,1)} %get-tuple-element.18), channel_id=1, source_target_pairs={{0,128},{128,0},{1,129},{129,1},{2,130},{130,2},{3,131},{131,3},{4... | collective-permute-start | bytes 1179656 | tf_op jit(solution)/shard_map/ppermute | solution.py:23
  67.6 1.9 collective-permute-start.7
  71.1 2.4 collective-permute-start.8
  73.5 4.3 %collective-permute-done.2 = bf16[192,1024]{1,0:T(8,128)(2,1)} collective-permute-done((bf16[192,1024]{1,0:T(8,128)(2,1)}, bf16[192,1024]{1,0:T(8,128)(2,1)}, u32[]{:S(2)}, u32[]{:S(2)}) %collective-permute-start.2) | collective-permute-done | bytes 393248 | tf_op jit(solution)/shard_map/ppermute | solution.py:23
  78.9 3.0 %fusion.20 = bf16[512,384]{1,0:T(8,128)(2,1)} fusion(bf16[512,1024]{1,0:T(8,128)(2,1)} %bitcast.15, bf16[192,1024]{1,0:T(8,128)(2,1)S(1)} %get-tuple-element.44, bf16[192,1024]{1,0:T(8,128)(2,1)S(1)} %get-tuple-element.43), kind=kOutput, calls=%fused_computation.49 | convolution fusion | flops 404226048 | bytes 2228224 | tf_op jit(solution)/shard_map/dot_general | solution.py:18
  81.9 1.9 collective-permute-start.3
  83.8 10.7 %all-gather.2.cloned.1.call-done = bf16[576,1024]{1,0:T(8,128)(2,1)} async-done(((bf16[72,1024]{1,0:T(8,128)(2,1)}), bf16[576,1024]{1,0:T(8,128)(2,1)}) %all-gather.2.cloned.1.call-update) | async-done | bytes 1179664 | tf_op jit(solution)/shard_map/all_gather | solution.py:138
  97.5 2.3 select_reduce_fusion.5
  100.0 3.3 %fusion = bf16[512,1024]{1,0:T(8,128)(2,1)} fusion(bf16[576,1024]{1,0:T(8,128)(2,1)} %all-gather.2.cloned.1.call-done, s32[512]{0:T(512)S(1)} %eq.386), kind=kOutput, calls=%fused_computation.6 | convolution fusion | flops 604274688 | bytes 2230272 | tf_op jit(solution)/shard_map/dot_general | solution.py:18
  103.2 4.9 %all-to-all-start.3 = ((bf16[4,128,1024]{2,1,0:T(8,128)(2,1)}), bf16[4,128,1024]{2,1,0:T(8,128)(2,1)S(1)}, u32[]{:S(2)}, u32[]{:S(2)}) async-start(bf16[4,128,1024]{2,1,0:T(8,128)(2,1)} %bitcast.26), calls=%async_computation.4 | async-start | bytes 2097152 | tf_op jit(solution)/shard_map/all_to_all | solution.py:172
  108.4 3.3 %fusion.96 = (bf16[512,384]{1,0:T(8,128)(2,1)}, f32[512,384]{1,0:T(8,128)}) fusion(bf16[512,384]{1,0:T(8,128)(2,1)} %collective-permute-done.3, bf16[512,1024]{1,0:T(8,128)(2,1)} %bitcast.15, bf16[192,1024]{1,0:T(8,128)(2,1)S(1)} %get-tuple-element.42, bf16[192,1024]{1,0:T(8,128)(2,1)S(1)} %get-tuple-element.41), kind=kOutput, calls=%fused_computation.203 | convolution fusion | flops 404815872 | bytes 3407872 | tf_op jit(solution)/shard_map/dot_general | solution.py:18
  111.6 5.9 %collective-permute-start.4 = (bf16[512,384]{1,0:T(8,128)(2,1)}, bf16[512,384]{1,0:T(8,128)(2,1)}, u32[]{:S(2)}, u32[]{:S(2)}) collective-permute-start(bf16[512,384]{1,0:T(8,128)(2,1)} %get-tuple-element.80), channel_id=1, source_target_pairs={{0,128},{128,0},{1,129},{129,1},{2,130},{130,2},{3,131},{131,3},{4... | collective-permute-start | bytes 1179656 | tf_op jit(solution)/shard_map/ppermute | solution.py:23
  118.4 2.1 collective-permute-start.9
  120.6 3.1 %collective-permute-done.4 = bf16[512,384]{1,0:T(8,128)(2,1)} collective-permute-done((bf16[512,384]{1,0:T(8,128)(2,1)}, bf16[512,384]{1,0:T(8,128)(2,1)}, u32[]{:S(2)}, u32[]{:S(2)}) %collective-permute-start.4) | collective-permute-done | bytes 393248 | tf_op jit(solution)/shard_map/ppermute | solution.py:23
  124.9 2.1 collective-permute-start.6
  128.8 3.9 %collective-permute-start.10 = (bf16[512,384]{1,0:T(8,128)(2,1)}, bf16[512,384]{1,0:T(8,128)(2,1)S(1)}, u32[]{:S(2)}, u32[]{:S(2)}) collective-permute-start(bf16[512,384]{1,0:T(8,128)(2,1)} %get-tuple-element.78), channel_id=1, source_target_pairs={{0,128},{128,0},{1,129},{129,1},{2,130},{130,2},{3,131},{131,3},{4... | collective-permute-start | bytes 1179656 | tf_op jit(solution)/shard_map/ppermute | solution.py:23
  133.7 8.9 %collective-permute-done.10 = bf16[512,384]{1,0:T(8,128)(2,1)S(1)} collective-permute-done((bf16[512,384]{1,0:T(8,128)(2,1)}, bf16[512,384]{1,0:T(8,128)(2,1)S(1)}, u32[]{:S(2)}, u32[]{:S(2)}) %collective-permute-start.10) | collective-permute-done | bytes 393248 | tf_op jit(solution)/shard_map/ppermute | solution.py:23
  142.9 1.9 collective-permute-start.11
  146.6 5.1 %all-to-all-start.2 = ((bf16[4,128,1024]{2,1,0:T(8,128)(2,1)}), bf16[4,128,1024]{2,1,0:T(8,128)(2,1)S(1)}, u32[]{:S(2)}, u32[]{:S(2)}) async-start(bf16[4,128,1024]{2,1,0:T(8,128)(2,1)} %bitcast.20), calls=%async_computation.2 | async-start | bytes 2097152 | tf_op jit(solution)/shard_map/all_to_all | solution.py:176
  155.5 9.3 %all-to-all-done.2 = bf16[4,128,1024]{2,1,0:T(8,128)(2,1)S(1)} async-done(((bf16[4,128,1024]{2,1,0:T(8,128)(2,1)}), bf16[4,128,1024]{2,1,0:T(8,128)(2,1)S(1)}, u32[]{:S(2)}, u32[]{:S(2)}) %all-to-all-start.2) | async-done | bytes 1048608 | tf_op jit(solution)/shard_map/all_to_all | solution.py:176
  164.8 8.2 %all-to-all-start.4 = ((bf16[32,16,1024]{2,1,0:T(8,128)(2,1)}), bf16[32,16,1024]{2,1,0:T(8,128)(2,1)S(1)}, u32[]{:S(2)}, u32[]{:S(2)}) async-start(bf16[32,16,1024]{2,1,0:T(8,128)(2,1)} %bitcast.30), calls=%async_computation.5 | async-start | bytes 2097152 | tf_op jit(solution)/shard_map/all_to_all | solution.py:182
  176.4 27.8 %all-to-all-done.4 = bf16[32,16,1024]{2,1,0:T(8,128)(2,1)S(1)} async-done(((bf16[32,16,1024]{2,1,0:T(8,128)(2,1)}), bf16[32,16,1024]{2,1,0:T(8,128)(2,1)S(1)}, u32[]{:S(2)}, u32[]{:S(2)}) %all-to-all-start.4) | async-done | bytes 1048608 | tf_op jit(solution)/shard_map/all_to_all | solution.py:182
  205.5 14.0 %reduce-scatter.2.cloned.1.call-done = bf16[64,1024]{1,0:T(8,128)(2,1)} async-done(((bf16[512,1024]{1,0:T(8,128)(2,1)}), bf16[64,1024]{1,0:T(8,128)(2,1)}) %reduce-scatter.2.cloned.1.call-update) | async-done | bytes 131088 | tf_op jit(solution)/shard_map/reduce_scatter | solution.py:179
  220.6 15.6 %all_to_all.30 = bf16[4,64,512]{2,1,0:T(8,128)(2,1)S(1)} all-to-all(bf16[4,64,512]{2,1,0:T(8,128)(2,1)S(1)} %bitcast.101), channel_id=1, replica_groups=mesh['p'=2,'m'=2,'k'=2,'zh'=2,'y'=8,'x'=4] {'p','zh'}, dimensions={0} | all-to-all | bytes 524288 | tf_op jit(solution)/shard_map/all_to_all | solution.py:188
  (171 shorter events, 35.8 us)
Async XLA Ops:
  10.4 22.7 %all-to-all-start = ((bf16[4,80,512]{2,1,0:T(8,128)(2,1)}), bf16[4,80,512]{2,1,0:T(8,128)(2,1)S(1)}, u32[]{:S(2)}, u32[]{:S(2)}) async-start(bf16[4,80,512]{2,1,0:T(8,128)(2,1)} %broadcast_in_dim.224), calls=%async_computation | async-start | bytes 655360 | tf_op jit(solution)/shard_map/all_to_all | solution.py:126
  20.7 15.6 %copy-start.22 = (s32[256]{0:T(256)}, s32[256]{0:T(256)S(1)}, u32[]{:S(2)}) copy-start(s32[256]{0:T(256)S(1)} %fusion.72) | copy-start | bytes 3076
  39.8 11.9 %copy-start.20 = (bf16[1,2,4,512]{3,2,1,0:T(4,128)(2,1)S(1)}, bf16[1,2,4,512]{3,2,1,0:T(4,128)(2,1)}, u32[]{:S(2)}) copy-start(bf16[1,2,4,512]{3,2,1,0:T(4,128)(2,1)} %get-tuple-element.46) | copy-start | bytes 24580
  39.8 12.0 %copy-start.7 = (bf16[1,2,32,2,512]{4,2,0,1,3:T(8,128)(2,1)S(1)}, bf16[1,2,32,2,512]{4,2,0,1,3:T(8,128)(2,1)}, u32[]{:S(2)}) copy-start(bf16[1,2,32,2,512]{4,2,0,1,3:T(8,128)(2,1)} %get-tuple-element.48) | copy-start | bytes 393220
  39.8 12.9 %copy-start.1 = (bf16[1,192,4096]{2,1,0:T(8,128)(2,1)S(1)}, bf16[1,192,4096]{2,1,0:T(8,128)(2,1)}, u32[]{:S(2)}) copy-start(bf16[1,192,4096]{2,1,0:T(8,128)(2,1)} %down.1) | copy-start | bytes 4718596
  41.3 11.5 %copy-start = (bf16[1,192,4096]{2,1,0:T(8,128)(2,1)S(1)}, bf16[1,192,4096]{2,1,0:T(8,128)(2,1)}, u32[]{:S(2)}) copy-start(bf16[1,192,4096]{2,1,0:T(8,128)(2,1)} %gate.1) | copy-start | bytes 4718596
  41.3 37.6 %all-to-all-start.1 = ((bf16[32,16,1024]{2,1,0:T(8,128)(2,1)}), bf16[32,16,1024]{2,1,0:T(8,128)(2,1)}, u32[]{:S(2)}, u32[]{:S(2)}) async-start(bf16[32,16,1024]{2,1,0:T(8,128)(2,1)} %fusion.38), calls=%async_computation.1 | async-start | bytes 2097152 | tf_op jit(solution)/shard_map/all_to_all | solution.py:165
  51.7 42.8 %all-gather.2.cloned.1.call-start = ((), (), s32[]{:S(2)}) async-start(), calls=%async_computation.7 | async-start | bytes 1327104 | tf_op jit(solution)/shard_map/all_gather | solution.py:138
  56.2 52.0 %collective-permute-start = (bf16[192,1024]{1,0:T(8,128)(2,1)}, bf16[192,1024]{1,0:T(8,128)(2,1)S(1)}, u32[]{:S(2)}, u32[]{:S(2)}) collective-permute-start(bf16[192,1024]{1,0:T(8,128)(2,1)} %get-tuple-element.14), channel_id=1, source_target_pairs={{0,128},{128,0},{1,129},{129,1},{2,130},{130,2},{3,131},{131,3},{4... | collective-permute-start | bytes 1179656 | tf_op jit(solution)/shard_map/ppermute | solution.py:23
  59.7 11.4 %collective-permute-start.1 = (bf16[192,1024]{1,0:T(8,128)(2,1)}, bf16[192,1024]{1,0:T(8,128)(2,1)S(1)}, u32[]{:S(2)}, u32[]{:S(2)}) collective-permute-start(bf16[192,1024]{1,0:T(8,128)(2,1)} %get-tuple-element.15), channel_id=1, source_target_pairs={{0,64},{64,0},{1,65},{65,1},{2,66},{66,2},{3,67},{67,3},{4,68},{68... | collective-permute-start | bytes 1179656 | tf_op jit(solution)/shard_map/ppermute | solution.py:23
  61.6 16.1 %collective-permute-start.2 = (bf16[192,1024]{1,0:T(8,128)(2,1)}, bf16[192,1024]{1,0:T(8,128)(2,1)}, u32[]{:S(2)}, u32[]{:S(2)}) collective-permute-start(bf16[192,1024]{1,0:T(8,128)(2,1)} %get-tuple-element.16), channel_id=1, source_target_pairs={{0,192},{64,128},{128,64},{192,0},{1,193},{65,129},{129,65},{193,1... | collective-permute-start | bytes 1179656 | tf_op jit(solution)/shard_map/ppermute | solution.py:23
  64.1 44.2 %collective-permute-start.5 = (bf16[192,1024]{1,0:T(8,128)(2,1)}, bf16[192,1024]{1,0:T(8,128)(2,1)S(1)}, u32[]{:S(2)}, u32[]{:S(2)}) collective-permute-start(bf16[192,1024]{1,0:T(8,128)(2,1)} %get-tuple-element.18), channel_id=1, source_target_pairs={{0,128},{128,0},{1,129},{129,1},{2,130},{130,2},{3,131},{131,3},{4... | collective-permute-start | bytes 1179656 | tf_op jit(solution)/shard_map/ppermute | solution.py:23
  67.6 52.8 %collective-permute-start.7 = (bf16[192,1024]{1,0:T(8,128)(2,1)}, bf16[192,1024]{1,0:T(8,128)(2,1)S(1)}, u32[]{:S(2)}, u32[]{:S(2)}) collective-permute-start(bf16[192,1024]{1,0:T(8,128)(2,1)} %get-tuple-element.19), channel_id=1, source_target_pairs={{0,64},{64,0},{1,65},{65,1},{2,66},{66,2},{3,67},{67,3},{4,68},{68... | collective-permute-start | bytes 1179656 | tf_op jit(solution)/shard_map/ppermute | solution.py:23
  71.1 49.4 %collective-permute-start.8 = (bf16[192,1024]{1,0:T(8,128)(2,1)}, bf16[192,1024]{1,0:T(8,128)(2,1)S(1)}, u32[]{:S(2)}, u32[]{:S(2)}) collective-permute-start(bf16[192,1024]{1,0:T(8,128)(2,1)} %copy-done.4), channel_id=1, source_target_pairs={{0,192},{64,128},{128,64},{192,0},{1,193},{65,129},{129,65},{193,1... | collective-permute-start | bytes 1179656 | tf_op jit(solution)/shard_map/ppermute | solution.py:23
  81.9 15.6 %copy-start.23 = (s32[256]{0:T(256)S(1)}, s32[256]{0:T(256)}, u32[]{:S(2)}) copy-start(s32[256]{0:T(256)} %copy-done.22) | copy-start | bytes 3076
  81.9 26.5 %collective-permute-start.3 = (bf16[512,384]{1,0:T(8,128)(2,1)}, bf16[512,384]{1,0:T(8,128)(2,1)}, u32[]{:S(2)}, u32[]{:S(2)}) collective-permute-start(bf16[512,384]{1,0:T(8,128)(2,1)} %fusion.20), channel_id=1, source_target_pairs={{0,64},{64,0},{1,65},{65,1},{2,66},{66,2},{3,67},{67,3},{4,68},{68... | collective-permute-start | bytes 1179656 | tf_op jit(solution)/shard_map/ppermute | solution.py:23
  103.2 14.3 %all-to-all-start.3 = ((bf16[4,128,1024]{2,1,0:T(8,128)(2,1)}), bf16[4,128,1024]{2,1,0:T(8,128)(2,1)S(1)}, u32[]{:S(2)}, u32[]{:S(2)}) async-start(bf16[4,128,1024]{2,1,0:T(8,128)(2,1)} %bitcast.26), calls=%async_computation.4 | async-start | bytes 2097152 | tf_op jit(solution)/shard_map/all_to_all | solution.py:172
  108.3 9.3 %copy-start.9 = (bf16[192,1024]{1,0:T(8,128)(2,1)S(1)}, bf16[192,1024]{1,0:T(8,128)(2,1)}, u32[]{:S(2)}) copy-start(bf16[192,1024]{1,0:T(8,128)(2,1)} %copy-done.8) | copy-start | bytes 1179652
  108.3 9.3 %copy-start.11 = (bf16[192,1024]{1,0:T(8,128)(2,1)S(1)}, bf16[192,1024]{1,0:T(8,128)(2,1)}, u32[]{:S(2)}) copy-start(bf16[192,1024]{1,0:T(8,128)(2,1)} %copy-done.10) | copy-start | bytes 1179652
  111.6 12.0 %collective-permute-start.4 = (bf16[512,384]{1,0:T(8,128)(2,1)}, bf16[512,384]{1,0:T(8,128)(2,1)}, u32[]{:S(2)}, u32[]{:S(2)}) collective-permute-start(bf16[512,384]{1,0:T(8,128)(2,1)} %get-tuple-element.80), channel_id=1, source_target_pairs={{0,128},{128,0},{1,129},{129,1},{2,130},{130,2},{3,131},{131,3},{4... | collective-permute-start | bytes 1179656 | tf_op jit(solution)/shard_map/ppermute | solution.py:23
  118.4 5.3 %copy-start.5 = (f32[512,384]{1,0:T(8,128)S(1)}, f32[512,384]{1,0:T(8,128)}, u32[]{:S(2)}) copy-start(f32[512,384]{1,0:T(8,128)} %get-tuple-element.81) | copy-start | bytes 2359300
  118.4 8.6 %copy-start.13 = (bf16[192,1024]{1,0:T(8,128)(2,1)S(1)}, bf16[192,1024]{1,0:T(8,128)(2,1)}, u32[]{:S(2)}) copy-start(bf16[192,1024]{1,0:T(8,128)(2,1)} %copy-done.12) | copy-start | bytes 1179652
  118.4 8.6 %copy-start.15 = (bf16[192,1024]{1,0:T(8,128)(2,1)S(1)}, bf16[192,1024]{1,0:T(8,128)(2,1)}, u32[]{:S(2)}) copy-start(bf16[192,1024]{1,0:T(8,128)(2,1)} %copy-done.14) | copy-start | bytes 1179652
  118.4 8.6 %collective-permute-start.9 = (bf16[512,384]{1,0:T(8,128)(2,1)S(1)}, bf16[512,384]{1,0:T(8,128)(2,1)S(1)}, u32[]{:S(2)}, u32[]{:S(2)}) collective-permute-start(bf16[512,384]{1,0:T(8,128)(2,1)S(1)} %fusion.19), channel_id=1, source_target_pairs={{0,64},{64,0},{1,65},{65,1},{2,66},{66,2},{3,67},{67,3},{4,68},{68... | collective-permute-start | bytes 1179656 | tf_op jit(solution)/shard_map/ppermute | solution.py:23
  124.9 8.1 %collective-permute-start.6 = (bf16[512,384]{1,0:T(8,128)(2,1)S(1)}, bf16[512,384]{1,0:T(8,128)(2,1)S(1)}, u32[]{:S(2)}, u32[]{:S(2)}) collective-permute-start(bf16[512,384]{1,0:T(8,128)(2,1)S(1)} %multiply_convert_fusion.1), channel_id=1, source_target_pairs={{0,64},{64,0},{1,65},{65,1},{2,66},{66,2},{3,67},{67,3},{4,68},{68... | collective-permute-start | bytes 1179656 | tf_op jit(solution)/shard_map/ppermute | solution.py:23
  128.8 13.9 %collective-permute-start.10 = (bf16[512,384]{1,0:T(8,128)(2,1)}, bf16[512,384]{1,0:T(8,128)(2,1)S(1)}, u32[]{:S(2)}, u32[]{:S(2)}) collective-permute-start(bf16[512,384]{1,0:T(8,128)(2,1)} %get-tuple-element.78), channel_id=1, source_target_pairs={{0,128},{128,0},{1,129},{129,1},{2,130},{130,2},{3,131},{131,3},{4... | collective-permute-start | bytes 1179656 | tf_op jit(solution)/shard_map/ppermute | solution.py:23
  133.0 9.6 %copy-start.6 = (f32[512,384]{1,0:T(8,128)S(1)}, f32[512,384]{1,0:T(8,128)}, u32[]{:S(2)}) copy-start(f32[512,384]{1,0:T(8,128)} %get-tuple-element.79) | copy-start | bytes 2359300
  142.9 9.1 %collective-permute-start.11 = (bf16[512,384]{1,0:T(8,128)(2,1)S(1)}, bf16[512,384]{1,0:T(8,128)(2,1)}, u32[]{:S(2)}, u32[]{:S(2)}) collective-permute-start(bf16[512,384]{1,0:T(8,128)(2,1)S(1)} %multiply_convert_fusion), channel_id=1, source_target_pairs={{0,64},{64,0},{1,65},{65,1},{2,66},{66,2},{3,67},{67,3},{4,68},{68... | collective-permute-start | bytes 1179656 | tf_op jit(solution)/shard_map/ppermute | solution.py:23
  146.6 5.1 %copy-start.24 = (s32[16]{0:T(128)S(1)}, s32[16]{0:T(128)}, u32[]{:S(2)}) copy-start(s32[16]{0:T(128)} %iota_multiply_fusion.1) | copy-start | bytes 196
  146.6 18.2 %all-to-all-start.2 = ((bf16[4,128,1024]{2,1,0:T(8,128)(2,1)}), bf16[4,128,1024]{2,1,0:T(8,128)(2,1)S(1)}, u32[]{:S(2)}, u32[]{:S(2)}) async-start(bf16[4,128,1024]{2,1,0:T(8,128)(2,1)} %bitcast.20), calls=%async_computation.2 | async-start | bytes 2097152 | tf_op jit(solution)/shard_map/all_to_all | solution.py:176
  164.8 39.4 %all-to-all-start.4 = ((bf16[32,16,1024]{2,1,0:T(8,128)(2,1)}), bf16[32,16,1024]{2,1,0:T(8,128)(2,1)S(1)}, u32[]{:S(2)}, u32[]{:S(2)}) async-start(bf16[32,16,1024]{2,1,0:T(8,128)(2,1)} %bitcast.30), calls=%async_computation.5 | async-start | bytes 2097152 | tf_op jit(solution)/shard_map/all_to_all | solution.py:182
  173.1 46.5 %reduce-scatter.2.cloned.1.call-start = ((), (), s32[]{:S(2)}) async-start(), calls=%async_computation.8 | async-start | bytes 1179648 | tf_op jit(solution)/shard_map/reduce_scatter | solution.py:179
  (12 other events, 29.0 us)
Sparse Core Ops, SparseCore 0:
  54.6 39.8 all-gather.1
  176.7 42.7 reduce-scatter.1

commit v6 on v4

--- a/solution.py
+++ b/solution.py
@@ -38,12 +38,14 @@
 def cut_weights(gate, down):
     _, hidden, feats = gate.shape
     place = jnp.stack([lax.axis_index("m"), lax.axis_index("k")]).astype(jnp.int32)
-    vmem = pl.BlockSpec(memory_space=pltpu.VMEM)
+    rows = hidden // 2
+    whole = pl.BlockSpec((1, rows, feats), lambda i: (0, i, 0))
     parts = pl.pallas_call(
         cut_kernel,
         out_shape=[jax.ShapeDtypeStruct((hidden, feats // 4), BF)] * 8,
-        in_specs=[pl.BlockSpec(memory_space=pltpu.SMEM), vmem, vmem],
-        out_specs=[vmem] * 8,
+        grid=(2,),
+        in_specs=[pl.BlockSpec(memory_space=pltpu.SMEM), whole, whole],
+        out_specs=[pl.BlockSpec((rows, feats // 4), lambda i: (i, 0))] * 8,
         compiler_params=pltpu.CompilerParams(vmem_limit_bytes=32 << 20),
         cost_estimate=pl.CostEstimate(flops=0, bytes_accessed=4 * gate.size * 2, transcendentals=0),
     )(place, gate, down)
@@ -119,16 +121,14 @@
     weight = info[:, 1] + info[:, 2] + info[:, 3]
 
     gate_parts, down_parts = cut_weights(w_gate, w_down)
+    gate_own, gate_other = recut(gate_parts)
+    down_own, down_other = recut(down_parts)
     outputs = []
     for index, plan in ((0, old_plan), (1, new_plan)):
         slot_token, slot_weight = slots(code[:, index], weight[:, index], plan)
         pick = slot_token[:, None] == jnp.arange(2 * group, dtype=jnp.int32)[None, :]
         rows = dot(pick.astype(BF), tok[index], ((1,), (0,)), BF)
         rows = rows.reshape(peers, -1, rows.shape[1])
-        if index == 0:
-            rows, gate_parts, down_parts = lax.optimization_barrier((rows, gate_parts, down_parts))
-            gate_own, gate_other = recut(gate_parts)
-            down_own, down_other = recut(down_parts)
         rows = lax.all_to_all(rows, ("y", "x"), 0, 0, tiled=True).reshape(-1, rows.shape[2])
 
         send = dot(rows, gate_other, ((1,), (1,)), BF)

time: 206 us -> 207 us (level)
    unnamed x60 -> x48, local copies, waits for them, and re-layouts: 5.83 us -> 3.13 us
  transfers between devices with their start and end apart: 17 -> 17, of which waited for: 8 -> 8; matrix products, arithmetic and copies ran while one was open for 10% -> 10% of each run, Pallas kernels for 0% -> 1%
where the time goes in v6:
time: 207 us; the launch traced here: 206 us
  starting transfers between devices  76.4 us (37%)
  waiting for transfers between devices  76 us (37%)
  matrix products  20.7 us (10%)
  blocking collectives  12.5 us (6%)
  local copies, waits for them, and re-layouts  9.06 us (4%)
  other arithmetic  8.99 us (4%)
    ppermute x12, starting transfers between devices, swap(): return lax.ppermute(array, axes, [(i, last - i) for i in range(last + 1)])  34.6 us
    all_to_all x2, waiting for transfers between devices, local(): lax.all_to_all(out, ('y', 'x'), 0, 0, tiled=True).reshape(-1, out.shape[2])  32.6 us
    ppermute x12, waiting for transfers between devices, swap(): return lax.ppermute(array, axes, [(i, last - i) for i in range(last + 1)])  24.7 us
    dot_general x18, matrix products, dot(): return lax.dot_general(a, b, (dims, ((), ())), preferred_element_type=out)  20.7 us
    all_to_all x2, starting transfers between devices, local(): lax.all_to_all(rows, ('y', 'x'), 0, 0, tiled=True)  15.9 us
    all_to_all x2, starting transfers between devices, local(): lax.all_to_all(out, ('y', 'x'), 0, 0, tiled=True).reshape(-1, out.shape[2])  15.5 us
    all_to_all x1, blocking collectives, local(): terms = lax.all_to_all(mixed, ('p', 'zh'), 0, 0, tiled=True)  12.5 us
    all_to_all x1, waiting for transfers between devices, local(): lax.all_to_all(sent, ('p', 'zh'), 0, 0, tiled=True).reshape(2, 2, -1, feats)  11.4 us
  transfers between devices with their start and end apart: 17, of which 8 were waited for; matrix products, arithmetic and copies ran while one was open for 10% of the time, Pallas kernels for 1%

profile of v6, /device:TPU:2, one launch (start us, length us, event | category | flops | bytes accessed | tf_op | source)
XLA Modules:
  0.0 206.1 jit_solution(8072521412238759013)
XLA Ops:
  3.8 10.3 %all-to-all-start = ((bf16[4,80,512]{2,1,0:T(8,128)(2,1)}), bf16[4,80,512]{2,1,0:T(8,128)(2,1)S(1)}, u32[]{:S(2)}, u32[]{:S(2)}) async-start(bf16[4,80,512]{2,1,0:T(8,128)(2,1)} %broadcast_in_dim.131), calls=%async_computation | async-start | bytes 655360 | tf_op jit(solution)/shard_map/all_to_all | solution.py:115
  15.1 11.4 %all-to-all-done = bf16[4,80,512]{2,1,0:T(8,128)(2,1)S(1)} async-done(((bf16[4,80,512]{2,1,0:T(8,128)(2,1)}), bf16[4,80,512]{2,1,0:T(8,128)(2,1)S(1)}, u32[]{:S(2)}, u32[]{:S(2)}) %all-to-all-start) | async-done | bytes 327712 | tf_op jit(solution)/shard_map/all_to_all | solution.py:115
  29.0 2.2 %select_reduce_fusion.3 = (s32[2,32,8]{2,1,0:T(8,128)S(1)}, s32[2,32,8]{2,1,0:T(8,128)S(1)}) fusion(s32[256]{0:T(256)S(1)} %fusion.57, f32[2,32,256]{2,1,0:T(8,128)S(1)} %fusion.16, pred[2,32,256]{2,1,0:T(8,128)(4,1)S(1)} %fusion.46, f32[2,32,256]{2,1,0:T(8,128)S(1)} %fusion.13, pred[2,32,256]{2,1,0:T(8,128)(4,1)S(1)} %fusion.45), kind=kLoop, calls=%fused_computation.20 | loop fusion | flops 1047552 | bytes 168960 | tf_op jit(solution)/shard_map/reduce_sum | solution.py:92
  32.9 2.3 %fusion.23 = bf16[32,16,1024]{2,1,0:T(8,128)(2,1)} fusion(bf16[64,1024,1]{1,0,2:T(8,128)(2,1)S(1)} %reshape.205, s32[32,16]{1,0:T(8,128)} %copy.33), kind=kOutput, calls=%fused_computation.56 | convolution fusion | flops 67141632 | bytes 1181696 | tf_op jit(solution)/shard_map/dot_general | solution.py:18
  35.3 10.3 %all-to-all-start.3 = ((bf16[32,16,1024]{2,1,0:T(8,128)(2,1)}), bf16[32,16,1024]{2,1,0:T(8,128)(2,1)}, u32[]{:S(2)}, u32[]{:S(2)}) async-start(bf16[32,16,1024]{2,1,0:T(8,128)(2,1)} %fusion.23), calls=%async_computation.3 | async-start | bytes 2097152 | tf_op jit(solution)/shard_map/all_to_all | solution.py:132
  50.4 1.9 collective-permute-start.1
  52.3 3.6 %collective-permute-start.2 = (bf16[192,1024]{1,0:T(8,128)(2,1)}, bf16[192,1024]{1,0:T(8,128)(2,1)S(1)}, u32[]{:S(2)}, u32[]{:S(2)}) collective-permute-start(bf16[192,1024]{1,0:T(8,128)(2,1)} %get-tuple-element.16), channel_id=1, source_target_pairs={{0,192},{64,128},{128,64},{192,0},{1,193},{65,129},{129,65},{193,1... | collective-permute-start | bytes 1179656 | tf_op jit(solution)/shard_map/ppermute | solution.py:23
  55.9 2.3 %collective-permute-start = (bf16[192,1024]{1,0:T(8,128)(2,1)}, bf16[192,1024]{1,0:T(8,128)(2,1)S(1)}, u32[]{:S(2)}, u32[]{:S(2)}) collective-permute-start(bf16[192,1024]{1,0:T(8,128)(2,1)} %get-tuple-element.14), channel_id=1, source_target_pairs={{0,128},{128,0},{1,129},{129,1},{2,130},{130,2},{3,131},{131,3},{4... | collective-permute-start | bytes 1179656 | tf_op jit(solution)/shard_map/ppermute | solution.py:23
  61.7 7.3 %all-to-all-done.3 = bf16[32,16,1024]{2,1,0:T(8,128)(2,1)} async-done(((bf16[32,16,1024]{2,1,0:T(8,128)(2,1)}), bf16[32,16,1024]{2,1,0:T(8,128)(2,1)}, u32[]{:S(2)}, u32[]{:S(2)}) %all-to-all-start.3) | async-done | bytes 1048608 | tf_op jit(solution)/shard_map/all_to_all | solution.py:132
  69.0 5.6 %all-to-all-start.1 = ((bf16[32,16,1024]{2,1,0:T(8,128)(2,1)}), bf16[32,16,1024]{2,1,0:T(8,128)(2,1)}, u32[]{:S(2)}, u32[]{:S(2)}) async-start(bf16[32,16,1024]{2,1,0:T(8,128)(2,1)} %fusion.20), calls=%async_computation.1 | async-start | bytes 2097152 | tf_op jit(solution)/shard_map/all_to_all | solution.py:132
  74.8 2.1 %fusion.6 = bf16[512,384]{1,0:T(8,128)(2,1)S(1)} fusion(bf16[512,1024]{1,0:T(8,128)(2,1)} %bitcast.21, bf16[192,1024]{1,0:T(8,128)(2,1)S(1)} %get-tuple-element.36, bf16[192,1024]{1,0:T(8,128)(2,1)S(1)} %get-tuple-element.35), kind=kOutput, calls=%fused_computation.26 | convolution fusion | flops 404226048 | bytes 2228224 | tf_op jit(solution)/shard_map/dot_general | solution.py:18
  76.9 1.9 collective-permute-start.9
  78.8 7.5 %collective-permute-start.5 = (bf16[192,1024]{1,0:T(8,128)(2,1)S(1)}, bf16[192,1024]{1,0:T(8,128)(2,1)S(1)}, u32[]{:S(2)}, u32[]{:S(2)}) collective-permute-start(bf16[192,1024]{1,0:T(8,128)(2,1)S(1)} %copy-done.9), channel_id=1, source_target_pairs={{0,128},{128,0},{1,129},{129,1},{2,130},{130,2},{3,131},{131,3},{4... | collective-permute-start | bytes 1179656 | tf_op jit(solution)/shard_map/ppermute | solution.py:23
  86.4 2.1 %fusion.75 = (bf16[512,384]{1,0:T(8,128)(2,1)S(1)}, f32[512,384]{1,0:T(8,128)S(1)}) fusion(bf16[512,384]{1,0:T(8,128)(2,1)S(1)} %collective-permute-done.9, bf16[512,1024]{1,0:T(8,128)(2,1)} %bitcast.21, bf16[192,1024]{1,0:T(8,128)(2,1)S(1)} %get-tuple-element.34, bf16[192,1024]{1,0:T(8,128)(2,1)S(1)} %get-tuple-element.33), kind=kOutput, calls=%fused_computation.146 | convolution fusion | flops 404815872 | bytes 3407872 | tf_op jit(solution)/shard_map/dot_general | solution.py:18
  88.6 1.9 collective-permute-start.10
  90.5 2.1 %collective-permute-start.7 = (bf16[192,1024]{1,0:T(8,128)(2,1)S(1)}, bf16[192,1024]{1,0:T(8,128)(2,1)S(1)}, u32[]{:S(2)}, u32[]{:S(2)}) collective-permute-start(bf16[192,1024]{1,0:T(8,128)(2,1)S(1)} %copy-done.7), channel_id=1, source_target_pairs={{0,64},{64,0},{1,65},{65,1},{2,66},{66,2},{3,67},{67,3},{4,68},{68... | collective-permute-start | bytes 1179656 | tf_op jit(solution)/shard_map/ppermute | solution.py:23
  92.6 3.8 %collective-permute-start.8 = (bf16[192,1024]{1,0:T(8,128)(2,1)S(1)}, bf16[192,1024]{1,0:T(8,128)(2,1)S(1)}, u32[]{:S(2)}, u32[]{:S(2)}) collective-permute-start(bf16[192,1024]{1,0:T(8,128)(2,1)S(1)} %copy-done.5), channel_id=1, source_target_pairs={{0,192},{64,128},{128,64},{192,0},{1,193},{65,129},{129,65},{193,1... | collective-permute-start | bytes 1179656 | tf_op jit(solution)/shard_map/ppermute | solution.py:23
  96.6 8.1 %collective-permute-done.10 = bf16[512,384]{1,0:T(8,128)(2,1)S(1)} collective-permute-done((bf16[512,384]{1,0:T(8,128)(2,1)S(1)}, bf16[512,384]{1,0:T(8,128)(2,1)S(1)}, u32[]{:S(2)}, u32[]{:S(2)}) %collective-permute-start.10) | collective-permute-done | bytes 393248 | tf_op jit(solution)/shard_map/ppermute | solution.py:23
  104.9 1.9 collective-permute-start.11
  106.9 5.9 %collective-permute-done.8 = bf16[192,1024]{1,0:T(8,128)(2,1)S(1)} collective-permute-done((bf16[192,1024]{1,0:T(8,128)(2,1)S(1)}, bf16[192,1024]{1,0:T(8,128)(2,1)S(1)}, u32[]{:S(2)}, u32[]{:S(2)}) %collective-permute-start.8) | collective-permute-done | bytes 393248 | tf_op jit(solution)/shard_map/ppermute | solution.py:23
  112.8 2.8 %fusion.7 = bf16[512,384]{1,0:T(8,128)(2,1)} fusion(bf16[512,1024]{1,0:T(8,128)(2,1)} %bitcast.11, bf16[192,1024]{1,0:T(8,128)(2,1)} %copy-done.12, bf16[192,1024]{1,0:T(8,128)(2,1)S(1)} %get-tuple-element.35), kind=kOutput, calls=%fused_computation.27 | convolution fusion | flops 404226048 | bytes 2228224 | tf_op jit(solution)/shard_map/dot_general | solution.py:18
  115.6 2.0 collective-permute-start.3
  118.3 1.7 add_convert_fusion
  120.1 9.9 %all-to-all-start.4 = ((bf16[32,16,1024]{2,1,0:T(8,128)(2,1)}), bf16[32,16,1024]{2,1,0:T(8,128)(2,1)S(1)}, u32[]{:S(2)}, u32[]{:S(2)}) async-start(bf16[32,16,1024]{2,1,0:T(8,128)(2,1)} %bitcast.22), calls=%async_computation.4 | async-start | bytes 2097152 | tf_op jit(solution)/shard_map/all_to_all | solution.py:142
  130.0 2.0 fusion.76
  132.1 3.5 %collective-permute-start.4 = (bf16[512,384]{1,0:T(8,128)(2,1)S(1)}, bf16[512,384]{1,0:T(8,128)(2,1)S(1)}, u32[]{:S(2)}, u32[]{:S(2)}) collective-permute-start(bf16[512,384]{1,0:T(8,128)(2,1)S(1)} %get-tuple-element.60), channel_id=1, source_target_pairs={{0,128},{128,0},{1,129},{129,1},{2,130},{130,2},{3,131},{131,3},{4... | collective-permute-start | bytes 1179656 | tf_op jit(solution)/shard_map/ppermute | solution.py:23
  135.6 9.2 %collective-permute-done.4 = bf16[512,384]{1,0:T(8,128)(2,1)S(1)} collective-permute-done((bf16[512,384]{1,0:T(8,128)(2,1)S(1)}, bf16[512,384]{1,0:T(8,128)(2,1)S(1)}, u32[]{:S(2)}, u32[]{:S(2)}) %collective-permute-start.4) | collective-permute-done | bytes 393248 | tf_op jit(solution)/shard_map/ppermute | solution.py:23
  145.0 2.1 %collective-permute-start.6 = (bf16[512,384]{1,0:T(8,128)(2,1)S(1)}, bf16[512,384]{1,0:T(8,128)(2,1)S(1)}, u32[]{:S(2)}, u32[]{:S(2)}) collective-permute-start(bf16[512,384]{1,0:T(8,128)(2,1)S(1)} %multiply_convert_fusion.1), channel_id=1, source_target_pairs={{0,64},{64,0},{1,65},{65,1},{2,66},{66,2},{3,67},{67,3},{4,68},{68... | collective-permute-start | bytes 1179656 | tf_op jit(solution)/shard_map/ppermute | solution.py:23
  151.1 7.5 %all-to-all-done.4 = bf16[32,16,1024]{2,1,0:T(8,128)(2,1)S(1)} async-done(((bf16[32,16,1024]{2,1,0:T(8,128)(2,1)}), bf16[32,16,1024]{2,1,0:T(8,128)(2,1)S(1)}, u32[]{:S(2)}, u32[]{:S(2)}) %all-to-all-start.4) | async-done | bytes 1048608 | tf_op jit(solution)/shard_map/all_to_all | solution.py:142
  158.6 5.6 %all-to-all-start.2 = ((bf16[32,16,1024]{2,1,0:T(8,128)(2,1)}), bf16[32,16,1024]{2,1,0:T(8,128)(2,1)S(1)}, u32[]{:S(2)}, u32[]{:S(2)}) async-start(bf16[32,16,1024]{2,1,0:T(8,128)(2,1)} %bitcast.14), calls=%async_computation.2 | async-start | bytes 2097152 | tf_op jit(solution)/shard_map/all_to_all | solution.py:142
  166.5 25.1 %all-to-all-done.2 = bf16[32,16,1024]{2,1,0:T(8,128)(2,1)S(1)} async-done(((bf16[32,16,1024]{2,1,0:T(8,128)(2,1)}), bf16[32,16,1024]{2,1,0:T(8,128)(2,1)S(1)}, u32[]{:S(2)}, u32[]{:S(2)}) %all-to-all-start.2) | async-done | bytes 1048608 | tf_op jit(solution)/shard_map/all_to_all | solution.py:142
  192.9 12.5 %all_to_all.30 = bf16[4,64,512]{2,1,0:T(8,128)(2,1)S(1)} all-to-all(bf16[4,64,512]{2,1,0:T(8,128)(2,1)S(1)} %bitcast.72), channel_id=1, replica_groups=mesh['p'=2,'m'=2,'k'=2,'zh'=2,'y'=8,'x'=4] {'p','zh'}, dimensions={0} | all-to-all | bytes 524288 | tf_op jit(solution)/shard_map/all_to_all | solution.py:149
  (132 shorter events, 26.6 us)
Async XLA Ops:
  3.8 22.7 %all-to-all-start = ((bf16[4,80,512]{2,1,0:T(8,128)(2,1)}), bf16[4,80,512]{2,1,0:T(8,128)(2,1)S(1)}, u32[]{:S(2)}, u32[]{:S(2)}) async-start(bf16[4,80,512]{2,1,0:T(8,128)(2,1)} %broadcast_in_dim.131), calls=%async_computation | async-start | bytes 655360 | tf_op jit(solution)/shard_map/all_to_all | solution.py:115
  28.6 4.2 %copy-start.20 = (pred[2,32,256]{2,1,0:T(8,128)(4,1)}, pred[2,32,256]{2,1,0:T(8,128)(4,1)S(1)}, u32[]{:S(2)}) copy-start(pred[2,32,256]{2,1,0:T(8,128)(4,1)S(1)} %fusion.45) | copy-start | bytes 49156
  28.8 2.5 %copy-start.18 = (f32[2,32,256]{2,1,0:T(8,128)}, f32[2,32,256]{2,1,0:T(8,128)S(1)}, u32[]{:S(2)}) copy-start(f32[2,32,256]{2,1,0:T(8,128)S(1)} %fusion.13) | copy-start | bytes 196612
  32.9 12.8 %copy-start = (bf16[1,192,4096]{2,1,0:T(8,128)(2,1)S(1)}, bf16[1,192,4096]{2,1,0:T(8,128)(2,1)}, u32[]{:S(2)}) copy-start(bf16[1,192,4096]{2,1,0:T(8,128)(2,1)} %gate.1) | copy-start | bytes 4718596
  32.9 12.7 %copy-start.1 = (bf16[1,192,4096]{2,1,0:T(8,128)(2,1)S(1)}, bf16[1,192,4096]{2,1,0:T(8,128)(2,1)}, u32[]{:S(2)}) copy-start(bf16[1,192,4096]{2,1,0:T(8,128)(2,1)} %down.1) | copy-start | bytes 4718596
  35.3 33.8 %all-to-all-start.3 = ((bf16[32,16,1024]{2,1,0:T(8,128)(2,1)}), bf16[32,16,1024]{2,1,0:T(8,128)(2,1)}, u32[]{:S(2)}, u32[]{:S(2)}) async-start(bf16[32,16,1024]{2,1,0:T(8,128)(2,1)} %fusion.23), calls=%async_computation.3 | async-start | bytes 2097152 | tf_op jit(solution)/shard_map/all_to_all | solution.py:132
  50.4 24.3 %collective-permute-start.1 = (bf16[192,1024]{1,0:T(8,128)(2,1)}, bf16[192,1024]{1,0:T(8,128)(2,1)S(1)}, u32[]{:S(2)}, u32[]{:S(2)}) collective-permute-start(bf16[192,1024]{1,0:T(8,128)(2,1)} %get-tuple-element.15), channel_id=1, source_target_pairs={{0,64},{64,0},{1,65},{65,1},{2,66},{66,2},{3,67},{67,3},{4,68},{68... | collective-permute-start | bytes 1179656 | tf_op jit(solution)/shard_map/ppermute | solution.py:23
  52.3 22.4 %collective-permute-start.2 = (bf16[192,1024]{1,0:T(8,128)(2,1)}, bf16[192,1024]{1,0:T(8,128)(2,1)S(1)}, u32[]{:S(2)}, u32[]{:S(2)}) collective-permute-start(bf16[192,1024]{1,0:T(8,128)(2,1)} %get-tuple-element.16), channel_id=1, source_target_pairs={{0,192},{64,128},{128,64},{192,0},{1,193},{65,129},{129,65},{193,1... | collective-permute-start | bytes 1179656 | tf_op jit(solution)/shard_map/ppermute | solution.py:23
  55.9 30.4 %collective-permute-start = (bf16[192,1024]{1,0:T(8,128)(2,1)}, bf16[192,1024]{1,0:T(8,128)(2,1)S(1)}, u32[]{:S(2)}, u32[]{:S(2)}) collective-permute-start(bf16[192,1024]{1,0:T(8,128)(2,1)} %get-tuple-element.14), channel_id=1, source_target_pairs={{0,128},{128,0},{1,129},{129,1},{2,130},{130,2},{3,131},{131,3},{4... | collective-permute-start | bytes 1179656 | tf_op jit(solution)/shard_map/ppermute | solution.py:23
  69.0 43.8 %all-to-all-start.1 = ((bf16[32,16,1024]{2,1,0:T(8,128)(2,1)}), bf16[32,16,1024]{2,1,0:T(8,128)(2,1)}, u32[]{:S(2)}, u32[]{:S(2)}) async-start(bf16[32,16,1024]{2,1,0:T(8,128)(2,1)} %fusion.20), calls=%async_computation.1 | async-start | bytes 2097152 | tf_op jit(solution)/shard_map/all_to_all | solution.py:132
  74.8 4.1 %copy-start.9 = (bf16[192,1024]{1,0:T(8,128)(2,1)S(1)}, bf16[192,1024]{1,0:T(8,128)(2,1)}, u32[]{:S(2)}) copy-start(bf16[192,1024]{1,0:T(8,128)(2,1)} %copy-done.8) | copy-start | bytes 1179652
  74.8 11.5 %copy-start.3 = (bf16[192,1024]{1,0:T(8,128)(2,1)S(1)}, bf16[192,1024]{1,0:T(8,128)(2,1)}, u32[]{:S(2)}) copy-start(bf16[192,1024]{1,0:T(8,128)(2,1)} %copy-done.2) | copy-start | bytes 1179652
  76.9 9.5 %collective-permute-start.9 = (bf16[512,384]{1,0:T(8,128)(2,1)S(1)}, bf16[512,384]{1,0:T(8,128)(2,1)S(1)}, u32[]{:S(2)}, u32[]{:S(2)}) collective-permute-start(bf16[512,384]{1,0:T(8,128)(2,1)S(1)} %fusion.6), channel_id=1, source_target_pairs={{0,64},{64,0},{1,65},{65,1},{2,66},{66,2},{3,67},{67,3},{4,68},{68... | collective-permute-start | bytes 1179656 | tf_op jit(solution)/shard_map/ppermute | solution.py:23
  78.8 17.6 %collective-permute-start.5 = (bf16[192,1024]{1,0:T(8,128)(2,1)S(1)}, bf16[192,1024]{1,0:T(8,128)(2,1)S(1)}, u32[]{:S(2)}, u32[]{:S(2)}) collective-permute-start(bf16[192,1024]{1,0:T(8,128)(2,1)S(1)} %copy-done.9), channel_id=1, source_target_pairs={{0,128},{128,0},{1,129},{129,1},{2,130},{130,2},{3,131},{131,3},{4... | collective-permute-start | bytes 1179656 | tf_op jit(solution)/shard_map/ppermute | solution.py:23
  86.4 4.1 %copy-start.7 = (bf16[192,1024]{1,0:T(8,128)(2,1)S(1)}, bf16[192,1024]{1,0:T(8,128)(2,1)}, u32[]{:S(2)}) copy-start(bf16[192,1024]{1,0:T(8,128)(2,1)} %copy-done.6) | copy-start | bytes 1179652
  86.4 6.2 %copy-start.5 = (bf16[192,1024]{1,0:T(8,128)(2,1)S(1)}, bf16[192,1024]{1,0:T(8,128)(2,1)}, u32[]{:S(2)}) copy-start(bf16[192,1024]{1,0:T(8,128)(2,1)} %copy-done.4) | copy-start | bytes 1179652
  88.6 16.1 %collective-permute-start.10 = (bf16[512,384]{1,0:T(8,128)(2,1)S(1)}, bf16[512,384]{1,0:T(8,128)(2,1)S(1)}, u32[]{:S(2)}, u32[]{:S(2)}) collective-permute-start(bf16[512,384]{1,0:T(8,128)(2,1)S(1)} %get-tuple-element.58), channel_id=1, source_target_pairs={{0,128},{128,0},{1,129},{129,1},{2,130},{130,2},{3,131},{131,3},{4... | collective-permute-start | bytes 1179656 | tf_op jit(solution)/shard_map/ppermute | solution.py:23
  90.5 16.4 %collective-permute-start.7 = (bf16[192,1024]{1,0:T(8,128)(2,1)S(1)}, bf16[192,1024]{1,0:T(8,128)(2,1)S(1)}, u32[]{:S(2)}, u32[]{:S(2)}) collective-permute-start(bf16[192,1024]{1,0:T(8,128)(2,1)S(1)} %copy-done.7), channel_id=1, source_target_pairs={{0,64},{64,0},{1,65},{65,1},{2,66},{66,2},{3,67},{67,3},{4,68},{68... | collective-permute-start | bytes 1179656 | tf_op jit(solution)/shard_map/ppermute | solution.py:23
  92.6 20.1 %collective-permute-start.8 = (bf16[192,1024]{1,0:T(8,128)(2,1)S(1)}, bf16[192,1024]{1,0:T(8,128)(2,1)S(1)}, u32[]{:S(2)}, u32[]{:S(2)}) collective-permute-start(bf16[192,1024]{1,0:T(8,128)(2,1)S(1)} %copy-done.5), channel_id=1, source_target_pairs={{0,192},{64,128},{128,64},{192,0},{1,193},{65,129},{129,65},{193,1... | collective-permute-start | bytes 1179656 | tf_op jit(solution)/shard_map/ppermute | solution.py:23
  104.9 12.7 %collective-permute-start.11 = (bf16[512,384]{1,0:T(8,128)(2,1)S(1)}, bf16[512,384]{1,0:T(8,128)(2,1)S(1)}, u32[]{:S(2)}, u32[]{:S(2)}) collective-permute-start(bf16[512,384]{1,0:T(8,128)(2,1)S(1)} %multiply_convert_fusion), channel_id=1, source_target_pairs={{0,64},{64,0},{1,65},{65,1},{2,66},{66,2},{3,67},{67,3},{4,68},{68... | collective-permute-start | bytes 1179656 | tf_op jit(solution)/shard_map/ppermute | solution.py:23
  115.6 14.4 %collective-permute-start.3 = (bf16[512,384]{1,0:T(8,128)(2,1)}, bf16[512,384]{1,0:T(8,128)(2,1)}, u32[]{:S(2)}, u32[]{:S(2)}) collective-permute-start(bf16[512,384]{1,0:T(8,128)(2,1)} %fusion.7), channel_id=1, source_target_pairs={{0,64},{64,0},{1,65},{65,1},{2,66},{66,2},{3,67},{67,3},{4,68},{68... | collective-permute-start | bytes 1179656 | tf_op jit(solution)/shard_map/ppermute | solution.py:23
  120.1 10.0 %copy-start.11 = (bf16[192,1024]{1,0:T(8,128)(2,1)S(1)}, bf16[192,1024]{1,0:T(8,128)(2,1)}, u32[]{:S(2)}) copy-start(bf16[192,1024]{1,0:T(8,128)(2,1)} %copy-done.10) | copy-start | bytes 1179652
  120.1 38.5 %all-to-all-start.4 = ((bf16[32,16,1024]{2,1,0:T(8,128)(2,1)}), bf16[32,16,1024]{2,1,0:T(8,128)(2,1)S(1)}, u32[]{:S(2)}, u32[]{:S(2)}) async-start(bf16[32,16,1024]{2,1,0:T(8,128)(2,1)} %bitcast.22), calls=%async_computation.4 | async-start | bytes 2097152 | tf_op jit(solution)/shard_map/all_to_all | solution.py:142
  132.1 12.7 %collective-permute-start.4 = (bf16[512,384]{1,0:T(8,128)(2,1)S(1)}, bf16[512,384]{1,0:T(8,128)(2,1)S(1)}, u32[]{:S(2)}, u32[]{:S(2)}) collective-permute-start(bf16[512,384]{1,0:T(8,128)(2,1)S(1)} %get-tuple-element.60), channel_id=1, source_target_pairs={{0,128},{128,0},{1,129},{129,1},{2,130},{130,2},{3,131},{131,3},{4... | collective-permute-start | bytes 1179656 | tf_op jit(solution)/shard_map/ppermute | solution.py:23
  145.0 3.6 %collective-permute-start.6 = (bf16[512,384]{1,0:T(8,128)(2,1)S(1)}, bf16[512,384]{1,0:T(8,128)(2,1)S(1)}, u32[]{:S(2)}, u32[]{:S(2)}) collective-permute-start(bf16[512,384]{1,0:T(8,128)(2,1)S(1)} %multiply_convert_fusion.1), channel_id=1, source_target_pairs={{0,64},{64,0},{1,65},{65,1},{2,66},{66,2},{3,67},{67,3},{4,68},{68... | collective-permute-start | bytes 1179656 | tf_op jit(solution)/shard_map/ppermute | solution.py:23
  151.0 13.1 %copy-start.15 = (s32[32,2,8]{2,0,1:T(8,128)S(1)}, s32[32,2,8]{2,0,1:T(8,128)}, u32[]{:S(2)}) copy-start(s32[32,2,8]{2,0,1:T(8,128)} %get-tuple-element.52) | copy-start | bytes 6148
  151.1 13.2 %copy-start.14 = (s32[32,2,8]{2,0,1:T(8,128)S(1)}, s32[32,2,8]{2,0,1:T(8,128)}, u32[]{:S(2)}) copy-start(s32[32,2,8]{2,0,1:T(8,128)} %copy-done.13) | copy-start | bytes 6148
  151.1 13.2 %copy-start.22 = (f32[2,2,256]{2,1,0:T(2,128)S(1)}, f32[2,2,256]{2,1,0:T(2,128)}, u32[]{:S(2)}) copy-start(f32[2,2,256]{2,1,0:T(2,128)} %get-tuple-element.39) | copy-start | bytes 12292
  151.1 13.2 %copy-start.19 = (f32[2,32,256]{2,1,0:T(8,128)S(1)}, f32[2,32,256]{2,1,0:T(8,128)}, u32[]{:S(2)}) copy-start(f32[2,32,256]{2,1,0:T(8,128)} %copy-done.18) | copy-start | bytes 196612
  151.1 13.2 %copy-start.21 = (pred[2,32,256]{2,1,0:T(8,128)(4,1)S(1)}, pred[2,32,256]{2,1,0:T(8,128)(4,1)}, u32[]{:S(2)}) copy-start(pred[2,32,256]{2,1,0:T(8,128)(4,1)} %copy-done.20) | copy-start | bytes 49156
  151.1 13.6 %copy-start.17 = (f32[2,32,256]{2,1,0:T(8,128)S(1)}, f32[2,32,256]{2,1,0:T(8,128)}, u32[]{:S(2)}) copy-start(f32[2,32,256]{2,1,0:T(8,128)} %copy-done.16) | copy-start | bytes 196612
  158.6 33.0 %all-to-all-start.2 = ((bf16[32,16,1024]{2,1,0:T(8,128)(2,1)}), bf16[32,16,1024]{2,1,0:T(8,128)(2,1)S(1)}, u32[]{:S(2)}, u32[]{:S(2)}) async-start(bf16[32,16,1024]{2,1,0:T(8,128)(2,1)} %bitcast.14), calls=%async_computation.2 | async-start | bytes 2097152 | tf_op jit(solution)/shard_map/all_to_all | solution.py:142
  (8 other events, 10.3 us)

commit v7 on v6

--- a/solution.py
+++ b/solution.py
@@ -27,12 +27,11 @@
     m, k = place[0], place[1]
     width = gate.shape[2] // 8
     for which, weight in enumerate((gate, down)):
-        for dm in range(2):
-            for dk in range(2):
-                out = outs[4 * which + 2 * dm + dk]
-                for p in range(2):
-                    at = (4 * p + 2 * (m ^ dm) + (k ^ dk)) * width
-                    out[:, p * width : (p + 1) * width] = weight[0, :, pl.ds(pl.multiple_of(at, width), width)]
+        mine, for_k, for_m = outs[3 * which : 3 * which + 3]
+        for dm, dk, out in ((0, 0, mine), (0, 1, for_k), (1, 0, for_m.at[0]), (1, 1, for_m.at[1])):
+            for p in range(2):
+                at = (4 * p + 2 * (m ^ dm) + (k ^ dk)) * width
+                out[:, p * width : (p + 1) * width] = weight[0, :, pl.ds(pl.multiple_of(at, width), width)]
 
 
 def cut_weights(gate, down):
@@ -40,31 +39,26 @@
     place = jnp.stack([lax.axis_index("m"), lax.axis_index("k")]).astype(jnp.int32)
     rows = hidden // 2
     whole = pl.BlockSpec((1, rows, feats), lambda i: (0, i, 0))
+    one = pl.BlockSpec((rows, feats // 4), lambda i: (i, 0))
+    two = pl.BlockSpec((2, rows, feats // 4), lambda i: (0, i, 0))
+    shape = lambda *lead: jax.ShapeDtypeStruct((*lead, hidden, feats // 4), BF)
     parts = pl.pallas_call(
         cut_kernel,
-        out_shape=[jax.ShapeDtypeStruct((hidden, feats // 4), BF)] * 8,
+        out_shape=[shape(), shape(), shape(2)] * 2,
         grid=(2,),
         in_specs=[pl.BlockSpec(memory_space=pltpu.SMEM), whole, whole],
-        out_specs=[pl.BlockSpec((rows, feats // 4), lambda i: (i, 0))] * 8,
+        out_specs=[one, one, two] * 2,
         compiler_params=pltpu.CompilerParams(vmem_limit_bytes=32 << 20),
         cost_estimate=pl.CostEstimate(flops=0, bytes_accessed=4 * gate.size * 2, transcendentals=0),
     )(place, gate, down)
-    return parts[:4], parts[4:]
+    return parts[:3], parts[3:]
 
 
-def recut(parts):
+def order(near, far):
     m = lax.axis_index("m")
-    mine, for_k, for_m, for_mk = parts
-    far_own = swap(for_m, "m")
-    near_other = swap(for_k, "k")
-    far_other = swap(for_mk, "m", "k")
-
-    def order(near, far):
-        first = jnp.where(m == 0, near, far)
-        second = jnp.where(m == 0, far, near)
-        return jnp.concatenate([first, second], axis=0)
-
-    return order(mine, far_own), order(near_other, far_other)
+    first = jnp.where(m == 0, near, far)
+    second = jnp.where(m == 0, far, near)
+    return jnp.concatenate([first, second], axis=0)
 
 
 def slots(codes, weights, plan):
@@ -121,14 +115,23 @@
     weight = info[:, 1] + info[:, 2] + info[:, 3]
 
     gate_parts, down_parts = cut_weights(w_gate, w_down)
-    gate_own, gate_other = recut(gate_parts)
-    down_own, down_other = recut(down_parts)
+    gate_far = swap(gate_parts[2], "m")
+
     outputs = []
     for index, plan in ((0, old_plan), (1, new_plan)):
         slot_token, slot_weight = slots(code[:, index], weight[:, index], plan)
         pick = slot_token[:, None] == jnp.arange(2 * group, dtype=jnp.int32)[None, :]
         rows = dot(pick.astype(BF), tok[index], ((1,), (0,)), BF)
         rows = rows.reshape(peers, -1, rows.shape[1])
+        if index == 0:
+            rows, gate_far, down_ready = lax.optimization_barrier((rows, gate_far, down_parts[2]))
+            down_far = swap(down_ready, "m")
+            gate_own = order(gate_parts[0], gate_far[0])
+            gate_other = swap(order(gate_parts[1], gate_far[1]), "k")
+            down_own = order(down_parts[0], down_far[0])
+            down_other = swap(order(down_parts[1], down_far[1]), "k")
+        else:
+            rows, gate_other, down_other = lax.optimization_barrier((rows, gate_other, down_other))
         rows = lax.all_to_all(rows, ("y", "x"), 0, 0, tiled=True).reshape(-1, rows.shape[2])
 
         send = dot(rows, gate_other, ((1,), (1,)), BF)

time: 207 us -> 208 us (level)
  starting transfers between devices: 76.4 us -> 68.1 us
  other arithmetic: 8.99 us -> 16.1 us
    ppermute x12 -> x10, waiting for transfers between devices: 24.7 us -> 33.7 us  [swap(): return lax.ppermute(array, axes, [(i, last - i) for i in range(last + 1)])]
    ppermute x12 -> x10, starting transfers between devices: 34.6 us -> 26.2 us  [swap(): return lax.ppermute(array, axes, [(i, last - i) for i in range(last + 1)])]
    all_to_all x1, waiting for transfers between devices: 11.4 us -> 3.76 us  [local(): lax.all_to_all(sent, ('p', 'zh'), 0, 0, tiled=True).reshape(2, 2, -1, feats)]
    all_to_all x2, starting transfers between devices: 15.9 us -> 19.3 us  [local(): lax.all_to_all(rows, ('y', 'x'), 0, 0, tiled=True)]
    all_to_all x2, starting transfers between devices: 15.5 us -> 12.4 us  [local(): lax.all_to_all(out, ('y', 'x'), 0, 0, tiled=True).reshape(-1, out.shape[2])]
  transfers between devices with their start and end apart: 17 -> 15, of which waited for: 8 -> 10; matrix products, arithmetic and copies ran while one was open for 10% -> 19% of each run, Pallas kernels for 1% -> 0%
where the time goes in v7:
time: 208 us; the launch traced here: 206 us
  waiting for transfers between devices  74.3 us (36%)
  starting transfers between devices  68.1 us (33%)
  matrix products  22.7 us (11%)
  other arithmetic  16.1 us (8%)
  blocking collectives  13.6 us (7%)
  local copies, waits for them, and re-layouts  10.1 us (5%)
    ppermute x10, waiting for transfers between devices, swap(): return lax.ppermute(array, axes, [(i, last - i) for i in range(last + 1)])  33.7 us
    all_to_all x2, waiting for transfers between devices, local(): lax.all_to_all(out, ('y', 'x'), 0, 0, tiled=True).reshape(-1, out.shape[2])  30.9 us
    ppermute x10, starting transfers between devices, swap(): return lax.ppermute(array, axes, [(i, last - i) for i in range(last + 1)])  26.2 us
    dot_general x18, matrix products, dot(): return lax.dot_general(a, b, (dims, ((), ())), preferred_element_type=out)  22.7 us
    all_to_all x2, starting transfers between devices, local(): lax.all_to_all(rows, ('y', 'x'), 0, 0, tiled=True)  19.3 us
    all_to_all x1, blocking collectives, local(): terms = lax.all_to_all(mixed, ('p', 'zh'), 0, 0, tiled=True)  13.6 us
    all_to_all x2, starting transfers between devices, local(): lax.all_to_all(out, ('y', 'x'), 0, 0, tiled=True).reshape(-1, out.shape[2])  12.4 us
    all_to_all x1, starting transfers between devices, local(): lax.all_to_all(sent, ('p', 'zh'), 0, 0, tiled=True).reshape(2, 2, -1, feats)  10.3 us
  transfers between devices with their start and end apart: 15, of which 10 were waited for; matrix products, arithmetic and copies ran while one was open for 19% of the time, Pallas kernels for 0%

profile of v7, /device:TPU:2, one launch (start us, length us, event | category | flops | bytes accessed | tf_op | source)
XLA Modules:
  0.0 206.3 jit_solution(13482344651181179656)
XLA Ops:
  3.8 10.3 %all-to-all-start = ((bf16[4,80,512]{2,1,0:T(8,128)(2,1)}), bf16[4,80,512]{2,1,0:T(8,128)(2,1)S(1)}, u32[]{:S(2)}, u32[]{:S(2)}) async-start(bf16[4,80,512]{2,1,0:T(8,128)(2,1)} %broadcast_in_dim.131), calls=%async_computation | async-start | bytes 655360 | tf_op jit(solution)/shard_map/all_to_all | solution.py:109
  18.0 3.4 %collective-permute-start = (bf16[2,192,1024]{2,1,0:T(8,128)(2,1)S(1)}, bf16[2,192,1024]{2,1,0:T(8,128)(2,1)}, u32[]{:S(2)}, u32[]{:S(2)}) collective-permute-start(bf16[2,192,1024]{2,1,0:T(8,128)(2,1)S(1)} %get-tuple-element.17), channel_id=1, source_target_pairs={{0,128},{128,0},{1,129},{129,1},{2,130},{130,2},{3,131},{131,3},{4... | collective-permute-start | bytes 2359304 | tf_op jit(solution)/shard_map/ppermute | solution.py:23
  22.8 3.8 %all-to-all-done = bf16[4,80,512]{2,1,0:T(8,128)(2,1)S(1)} async-done(((bf16[4,80,512]{2,1,0:T(8,128)(2,1)}), bf16[4,80,512]{2,1,0:T(8,128)(2,1)S(1)}, u32[]{:S(2)}, u32[]{:S(2)}) %all-to-all-start) | async-done | bytes 327712 | tf_op jit(solution)/shard_map/all_to_all | solution.py:109
  34.3 2.9 %select_reduce_fusion.3 = (s32[2,32,8]{2,1,0:T(8,128)S(1)}, s32[2,32,8]{2,1,0:T(8,128)S(1)}) fusion(s32[256]{0:T(256)} %fusion.57, f32[2,32,256]{2,1,0:T(8,128)S(1)} %fusion.16, pred[2,32,256]{2,1,0:T(8,128)(4,1)S(1)} %fusion.46, f32[2,32,256]{2,1,0:T(8,128)S(1)} %fusion.13, pred[2,32,256]{2,1,0:T(8,128)(4,1)S(1)} %fusion.45), kind=kLoop, calls=%fused_computation.22 | loop fusion | flops 1047552 | bytes 168960 | tf_op jit(solution)/shard_map/reduce_sum | solution.py:86
  40.0 2.2 %fusion.20 = bf16[32,16,1024]{2,1,0:T(8,128)(2,1)} fusion(bf16[64,1024,1]{1,0,2:T(8,128)(2,1)S(1)} %reshape.204, s32[32,16]{1,0:T(8,128)} %copy.28), kind=kOutput, calls=%fused_computation.56 | convolution fusion | flops 67141632 | bytes 1181696 | tf_op jit(solution)/shard_map/dot_general | solution.py:18
  42.1 10.3 %all-to-all-start.1 = ((bf16[32,16,1024]{2,1,0:T(8,128)(2,1)}), bf16[32,16,1024]{2,1,0:T(8,128)(2,1)}, u32[]{:S(2)}, u32[]{:S(2)}) async-start(bf16[32,16,1024]{2,1,0:T(8,128)(2,1)} %fusion.20), calls=%async_computation.1 | async-start | bytes 2097152 | tf_op jit(solution)/shard_map/all_to_all | solution.py:135
  52.4 3.8 %collective-permute-start.4 = (bf16[2,192,1024]{2,1,0:T(8,128)(2,1)S(1)}, bf16[2,192,1024]{2,1,0:T(8,128)(2,1)S(1)}, u32[]{:S(2)}, u32[]{:S(2)}) collective-permute-start(bf16[2,192,1024]{2,1,0:T(8,128)(2,1)S(1)} %get-tuple-element.24), channel_id=1, source_target_pairs={{0,128},{128,0},{1,129},{129,1},{2,130},{130,2},{3,131},{131,3},{4... | collective-permute-start | bytes 2359304 | tf_op jit(solution)/shard_map/ppermute | solution.py:23
  56.3 2.1 %bitcast_select_fusion.3 = (bf16[192,1024]{1,0:T(8,128)(2,1)}, bf16[192,1024]{1,0:T(8,128)(2,1)}, bf16[192,1024]{1,0:T(8,128)(2,1)S(1)}, bf16[192,1024]{1,0:T(8,128)(2,1)S(1)}) fusion(bf16[192,1024]{1,0:T(8,128)(2,1)S(1)} %get-tuple-element.20, pred[]{:T(512)S(6)} %eq.228, bf16[2,192,1024]{2,1,0:T(8,128)(2,1)} %collective-permute-done, ...), kind=kLoop, calls=%fused_computation.33 | loop fusion | flops 786432 | bytes 3145729 | tf_op jit(solution)/shard_map/jit(_where)/select_n | solution.py:59
  58.5 1.9 collective-permute-start.1
  60.4 11.8 %collective-permute-done.4 = bf16[2,192,1024]{2,1,0:T(8,128)(2,1)S(1)} collective-permute-done((bf16[2,192,1024]{2,1,0:T(8,128)(2,1)S(1)}, bf16[2,192,1024]{2,1,0:T(8,128)(2,1)S(1)}, u32[]{:S(2)}, u32[]{:S(2)}) %collective-permute-start.4) | collective-permute-done | bytes 786464 | tf_op jit(solution)/shard_map/ppermute | solution.py:23
  72.4 1.9 collective-permute-start.6
  75.3 2.2 %fusion.23 = bf16[32,16,1024]{2,1,0:T(8,128)(2,1)} fusion(bf16[64,1024,1]{1,0,2:T(8,128)(2,1)S(1)} %reshape.205, s32[32,16]{1,0:T(8,128)} %copy.33), kind=kOutput, calls=%fused_computation.58 | convolution fusion | flops 67141632 | bytes 1181696 | tf_op jit(solution)/shard_map/dot_general | solution.py:18
  78.4 8.9 %all-to-all-start.3 = ((bf16[32,16,1024]{2,1,0:T(8,128)(2,1)}), bf16[32,16,1024]{2,1,0:T(8,128)(2,1)}, u32[]{:S(2)}, u32[]{:S(2)}) async-start(bf16[32,16,1024]{2,1,0:T(8,128)(2,1)} %fusion.23), calls=%async_computation.3 | async-start | bytes 2097152 | tf_op jit(solution)/shard_map/all_to_all | solution.py:135
  87.4 2.2 %fusion.71 = bf16[512,384]{1,0:T(8,128)(2,1)S(1)} fusion(bf16[512,1024]{1,0:T(8,128)(2,1)} %bitcast.13, bf16[384,1024]{1,0:T(8,128)(2,1)} %collective-permute-done.1), kind=kOutput, calls=%fused_computation.144 | convolution fusion | flops 402653184 | bytes 2228224 | tf_op jit(solution)/shard_map/dot_general | solution.py:18
  89.6 1.9 collective-permute-start.2
  93.3 1.9 fusion.2
  95.2 3.6 %collective-permute-start.3 = (bf16[512,384]{1,0:T(8,128)(2,1)S(1)}, bf16[512,384]{1,0:T(8,128)(2,1)S(1)}, u32[]{:S(2)}, u32[]{:S(2)}) collective-permute-start(bf16[512,384]{1,0:T(8,128)(2,1)S(1)} %get-tuple-element.72), channel_id=1, source_target_pairs={{0,128},{128,0},{1,129},{129,1},{2,130},{130,2},{3,131},{131,3},{4... | collective-permute-start | bytes 1179656 | tf_op jit(solution)/shard_map/ppermute | solution.py:23
  98.9 9.4 %collective-permute-done.3 = bf16[512,384]{1,0:T(8,128)(2,1)S(1)} collective-permute-done((bf16[512,384]{1,0:T(8,128)(2,1)S(1)}, bf16[512,384]{1,0:T(8,128)(2,1)S(1)}, u32[]{:S(2)}, u32[]{:S(2)}) %collective-permute-start.3) | collective-permute-done | bytes 393248 | tf_op jit(solution)/shard_map/ppermute | solution.py:23
  108.5 1.9 collective-permute-start.5
  110.5 5.1 %all-to-all-done.3 = bf16[32,16,1024]{2,1,0:T(8,128)(2,1)} async-done(((bf16[32,16,1024]{2,1,0:T(8,128)(2,1)}), bf16[32,16,1024]{2,1,0:T(8,128)(2,1)}, u32[]{:S(2)}, u32[]{:S(2)}) %all-to-all-start.3) | async-done | bytes 1048608 | tf_op jit(solution)/shard_map/all_to_all | solution.py:135
  115.5 2.9 %fusion.73 = bf16[512,384]{1,0:T(8,128)(2,1)} fusion(bf16[512,1024]{1,0:T(8,128)(2,1)} %bitcast.25, bf16[384,1024]{1,0:T(8,128)(2,1)} %collective-permute-done.1), kind=kOutput, calls=%fused_computation.146 | convolution fusion | flops 402653184 | bytes 2228224 | tf_op jit(solution)/shard_map/dot_general | solution.py:18
  118.5 1.9 collective-permute-start.7
  122.8 6.2 %all-to-all-start.2 = ((bf16[32,16,1024]{2,1,0:T(8,128)(2,1)}), bf16[32,16,1024]{2,1,0:T(8,128)(2,1)S(1)}, u32[]{:S(2)}, u32[]{:S(2)}) async-start(bf16[32,16,1024]{2,1,0:T(8,128)(2,1)} %bitcast.18), calls=%async_computation.2 | async-start | bytes 2097152 | tf_op jit(solution)/shard_map/all_to_all | solution.py:145
  129.0 2.0 fusion.3
  131.1 3.6 %collective-permute-start.8 = (bf16[512,384]{1,0:T(8,128)(2,1)S(1)}, bf16[512,384]{1,0:T(8,128)(2,1)S(1)}, u32[]{:S(2)}, u32[]{:S(2)}) collective-permute-start(bf16[512,384]{1,0:T(8,128)(2,1)S(1)} %get-tuple-element.70), channel_id=1, source_target_pairs={{0,128},{128,0},{1,129},{129,1},{2,130},{130,2},{3,131},{131,3},{4... | collective-permute-start | bytes 1179656 | tf_op jit(solution)/shard_map/ppermute | solution.py:23
  134.7 9.2 %collective-permute-done.8 = bf16[512,384]{1,0:T(8,128)(2,1)S(1)} collective-permute-done((bf16[512,384]{1,0:T(8,128)(2,1)S(1)}, bf16[512,384]{1,0:T(8,128)(2,1)S(1)}, u32[]{:S(2)}, u32[]{:S(2)}) %collective-permute-start.8) | collective-permute-done | bytes 393248 | tf_op jit(solution)/shard_map/ppermute | solution.py:23
  145.2 2.1 %collective-permute-start.9 = (bf16[512,384]{1,0:T(8,128)(2,1)S(1)}, bf16[512,384]{1,0:T(8,128)(2,1)S(1)}, u32[]{:S(2)}, u32[]{:S(2)}) collective-permute-start(bf16[512,384]{1,0:T(8,128)(2,1)S(1)} %multiply_convert_fusion), channel_id=1, source_target_pairs={{0,64},{64,0},{1,65},{65,1},{2,66},{66,2},{3,67},{67,3},{4,68},{68... | collective-permute-start | bytes 1179656 | tf_op jit(solution)/shard_map/ppermute | solution.py:23
  149.5 1.7 add_convert_fusion
  151.3 5.8 %all-to-all-done.2 = bf16[32,16,1024]{2,1,0:T(8,128)(2,1)S(1)} async-done(((bf16[32,16,1024]{2,1,0:T(8,128)(2,1)}), bf16[32,16,1024]{2,1,0:T(8,128)(2,1)S(1)}, u32[]{:S(2)}, u32[]{:S(2)}) %all-to-all-start.2) | async-done | bytes 1048608 | tf_op jit(solution)/shard_map/all_to_all | solution.py:145
  157.1 6.2 %all-to-all-start.4 = ((bf16[32,16,1024]{2,1,0:T(8,128)(2,1)}), bf16[32,16,1024]{2,1,0:T(8,128)(2,1)S(1)}, u32[]{:S(2)}, u32[]{:S(2)}) async-start(bf16[32,16,1024]{2,1,0:T(8,128)(2,1)} %bitcast.26), calls=%async_computation.4 | async-start | bytes 2097152 | tf_op jit(solution)/shard_map/all_to_all | solution.py:145
  165.6 25.1 %all-to-all-done.4 = bf16[32,16,1024]{2,1,0:T(8,128)(2,1)S(1)} async-done(((bf16[32,16,1024]{2,1,0:T(8,128)(2,1)}), bf16[32,16,1024]{2,1,0:T(8,128)(2,1)S(1)}, u32[]{:S(2)}, u32[]{:S(2)}) %all-to-all-start.4) | async-done | bytes 1048608 | tf_op jit(solution)/shard_map/all_to_all | solution.py:145
  192.0 13.6 %all_to_all.30 = bf16[4,64,512]{2,1,0:T(8,128)(2,1)S(1)} all-to-all(bf16[4,64,512]{2,1,0:T(8,128)(2,1)S(1)} %bitcast.94), channel_id=1, replica_groups=mesh['p'=2,'m'=2,'k'=2,'zh'=2,'y'=8,'x'=4] {'p','zh'}, dimensions={0} | all-to-all | bytes 524288 | tf_op jit(solution)/shard_map/all_to_all | solution.py:152
  (116 shorter events, 33.6 us)
Async XLA Ops:
  3.8 22.7 %all-to-all-start = ((bf16[4,80,512]{2,1,0:T(8,128)(2,1)}), bf16[4,80,512]{2,1,0:T(8,128)(2,1)S(1)}, u32[]{:S(2)}, u32[]{:S(2)}) async-start(bf16[4,80,512]{2,1,0:T(8,128)(2,1)} %broadcast_in_dim.131), calls=%async_computation | async-start | bytes 655360 | tf_op jit(solution)/shard_map/all_to_all | solution.py:109
  14.2 1.4 copy-start
  15.6 1.4 copy-start.1
  17.0 5.5 %copy-start.15 = (s32[64]{0:T(128)S(1)}, s32[64]{0:T(128)}, u32[]{:S(2)}) copy-start(s32[64]{0:T(128)} %param.14) | copy-start | bytes 772
  17.0 5.5 %copy-start.16 = (s32[64]{0:T(128)S(1)}, s32[64]{0:T(128)}, u32[]{:S(2)}) copy-start(s32[64]{0:T(128)} %param.15) | copy-start | bytes 772
  18.0 24.1 %collective-permute-start = (bf16[2,192,1024]{2,1,0:T(8,128)(2,1)S(1)}, bf16[2,192,1024]{2,1,0:T(8,128)(2,1)}, u32[]{:S(2)}, u32[]{:S(2)}) collective-permute-start(bf16[2,192,1024]{2,1,0:T(8,128)(2,1)S(1)} %get-tuple-element.17), channel_id=1, source_target_pairs={{0,128},{128,0},{1,129},{129,1},{2,130},{130,2},{3,131},{131,3},{4... | collective-permute-start | bytes 2359304 | tf_op jit(solution)/shard_map/ppermute | solution.py:23
  33.1 4.1 %copy-start.12 = (pred[2,32,256]{2,1,0:T(8,128)(4,1)}, pred[2,32,256]{2,1,0:T(8,128)(4,1)S(1)}, u32[]{:S(2)}) copy-start(pred[2,32,256]{2,1,0:T(8,128)(4,1)S(1)} %fusion.45) | copy-start | bytes 49156
  33.3 8.8 %copy-start.10 = (f32[2,32,256]{2,1,0:T(8,128)}, f32[2,32,256]{2,1,0:T(8,128)S(1)}, u32[]{:S(2)}) copy-start(f32[2,32,256]{2,1,0:T(8,128)S(1)} %fusion.13) | copy-start | bytes 196612
  34.3 2.9 %copy-start.8 = (f32[2,32,256]{2,1,0:T(8,128)}, f32[2,32,256]{2,1,0:T(8,128)S(1)}, u32[]{:S(2)}) copy-start(f32[2,32,256]{2,1,0:T(8,128)S(1)} %fusion.16) | copy-start | bytes 196612
  37.9 4.2 %copy-start.6 = (s32[32,2,8]{2,0,1:T(8,128)}, s32[32,2,8]{2,0,1:T(8,128)S(1)}, u32[]{:S(2)}) copy-start(s32[32,2,8]{2,0,1:T(8,128)S(1)} %get-tuple-element.64) | copy-start | bytes 6148
  37.9 36.4 %copy-start.4 = (s32[32,2,8]{2,0,1:T(8,128)}, s32[32,2,8]{2,0,1:T(8,128)S(1)}, u32[]{:S(2)}) copy-start(s32[32,2,8]{2,0,1:T(8,128)S(1)} %get-tuple-element.65) | copy-start | bytes 6148
  42.1 36.3 %all-to-all-start.1 = ((bf16[32,16,1024]{2,1,0:T(8,128)(2,1)}), bf16[32,16,1024]{2,1,0:T(8,128)(2,1)}, u32[]{:S(2)}, u32[]{:S(2)}) async-start(bf16[32,16,1024]{2,1,0:T(8,128)(2,1)} %fusion.20), calls=%async_computation.1 | async-start | bytes 2097152 | tf_op jit(solution)/shard_map/all_to_all | solution.py:135
  52.4 19.8 %collective-permute-start.4 = (bf16[2,192,1024]{2,1,0:T(8,128)(2,1)S(1)}, bf16[2,192,1024]{2,1,0:T(8,128)(2,1)S(1)}, u32[]{:S(2)}, u32[]{:S(2)}) collective-permute-start(bf16[2,192,1024]{2,1,0:T(8,128)(2,1)S(1)} %get-tuple-element.24), channel_id=1, source_target_pairs={{0,128},{128,0},{1,129},{129,1},{2,130},{130,2},{3,131},{131,3},{4... | collective-permute-start | bytes 2359304 | tf_op jit(solution)/shard_map/ppermute | solution.py:23
  58.5 19.0 %collective-permute-start.1 = (bf16[384,1024]{1,0:T(8,128)(2,1)S(1)}, bf16[384,1024]{1,0:T(8,128)(2,1)}, u32[]{:S(2)}, u32[]{:S(2)}) collective-permute-start(bf16[384,1024]{1,0:T(8,128)(2,1)S(1)} %pad_maximum_fusion.1), channel_id=1, source_target_pairs={{0,64},{64,0},{1,65},{65,1},{2,66},{66,2},{3,67},{67,3},{4,68},{68... | collective-permute-start | bytes 2359304 | tf_op jit(solution)/shard_map/ppermute | solution.py:23
  72.4 5.1 %collective-permute-start.6 = (bf16[384,1024]{1,0:T(8,128)(2,1)S(1)}, bf16[384,1024]{1,0:T(8,128)(2,1)S(1)}, u32[]{:S(2)}, u32[]{:S(2)}) collective-permute-start(bf16[384,1024]{1,0:T(8,128)(2,1)S(1)} %pad_maximum_fusion.3), channel_id=1, source_target_pairs={{0,64},{64,0},{1,65},{65,1},{2,66},{66,2},{3,67},{67,3},{4,68},{68... | collective-permute-start | bytes 2359304 | tf_op jit(solution)/shard_map/ppermute | solution.py:23
  78.4 37.1 %all-to-all-start.3 = ((bf16[32,16,1024]{2,1,0:T(8,128)(2,1)}), bf16[32,16,1024]{2,1,0:T(8,128)(2,1)}, u32[]{:S(2)}, u32[]{:S(2)}) async-start(bf16[32,16,1024]{2,1,0:T(8,128)(2,1)} %fusion.23), calls=%async_computation.3 | async-start | bytes 2097152 | tf_op jit(solution)/shard_map/all_to_all | solution.py:135
  87.4 5.9 %copy-start.2 = (bf16[192,1024]{1,0:T(8,128)(2,1)S(1)}, bf16[192,1024]{1,0:T(8,128)(2,1)}, u32[]{:S(2)}) copy-start(bf16[192,1024]{1,0:T(8,128)(2,1)} %get-tuple-element.39) | copy-start | bytes 1179652
  87.4 5.9 %copy-start.3 = (bf16[192,1024]{1,0:T(8,128)(2,1)S(1)}, bf16[192,1024]{1,0:T(8,128)(2,1)}, u32[]{:S(2)}) copy-start(bf16[192,1024]{1,0:T(8,128)(2,1)} %get-tuple-element.40) | copy-start | bytes 1179652
  89.6 3.6 %collective-permute-start.2 = (bf16[512,384]{1,0:T(8,128)(2,1)S(1)}, bf16[512,384]{1,0:T(8,128)(2,1)S(1)}, u32[]{:S(2)}, u32[]{:S(2)}) collective-permute-start(bf16[512,384]{1,0:T(8,128)(2,1)S(1)} %fusion.71), channel_id=1, source_target_pairs={{0,64},{64,0},{1,65},{65,1},{2,66},{66,2},{3,67},{67,3},{4,68},{68... | collective-permute-start | bytes 1179656 | tf_op jit(solution)/shard_map/ppermute | solution.py:23
  95.2 13.1 %collective-permute-start.3 = (bf16[512,384]{1,0:T(8,128)(2,1)S(1)}, bf16[512,384]{1,0:T(8,128)(2,1)S(1)}, u32[]{:S(2)}, u32[]{:S(2)}) collective-permute-start(bf16[512,384]{1,0:T(8,128)(2,1)S(1)} %get-tuple-element.72), channel_id=1, source_target_pairs={{0,128},{128,0},{1,129},{129,1},{2,130},{130,2},{3,131},{131,3},{4... | collective-permute-start | bytes 1179656 | tf_op jit(solution)/shard_map/ppermute | solution.py:23
  108.5 11.8 %collective-permute-start.5 = (bf16[512,384]{1,0:T(8,128)(2,1)S(1)}, bf16[512,384]{1,0:T(8,128)(2,1)S(1)}, u32[]{:S(2)}, u32[]{:S(2)}) collective-permute-start(bf16[512,384]{1,0:T(8,128)(2,1)S(1)} %multiply_convert_fusion.1), channel_id=1, source_target_pairs={{0,64},{64,0},{1,65},{65,1},{2,66},{66,2},{3,67},{67,3},{4,68},{68... | collective-permute-start | bytes 1179656 | tf_op jit(solution)/shard_map/ppermute | solution.py:23
  118.5 10.6 %collective-permute-start.7 = (bf16[512,384]{1,0:T(8,128)(2,1)}, bf16[512,384]{1,0:T(8,128)(2,1)}, u32[]{:S(2)}, u32[]{:S(2)}) collective-permute-start(bf16[512,384]{1,0:T(8,128)(2,1)} %fusion.73), channel_id=1, source_target_pairs={{0,64},{64,0},{1,65},{65,1},{2,66},{66,2},{3,67},{67,3},{4,68},{68... | collective-permute-start | bytes 1179656 | tf_op jit(solution)/shard_map/ppermute | solution.py:23
  122.8 34.3 %all-to-all-start.2 = ((bf16[32,16,1024]{2,1,0:T(8,128)(2,1)}), bf16[32,16,1024]{2,1,0:T(8,128)(2,1)S(1)}, u32[]{:S(2)}, u32[]{:S(2)}) async-start(bf16[32,16,1024]{2,1,0:T(8,128)(2,1)} %bitcast.18), calls=%async_computation.2 | async-start | bytes 2097152 | tf_op jit(solution)/shard_map/all_to_all | solution.py:145
  131.1 12.8 %collective-permute-start.8 = (bf16[512,384]{1,0:T(8,128)(2,1)S(1)}, bf16[512,384]{1,0:T(8,128)(2,1)S(1)}, u32[]{:S(2)}, u32[]{:S(2)}) collective-permute-start(bf16[512,384]{1,0:T(8,128)(2,1)S(1)} %get-tuple-element.70), channel_id=1, source_target_pairs={{0,128},{128,0},{1,129},{129,1},{2,130},{130,2},{3,131},{131,3},{4... | collective-permute-start | bytes 1179656 | tf_op jit(solution)/shard_map/ppermute | solution.py:23
  145.2 3.6 %collective-permute-start.9 = (bf16[512,384]{1,0:T(8,128)(2,1)S(1)}, bf16[512,384]{1,0:T(8,128)(2,1)S(1)}, u32[]{:S(2)}, u32[]{:S(2)}) collective-permute-start(bf16[512,384]{1,0:T(8,128)(2,1)S(1)} %multiply_convert_fusion), channel_id=1, source_target_pairs={{0,64},{64,0},{1,65},{65,1},{2,66},{66,2},{3,67},{67,3},{4,68},{68... | collective-permute-start | bytes 1179656 | tf_op jit(solution)/shard_map/ppermute | solution.py:23
  151.2 12.1 %copy-start.7 = (s32[32,2,8]{2,0,1:T(8,128)S(1)}, s32[32,2,8]{2,0,1:T(8,128)}, u32[]{:S(2)}) copy-start(s32[32,2,8]{2,0,1:T(8,128)} %copy-done.6) | copy-start | bytes 6148
  151.2 12.1 %copy-start.5 = (s32[32,2,8]{2,0,1:T(8,128)S(1)}, s32[32,2,8]{2,0,1:T(8,128)}, u32[]{:S(2)}) copy-start(s32[32,2,8]{2,0,1:T(8,128)} %copy-done.4) | copy-start | bytes 6148
  151.2 12.2 %copy-start.14 = (f32[2,2,256]{2,1,0:T(2,128)S(1)}, f32[2,2,256]{2,1,0:T(2,128)}, u32[]{:S(2)}) copy-start(f32[2,2,256]{2,1,0:T(2,128)} %get-tuple-element.51) | copy-start | bytes 12292
  151.2 12.2 %copy-start.11 = (f32[2,32,256]{2,1,0:T(8,128)S(1)}, f32[2,32,256]{2,1,0:T(8,128)}, u32[]{:S(2)}) copy-start(f32[2,32,256]{2,1,0:T(8,128)} %copy-done.10) | copy-start | bytes 196612
  151.2 12.2 %copy-start.13 = (pred[2,32,256]{2,1,0:T(8,128)(4,1)S(1)}, pred[2,32,256]{2,1,0:T(8,128)(4,1)}, u32[]{:S(2)}) copy-start(pred[2,32,256]{2,1,0:T(8,128)(4,1)} %copy-done.12) | copy-start | bytes 49156
  151.3 12.5 %copy-start.9 = (f32[2,32,256]{2,1,0:T(8,128)S(1)}, f32[2,32,256]{2,1,0:T(8,128)}, u32[]{:S(2)}) copy-start(f32[2,32,256]{2,1,0:T(8,128)} %copy-done.8) | copy-start | bytes 196612
  157.1 33.6 %all-to-all-start.4 = ((bf16[32,16,1024]{2,1,0:T(8,128)(2,1)}), bf16[32,16,1024]{2,1,0:T(8,128)(2,1)S(1)}, u32[]{:S(2)}, u32[]{:S(2)}) async-start(bf16[32,16,1024]{2,1,0:T(8,128)(2,1)} %bitcast.26), calls=%async_computation.4 | async-start | bytes 2097152 | tf_op jit(solution)/shard_map/all_to_all | solution.py:145

commit v8 on v7

--- a/solution.py
+++ b/solution.py
@@ -1,3 +1,5 @@
+import functools
+
 import jax
 import jax.numpy as jnp
 from jax import lax
@@ -91,37 +93,100 @@
     return order(tokens_of), order(weight_of)
 
 
-def thirds(value):
+def halves(value):
     high = lax.reduce_precision(value, 8, 7)
-    mid = lax.reduce_precision(value - high, 8, 7)
-    return high.astype(BF), mid.astype(BF), (value - high - mid).astype(BF)
+    return high.astype(BF), (value - high).astype(BF)
+
+
+def host_codes(plan):
+    hosts = plan.shape[0]
+    count = hosts // lax.axis_size("zh")
+    experts = lax.axis_index("zh") * count + jnp.arange(count, dtype=jnp.int32)
+    ids = jnp.arange(hosts, dtype=jnp.int32)
+    spare_host = jnp.sum(jnp.where(plan[None, :] == experts[:, None], ids[None, :], 0), axis=1)
+    here = jnp.sum(jnp.where(ids[None, :] == experts[:, None], plan[None, :], 0), axis=1)
+    own_code = 2 * jnp.concatenate([experts, spare_host])
+    spare_code = 2 * jnp.concatenate([here, experts]) + 1
+    return jnp.stack([own_code, spare_code], axis=1).astype(F32)
+
+
+def ahead(shape, axis):
+    return lax.broadcasted_iota(jnp.int32, shape, axis)
+
+
+def one(mask, dtype=F32):
+    return jnp.where(mask, 1.0, 0.0).astype(dtype)
+
+
+def route_kernel(index, group, came, codes, rows_out, high_out, mid_out):
+    count, rows = codes.shape[0] // 2, group * TOPK
+    feats, lines = came.shape[2], 2 * group
+    before = one(ahead((rows, rows), 0) < ahead((rows, rows), 1), BF)
+    own_code, spare_code = codes[:, 0:1], codes[:, 1:2]
+    table = jnp.zeros((4 * count, 2 * group), F32)
+    for g in range(2):
+        info = came[g, lines : lines + 16, index * rows : (index + 1) * rows].astype(F32)
+        code, high, mid = info[0:1], info[1:2], info[2:3]
+        own, spare = one(code == own_code), one(code == spare_code)
+        position = dot((own + spare).astype(BF), before, ((1,), (0,)))
+        fits = position < CAP
+        own, spare = jnp.where(fits, own, 0.0), jnp.where(fits, spare, 0.0)
+        kept = own[:count] + spare[count:]
+        rank = dot(kept.astype(BF), before, ((1,), (0,)))
+        facts = jnp.concatenate([kept, kept * rank, kept * high, kept * mid], axis=0).astype(BF)
+        shape = (rows, 2 * group)
+        to_token = one(ahead(shape, 0) // TOPK + g * group == ahead(shape, 1), BF)
+        table = table + dot(facts, to_token, ((1,), (0,)))
+    table = table.astype(BF)
+    slots = count * 4 * CAP
+    shape = (slots, count)
+    spread = one(ahead(shape, 0) // (4 * CAP) == ahead(shape, 1), BF)
+    kept, rank, high, mid = (
+        dot(spread, table[i * count : (i + 1) * count], ((1,), (0,))) for i in range(4)
+    )
+    shape = (slots, 2 * group)
+    slot, token = ahead(shape, 0), ahead(shape, 1)
+    turn = (slot % (2 * CAP)).astype(F32)
+    hot = (kept > 0.5) & (rank == turn) & ((slot // (2 * CAP)) % 2 == token // group)
+    high_out[...] = jnp.where(hot, high, 0.0).astype(BF)
+    mid_out[...] = jnp.where(hot, mid, 0.0).astype(BF)
+    hot = one(hot, BF)
+    for p in range(2):
+        both = jnp.concatenate([came[2 * p + g, index * group : (index + 1) * group] for g in range(2)], axis=0)
+        rows_out[:, p * feats : (p + 1) * feats] = dot(hot, both, ((1,), (0,))).astype(BF)
+
+
+def route(came, codes, index, group):
+    slots, feats = codes.shape[0] // 2 * 4 * CAP, came.shape[2]
+    vmem = pl.BlockSpec(memory_space=pltpu.VMEM)
+    shape = lambda width: jax.ShapeDtypeStruct((slots, width), BF)
+    return pl.pallas_call(
+        functools.partial(route_kernel, index, group),
+        out_shape=[shape(2 * feats), shape(2 * group), shape(2 * group)],
+        in_specs=[vmem, vmem],
+        out_specs=[vmem, vmem, vmem],
+        compiler_params=pltpu.CompilerParams(vmem_limit_bytes=32 << 20),
+        cost_estimate=pl.CostEstimate(flops=2 * slots * 2 * group * 2 * feats, bytes_accessed=2 << 20, transcendentals=0),
+    )(came, codes)
 
 
 def local(tokens, w_gate, w_down, expert_ids, route_weight, replica_pick, old_plan, new_plan):
     batches, group, feats = tokens.shape
     peers = lax.axis_size("y") * lax.axis_size("x")
     code = (2 * expert_ids + (replica_pick & 1)).astype(BF)
-    parts = [code, *thirds(route_weight)]
-    info = jnp.stack(parts).reshape(-1, feats)
-    count = info.shape[0]
-    sent = jnp.concatenate([tokens.reshape(-1, feats), jnp.pad(info, ((0, 16 - count), (0, 0)))])
+    info = jnp.stack([code, *halves(route_weight)]).reshape(3, feats)
+    sent = jnp.concatenate([tokens.reshape(-1, feats), jnp.pad(info, ((0, 13), (0, 0)))])
     sent = jnp.broadcast_to(sent[None], (4, *sent.shape))
-    came = lax.all_to_all(sent, ("p", "zh"), 0, 0, tiled=True).reshape(2, 2, -1, feats)
-    tok = came[:, :, : batches * group].reshape(2, 2, batches, group, feats)
-    tok = tok.transpose(2, 1, 3, 0, 4).reshape(batches, 2 * group, 2 * feats)
-    info = came[0, :, batches * group : batches * group + count]
-    info = info.reshape(2, 4, batches, group * TOPK).astype(F32)
-    code = info[:, 0].astype(jnp.int32)
-    weight = info[:, 1] + info[:, 2] + info[:, 3]
+    came = lax.all_to_all(sent, ("p", "zh"), 0, 0, tiled=True)
+    plans = [host_codes(old_plan), host_codes(new_plan)]
 
     gate_parts, down_parts = cut_weights(w_gate, w_down)
     gate_far = swap(gate_parts[2], "m")
 
-    outputs = []
-    for index, plan in ((0, old_plan), (1, new_plan)):
-        slot_token, slot_weight = slots(code[:, index], weight[:, index], plan)
-        pick = slot_token[:, None] == jnp.arange(2 * group, dtype=jnp.int32)[None, :]
-        rows = dot(pick.astype(BF), tok[index], ((1,), (0,)), BF)
+    outs, scales = [], []
+    for index in range(batches):
+        rows, high, mid = route(came, plans[index], index, group)
+        scales.append((high, mid))
         rows = rows.reshape(peers, -1, rows.shape[1])
         if index == 0:
             rows, gate_far, down_ready = lax.optimization_barrier((rows, gate_far, down_parts[2]))
@@ -133,6 +198,8 @@
         else:
             rows, gate_other, down_other = lax.optimization_barrier((rows, gate_other, down_other))
         rows = lax.all_to_all(rows, ("y", "x"), 0, 0, tiled=True).reshape(-1, rows.shape[2])
+        if outs:
+            rows, _ = lax.optimization_barrier((rows, outs[0]))
 
         send = dot(rows, gate_other, ((1,), (1,)), BF)
         part = dot(rows, gate_own, ((1,), (1,)))
@@ -141,12 +208,12 @@
         hidden = jax.nn.silu(gate).astype(BF)
         hidden_other = swap(hidden, "k")
         out = dot(hidden, down_own, ((1,), (0,))) + dot(hidden_other, down_other, ((1,), (0,)))
-        out = out.astype(BF).reshape(peers, -1, out.shape[1])
+        outs.append(out.astype(BF).reshape(peers, -1, out.shape[1]))
+
+    outputs = []
+    for out, (high, mid) in zip(outs, scales):
         back = lax.all_to_all(out, ("y", "x"), 0, 0, tiled=True).reshape(-1, out.shape[2])
-
-        scale = jnp.where(pick, slot_weight[:, None], 0.0)
-        high, low, _ = thirds(scale)
-        mixed = dot(high, back, ((0,), (0,))) + dot(low, back, ((0,), (0,)))
+        mixed = dot(high, back, ((0,), (0,))) + dot(mid, back, ((0,), (0,)))
         outputs.append(mixed.astype(BF).reshape(2, group, 2, feats))
     mixed = jnp.stack(outputs).transpose(3, 1, 0, 2, 4).reshape(4, batches * group, feats)
     terms = lax.all_to_all(mixed, ("p", "zh"), 0, 0, tiled=True)

time: 208 us -> 210 us (level)
  waiting for transfers between devices: 74.3 us -> 94.8 us
  other arithmetic: 16.1 us -> 6.94 us
  local copies, waits for them, and re-layouts: 10.1 us -> 4.58 us
  starting transfers between devices: 68.1 us -> 62.6 us
  Pallas kernels: 0.92 us -> 5.7 us
  matrix products: 22.7 us -> 18.4 us
    all_to_all x1, waiting for transfers between devices: 3.76 us -> 20.5 us  [local(): came = lax.all_to_all(sent, ('p', 'zh'), 0, 0, tiled=True)]
    dot_general x18 -> x12, matrix products: 22.7 us -> 18.4 us  [dot(): return lax.dot_general(a, b, (dims, ((), ())), preferred_element_type=out)]
    pallas_call x0 -> x2, Pallas kernels: none -> 4.07 us  [route(): pl.pallas_call(functools.partial(route_kernel, index, group), out_shape=[...]
    all_to_all x2, waiting for transfers between devices: 5.96 us -> 9.52 us  [local(): lax.all_to_all(rows, ('y', 'x'), 0, 0, tiled=True)]
    reduce_sum x4 -> x1, other arithmetic: 3.54 us -> 0.21 us  [host_codes(): jnp.sum(jnp.where(plan[None, :] == experts[:, None], ids[None, :], 0), ax...]
    all_to_all x2, starting transfers between devices: 19.3 us -> 16.4 us  [local(): lax.all_to_all(rows, ('y', 'x'), 0, 0, tiled=True)]
    eq x4 -> x0, local copies, waits for them, and re-layouts: 2.25 us -> none  [local(): slot_token[:, None] == jnp.arange(2 * group, dtype=jnp.int32)[None, :]]
  transfers between devices with their start and end apart: 15 -> 15, of which waited for: 10 -> 10; matrix products, arithmetic and copies ran while one was open for 19% -> 11% of each run, Pallas kernels for 0% -> 2%
where the time goes in v8:
time: 210 us; the launch traced here: 209 us
  waiting for transfers between devices  94.8 us (45%)
  starting transfers between devices  62.6 us (30%)
  matrix products  18.4 us (9%)
  blocking collectives  15.2 us (7%)
  other arithmetic  6.94 us (3%)
  Pallas kernels  5.7 us (3%)
  local copies, waits for them, and re-layouts  4.58 us (2%)
    ppermute x10, waiting for transfers between devices, swap(): return lax.ppermute(array, axes, [(i, last - i) for i in range(last + 1)])  33.3 us
    all_to_all x2, waiting for transfers between devices, local(): lax.all_to_all(out, ('y', 'x'), 0, 0, tiled=True).reshape(-1, out.shape[2])  31.4 us
    ppermute x10, starting transfers between devices, swap(): return lax.ppermute(array, axes, [(i, last - i) for i in range(last + 1)])  25.1 us
    all_to_all x1, waiting for transfers between devices, local(): came = lax.all_to_all(sent, ('p', 'zh'), 0, 0, tiled=True)  20.5 us
    dot_general x12, matrix products, dot(): return lax.dot_general(a, b, (dims, ((), ())), preferred_element_type=out)  18.4 us
    all_to_all x2, starting transfers between devices, local(): lax.all_to_all(rows, ('y', 'x'), 0, 0, tiled=True)  16.4 us
    all_to_all x1, blocking collectives, local(): terms = lax.all_to_all(mixed, ('p', 'zh'), 0, 0, tiled=True)  15.2 us
    all_to_all x2, starting transfers between devices, local(): lax.all_to_all(out, ('y', 'x'), 0, 0, tiled=True).reshape(-1, out.shape[2])  11.8 us
  transfers between devices with their start and end apart: 15, of which 10 were waited for; matrix products, arithmetic and copies ran while one was open for 11% of the time, Pallas kernels for 2%

profile of v8, /device:TPU:2, one launch (start us, length us, event | category | flops | bytes accessed | tf_op | source)
XLA Modules:
  0.0 208.6 jit_solution(13698251270512401105)
XLA Ops:
  4.6 4.3 %collective-permute-start = (bf16[2,192,1024]{2,1,0:T(8,128)(2,1)}, bf16[2,192,1024]{2,1,0:T(8,128)(2,1)}, u32[]{:S(2)}, u32[]{:S(2)}) collective-permute-start(bf16[2,192,1024]{2,1,0:T(8,128)(2,1)} %get-tuple-element.26), channel_id=1, source_target_pairs={{0,128},{128,0},{1,129},{129,1},{2,130},{130,2},{3,131},{131,3},{4... | collective-permute-start | bytes 2359304 | tf_op jit(solution)/shard_map/ppermute | solution.py:25
  10.3 9.4 %all-to-all-start = ((bf16[4,80,512]{2,1,0:T(8,128)(2,1)}), bf16[4,80,512]{2,1,0:T(8,128)(2,1)S(1)}, u32[]{:S(2)}, u32[]{:S(2)}) async-start(bf16[4,80,512]{2,1,0:T(8,128)(2,1)} %broadcast_in_dim.46), calls=%async_computation | async-start | bytes 655360 | tf_op jit(solution)/shard_map/all_to_all | solution.py:180
  20.1 20.5 %all-to-all-done.came = bf16[4,80,512]{2,1,0:T(8,128)(2,1)S(1)} async-done(((bf16[4,80,512]{2,1,0:T(8,128)(2,1)}), bf16[4,80,512]{2,1,0:T(8,128)(2,1)S(1)}, u32[]{:S(2)}, u32[]{:S(2)}) %all-to-all-start) | async-done | bytes 327712 | tf_op jit(solution)/shard_map/all_to_all | solution.py:180
  40.6 2.0 shard_map.82
  42.7 10.3 %all-to-all-start.1 = ((bf16[32,16,1024]{2,1,0:T(8,128)(2,1)}), bf16[32,16,1024]{2,1,0:T(8,128)(2,1)}, u32[]{:S(2)}, u32[]{:S(2)}) async-start(bf16[32,16,1024]{2,1,0:T(8,128)(2,1)} %bitcast.4), calls=%async_computation.1 | async-start | bytes 2097152 | tf_op jit(solution)/shard_map/all_to_all | solution.py:200
  53.0 2.4 %collective-permute-start.4 = (bf16[2,192,1024]{2,1,0:T(8,128)(2,1)S(1)}, bf16[2,192,1024]{2,1,0:T(8,128)(2,1)}, u32[]{:S(2)}, u32[]{:S(2)}) collective-permute-start(bf16[2,192,1024]{2,1,0:T(8,128)(2,1)S(1)} %get-tuple-element.33), channel_id=1, source_target_pairs={{0,128},{128,0},{1,129},{129,1},{2,130},{130,2},{3,131},{131,3},{4... | collective-permute-start | bytes 2359304 | tf_op jit(solution)/shard_map/ppermute | solution.py:25
  55.4 2.0 bitcast_select_fusion.3
  57.4 1.9 collective-permute-start.1
  59.3 11.4 %collective-permute-done.4 = bf16[2,192,1024]{2,1,0:T(8,128)(2,1)} collective-permute-done((bf16[2,192,1024]{2,1,0:T(8,128)(2,1)S(1)}, bf16[2,192,1024]{2,1,0:T(8,128)(2,1)}, u32[]{:S(2)}, u32[]{:S(2)}) %collective-permute-start.4) | collective-permute-done | bytes 786464 | tf_op jit(solution)/shard_map/ppermute | solution.py:25
  72.0 1.9 collective-permute-start.6
  73.9 4.2 %all-to-all-done.1 = bf16[32,16,1024]{2,1,0:T(8,128)(2,1)} async-done(((bf16[32,16,1024]{2,1,0:T(8,128)(2,1)}), bf16[32,16,1024]{2,1,0:T(8,128)(2,1)}, u32[]{:S(2)}, u32[]{:S(2)}) %all-to-all-start.1) | async-done | bytes 1048608 | tf_op jit(solution)/shard_map/all_to_all | solution.py:200
  78.1 2.9 %fusion.19 = bf16[512,384]{1,0:T(8,128)(2,1)} fusion(bf16[512,1024]{1,0:T(8,128)(2,1)} %bitcast.7, bf16[384,1024]{1,0:T(8,128)(2,1)} %collective-permute-done.1), kind=kOutput, calls=%fused_computation.60 | convolution fusion | flops 402653184 | bytes 2228224 | tf_op jit(solution)/shard_map/dot_general | solution.py:20
  81.0 2.0 collective-permute-start.2
  83.2 2.0 shard_map.84
  85.2 6.1 %all-to-all-start.3 = ((bf16[32,16,1024]{2,1,0:T(8,128)(2,1)}), bf16[32,16,1024]{2,1,0:T(8,128)(2,1)S(1)}, u32[]{:S(2)}, u32[]{:S(2)}) async-start(bf16[32,16,1024]{2,1,0:T(8,128)(2,1)} %bitcast.16), calls=%async_computation.3 | async-start | bytes 2097152 | tf_op jit(solution)/shard_map/all_to_all | solution.py:200
  91.3 2.0 fusion.2
  93.4 3.3 %collective-permute-start.3 = (bf16[512,384]{1,0:T(8,128)(2,1)S(1)}, bf16[512,384]{1,0:T(8,128)(2,1)S(1)}, u32[]{:S(2)}, u32[]{:S(2)}) collective-permute-start(bf16[512,384]{1,0:T(8,128)(2,1)S(1)} %get-tuple-element.67), channel_id=1, source_target_pairs={{0,128},{128,0},{1,129},{129,1},{2,130},{130,2},{3,131},{131,3},{4... | collective-permute-start | bytes 1179656 | tf_op jit(solution)/shard_map/ppermute | solution.py:25
  96.7 9.0 %collective-permute-done.3 = bf16[512,384]{1,0:T(8,128)(2,1)S(1)} collective-permute-done((bf16[512,384]{1,0:T(8,128)(2,1)S(1)}, bf16[512,384]{1,0:T(8,128)(2,1)S(1)}, u32[]{:S(2)}, u32[]{:S(2)}) %collective-permute-start.3) | collective-permute-done | bytes 393248 | tf_op jit(solution)/shard_map/ppermute | solution.py:25
  107.0 1.9 collective-permute-start.5
  110.6 1.8 fusion.20
  114.2 5.3 %all-to-all-done.3 = bf16[32,16,1024]{2,1,0:T(8,128)(2,1)S(1)} async-done(((bf16[32,16,1024]{2,1,0:T(8,128)(2,1)}), bf16[32,16,1024]{2,1,0:T(8,128)(2,1)S(1)}, u32[]{:S(2)}, u32[]{:S(2)}) %all-to-all-start.3) | async-done | bytes 1048608 | tf_op jit(solution)/shard_map/all_to_all | solution.py:200
  119.6 3.0 %fusion.22 = bf16[512,384]{1,0:T(8,128)(2,1)} fusion(bf16[512,1024]{1,0:T(8,128)(2,1)S(1)} %bitcast.64, bf16[384,1024]{1,0:T(8,128)(2,1)} %collective-permute-done.1), kind=kOutput, calls=%fused_computation.63 | convolution fusion | flops 402653184 | bytes 2228224 | tf_op jit(solution)/shard_map/dot_general | solution.py:20
  122.6 2.0 collective-permute-start.7
  124.6 5.6 %all-to-all-start.2 = ((bf16[32,16,1024]{2,1,0:T(8,128)(2,1)}), bf16[32,16,1024]{2,1,0:T(8,128)(2,1)S(1)}, u32[]{:S(2)}, u32[]{:S(2)}) async-start(bf16[32,16,1024]{2,1,0:T(8,128)(2,1)} %bitcast.12), calls=%async_computation.2 | async-start | bytes 2097152 | tf_op jit(solution)/shard_map/all_to_all | solution.py:215
  130.2 2.0 fusion.3
  132.3 3.3 %collective-permute-start.8 = (bf16[512,384]{1,0:T(8,128)(2,1)S(1)}, bf16[512,384]{1,0:T(8,128)(2,1)S(1)}, u32[]{:S(2)}, u32[]{:S(2)}) collective-permute-start(bf16[512,384]{1,0:T(8,128)(2,1)S(1)} %get-tuple-element.69), channel_id=1, source_target_pairs={{0,128},{128,0},{1,129},{129,1},{2,130},{130,2},{3,131},{131,3},{4... | collective-permute-start | bytes 1179656 | tf_op jit(solution)/shard_map/ppermute | solution.py:25
  135.6 9.5 %collective-permute-done.8 = bf16[512,384]{1,0:T(8,128)(2,1)S(1)} collective-permute-done((bf16[512,384]{1,0:T(8,128)(2,1)S(1)}, bf16[512,384]{1,0:T(8,128)(2,1)S(1)}, u32[]{:S(2)}, u32[]{:S(2)}) %collective-permute-start.8) | collective-permute-done | bytes 393248 | tf_op jit(solution)/shard_map/ppermute | solution.py:25
  146.4 1.9 collective-permute-start.9
  153.5 4.8 %all-to-all-done.2 = bf16[32,16,1024]{2,1,0:T(8,128)(2,1)S(1)} async-done(((bf16[32,16,1024]{2,1,0:T(8,128)(2,1)}), bf16[32,16,1024]{2,1,0:T(8,128)(2,1)S(1)}, u32[]{:S(2)}, u32[]{:S(2)}) %all-to-all-start.2) | async-done | bytes 1048608 | tf_op jit(solution)/shard_map/all_to_all | solution.py:215
  158.3 6.2 %all-to-all-start.4 = ((bf16[32,16,1024]{2,1,0:T(8,128)(2,1)}), bf16[32,16,1024]{2,1,0:T(8,128)(2,1)S(1)}, u32[]{:S(2)}, u32[]{:S(2)}) async-start(bf16[32,16,1024]{2,1,0:T(8,128)(2,1)} %bitcast.63), calls=%async_computation.4 | async-start | bytes 2097152 | tf_op jit(solution)/shard_map/all_to_all | solution.py:215
  165.3 26.6 %all-to-all-done.4 = bf16[32,16,1024]{2,1,0:T(8,128)(2,1)S(1)} async-done(((bf16[32,16,1024]{2,1,0:T(8,128)(2,1)}), bf16[32,16,1024]{2,1,0:T(8,128)(2,1)S(1)}, u32[]{:S(2)}, u32[]{:S(2)}) %all-to-all-start.4) | async-done | bytes 1048608 | tf_op jit(solution)/shard_map/all_to_all | solution.py:215
  192.7 15.2 %all_to_all.30 = bf16[4,64,512]{2,1,0:T(8,128)(2,1)S(1)} all-to-all(bf16[4,64,512]{2,1,0:T(8,128)(2,1)S(1)} %bitcast.66), channel_id=1, replica_groups=mesh['p'=2,'m'=2,'k'=2,'zh'=2,'y'=8,'x'=4] {'p','zh'}, dimensions={0} | all-to-all | bytes 524288 | tf_op jit(solution)/shard_map/all_to_all | solution.py:219
  (67 shorter events, 21.1 us)
Async XLA Ops:
  0.1 1.4 copy-start
  1.5 1.4 copy-start.1
  2.9 5.9 %copy-start.6 = (f32[2,32,8]{1,2,0:T(8,128)S(1)}, f32[2,32,8]{1,2,0:T(8,128)}, u32[]{:S(2)}) copy-start(f32[2,32,8]{1,2,0:T(8,128)} %param.12) | copy-start | bytes 6148
  2.9 6.4 %copy-start.7 = (s32[2,32,8]{1,2,0:T(8,128)S(1)}, s32[2,32,8]{1,2,0:T(8,128)}, u32[]{:S(2)}) copy-start(s32[2,32,8]{1,2,0:T(8,128)} %param.13) | copy-start | bytes 6148
  2.9 6.4 %copy-start.8 = (s32[2,32,8]{1,2,0:T(8,128)S(1)}, s32[2,32,8]{1,2,0:T(8,128)}, u32[]{:S(2)}) copy-start(s32[2,32,8]{1,2,0:T(8,128)} %param.11) | copy-start | bytes 6148
  2.9 6.6 %copy-start.5 = (bf16[2,32,512]{2,1,0:T(8,128)(2,1)S(1)}, bf16[2,32,512]{2,1,0:T(8,128)(2,1)}, u32[]{:S(2)}) copy-start(bf16[2,32,512]{2,1,0:T(8,128)(2,1)} %param.8) | copy-start | bytes 196612
  2.9 16.8 %copy-start.9 = (s32[64]{0:T(128)S(1)}, s32[64]{0:T(128)}, u32[]{:S(2)}) copy-start(s32[64]{0:T(128)} %param.14) | copy-start | bytes 772
  2.9 16.8 %copy-start.10 = (s32[64]{0:T(128)S(1)}, s32[64]{0:T(128)}, u32[]{:S(2)}) copy-start(s32[64]{0:T(128)} %param.15) | copy-start | bytes 772
  4.6 38.1 %collective-permute-start = (bf16[2,192,1024]{2,1,0:T(8,128)(2,1)}, bf16[2,192,1024]{2,1,0:T(8,128)(2,1)}, u32[]{:S(2)}, u32[]{:S(2)}) collective-permute-start(bf16[2,192,1024]{2,1,0:T(8,128)(2,1)} %get-tuple-element.26), channel_id=1, source_target_pairs={{0,128},{128,0},{1,129},{129,1},{2,130},{130,2},{3,131},{131,3},{4... | collective-permute-start | bytes 2359304 | tf_op jit(solution)/shard_map/ppermute | solution.py:25
  10.3 30.3 %all-to-all-start = ((bf16[4,80,512]{2,1,0:T(8,128)(2,1)}), bf16[4,80,512]{2,1,0:T(8,128)(2,1)S(1)}, u32[]{:S(2)}, u32[]{:S(2)}) async-start(bf16[4,80,512]{2,1,0:T(8,128)(2,1)} %broadcast_in_dim.46), calls=%async_computation | async-start | bytes 655360 | tf_op jit(solution)/shard_map/all_to_all | solution.py:180
  42.7 35.4 %all-to-all-start.1 = ((bf16[32,16,1024]{2,1,0:T(8,128)(2,1)}), bf16[32,16,1024]{2,1,0:T(8,128)(2,1)}, u32[]{:S(2)}, u32[]{:S(2)}) async-start(bf16[32,16,1024]{2,1,0:T(8,128)(2,1)} %bitcast.4), calls=%async_computation.1 | async-start | bytes 2097152 | tf_op jit(solution)/shard_map/all_to_all | solution.py:200
  53.0 17.7 %collective-permute-start.4 = (bf16[2,192,1024]{2,1,0:T(8,128)(2,1)S(1)}, bf16[2,192,1024]{2,1,0:T(8,128)(2,1)}, u32[]{:S(2)}, u32[]{:S(2)}) collective-permute-start(bf16[2,192,1024]{2,1,0:T(8,128)(2,1)S(1)} %get-tuple-element.33), channel_id=1, source_target_pairs={{0,128},{128,0},{1,129},{129,1},{2,130},{130,2},{3,131},{131,3},{4... | collective-permute-start | bytes 2359304 | tf_op jit(solution)/shard_map/ppermute | solution.py:25
  57.4 16.5 %collective-permute-start.1 = (bf16[384,1024]{1,0:T(8,128)(2,1)S(1)}, bf16[384,1024]{1,0:T(8,128)(2,1)}, u32[]{:S(2)}, u32[]{:S(2)}) collective-permute-start(bf16[384,1024]{1,0:T(8,128)(2,1)S(1)} %pad_maximum_fusion.1), channel_id=1, source_target_pairs={{0,64},{64,0},{1,65},{65,1},{2,66},{66,2},{3,67},{67,3},{4,68},{68... | collective-permute-start | bytes 2359304 | tf_op jit(solution)/shard_map/ppermute | solution.py:25
  72.0 13.2 %collective-permute-start.6 = (bf16[384,1024]{1,0:T(8,128)(2,1)S(1)}, bf16[384,1024]{1,0:T(8,128)(2,1)}, u32[]{:S(2)}, u32[]{:S(2)}) collective-permute-start(bf16[384,1024]{1,0:T(8,128)(2,1)S(1)} %pad_maximum_fusion.3), channel_id=1, source_target_pairs={{0,64},{64,0},{1,65},{65,1},{2,66},{66,2},{3,67},{67,3},{4,68},{68... | collective-permute-start | bytes 2359304 | tf_op jit(solution)/shard_map/ppermute | solution.py:25
  81.0 10.3 %copy-start.3 = (bf16[192,1024]{1,0:T(8,128)(2,1)S(1)}, bf16[192,1024]{1,0:T(8,128)(2,1)}, u32[]{:S(2)}) copy-start(bf16[192,1024]{1,0:T(8,128)(2,1)} %get-tuple-element.52) | copy-start | bytes 1179652
  81.0 10.3 %collective-permute-start.2 = (bf16[512,384]{1,0:T(8,128)(2,1)}, bf16[512,384]{1,0:T(8,128)(2,1)}, u32[]{:S(2)}, u32[]{:S(2)}) collective-permute-start(bf16[512,384]{1,0:T(8,128)(2,1)} %fusion.19), channel_id=1, source_target_pairs={{0,64},{64,0},{1,65},{65,1},{2,66},{66,2},{3,67},{67,3},{4,68},{68... | collective-permute-start | bytes 1179656 | tf_op jit(solution)/shard_map/ppermute | solution.py:25
  85.2 34.4 %all-to-all-start.3 = ((bf16[32,16,1024]{2,1,0:T(8,128)(2,1)}), bf16[32,16,1024]{2,1,0:T(8,128)(2,1)S(1)}, u32[]{:S(2)}, u32[]{:S(2)}) async-start(bf16[32,16,1024]{2,1,0:T(8,128)(2,1)} %bitcast.16), calls=%async_computation.3 | async-start | bytes 2097152 | tf_op jit(solution)/shard_map/all_to_all | solution.py:200
  93.4 12.4 %collective-permute-start.3 = (bf16[512,384]{1,0:T(8,128)(2,1)S(1)}, bf16[512,384]{1,0:T(8,128)(2,1)S(1)}, u32[]{:S(2)}, u32[]{:S(2)}) collective-permute-start(bf16[512,384]{1,0:T(8,128)(2,1)S(1)} %get-tuple-element.67), channel_id=1, source_target_pairs={{0,128},{128,0},{1,129},{129,1},{2,130},{130,2},{3,131},{131,3},{4... | collective-permute-start | bytes 1179656 | tf_op jit(solution)/shard_map/ppermute | solution.py:25
  107.0 3.6 %collective-permute-start.5 = (bf16[512,384]{1,0:T(8,128)(2,1)S(1)}, bf16[512,384]{1,0:T(8,128)(2,1)S(1)}, u32[]{:S(2)}, u32[]{:S(2)}) collective-permute-start(bf16[512,384]{1,0:T(8,128)(2,1)S(1)} %multiply_convert_fusion.1), channel_id=1, source_target_pairs={{0,64},{64,0},{1,65},{65,1},{2,66},{66,2},{3,67},{67,3},{4,68},{68... | collective-permute-start | bytes 1179656 | tf_op jit(solution)/shard_map/ppermute | solution.py:25
  119.6 5.0 %copy-start.2 = (bf16[32,16,1024]{2,1,0:T(8,128)(2,1)}, bf16[32,16,1024]{2,1,0:T(8,128)(2,1)S(1)}, u32[]{:S(2)}) copy-start(bf16[32,16,1024]{2,1,0:T(8,128)(2,1)S(1)} %all-to-all-done.3) | copy-start | bytes 3145732
  122.6 7.7 %copy-start.4 = (bf16[192,1024]{1,0:T(8,128)(2,1)S(1)}, bf16[192,1024]{1,0:T(8,128)(2,1)}, u32[]{:S(2)}) copy-start(bf16[192,1024]{1,0:T(8,128)(2,1)} %get-tuple-element.52) | copy-start | bytes 1179652
  122.6 7.6 %collective-permute-start.7 = (bf16[512,384]{1,0:T(8,128)(2,1)}, bf16[512,384]{1,0:T(8,128)(2,1)}, u32[]{:S(2)}, u32[]{:S(2)}) collective-permute-start(bf16[512,384]{1,0:T(8,128)(2,1)} %fusion.22), channel_id=1, source_target_pairs={{0,64},{64,0},{1,65},{65,1},{2,66},{66,2},{3,67},{67,3},{4,68},{68... | collective-permute-start | bytes 1179656 | tf_op jit(solution)/shard_map/ppermute | solution.py:25
  124.6 33.7 %all-to-all-start.2 = ((bf16[32,16,1024]{2,1,0:T(8,128)(2,1)}), bf16[32,16,1024]{2,1,0:T(8,128)(2,1)S(1)}, u32[]{:S(2)}, u32[]{:S(2)}) async-start(bf16[32,16,1024]{2,1,0:T(8,128)(2,1)} %bitcast.12), calls=%async_computation.2 | async-start | bytes 2097152 | tf_op jit(solution)/shard_map/all_to_all | solution.py:215
  132.3 12.9 %collective-permute-start.8 = (bf16[512,384]{1,0:T(8,128)(2,1)S(1)}, bf16[512,384]{1,0:T(8,128)(2,1)S(1)}, u32[]{:S(2)}, u32[]{:S(2)}) collective-permute-start(bf16[512,384]{1,0:T(8,128)(2,1)S(1)} %get-tuple-element.69), channel_id=1, source_target_pairs={{0,128},{128,0},{1,129},{129,1},{2,130},{130,2},{3,131},{131,3},{4... | collective-permute-start | bytes 1179656 | tf_op jit(solution)/shard_map/ppermute | solution.py:25
  146.4 3.6 %collective-permute-start.9 = (bf16[512,384]{1,0:T(8,128)(2,1)S(1)}, bf16[512,384]{1,0:T(8,128)(2,1)S(1)}, u32[]{:S(2)}, u32[]{:S(2)}) collective-permute-start(bf16[512,384]{1,0:T(8,128)(2,1)S(1)} %multiply_convert_fusion), channel_id=1, source_target_pairs={{0,64},{64,0},{1,65},{65,1},{2,66},{66,2},{3,67},{67,3},{4,68},{68... | collective-permute-start | bytes 1179656 | tf_op jit(solution)/shard_map/ppermute | solution.py:25
  158.3 33.6 %all-to-all-start.4 = ((bf16[32,16,1024]{2,1,0:T(8,128)(2,1)}), bf16[32,16,1024]{2,1,0:T(8,128)(2,1)S(1)}, u32[]{:S(2)}, u32[]{:S(2)}) async-start(bf16[32,16,1024]{2,1,0:T(8,128)(2,1)} %bitcast.63), calls=%async_computation.4 | async-start | bytes 2097152 | tf_op jit(solution)/shard_map/all_to_all | solution.py:215

commit v9 on v8

--- a/solution.py
+++ b/solution.py
@@ -181,22 +181,22 @@
     plans = [host_codes(old_plan), host_codes(new_plan)]
 
     gate_parts, down_parts = cut_weights(w_gate, w_down)
-    gate_far = swap(gate_parts[2], "m")
+    came, gate_sent = lax.optimization_barrier((came, gate_parts[2]))
+    gate_far = swap(gate_sent, "m")
+    gate_own = order(gate_parts[0], gate_far[0])
+    gate_other = swap(order(gate_parts[1], gate_far[1]), "k")
+    _, down_sent = lax.optimization_barrier((gate_far, down_parts[2]))
+    down_far = swap(down_sent, "m")
+    down_own = order(down_parts[0], down_far[0])
+    down_other = swap(order(down_parts[1], down_far[1]), "k")
 
     outs, scales = [], []
     for index in range(batches):
         rows, high, mid = route(came, plans[index], index, group)
         scales.append((high, mid))
         rows = rows.reshape(peers, -1, rows.shape[1])
-        if index == 0:
-            rows, gate_far, down_ready = lax.optimization_barrier((rows, gate_far, down_parts[2]))
-            down_far = swap(down_ready, "m")
-            gate_own = order(gate_parts[0], gate_far[0])
-            gate_other = swap(order(gate_parts[1], gate_far[1]), "k")
-            down_own = order(down_parts[0], down_far[0])
-            down_other = swap(order(down_parts[1], down_far[1]), "k")
-        else:
-            rows, gate_other, down_other = lax.optimization_barrier((rows, gate_other, down_other))
+        if outs:
+            rows, gate_other = lax.optimization_barrier((rows, gate_other))
         rows = lax.all_to_all(rows, ("y", "x"), 0, 0, tiled=True).reshape(-1, rows.shape[2])
         if outs:
             rows, _ = lax.optimization_barrier((rows, outs[0]))

time: 210 us -> 199 us (0.948)
  the two profiles are of different devices: /device:TPU:2 before, /device:TPU:16 now
where the time goes in v9:
time: 199 us; the launch traced here: 198 us
  waiting for transfers between devices  84.5 us (42%)
  starting transfers between devices  65 us (33%)
  matrix products  16.6 us (8%)
  blocking collectives  12.1 us (6%)
  other arithmetic  8.89 us (4%)
  local copies, waits for them, and re-layouts  5.41 us (3%)
  Pallas kernels  5.05 us (3%)
    ppermute x10, waiting for transfers between devices, swap(): return lax.ppermute(array, axes, [(i, last - i) for i in range(last + 1)])  38.7 us
    all_to_all x2, waiting for transfers between devices, local(): lax.all_to_all(out, ('y', 'x'), 0, 0, tiled=True).reshape(-1, out.shape[2])  32.9 us
    ppermute x10, starting transfers between devices, swap(): return lax.ppermute(array, axes, [(i, last - i) for i in range(last + 1)])  23.5 us
    all_to_all x2, starting transfers between devices, local(): lax.all_to_all(rows, ('y', 'x'), 0, 0, tiled=True)  19.9 us
    dot_general x12, matrix products, dot(): return lax.dot_general(a, b, (dims, ((), ())), preferred_element_type=out)  16.6 us
    all_to_all x1, blocking collectives, local(): terms = lax.all_to_all(mixed, ('p', 'zh'), 0, 0, tiled=True)  12.1 us
    all_to_all x2, starting transfers between devices, local(): lax.all_to_all(out, ('y', 'x'), 0, 0, tiled=True).reshape(-1, out.shape[2])  11.2 us
    all_to_all x1, starting transfers between devices, local(): came = lax.all_to_all(sent, ('p', 'zh'), 0, 0, tiled=True)  10.3 us
  transfers between devices with their start and end apart: 15, of which 9 were waited for; matrix products, arithmetic and copies ran while one was open for 10% of the time, Pallas kernels for 2%

profile of v9, /device:TPU:16, one launch (start us, length us, event | category | flops | bytes accessed | tf_op | source)
XLA Modules:
  0.0 197.8 jit_solution(15148447298961216169)
XLA Ops:
  3.6 10.3 %all-to-all-start = ((bf16[4,80,512]{2,1,0:T(8,128)(2,1)}), bf16[4,80,512]{2,1,0:T(8,128)(2,1)S(1)}, u32[]{:S(2)}, u32[]{:S(2)}) async-start(bf16[4,80,512]{2,1,0:T(8,128)(2,1)} %broadcast_in_dim.46), calls=%async_computation | async-start | bytes 655360 | tf_op jit(solution)/shard_map/all_to_all | solution.py:180
  19.8 6.6 %all-to-all-done.came = bf16[4,80,512]{2,1,0:T(8,128)(2,1)S(1)} async-done(((bf16[4,80,512]{2,1,0:T(8,128)(2,1)}), bf16[4,80,512]{2,1,0:T(8,128)(2,1)S(1)}, u32[]{:S(2)}, u32[]{:S(2)}) %all-to-all-start) | async-done | bytes 327712 | tf_op jit(solution)/shard_map/all_to_all | solution.py:180
  26.3 2.1 %shard_map.83 = (bf16[512,1024]{1,0:T(8,128)(2,1)}, bf16[512,64]{1,0:T(8,128)(2,1)S(1)}, bf16[512,64]{1,0:T(8,128)(2,1)S(1)}) custom-call(bf16[4,80,512]{2,1,0:T(8,128)(2,1)S(1)} %all-to-all-done.came, f32[64,2]{1,0:T(8,128)S(1)} %copy.47.codes), custom_call_target="tpu_custom_call" | custom-call | flops 67108864 | bytes 2097152 | tf_op jit(solution)/shard_map/pallas_call | solution.py:163
  28.4 10.1 %all-to-all-start.1 = ((bf16[32,16,1024]{2,1,0:T(8,128)(2,1)}), bf16[32,16,1024]{2,1,0:T(8,128)(2,1)}, u32[]{:S(2)}, u32[]{:S(2)}) async-start(bf16[32,16,1024]{2,1,0:T(8,128)(2,1)} %bitcast.6), calls=%async_computation.1 | async-start | bytes 2097152 | tf_op jit(solution)/shard_map/all_to_all | solution.py:200
  38.5 3.5 %collective-permute-start = (bf16[2,192,1024]{2,1,0:T(8,128)(2,1)}, bf16[2,192,1024]{2,1,0:T(8,128)(2,1)}, u32[]{:S(2)}, u32[]{:S(2)}) collective-permute-start(bf16[2,192,1024]{2,1,0:T(8,128)(2,1)} %copy-done.2), channel_id=1, source_target_pairs={{0,128},{128,0},{1,129},{129,1},{2,130},{130,2},{3,131},{131,3},{4... | collective-permute-start | bytes 2359304 | tf_op jit(solution)/shard_map/ppermute | solution.py:25
  42.1 16.6 %collective-permute-done = bf16[2,192,1024]{2,1,0:T(8,128)(2,1)} collective-permute-done((bf16[2,192,1024]{2,1,0:T(8,128)(2,1)}, bf16[2,192,1024]{2,1,0:T(8,128)(2,1)}, u32[]{:S(2)}, u32[]{:S(2)}) %collective-permute-start) | collective-permute-done | bytes 786464 | tf_op jit(solution)/shard_map/ppermute | solution.py:25
  58.6 2.1 %broadcast_select_fusion.7 = (bf16[192,1024]{1,0:T(8,128)(2,1)}, bf16[192,1024]{1,0:T(8,128)(2,1)}, bf16[192,1024]{1,0:T(8,128)(2,1)S(1)}, bf16[192,1024]{1,0:T(8,128)(2,1)S(1)}) fusion(bf16[192,1024]{1,0:T(8,128)(2,1)S(1)} %get-tuple-element.27, pred[]{:T(512)S(6)} %eq.18, bf16[2,192,1024]{2,1,0:T(8,128)(2,1)} %collective-permute-done, ...), kind=kLoop, calls=%fused_computation.29 | loop fusion | flops 786432 | bytes 3145729 | tf_op jit(solution)/shard_map/jit(_where)/select_n | solution.py:61
  60.8 1.9 collective-permute-start.1
  62.7 3.6 %collective-permute-start.4 = (bf16[2,192,1024]{2,1,0:T(8,128)(2,1)S(1)}, bf16[2,192,1024]{2,1,0:T(8,128)(2,1)S(1)}, u32[]{:S(2)}, u32[]{:S(2)}) collective-permute-start(bf16[2,192,1024]{2,1,0:T(8,128)(2,1)S(1)} %get-tuple-element.32), channel_id=1, source_target_pairs={{0,128},{128,0},{1,129},{129,1},{2,130},{130,2},{3,131},{131,3},{4... | collective-permute-start | bytes 2359304 | tf_op jit(solution)/shard_map/ppermute | solution.py:25
  66.4 3.0 %fusion.19 = bf16[512,384]{1,0:T(8,128)(2,1)} fusion(bf16[512,1024]{1,0:T(8,128)(2,1)} %bitcast.7, bf16[384,1024]{1,0:T(8,128)(2,1)} %collective-permute-done.1), kind=kOutput, calls=%fused_computation.62 | convolution fusion | flops 402653184 | bytes 2228224 | tf_op jit(solution)/shard_map/dot_general | solution.py:20
  69.3 2.1 %collective-permute-start.2 = (bf16[512,384]{1,0:T(8,128)(2,1)}, bf16[512,384]{1,0:T(8,128)(2,1)}, u32[]{:S(2)}, u32[]{:S(2)}) collective-permute-start(bf16[512,384]{1,0:T(8,128)(2,1)} %fusion.19), channel_id=1, source_target_pairs={{0,64},{64,0},{1,65},{65,1},{2,66},{66,2},{3,67},{67,3},{4,68},{68... | collective-permute-start | bytes 1179656 | tf_op jit(solution)/shard_map/ppermute | solution.py:25
  71.6 2.1 %shard_map.84 = (bf16[512,1024]{1,0:T(8,128)(2,1)}, bf16[512,64]{1,0:T(8,128)(2,1)S(1)}, bf16[512,64]{1,0:T(8,128)(2,1)S(1)}) custom-call(bf16[4,80,512]{2,1,0:T(8,128)(2,1)S(1)} %all-to-all-done.came, f32[64,2]{1,0:T(8,128)S(1)} %copy.48.codes), custom_call_target="tpu_custom_call" | custom-call | flops 67108864 | bytes 2097152 | tf_op jit(solution)/shard_map/pallas_call | solution.py:163
  73.6 9.8 %all-to-all-start.3 = ((bf16[32,16,1024]{2,1,0:T(8,128)(2,1)}), bf16[32,16,1024]{2,1,0:T(8,128)(2,1)}, u32[]{:S(2)}, u32[]{:S(2)}) async-start(bf16[32,16,1024]{2,1,0:T(8,128)(2,1)} %bitcast.16), calls=%async_computation.3 | async-start | bytes 2097152 | tf_op jit(solution)/shard_map/all_to_all | solution.py:200
  83.5 2.3 %fusion.2 = (bf16[512,384]{1,0:T(8,128)(2,1)S(1)}, f32[512,384]{1,0:T(8,128)S(1)}) fusion(bf16[512,384]{1,0:T(8,128)(2,1)} %collective-permute-done.2, bf16[512,1024]{1,0:T(8,128)(2,1)} %bitcast.7, bf16[192,1024]{1,0:T(8,128)(2,1)} %get-tuple-element.52, bf16[192,1024]{1,0:T(8,128)(2,1)} %get-tuple-element.51), kind=kOutput, calls=%fused_computation.14 | convolution fusion | flops 404815872 | bytes 3407872 | tf_op jit(solution)/shard_map/dot_general | solution.py:20
  85.8 2.3 %collective-permute-start.3 = (bf16[512,384]{1,0:T(8,128)(2,1)S(1)}, bf16[512,384]{1,0:T(8,128)(2,1)S(1)}, u32[]{:S(2)}, u32[]{:S(2)}) collective-permute-start(bf16[512,384]{1,0:T(8,128)(2,1)S(1)} %get-tuple-element.65), channel_id=1, source_target_pairs={{0,128},{128,0},{1,129},{129,1},{2,130},{130,2},{3,131},{131,3},{4... | collective-permute-start | bytes 1179656 | tf_op jit(solution)/shard_map/ppermute | solution.py:25
  88.2 1.9 collective-permute-start.6
  90.2 8.2 %collective-permute-done.3 = bf16[512,384]{1,0:T(8,128)(2,1)S(1)} collective-permute-done((bf16[512,384]{1,0:T(8,128)(2,1)S(1)}, bf16[512,384]{1,0:T(8,128)(2,1)S(1)}, u32[]{:S(2)}, u32[]{:S(2)}) %collective-permute-start.3) | collective-permute-done | bytes 393248 | tf_op jit(solution)/shard_map/ppermute | solution.py:25
  99.7 1.9 collective-permute-start.5
  104.0 1.7 add_convert_fusion.1
  105.7 6.3 %all-to-all-done.3 = bf16[32,16,1024]{2,1,0:T(8,128)(2,1)} async-done(((bf16[32,16,1024]{2,1,0:T(8,128)(2,1)}), bf16[32,16,1024]{2,1,0:T(8,128)(2,1)}, u32[]{:S(2)}, u32[]{:S(2)}) %all-to-all-start.3) | async-done | bytes 1048608 | tf_op jit(solution)/shard_map/all_to_all | solution.py:200
  112.0 2.9 %fusion.22 = bf16[512,384]{1,0:T(8,128)(2,1)} fusion(bf16[512,1024]{1,0:T(8,128)(2,1)} %bitcast.17, bf16[384,1024]{1,0:T(8,128)(2,1)} %collective-permute-done.1), kind=kOutput, calls=%fused_computation.65 | convolution fusion | flops 402653184 | bytes 2228224 | tf_op jit(solution)/shard_map/dot_general | solution.py:20
  115.0 1.9 collective-permute-start.7
  116.9 5.6 %all-to-all-start.2 = ((bf16[32,16,1024]{2,1,0:T(8,128)(2,1)}), bf16[32,16,1024]{2,1,0:T(8,128)(2,1)S(1)}, u32[]{:S(2)}, u32[]{:S(2)}) async-start(bf16[32,16,1024]{2,1,0:T(8,128)(2,1)} %bitcast.12), calls=%async_computation.2 | async-start | bytes 2097152 | tf_op jit(solution)/shard_map/all_to_all | solution.py:215
  122.5 2.3 %fusion.3 = (bf16[512,384]{1,0:T(8,128)(2,1)S(1)}, f32[512,384]{1,0:T(8,128)S(1)}) fusion(bf16[512,384]{1,0:T(8,128)(2,1)} %collective-permute-done.7, bf16[512,1024]{1,0:T(8,128)(2,1)} %bitcast.17, bf16[192,1024]{1,0:T(8,128)(2,1)} %get-tuple-element.52, bf16[192,1024]{1,0:T(8,128)(2,1)} %get-tuple-element.51), kind=kOutput, calls=%fused_computation.15 | convolution fusion | flops 404815872 | bytes 3407872 | tf_op jit(solution)/shard_map/dot_general | solution.py:20
  124.8 2.3 %collective-permute-start.8 = (bf16[512,384]{1,0:T(8,128)(2,1)S(1)}, bf16[512,384]{1,0:T(8,128)(2,1)S(1)}, u32[]{:S(2)}, u32[]{:S(2)}) collective-permute-start(bf16[512,384]{1,0:T(8,128)(2,1)S(1)} %get-tuple-element.67), channel_id=1, source_target_pairs={{0,128},{128,0},{1,129},{129,1},{2,130},{130,2},{3,131},{131,3},{4... | collective-permute-start | bytes 1179656 | tf_op jit(solution)/shard_map/ppermute | solution.py:25
  127.1 10.5 %collective-permute-done.8 = bf16[512,384]{1,0:T(8,128)(2,1)S(1)} collective-permute-done((bf16[512,384]{1,0:T(8,128)(2,1)S(1)}, bf16[512,384]{1,0:T(8,128)(2,1)S(1)}, u32[]{:S(2)}, u32[]{:S(2)}) %collective-permute-start.8) | collective-permute-done | bytes 393248 | tf_op jit(solution)/shard_map/ppermute | solution.py:25
  138.9 1.9 collective-permute-start.9
  143.2 1.7 add_convert_fusion
  144.9 6.2 %all-to-all-done.2 = bf16[32,16,1024]{2,1,0:T(8,128)(2,1)S(1)} async-done(((bf16[32,16,1024]{2,1,0:T(8,128)(2,1)}), bf16[32,16,1024]{2,1,0:T(8,128)(2,1)S(1)}, u32[]{:S(2)}, u32[]{:S(2)}) %all-to-all-start.2) | async-done | bytes 1048608 | tf_op jit(solution)/shard_map/all_to_all | solution.py:215
  151.1 5.6 %all-to-all-start.4 = ((bf16[32,16,1024]{2,1,0:T(8,128)(2,1)}), bf16[32,16,1024]{2,1,0:T(8,128)(2,1)S(1)}, u32[]{:S(2)}, u32[]{:S(2)}) async-start(bf16[32,16,1024]{2,1,0:T(8,128)(2,1)} %bitcast.69), calls=%async_computation.4 | async-start | bytes 2097152 | tf_op jit(solution)/shard_map/all_to_all | solution.py:215
  157.5 26.7 %all-to-all-done.4 = bf16[32,16,1024]{2,1,0:T(8,128)(2,1)S(1)} async-done(((bf16[32,16,1024]{2,1,0:T(8,128)(2,1)}), bf16[32,16,1024]{2,1,0:T(8,128)(2,1)S(1)}, u32[]{:S(2)}, u32[]{:S(2)}) %all-to-all-start.4) | async-done | bytes 1048608 | tf_op jit(solution)/shard_map/all_to_all | solution.py:215
  185.1 12.1 %all_to_all.30 = bf16[4,64,512]{2,1,0:T(8,128)(2,1)S(1)} all-to-all(bf16[4,64,512]{2,1,0:T(8,128)(2,1)S(1)} %bitcast.70), channel_id=1, replica_groups=mesh['p'=2,'m'=2,'k'=2,'zh'=2,'y'=8,'x'=4] {'p','zh'}, dimensions={0} | all-to-all | bytes 524288 | tf_op jit(solution)/shard_map/all_to_all | solution.py:219
  (51 shorter events, 19.2 us)
Async XLA Ops:
  3.6 22.7 %all-to-all-start = ((bf16[4,80,512]{2,1,0:T(8,128)(2,1)}), bf16[4,80,512]{2,1,0:T(8,128)(2,1)S(1)}, u32[]{:S(2)}, u32[]{:S(2)}) async-start(bf16[4,80,512]{2,1,0:T(8,128)(2,1)} %broadcast_in_dim.46), calls=%async_computation | async-start | bytes 655360 | tf_op jit(solution)/shard_map/all_to_all | solution.py:180
  15.1 1.4 copy-start
  16.5 1.4 copy-start.1
  18.9 0.9 copy-start.2
  28.4 38.0 %all-to-all-start.1 = ((bf16[32,16,1024]{2,1,0:T(8,128)(2,1)}), bf16[32,16,1024]{2,1,0:T(8,128)(2,1)}, u32[]{:S(2)}, u32[]{:S(2)}) async-start(bf16[32,16,1024]{2,1,0:T(8,128)(2,1)} %bitcast.6), calls=%async_computation.1 | async-start | bytes 2097152 | tf_op jit(solution)/shard_map/all_to_all | solution.py:200
  38.5 20.1 %collective-permute-start = (bf16[2,192,1024]{2,1,0:T(8,128)(2,1)}, bf16[2,192,1024]{2,1,0:T(8,128)(2,1)}, u32[]{:S(2)}, u32[]{:S(2)}) collective-permute-start(bf16[2,192,1024]{2,1,0:T(8,128)(2,1)} %copy-done.2), channel_id=1, source_target_pairs={{0,128},{128,0},{1,129},{129,1},{2,130},{130,2},{3,131},{131,3},{4... | collective-permute-start | bytes 2359304 | tf_op jit(solution)/shard_map/ppermute | solution.py:25
  60.8 5.6 %collective-permute-start.1 = (bf16[384,1024]{1,0:T(8,128)(2,1)S(1)}, bf16[384,1024]{1,0:T(8,128)(2,1)}, u32[]{:S(2)}, u32[]{:S(2)}) collective-permute-start(bf16[384,1024]{1,0:T(8,128)(2,1)S(1)} %pad_maximum_fusion.1), channel_id=1, source_target_pairs={{0,64},{64,0},{1,65},{65,1},{2,66},{66,2},{3,67},{67,3},{4,68},{68... | collective-permute-start | bytes 2359304 | tf_op jit(solution)/shard_map/ppermute | solution.py:25
  62.7 25.3 %collective-permute-start.4 = (bf16[2,192,1024]{2,1,0:T(8,128)(2,1)S(1)}, bf16[2,192,1024]{2,1,0:T(8,128)(2,1)S(1)}, u32[]{:S(2)}, u32[]{:S(2)}) collective-permute-start(bf16[2,192,1024]{2,1,0:T(8,128)(2,1)S(1)} %get-tuple-element.32), channel_id=1, source_target_pairs={{0,128},{128,0},{1,129},{129,1},{2,130},{130,2},{3,131},{131,3},{4... | collective-permute-start | bytes 2359304 | tf_op jit(solution)/shard_map/ppermute | solution.py:25
  69.3 14.1 %collective-permute-start.2 = (bf16[512,384]{1,0:T(8,128)(2,1)}, bf16[512,384]{1,0:T(8,128)(2,1)}, u32[]{:S(2)}, u32[]{:S(2)}) collective-permute-start(bf16[512,384]{1,0:T(8,128)(2,1)} %fusion.19), channel_id=1, source_target_pairs={{0,64},{64,0},{1,65},{65,1},{2,66},{66,2},{3,67},{67,3},{4,68},{68... | collective-permute-start | bytes 1179656 | tf_op jit(solution)/shard_map/ppermute | solution.py:25
  73.6 38.4 %all-to-all-start.3 = ((bf16[32,16,1024]{2,1,0:T(8,128)(2,1)}), bf16[32,16,1024]{2,1,0:T(8,128)(2,1)}, u32[]{:S(2)}, u32[]{:S(2)}) async-start(bf16[32,16,1024]{2,1,0:T(8,128)(2,1)} %bitcast.16), calls=%async_computation.3 | async-start | bytes 2097152 | tf_op jit(solution)/shard_map/all_to_all | solution.py:200
  85.8 12.6 %collective-permute-start.3 = (bf16[512,384]{1,0:T(8,128)(2,1)S(1)}, bf16[512,384]{1,0:T(8,128)(2,1)S(1)}, u32[]{:S(2)}, u32[]{:S(2)}) collective-permute-start(bf16[512,384]{1,0:T(8,128)(2,1)S(1)} %get-tuple-element.65), channel_id=1, source_target_pairs={{0,128},{128,0},{1,129},{129,1},{2,130},{130,2},{3,131},{131,3},{4... | collective-permute-start | bytes 1179656 | tf_op jit(solution)/shard_map/ppermute | solution.py:25
  88.2 13.4 %collective-permute-start.6 = (bf16[384,1024]{1,0:T(8,128)(2,1)S(1)}, bf16[384,1024]{1,0:T(8,128)(2,1)S(1)}, u32[]{:S(2)}, u32[]{:S(2)}) collective-permute-start(bf16[384,1024]{1,0:T(8,128)(2,1)S(1)} %pad_maximum_fusion.3), channel_id=1, source_target_pairs={{0,64},{64,0},{1,65},{65,1},{2,66},{66,2},{3,67},{67,3},{4,68},{68... | collective-permute-start | bytes 2359304 | tf_op jit(solution)/shard_map/ppermute | solution.py:25
  99.7 3.6 %collective-permute-start.5 = (bf16[512,384]{1,0:T(8,128)(2,1)S(1)}, bf16[512,384]{1,0:T(8,128)(2,1)S(1)}, u32[]{:S(2)}, u32[]{:S(2)}) collective-permute-start(bf16[512,384]{1,0:T(8,128)(2,1)S(1)} %multiply_convert_fusion.1), channel_id=1, source_target_pairs={{0,64},{64,0},{1,65},{65,1},{2,66},{66,2},{3,67},{67,3},{4,68},{68... | collective-permute-start | bytes 1179656 | tf_op jit(solution)/shard_map/ppermute | solution.py:25
  115.0 7.5 %collective-permute-start.7 = (bf16[512,384]{1,0:T(8,128)(2,1)}, bf16[512,384]{1,0:T(8,128)(2,1)}, u32[]{:S(2)}, u32[]{:S(2)}) collective-permute-start(bf16[512,384]{1,0:T(8,128)(2,1)} %fusion.22), channel_id=1, source_target_pairs={{0,64},{64,0},{1,65},{65,1},{2,66},{66,2},{3,67},{67,3},{4,68},{68... | collective-permute-start | bytes 1179656 | tf_op jit(solution)/shard_map/ppermute | solution.py:25
  116.9 34.2 %all-to-all-start.2 = ((bf16[32,16,1024]{2,1,0:T(8,128)(2,1)}), bf16[32,16,1024]{2,1,0:T(8,128)(2,1)S(1)}, u32[]{:S(2)}, u32[]{:S(2)}) async-start(bf16[32,16,1024]{2,1,0:T(8,128)(2,1)} %bitcast.12), calls=%async_computation.2 | async-start | bytes 2097152 | tf_op jit(solution)/shard_map/all_to_all | solution.py:215
  124.8 12.9 %collective-permute-start.8 = (bf16[512,384]{1,0:T(8,128)(2,1)S(1)}, bf16[512,384]{1,0:T(8,128)(2,1)S(1)}, u32[]{:S(2)}, u32[]{:S(2)}) collective-permute-start(bf16[512,384]{1,0:T(8,128)(2,1)S(1)} %get-tuple-element.67), channel_id=1, source_target_pairs={{0,128},{128,0},{1,129},{129,1},{2,130},{130,2},{3,131},{131,3},{4... | collective-permute-start | bytes 1179656 | tf_op jit(solution)/shard_map/ppermute | solution.py:25
  138.9 3.6 %collective-permute-start.9 = (bf16[512,384]{1,0:T(8,128)(2,1)S(1)}, bf16[512,384]{1,0:T(8,128)(2,1)S(1)}, u32[]{:S(2)}, u32[]{:S(2)}) collective-permute-start(bf16[512,384]{1,0:T(8,128)(2,1)S(1)} %multiply_convert_fusion), channel_id=1, source_target_pairs={{0,64},{64,0},{1,65},{65,1},{2,66},{66,2},{3,67},{67,3},{4,68},{68... | collective-permute-start | bytes 1179656 | tf_op jit(solution)/shard_map/ppermute | solution.py:25
  151.1 33.1 %all-to-all-start.4 = ((bf16[32,16,1024]{2,1,0:T(8,128)(2,1)}), bf16[32,16,1024]{2,1,0:T(8,128)(2,1)S(1)}, u32[]{:S(2)}, u32[]{:S(2)}) async-start(bf16[32,16,1024]{2,1,0:T(8,128)(2,1)} %bitcast.69), calls=%async_computation.4 | async-start | bytes 2097152 | tf_op jit(solution)/shard_map/all_to_all | solution.py:215

commit v10 on v9

--- a/solution.py
+++ b/solution.py
@@ -183,6 +183,8 @@
     gate_parts, down_parts = cut_weights(w_gate, w_down)
     came, gate_sent = lax.optimization_barrier((came, gate_parts[2]))
     gate_far = swap(gate_sent, "m")
+    routed = [route(came, plans[index], index, group) for index in range(batches)]
+    gate_far, routed[1] = lax.optimization_barrier((gate_far, routed[1]))
     gate_own = order(gate_parts[0], gate_far[0])
     gate_other = swap(order(gate_parts[1], gate_far[1]), "k")
     _, down_sent = lax.optimization_barrier((gate_far, down_parts[2]))
@@ -192,17 +194,15 @@
 
     outs, scales = [], []
     for index in range(batches):
-        rows, high, mid = route(came, plans[index], index, group)
+        rows, high, mid = routed[index]
         scales.append((high, mid))
         rows = rows.reshape(peers, -1, rows.shape[1])
-        if outs:
-            rows, gate_other = lax.optimization_barrier((rows, gate_other))
         rows = lax.all_to_all(rows, ("y", "x"), 0, 0, tiled=True).reshape(-1, rows.shape[2])
         if outs:
             rows, _ = lax.optimization_barrier((rows, outs[0]))
 
         send = dot(rows, gate_other, ((1,), (1,)), BF)
-        part = dot(rows, gate_own, ((1,), (1,)))
+        part = lax.optimization_barrier(dot(rows, gate_own, ((1,), (1,))))
         part = part + swap(send, "k").astype(F32)
         gate = part + swap(part.astype(BF), "m").astype(F32)
         hidden = jax.nn.silu(gate).astype(BF)

time: 199 us -> 198 us (level)
  waiting for transfers between devices: 84.5 us -> 81.4 us
    ppermute x10, waiting for transfers between devices: 38.7 us -> 35.4 us  [swap(): return lax.ppermute(array, axes, [(i, last - i) for i in range(last + 1)])]
    unnamed x6 -> x16, local copies, waits for them, and re-layouts: 3.7 us -> 4.61 us
where the time goes in v10:
time: 198 us; the launch traced here: 196 us
  waiting for transfers between devices  81.4 us (41%)
  starting transfers between devices  65.1 us (33%)
  matrix products  15.7 us (8%)
  blocking collectives  12.1 us (6%)
  other arithmetic  10.2 us (5%)
  local copies, waits for them, and re-layouts  6.32 us (3%)
  Pallas kernels  5.08 us (3%)
    ppermute x10, waiting for transfers between devices, swap(): return lax.ppermute(array, axes, [(i, last - i) for i in range(last + 1)])  35.4 us
    all_to_all x2, waiting for transfers between devices, local(): lax.all_to_all(out, ('y', 'x'), 0, 0, tiled=True).reshape(-1, out.shape[2])  32 us
    ppermute x10, starting transfers between devices, swap(): return lax.ppermute(array, axes, [(i, last - i) for i in range(last + 1)])  23.6 us
    all_to_all x2, starting transfers between devices, local(): lax.all_to_all(rows, ('y', 'x'), 0, 0, tiled=True)  20 us
    dot_general x12, matrix products, dot(): return lax.dot_general(a, b, (dims, ((), ())), preferred_element_type=out)  15.7 us
    all_to_all x1, blocking collectives, local(): terms = lax.all_to_all(mixed, ('p', 'zh'), 0, 0, tiled=True)  12.1 us
    all_to_all x2, starting transfers between devices, local(): lax.all_to_all(out, ('y', 'x'), 0, 0, tiled=True).reshape(-1, out.shape[2])  11.2 us
    all_to_all x1, starting transfers between devices, local(): came = lax.all_to_all(sent, ('p', 'zh'), 0, 0, tiled=True)  10.3 us
  transfers between devices with their start and end apart: 15, of which 9 were waited for; matrix products, arithmetic and copies ran while one was open for 10% of the time, Pallas kernels for 2%

profile of v10, /device:TPU:16, one launch (start us, length us, event | category | flops | bytes accessed | tf_op | source)
XLA Modules:
  0.0 196.2 jit_solution(16024530650366664966)
XLA Ops:
  3.6 10.3 %all-to-all-start = ((bf16[4,80,512]{2,1,0:T(8,128)(2,1)}), bf16[4,80,512]{2,1,0:T(8,128)(2,1)S(1)}, u32[]{:S(2)}, u32[]{:S(2)}) async-start(bf16[4,80,512]{2,1,0:T(8,128)(2,1)} %broadcast_in_dim.46), calls=%async_computation | async-start | bytes 655360 | tf_op jit(solution)/shard_map/all_to_all | solution.py:180
  19.8 6.6 %all-to-all-done.came = bf16[4,80,512]{2,1,0:T(8,128)(2,1)S(1)} async-done(((bf16[4,80,512]{2,1,0:T(8,128)(2,1)}), bf16[4,80,512]{2,1,0:T(8,128)(2,1)S(1)}, u32[]{:S(2)}, u32[]{:S(2)}) %all-to-all-start) | async-done | bytes 327712 | tf_op jit(solution)/shard_map/all_to_all | solution.py:180
  26.3 2.1 %shard_map.83 = (bf16[512,1024]{1,0:T(8,128)(2,1)}, bf16[512,64]{1,0:T(8,128)(2,1)S(1)}, bf16[512,64]{1,0:T(8,128)(2,1)S(1)}) custom-call(bf16[4,80,512]{2,1,0:T(8,128)(2,1)S(1)} %all-to-all-done.came, f32[64,2]{1,0:T(8,128)S(1)} %copy.47.codes), custom_call_target="tpu_custom_call" | custom-call | flops 67108864 | bytes 2097152 | tf_op jit(solution)/shard_map/pallas_call | solution.py:163
  28.4 10.1 %all-to-all-start.1 = ((bf16[32,16,1024]{2,1,0:T(8,128)(2,1)}), bf16[32,16,1024]{2,1,0:T(8,128)(2,1)}, u32[]{:S(2)}, u32[]{:S(2)}) async-start(bf16[32,16,1024]{2,1,0:T(8,128)(2,1)} %bitcast.6), calls=%async_computation.1 | async-start | bytes 2097152 | tf_op jit(solution)/shard_map/all_to_all | solution.py:200
  38.5 3.5 %collective-permute-start = (bf16[2,192,1024]{2,1,0:T(8,128)(2,1)}, bf16[2,192,1024]{2,1,0:T(8,128)(2,1)}, u32[]{:S(2)}, u32[]{:S(2)}) collective-permute-start(bf16[2,192,1024]{2,1,0:T(8,128)(2,1)} %copy-done.2), channel_id=1, source_target_pairs={{0,128},{128,0},{1,129},{129,1},{2,130},{130,2},{3,131},{131,3},{4... | collective-permute-start | bytes 2359304 | tf_op jit(solution)/shard_map/ppermute | solution.py:25
  42.2 2.1 %shard_map.84 = (bf16[512,1024]{1,0:T(8,128)(2,1)}, bf16[512,64]{1,0:T(8,128)(2,1)S(1)}, bf16[512,64]{1,0:T(8,128)(2,1)S(1)}) custom-call(bf16[4,80,512]{2,1,0:T(8,128)(2,1)S(1)} %all-to-all-done.came, f32[64,2]{1,0:T(8,128)S(1)} %copy.48.codes), custom_call_target="tpu_custom_call" | custom-call | flops 67108864 | bytes 2097152 | tf_op jit(solution)/shard_map/pallas_call | solution.py:163
  44.3 14.4 %collective-permute-done = bf16[2,192,1024]{2,1,0:T(8,128)(2,1)} collective-permute-done((bf16[2,192,1024]{2,1,0:T(8,128)(2,1)}, bf16[2,192,1024]{2,1,0:T(8,128)(2,1)}, u32[]{:S(2)}, u32[]{:S(2)}) %collective-permute-start) | collective-permute-done | bytes 786464 | tf_op jit(solution)/shard_map/ppermute | solution.py:25
  58.6 2.1 %bitcast_select_fusion.1 = (bf16[192,1024]{1,0:T(8,128)(2,1)S(1)}, bf16[192,1024]{1,0:T(8,128)(2,1)S(1)}, bf16[192,1024]{1,0:T(8,128)(2,1)}, bf16[192,1024]{1,0:T(8,128)(2,1)}) fusion(bf16[192,1024]{1,0:T(8,128)(2,1)S(1)} %get-tuple-element.35, pred[]{:T(512)S(6)} %eq.18, bf16[2,192,1024]{2,1,0:T(8,128)(2,1)} %collective-permute-done, ...), kind=kLoop, calls=%fused_computation.21 | loop fusion | flops 786432 | bytes 3145729 | tf_op jit(solution)/shard_map/jit(_where)/select_n | solution.py:61
  60.8 1.9 collective-permute-start.1
  62.7 3.6 %collective-permute-start.4 = (bf16[2,192,1024]{2,1,0:T(8,128)(2,1)S(1)}, bf16[2,192,1024]{2,1,0:T(8,128)(2,1)}, u32[]{:S(2)}, u32[]{:S(2)}) collective-permute-start(bf16[2,192,1024]{2,1,0:T(8,128)(2,1)S(1)} %get-tuple-element.38), channel_id=1, source_target_pairs={{0,128},{128,0},{1,129},{129,1},{2,130},{130,2},{3,131},{131,3},{4... | collective-permute-start | bytes 2359304 | tf_op jit(solution)/shard_map/ppermute | solution.py:25
  67.3 2.7 %fusion.19 = bf16[512,384]{1,0:T(8,128)(2,1)} fusion(bf16[512,1024]{1,0:T(8,128)(2,1)} %bitcast.7, bf16[384,1024]{1,0:T(8,128)(2,1)S(1)} %collective-permute-done.1), kind=kOutput, calls=%fused_computation.60 | convolution fusion | flops 402653184 | bytes 2228224 | tf_op jit(solution)/shard_map/dot_general | solution.py:20
  70.0 2.2 %collective-permute-start.2 = (bf16[512,384]{1,0:T(8,128)(2,1)}, bf16[512,384]{1,0:T(8,128)(2,1)S(1)}, u32[]{:S(2)}, u32[]{:S(2)}) collective-permute-start(bf16[512,384]{1,0:T(8,128)(2,1)} %fusion.19), channel_id=1, source_target_pairs={{0,64},{64,0},{1,65},{65,1},{2,66},{66,2},{3,67},{67,3},{4,68},{68... | collective-permute-start | bytes 1179656 | tf_op jit(solution)/shard_map/ppermute | solution.py:25
  72.3 9.8 %all-to-all-start.3 = ((bf16[32,16,1024]{2,1,0:T(8,128)(2,1)}), bf16[32,16,1024]{2,1,0:T(8,128)(2,1)}, u32[]{:S(2)}, u32[]{:S(2)}) async-start(bf16[32,16,1024]{2,1,0:T(8,128)(2,1)} %bitcast.16), calls=%async_computation.3 | async-start | bytes 2097152 | tf_op jit(solution)/shard_map/all_to_all | solution.py:200
  82.1 2.0 %fusion.5 = f32[512,384]{1,0:T(8,128)S(1)} fusion(bf16[512,1024]{1,0:T(8,128)(2,1)} %bitcast.7, bf16[192,1024]{1,0:T(8,128)(2,1)S(1)} %copy-done.5, bf16[192,1024]{1,0:T(8,128)(2,1)} %get-tuple-element.62), kind=kOutput, calls=%fused_computation.17 | convolution fusion | flops 404226048 | bytes 2621440 | tf_op jit(solution)/shard_map/dot_general | solution.py:20
  84.3 2.2 %collective-permute-start.3 = (bf16[512,384]{1,0:T(8,128)(2,1)S(1)}, bf16[512,384]{1,0:T(8,128)(2,1)S(1)}, u32[]{:S(2)}, u32[]{:S(2)}) collective-permute-start(bf16[512,384]{1,0:T(8,128)(2,1)S(1)} %fusion.2), channel_id=1, source_target_pairs={{0,128},{128,0},{1,129},{129,1},{2,130},{130,2},{3,131},{131,3},{4... | collective-permute-start | bytes 1179656 | tf_op jit(solution)/shard_map/ppermute | solution.py:25
  87.8 2.1 %collective-permute-start.6 = (bf16[384,1024]{1,0:T(8,128)(2,1)S(1)}, bf16[384,1024]{1,0:T(8,128)(2,1)S(1)}, u32[]{:S(2)}, u32[]{:S(2)}) collective-permute-start(bf16[384,1024]{1,0:T(8,128)(2,1)S(1)} %pad_maximum_fusion.3), channel_id=1, source_target_pairs={{0,64},{64,0},{1,65},{65,1},{2,66},{66,2},{3,67},{67,3},{4,68},{68... | collective-permute-start | bytes 2359304 | tf_op jit(solution)/shard_map/ppermute | solution.py:25
  89.9 7.1 %collective-permute-done.3 = bf16[512,384]{1,0:T(8,128)(2,1)S(1)} collective-permute-done((bf16[512,384]{1,0:T(8,128)(2,1)S(1)}, bf16[512,384]{1,0:T(8,128)(2,1)S(1)}, u32[]{:S(2)}, u32[]{:S(2)}) %collective-permute-start.3) | collective-permute-done | bytes 393248 | tf_op jit(solution)/shard_map/ppermute | solution.py:25
  97.2 1.9 collective-permute-start.5
  101.5 1.7 add_convert_fusion.1
  103.2 7.4 %all-to-all-done.3 = bf16[32,16,1024]{2,1,0:T(8,128)(2,1)} async-done(((bf16[32,16,1024]{2,1,0:T(8,128)(2,1)}), bf16[32,16,1024]{2,1,0:T(8,128)(2,1)}, u32[]{:S(2)}, u32[]{:S(2)}) %all-to-all-start.3) | async-done | bytes 1048608 | tf_op jit(solution)/shard_map/all_to_all | solution.py:200
  110.7 2.7 %fusion.22 = bf16[512,384]{1,0:T(8,128)(2,1)} fusion(bf16[512,1024]{1,0:T(8,128)(2,1)} %bitcast.17, bf16[384,1024]{1,0:T(8,128)(2,1)S(1)} %copy-done.7), kind=kOutput, calls=%fused_computation.63 | convolution fusion | flops 402653184 | bytes 2228224 | tf_op jit(solution)/shard_map/dot_general | solution.py:20
  113.4 1.9 collective-permute-start.7
  115.3 5.6 %all-to-all-start.2 = ((bf16[32,16,1024]{2,1,0:T(8,128)(2,1)}), bf16[32,16,1024]{2,1,0:T(8,128)(2,1)S(1)}, u32[]{:S(2)}, u32[]{:S(2)}) async-start(bf16[32,16,1024]{2,1,0:T(8,128)(2,1)} %bitcast.14), calls=%async_computation.2 | async-start | bytes 2097152 | tf_op jit(solution)/shard_map/all_to_all | solution.py:215
  120.9 2.2 %fusion.4 = f32[512,384]{1,0:T(8,128)S(1)} fusion(bf16[512,1024]{1,0:T(8,128)(2,1)} %bitcast.17, bf16[192,1024]{1,0:T(8,128)(2,1)} %get-tuple-element.61, bf16[192,1024]{1,0:T(8,128)(2,1)} %get-tuple-element.62), kind=kOutput, calls=%fused_computation.16 | convolution fusion | flops 404226048 | bytes 2621440 | tf_op jit(solution)/shard_map/dot_general | solution.py:20
  124.1 2.2 %collective-permute-start.8 = (bf16[512,384]{1,0:T(8,128)(2,1)S(1)}, bf16[512,384]{1,0:T(8,128)(2,1)S(1)}, u32[]{:S(2)}, u32[]{:S(2)}) collective-permute-start(bf16[512,384]{1,0:T(8,128)(2,1)S(1)} %fusion.3), channel_id=1, source_target_pairs={{0,128},{128,0},{1,129},{129,1},{2,130},{130,2},{3,131},{131,3},{4... | collective-permute-start | bytes 1179656 | tf_op jit(solution)/shard_map/ppermute | solution.py:25
  126.4 10.6 %collective-permute-done.8 = bf16[512,384]{1,0:T(8,128)(2,1)S(1)} collective-permute-done((bf16[512,384]{1,0:T(8,128)(2,1)S(1)}, bf16[512,384]{1,0:T(8,128)(2,1)S(1)}, u32[]{:S(2)}, u32[]{:S(2)}) %collective-permute-start.8) | collective-permute-done | bytes 393248 | tf_op jit(solution)/shard_map/ppermute | solution.py:25
  138.2 1.9 collective-permute-start.9
  142.6 1.7 add_convert_fusion
  144.3 5.2 %all-to-all-done.2 = bf16[32,16,1024]{2,1,0:T(8,128)(2,1)S(1)} async-done(((bf16[32,16,1024]{2,1,0:T(8,128)(2,1)}), bf16[32,16,1024]{2,1,0:T(8,128)(2,1)S(1)}, u32[]{:S(2)}, u32[]{:S(2)}) %all-to-all-start.2) | async-done | bytes 1048608 | tf_op jit(solution)/shard_map/all_to_all | solution.py:215
  149.5 5.6 %all-to-all-start.4 = ((bf16[32,16,1024]{2,1,0:T(8,128)(2,1)}), bf16[32,16,1024]{2,1,0:T(8,128)(2,1)S(1)}, u32[]{:S(2)}, u32[]{:S(2)}) async-start(bf16[32,16,1024]{2,1,0:T(8,128)(2,1)} %bitcast.63), calls=%async_computation.4 | async-start | bytes 2097152 | tf_op jit(solution)/shard_map/all_to_all | solution.py:215
  156.0 26.7 %all-to-all-done.4 = bf16[32,16,1024]{2,1,0:T(8,128)(2,1)S(1)} async-done(((bf16[32,16,1024]{2,1,0:T(8,128)(2,1)}), bf16[32,16,1024]{2,1,0:T(8,128)(2,1)S(1)}, u32[]{:S(2)}, u32[]{:S(2)}) %all-to-all-start.4) | async-done | bytes 1048608 | tf_op jit(solution)/shard_map/all_to_all | solution.py:215
  183.5 12.1 %all_to_all.30 = bf16[4,64,512]{2,1,0:T(8,128)(2,1)S(1)} all-to-all(bf16[4,64,512]{2,1,0:T(8,128)(2,1)S(1)} %bitcast.64), channel_id=1, replica_groups=mesh['p'=2,'m'=2,'k'=2,'zh'=2,'y'=8,'x'=4] {'p','zh'}, dimensions={0} | all-to-all | bytes 524288 | tf_op jit(solution)/shard_map/all_to_all | solution.py:219
  (63 shorter events, 21.4 us)
Async XLA Ops:
  3.6 22.7 %all-to-all-start = ((bf16[4,80,512]{2,1,0:T(8,128)(2,1)}), bf16[4,80,512]{2,1,0:T(8,128)(2,1)S(1)}, u32[]{:S(2)}, u32[]{:S(2)}) async-start(bf16[4,80,512]{2,1,0:T(8,128)(2,1)} %broadcast_in_dim.46), calls=%async_computation | async-start | bytes 655360 | tf_op jit(solution)/shard_map/all_to_all | solution.py:180
  15.1 1.4 copy-start
  16.5 1.4 copy-start.1
  18.9 0.9 copy-start.2
  28.4 38.0 %all-to-all-start.1 = ((bf16[32,16,1024]{2,1,0:T(8,128)(2,1)}), bf16[32,16,1024]{2,1,0:T(8,128)(2,1)}, u32[]{:S(2)}, u32[]{:S(2)}) async-start(bf16[32,16,1024]{2,1,0:T(8,128)(2,1)} %bitcast.6), calls=%async_computation.1 | async-start | bytes 2097152 | tf_op jit(solution)/shard_map/all_to_all | solution.py:200
  38.5 20.1 %collective-permute-start = (bf16[2,192,1024]{2,1,0:T(8,128)(2,1)}, bf16[2,192,1024]{2,1,0:T(8,128)(2,1)}, u32[]{:S(2)}, u32[]{:S(2)}) collective-permute-start(bf16[2,192,1024]{2,1,0:T(8,128)(2,1)} %copy-done.2), channel_id=1, source_target_pairs={{0,128},{128,0},{1,129},{129,1},{2,130},{130,2},{3,131},{131,3},{4... | collective-permute-start | bytes 2359304 | tf_op jit(solution)/shard_map/ppermute | solution.py:25
  60.8 5.6 %collective-permute-start.1 = (bf16[384,1024]{1,0:T(8,128)(2,1)S(1)}, bf16[384,1024]{1,0:T(8,128)(2,1)S(1)}, u32[]{:S(2)}, u32[]{:S(2)}) collective-permute-start(bf16[384,1024]{1,0:T(8,128)(2,1)S(1)} %pad_maximum_fusion.1), channel_id=1, source_target_pairs={{0,64},{64,0},{1,65},{65,1},{2,66},{66,2},{3,67},{67,3},{4,68},{68... | collective-permute-start | bytes 2359304 | tf_op jit(solution)/shard_map/ppermute | solution.py:25
  62.7 23.8 %collective-permute-start.4 = (bf16[2,192,1024]{2,1,0:T(8,128)(2,1)S(1)}, bf16[2,192,1024]{2,1,0:T(8,128)(2,1)}, u32[]{:S(2)}, u32[]{:S(2)}) collective-permute-start(bf16[2,192,1024]{2,1,0:T(8,128)(2,1)S(1)} %get-tuple-element.38), channel_id=1, source_target_pairs={{0,128},{128,0},{1,129},{129,1},{2,130},{130,2},{3,131},{131,3},{4... | collective-permute-start | bytes 2359304 | tf_op jit(solution)/shard_map/ppermute | solution.py:25
  66.4 0.9 copy-start.6
  70.0 12.1 %copy-start.5 = (bf16[192,1024]{1,0:T(8,128)(2,1)S(1)}, bf16[192,1024]{1,0:T(8,128)(2,1)}, u32[]{:S(2)}) copy-start(bf16[192,1024]{1,0:T(8,128)(2,1)} %get-tuple-element.61) | copy-start | bytes 1179652
  70.0 14.2 %collective-permute-start.2 = (bf16[512,384]{1,0:T(8,128)(2,1)}, bf16[512,384]{1,0:T(8,128)(2,1)S(1)}, u32[]{:S(2)}, u32[]{:S(2)}) collective-permute-start(bf16[512,384]{1,0:T(8,128)(2,1)} %fusion.19), channel_id=1, source_target_pairs={{0,64},{64,0},{1,65},{65,1},{2,66},{66,2},{3,67},{67,3},{4,68},{68... | collective-permute-start | bytes 1179656 | tf_op jit(solution)/shard_map/ppermute | solution.py:25
  72.3 38.4 %all-to-all-start.3 = ((bf16[32,16,1024]{2,1,0:T(8,128)(2,1)}), bf16[32,16,1024]{2,1,0:T(8,128)(2,1)}, u32[]{:S(2)}, u32[]{:S(2)}) async-start(bf16[32,16,1024]{2,1,0:T(8,128)(2,1)} %bitcast.16), calls=%async_computation.3 | async-start | bytes 2097152 | tf_op jit(solution)/shard_map/all_to_all | solution.py:200
  84.2 3.6 %copy-start.3 = (bf16[512,384]{1,0:T(8,128)(2,1)}, bf16[512,384]{1,0:T(8,128)(2,1)S(1)}, u32[]{:S(2)}) copy-start(bf16[512,384]{1,0:T(8,128)(2,1)S(1)} %collective-permute-done.2) | copy-start | bytes 1179652
  84.3 12.6 %collective-permute-start.3 = (bf16[512,384]{1,0:T(8,128)(2,1)S(1)}, bf16[512,384]{1,0:T(8,128)(2,1)S(1)}, u32[]{:S(2)}, u32[]{:S(2)}) collective-permute-start(bf16[512,384]{1,0:T(8,128)(2,1)S(1)} %fusion.2), channel_id=1, source_target_pairs={{0,128},{128,0},{1,129},{129,1},{2,130},{130,2},{3,131},{131,3},{4... | collective-permute-start | bytes 1179656 | tf_op jit(solution)/shard_map/ppermute | solution.py:25
  87.8 9.2 %copy-start.4 = (bf16[512,384]{1,0:T(8,128)(2,1)S(1)}, bf16[512,384]{1,0:T(8,128)(2,1)}, u32[]{:S(2)}) copy-start(bf16[512,384]{1,0:T(8,128)(2,1)} %copy-done.3) | copy-start | bytes 1179652
  87.8 11.3 %collective-permute-start.6 = (bf16[384,1024]{1,0:T(8,128)(2,1)S(1)}, bf16[384,1024]{1,0:T(8,128)(2,1)S(1)}, u32[]{:S(2)}, u32[]{:S(2)}) collective-permute-start(bf16[384,1024]{1,0:T(8,128)(2,1)S(1)} %pad_maximum_fusion.3), channel_id=1, source_target_pairs={{0,64},{64,0},{1,65},{65,1},{2,66},{66,2},{3,67},{67,3},{4,68},{68... | collective-permute-start | bytes 2359304 | tf_op jit(solution)/shard_map/ppermute | solution.py:25
  97.2 3.6 %collective-permute-start.5 = (bf16[512,384]{1,0:T(8,128)(2,1)S(1)}, bf16[512,384]{1,0:T(8,128)(2,1)S(1)}, u32[]{:S(2)}, u32[]{:S(2)}) collective-permute-start(bf16[512,384]{1,0:T(8,128)(2,1)S(1)} %multiply_convert_fusion.1), channel_id=1, source_target_pairs={{0,64},{64,0},{1,65},{65,1},{2,66},{66,2},{3,67},{67,3},{4,68},{68... | collective-permute-start | bytes 1179656 | tf_op jit(solution)/shard_map/ppermute | solution.py:25
  101.5 9.1 %copy-start.7 = (bf16[384,1024]{1,0:T(8,128)(2,1)S(1)}, bf16[384,1024]{1,0:T(8,128)(2,1)}, u32[]{:S(2)}) copy-start(bf16[384,1024]{1,0:T(8,128)(2,1)} %copy-done.6) | copy-start | bytes 2359300
  113.4 9.7 %collective-permute-start.7 = (bf16[512,384]{1,0:T(8,128)(2,1)}, bf16[512,384]{1,0:T(8,128)(2,1)}, u32[]{:S(2)}, u32[]{:S(2)}) collective-permute-start(bf16[512,384]{1,0:T(8,128)(2,1)} %fusion.22), channel_id=1, source_target_pairs={{0,64},{64,0},{1,65},{65,1},{2,66},{66,2},{3,67},{67,3},{4,68},{68... | collective-permute-start | bytes 1179656 | tf_op jit(solution)/shard_map/ppermute | solution.py:25
  115.3 34.2 %all-to-all-start.2 = ((bf16[32,16,1024]{2,1,0:T(8,128)(2,1)}), bf16[32,16,1024]{2,1,0:T(8,128)(2,1)S(1)}, u32[]{:S(2)}, u32[]{:S(2)}) async-start(bf16[32,16,1024]{2,1,0:T(8,128)(2,1)} %bitcast.14), calls=%async_computation.2 | async-start | bytes 2097152 | tf_op jit(solution)/shard_map/all_to_all | solution.py:215
  124.1 12.9 %collective-permute-start.8 = (bf16[512,384]{1,0:T(8,128)(2,1)S(1)}, bf16[512,384]{1,0:T(8,128)(2,1)S(1)}, u32[]{:S(2)}, u32[]{:S(2)}) collective-permute-start(bf16[512,384]{1,0:T(8,128)(2,1)S(1)} %fusion.3), channel_id=1, source_target_pairs={{0,128},{128,0},{1,129},{129,1},{2,130},{130,2},{3,131},{131,3},{4... | collective-permute-start | bytes 1179656 | tf_op jit(solution)/shard_map/ppermute | solution.py:25
  138.2 3.6 %collective-permute-start.9 = (bf16[512,384]{1,0:T(8,128)(2,1)S(1)}, bf16[512,384]{1,0:T(8,128)(2,1)S(1)}, u32[]{:S(2)}, u32[]{:S(2)}) collective-permute-start(bf16[512,384]{1,0:T(8,128)(2,1)S(1)} %multiply_convert_fusion), channel_id=1, source_target_pairs={{0,64},{64,0},{1,65},{65,1},{2,66},{66,2},{3,67},{67,3},{4,68},{68... | collective-permute-start | bytes 1179656 | tf_op jit(solution)/shard_map/ppermute | solution.py:25
  149.5 33.1 %all-to-all-start.4 = ((bf16[32,16,1024]{2,1,0:T(8,128)(2,1)}), bf16[32,16,1024]{2,1,0:T(8,128)(2,1)S(1)}, u32[]{:S(2)}, u32[]{:S(2)}) async-start(bf16[32,16,1024]{2,1,0:T(8,128)(2,1)} %bitcast.63), calls=%async_computation.4 | async-start | bytes 2097152 | tf_op jit(solution)/shard_map/all_to_all | solution.py:215

commit v11 on v10

--- a/solution.py
+++ b/solution.py
@@ -170,6 +170,35 @@
     )(came, codes)
 
 
+def gate_kernel(rows, own, other, send_out, part_out):
+    send_out[...] = dot(rows[...], other[...], ((1,), (1,))).astype(BF)
+    part_out[...] = dot(rows[...], own[...], ((1,), (1,)))
+
+
+def down_kernel(hidden, hidden_other, own, other, out):
+    total = dot(hidden[...], own[...], ((1,), (0,))) + dot(hidden_other[...], other[...], ((1,), (0,)))
+    out[...] = total.astype(BF)
+
+
+def on_rows(kernel, arrays, weights, widths, types):
+    count = arrays[0].shape[0]
+    block = count // 4
+    by_rows = lambda width: pl.BlockSpec((block, width), lambda i: (i, 0))
+    whole = lambda weight: pl.BlockSpec(weight.shape, lambda i: (0, 0))
+    moved = sum(a.size for a in (*arrays, *weights)) * 2 + 4 * count * sum(widths)
+    return pl.pallas_call(
+        kernel,
+        out_shape=[jax.ShapeDtypeStruct((count, width), held) for width, held in zip(widths, types)],
+        grid=(4,),
+        in_specs=[*(by_rows(a.shape[1]) for a in arrays), *(whole(w) for w in weights)],
+        out_specs=[by_rows(width) for width in widths],
+        compiler_params=pltpu.CompilerParams(vmem_limit_bytes=32 << 20),
+        cost_estimate=pl.CostEstimate(
+            flops=2 * count * sum(w.size for w in weights), bytes_accessed=moved, transcendentals=0
+        ),
+    )(*arrays, *weights)
+
+
 def local(tokens, w_gate, w_down, expert_ids, route_weight, replica_pick, old_plan, new_plan):
     batches, group, feats = tokens.shape
     peers = lax.axis_size("y") * lax.axis_size("x")
@@ -201,14 +230,14 @@
         if outs:
             rows, _ = lax.optimization_barrier((rows, outs[0]))
 
-        send = dot(rows, gate_other, ((1,), (1,)), BF)
-        part = lax.optimization_barrier(dot(rows, gate_own, ((1,), (1,))))
+        cut = gate_own.shape[0]
+        send, part = on_rows(gate_kernel, [rows], [gate_own, gate_other], [cut, cut], [BF, F32])
         part = part + swap(send, "k").astype(F32)
         gate = part + swap(part.astype(BF), "m").astype(F32)
         hidden = jax.nn.silu(gate).astype(BF)
         hidden_other = swap(hidden, "k")
-        out = dot(hidden, down_own, ((1,), (0,))) + dot(hidden_other, down_other, ((1,), (0,)))
-        outs.append(out.astype(BF).reshape(peers, -1, out.shape[1]))
+        (out,) = on_rows(down_kernel, [hidden, hidden_other], [down_own, down_other], [rows.shape[1]], [BF])
+        outs.append(out.reshape(peers, -1, out.shape[1]))
 
     outputs = []
     for out, (high, mid) in zip(outs, scales):

time: 198 us -> 196 us (0.990)
  the two profiles are of different devices: /device:TPU:16 before, /device:TPU:2 now
where the time goes in v11:
time: 196 us; the launch traced here: 194 us
  starting transfers between devices  71.6 us (37%)
  waiting for transfers between devices  71.2 us (36%)
  Pallas kernels  18.5 us (9%)
  blocking collectives  11.8 us (6%)
  other arithmetic  10.3 us (5%)
  local copies, waits for them, and re-layouts  6.72 us (3%)
  matrix products  3.78 us (2%)
    ppermute x10, waiting for transfers between devices, swap(): return lax.ppermute(array, axes, [(i, last - i) for i in range(last + 1)])  39.3 us
    all_to_all x2, waiting for transfers between devices, local(): lax.all_to_all(out, ('y', 'x'), 0, 0, tiled=True).reshape(-1, out.shape[2])  26.4 us
    ppermute x10, starting transfers between devices, swap(): return lax.ppermute(array, axes, [(i, last - i) for i in range(last + 1)])  23.1 us
    all_to_all x2, starting transfers between devices, local(): lax.all_to_all(rows, ('y', 'x'), 0, 0, tiled=True)  20 us
    all_to_all x2, starting transfers between devices, local(): lax.all_to_all(out, ('y', 'x'), 0, 0, tiled=True).reshape(-1, out.shape[2])  18.2 us
    pallas_call x4, Pallas kernels, on_rows(): pl.pallas_call(kernel, out_shape=[jax.ShapeDtypeStruct((count, width), he...  12.7 us
    all_to_all x1, blocking collectives, local(): terms = lax.all_to_all(mixed, ('p', 'zh'), 0, 0, tiled=True)  11.8 us
    all_to_all x1, starting transfers between devices, local(): came = lax.all_to_all(sent, ('p', 'zh'), 0, 0, tiled=True)  10.3 us
  transfers between devices with their start and end apart: 15, of which 11 were waited for; matrix products, arithmetic and copies ran while one was open for 6% of the time, Pallas kernels for 8%

profile of v11, /device:TPU:2, one launch (start us, length us, event | category | flops | bytes accessed | tf_op | source)
XLA Modules:
  0.0 194.3 jit_solution(10293999316504576676)
XLA Ops:
  3.6 10.3 %all-to-all-start = ((bf16[4,80,512]{2,1,0:T(8,128)(2,1)}), bf16[4,80,512]{2,1,0:T(8,128)(2,1)S(1)}, u32[]{:S(2)}, u32[]{:S(2)}) async-start(bf16[4,80,512]{2,1,0:T(8,128)(2,1)} %broadcast_in_dim.46), calls=%async_computation | async-start | bytes 655360 | tf_op jit(solution)/shard_map/all_to_all | solution.py:209
  17.9 1.6 shard_map.82
  21.1 5.3 %all-to-all-done.came = bf16[4,80,512]{2,1,0:T(8,128)(2,1)S(1)} async-done(((bf16[4,80,512]{2,1,0:T(8,128)(2,1)}), bf16[4,80,512]{2,1,0:T(8,128)(2,1)S(1)}, u32[]{:S(2)}, u32[]{:S(2)}) %all-to-all-start) | async-done | bytes 327712 | tf_op jit(solution)/shard_map/all_to_all | solution.py:209
  26.4 2.0 %shard_map.83 = (bf16[512,1024]{1,0:T(8,128)(2,1)}, bf16[512,64]{1,0:T(8,128)(2,1)S(1)}, bf16[512,64]{1,0:T(8,128)(2,1)S(1)}) custom-call(bf16[4,80,512]{2,1,0:T(8,128)(2,1)S(1)} %all-to-all-done.came, f32[64,2]{1,0:T(8,128)S(1)} %copy.47.codes), custom_call_target="tpu_custom_call" | custom-call | flops 67108864 | bytes 2097152 | tf_op jit(solution)/shard_map/pallas_call | solution.py:163
  29.0 10.3 %all-to-all-start.1 = ((bf16[32,16,1024]{2,1,0:T(8,128)(2,1)}), bf16[32,16,1024]{2,1,0:T(8,128)(2,1)S(1)}, u32[]{:S(2)}, u32[]{:S(2)}) async-start(bf16[32,16,1024]{2,1,0:T(8,128)(2,1)} %bitcast.6), calls=%async_computation.1 | async-start | bytes 2097152 | tf_op jit(solution)/shard_map/all_to_all | solution.py:229
  39.3 3.5 %collective-permute-start = (bf16[2,192,1024]{2,1,0:T(8,128)(2,1)S(1)}, bf16[2,192,1024]{2,1,0:T(8,128)(2,1)}, u32[]{:S(2)}, u32[]{:S(2)}) collective-permute-start(bf16[2,192,1024]{2,1,0:T(8,128)(2,1)S(1)} %get-tuple-element.34), channel_id=1, source_target_pairs={{0,128},{128,0},{1,129},{129,1},{2,130},{130,2},{3,131},{131,3},{4... | collective-permute-start | bytes 2359304 | tf_op jit(solution)/shard_map/ppermute | solution.py:25
  42.9 2.1 %shard_map.84 = (bf16[512,1024]{1,0:T(8,128)(2,1)}, bf16[512,64]{1,0:T(8,128)(2,1)S(1)}, bf16[512,64]{1,0:T(8,128)(2,1)S(1)}) custom-call(bf16[4,80,512]{2,1,0:T(8,128)(2,1)S(1)} %all-to-all-done.came, f32[64,2]{1,0:T(8,128)S(1)} %copy.48.codes), custom_call_target="tpu_custom_call" | custom-call | flops 67108864 | bytes 2097152 | tf_op jit(solution)/shard_map/pallas_call | solution.py:163
  45.1 14.1 %collective-permute-done = bf16[2,192,1024]{2,1,0:T(8,128)(2,1)} collective-permute-done((bf16[2,192,1024]{2,1,0:T(8,128)(2,1)S(1)}, bf16[2,192,1024]{2,1,0:T(8,128)(2,1)}, u32[]{:S(2)}, u32[]{:S(2)}) %collective-permute-start) | collective-permute-done | bytes 786464 | tf_op jit(solution)/shard_map/ppermute | solution.py:25
  59.2 2.1 %bitcast_select_fusion.1 = (bf16[192,1024]{1,0:T(8,128)(2,1)S(1)}, bf16[192,1024]{1,0:T(8,128)(2,1)S(1)}, bf16[192,1024]{1,0:T(8,128)(2,1)}, bf16[192,1024]{1,0:T(8,128)(2,1)}) fusion(bf16[192,1024]{1,0:T(8,128)(2,1)S(1)} %get-tuple-element.39, pred[]{:T(512)S(6)} %eq.18, bf16[2,192,1024]{2,1,0:T(8,128)(2,1)} %collective-permute-done, ...), kind=kLoop, calls=%fused_computation.17 | loop fusion | flops 786432 | bytes 3145729 | tf_op jit(solution)/shard_map/jit(_where)/select_n | solution.py:61
  62.3 1.9 collective-permute-start.1
  64.2 3.6 %collective-permute-start.5 = (bf16[2,192,1024]{2,1,0:T(8,128)(2,1)}, bf16[2,192,1024]{2,1,0:T(8,128)(2,1)}, u32[]{:S(2)}, u32[]{:S(2)}) collective-permute-start(bf16[2,192,1024]{2,1,0:T(8,128)(2,1)} %get-tuple-element.44), channel_id=1, source_target_pairs={{0,128},{128,0},{1,129},{129,1},{2,130},{130,2},{3,131},{131,3},{4... | collective-permute-start | bytes 2359304 | tf_op jit(solution)/shard_map/ppermute | solution.py:25
  67.9 9.8 %all-to-all-start.3 = ((bf16[32,16,1024]{2,1,0:T(8,128)(2,1)}), bf16[32,16,1024]{2,1,0:T(8,128)(2,1)S(1)}, u32[]{:S(2)}, u32[]{:S(2)}) async-start(bf16[32,16,1024]{2,1,0:T(8,128)(2,1)} %bitcast.16), calls=%async_computation.3 | async-start | bytes 2097152 | tf_op jit(solution)/shard_map/all_to_all | solution.py:229
  78.9 3.7 %shard_map.85 = (bf16[512,384]{1,0:T(8,128)(2,1)S(1)}, f32[512,384]{1,0:T(8,128)S(1)}) custom-call(bf16[512,1024]{1,0:T(8,128)(2,1)S(1)} %bitcast.48, bf16[384,1024]{1,0:T(8,128)(2,1)S(1)} %pad_maximum_fusion.own, bf16[384,1024]{1,0:T(8,128)(2,1)} %collective-permute-done.1.other), custom_call_target="tpu_custom_call" | custom-call | flops 805306368 | bytes 4194304 | tf_op jit(solution)/shard_map/pallas_call | solution.py:189
  82.5 1.9 collective-permute-start.2
  84.5 1.7 collective-permute-done.2
  86.2 2.2 %collective-permute-start.3 = (bf16[512,384]{1,0:T(8,128)(2,1)S(1)}, bf16[512,384]{1,0:T(8,128)(2,1)S(1)}, u32[]{:S(2)}, u32[]{:S(2)}) collective-permute-start(bf16[512,384]{1,0:T(8,128)(2,1)S(1)} %fusion.2), channel_id=1, source_target_pairs={{0,128},{128,0},{1,129},{129,1},{2,130},{130,2},{3,131},{131,3},{4... | collective-permute-start | bytes 1179656 | tf_op jit(solution)/shard_map/ppermute | solution.py:25
  89.7 1.9 collective-permute-start.6
  91.7 7.6 %collective-permute-done.3 = bf16[512,384]{1,0:T(8,128)(2,1)S(1)} collective-permute-done((bf16[512,384]{1,0:T(8,128)(2,1)S(1)}, bf16[512,384]{1,0:T(8,128)(2,1)S(1)}, u32[]{:S(2)}, u32[]{:S(2)}) %collective-permute-start.3) | collective-permute-done | bytes 393248 | tf_op jit(solution)/shard_map/ppermute | solution.py:25
  99.5 1.9 collective-permute-start.4
  103.2 2.7 %shard_map.86 = bf16[512,1024]{1,0:T(8,128)(2,1)} custom-call(bf16[512,384]{1,0:T(8,128)(2,1)S(1)} %multiply_convert_fusion.1.hidden, bf16[512,384]{1,0:T(8,128)(2,1)S(1)} %collective-permute-done.4.hidden_other, bf16[384,1024]{1,0:T(8,128)(2,1)S(1)} %pad_maximum_fusion.2.own, bf16[384,1024]{1,0:T(8,128)(2,1)S(1)} %collective-permute-done.6.other), custom_call_target="tpu_custom_call" | custom-call | flops 805306368 | bytes 4456448 | tf_op jit(solution)/shard_map/pallas_call | solution.py:189
  106.1 9.7 %all-to-all-start.2 = ((bf16[32,16,1024]{2,1,0:T(8,128)(2,1)}), bf16[32,16,1024]{2,1,0:T(8,128)(2,1)}, u32[]{:S(2)}, u32[]{:S(2)}) async-start(bf16[32,16,1024]{2,1,0:T(8,128)(2,1)} %bitcast.14), calls=%async_computation.2 | async-start | bytes 2097152 | tf_op jit(solution)/shard_map/all_to_all | solution.py:244
  115.8 3.6 %shard_map.87 = (bf16[512,384]{1,0:T(8,128)(2,1)S(1)}, f32[512,384]{1,0:T(8,128)S(1)}) custom-call(bf16[512,1024]{1,0:T(8,128)(2,1)S(1)} %bitcast.47, bf16[384,1024]{1,0:T(8,128)(2,1)S(1)} %pad_maximum_fusion.own, bf16[384,1024]{1,0:T(8,128)(2,1)} %collective-permute-done.1.other), custom_call_target="tpu_custom_call" | custom-call | flops 805306368 | bytes 4194304 | tf_op jit(solution)/shard_map/pallas_call | solution.py:189
  119.4 1.9 collective-permute-start.7
  121.3 1.7 collective-permute-done.7
  123.1 2.2 %collective-permute-start.8 = (bf16[512,384]{1,0:T(8,128)(2,1)S(1)}, bf16[512,384]{1,0:T(8,128)(2,1)S(1)}, u32[]{:S(2)}, u32[]{:S(2)}) collective-permute-start(bf16[512,384]{1,0:T(8,128)(2,1)S(1)} %fusion.3), channel_id=1, source_target_pairs={{0,128},{128,0},{1,129},{129,1},{2,130},{130,2},{3,131},{131,3},{4... | collective-permute-start | bytes 1179656 | tf_op jit(solution)/shard_map/ppermute | solution.py:25
  125.3 10.8 %collective-permute-done.8 = bf16[512,384]{1,0:T(8,128)(2,1)S(1)} collective-permute-done((bf16[512,384]{1,0:T(8,128)(2,1)S(1)}, bf16[512,384]{1,0:T(8,128)(2,1)S(1)}, u32[]{:S(2)}, u32[]{:S(2)}) %collective-permute-start.8) | collective-permute-done | bytes 393248 | tf_op jit(solution)/shard_map/ppermute | solution.py:25
  136.4 1.9 collective-permute-start.9
  138.3 1.7 collective-permute-done.9.hidden_other
  140.0 2.8 %shard_map.88 = bf16[512,1024]{1,0:T(8,128)(2,1)} custom-call(bf16[512,384]{1,0:T(8,128)(2,1)S(1)} %multiply_convert_fusion.hidden, bf16[512,384]{1,0:T(8,128)(2,1)S(1)} %collective-permute-done.9.hidden_other, bf16[384,1024]{1,0:T(8,128)(2,1)S(1)} %pad_maximum_fusion.2.own, bf16[384,1024]{1,0:T(8,128)(2,1)S(1)} %collective-permute-done.6.other), custom_call_target="tpu_custom_call" | custom-call | flops 805306368 | bytes 4456448 | tf_op jit(solution)/shard_map/pallas_call | solution.py:189
  144.2 8.5 %all-to-all-start.4 = ((bf16[32,16,1024]{2,1,0:T(8,128)(2,1)}), bf16[32,16,1024]{2,1,0:T(8,128)(2,1)S(1)}, u32[]{:S(2)}, u32[]{:S(2)}) async-start(bf16[32,16,1024]{2,1,0:T(8,128)(2,1)} %bitcast.18), calls=%async_computation.4 | async-start | bytes 2097152 | tf_op jit(solution)/shard_map/all_to_all | solution.py:244
  156.0 25.0 %all-to-all-done.4 = bf16[32,16,1024]{2,1,0:T(8,128)(2,1)S(1)} async-done(((bf16[32,16,1024]{2,1,0:T(8,128)(2,1)}), bf16[32,16,1024]{2,1,0:T(8,128)(2,1)S(1)}, u32[]{:S(2)}, u32[]{:S(2)}) %all-to-all-start.4) | async-done | bytes 1048608 | tf_op jit(solution)/shard_map/all_to_all | solution.py:244
  181.8 11.8 %all_to_all.30 = bf16[4,64,512]{2,1,0:T(8,128)(2,1)S(1)} all-to-all(bf16[4,64,512]{2,1,0:T(8,128)(2,1)S(1)} %bitcast.51), channel_id=1, replica_groups=mesh['p'=2,'m'=2,'k'=2,'zh'=2,'y'=8,'x'=4] {'p','zh'}, dimensions={0} | all-to-all | bytes 524288 | tf_op jit(solution)/shard_map/all_to_all | solution.py:248
  (69 shorter events, 22.0 us)
Async XLA Ops:
  3.6 22.7 %all-to-all-start = ((bf16[4,80,512]{2,1,0:T(8,128)(2,1)}), bf16[4,80,512]{2,1,0:T(8,128)(2,1)S(1)}, u32[]{:S(2)}, u32[]{:S(2)}) async-start(bf16[4,80,512]{2,1,0:T(8,128)(2,1)} %broadcast_in_dim.46), calls=%async_computation | async-start | bytes 655360 | tf_op jit(solution)/shard_map/all_to_all | solution.py:209
  15.1 1.4 copy-start
  16.5 1.4 copy-start.1
  19.6 0.7 copy-start.2
  20.3 0.8 copy-start.4
  28.4 0.7 copy-start.8
  29.0 38.8 %all-to-all-start.1 = ((bf16[32,16,1024]{2,1,0:T(8,128)(2,1)}), bf16[32,16,1024]{2,1,0:T(8,128)(2,1)S(1)}, u32[]{:S(2)}, u32[]{:S(2)}) async-start(bf16[32,16,1024]{2,1,0:T(8,128)(2,1)} %bitcast.6), calls=%async_computation.1 | async-start | bytes 2097152 | tf_op jit(solution)/shard_map/all_to_all | solution.py:229
  39.3 19.9 %collective-permute-start = (bf16[2,192,1024]{2,1,0:T(8,128)(2,1)S(1)}, bf16[2,192,1024]{2,1,0:T(8,128)(2,1)}, u32[]{:S(2)}, u32[]{:S(2)}) collective-permute-start(bf16[2,192,1024]{2,1,0:T(8,128)(2,1)S(1)} %get-tuple-element.34), channel_id=1, source_target_pairs={{0,128},{128,0},{1,129},{129,1},{2,130},{130,2},{3,131},{131,3},{4... | collective-permute-start | bytes 2359304 | tf_op jit(solution)/shard_map/ppermute | solution.py:25
  45.0 16.3 %copy-start.6 = (bf16[512,64]{1,0:T(8,128)(2,1)}, bf16[512,64]{1,0:T(8,128)(2,1)S(1)}, u32[]{:S(2)}) copy-start(bf16[512,64]{1,0:T(8,128)(2,1)S(1)} %get-tuple-element.47) | copy-start | bytes 196612
  45.1 16.3 %copy-start.10 = (bf16[512,64]{1,0:T(8,128)(2,1)}, bf16[512,64]{1,0:T(8,128)(2,1)S(1)}, u32[]{:S(2)}) copy-start(bf16[512,64]{1,0:T(8,128)(2,1)S(1)} %get-tuple-element.52) | copy-start | bytes 196612
  62.3 16.5 %collective-permute-start.1 = (bf16[384,1024]{1,0:T(8,128)(2,1)}, bf16[384,1024]{1,0:T(8,128)(2,1)}, u32[]{:S(2)}, u32[]{:S(2)}) collective-permute-start(bf16[384,1024]{1,0:T(8,128)(2,1)} %pad_maximum_fusion.1), channel_id=1, source_target_pairs={{0,64},{64,0},{1,65},{65,1},{2,66},{66,2},{3,67},{67,3},{4,68},{68... | collective-permute-start | bytes 2359304 | tf_op jit(solution)/shard_map/ppermute | solution.py:25
  64.2 24.2 %collective-permute-start.5 = (bf16[2,192,1024]{2,1,0:T(8,128)(2,1)}, bf16[2,192,1024]{2,1,0:T(8,128)(2,1)}, u32[]{:S(2)}, u32[]{:S(2)}) collective-permute-start(bf16[2,192,1024]{2,1,0:T(8,128)(2,1)} %get-tuple-element.44), channel_id=1, source_target_pairs={{0,128},{128,0},{1,129},{129,1},{2,130},{130,2},{3,131},{131,3},{4... | collective-permute-start | bytes 2359304 | tf_op jit(solution)/shard_map/ppermute | solution.py:25
  67.9 38.2 %all-to-all-start.3 = ((bf16[32,16,1024]{2,1,0:T(8,128)(2,1)}), bf16[32,16,1024]{2,1,0:T(8,128)(2,1)S(1)}, u32[]{:S(2)}, u32[]{:S(2)}) async-start(bf16[32,16,1024]{2,1,0:T(8,128)(2,1)} %bitcast.16), calls=%async_computation.3 | async-start | bytes 2097152 | tf_op jit(solution)/shard_map/all_to_all | solution.py:229
  78.8 9.6 %copy-start.3 = (bf16[192,1024]{1,0:T(8,128)(2,1)S(1)}, bf16[192,1024]{1,0:T(8,128)(2,1)}, u32[]{:S(2)}) copy-start(bf16[192,1024]{1,0:T(8,128)(2,1)} %copy-done.2) | copy-start | bytes 1179652
  78.9 9.6 %copy-start.5 = (bf16[192,1024]{1,0:T(8,128)(2,1)S(1)}, bf16[192,1024]{1,0:T(8,128)(2,1)}, u32[]{:S(2)}) copy-start(bf16[192,1024]{1,0:T(8,128)(2,1)} %copy-done.4) | copy-start | bytes 1179652
  82.5 3.6 %collective-permute-start.2 = (bf16[512,384]{1,0:T(8,128)(2,1)S(1)}, bf16[512,384]{1,0:T(8,128)(2,1)S(1)}, u32[]{:S(2)}, u32[]{:S(2)}) collective-permute-start(bf16[512,384]{1,0:T(8,128)(2,1)S(1)} %get-tuple-element.41), channel_id=1, source_target_pairs={{0,64},{64,0},{1,65},{65,1},{2,66},{66,2},{3,67},{67,3},{4,68},{68... | collective-permute-start | bytes 1179656 | tf_op jit(solution)/shard_map/ppermute | solution.py:25
  86.2 13.1 %collective-permute-start.3 = (bf16[512,384]{1,0:T(8,128)(2,1)S(1)}, bf16[512,384]{1,0:T(8,128)(2,1)S(1)}, u32[]{:S(2)}, u32[]{:S(2)}) collective-permute-start(bf16[512,384]{1,0:T(8,128)(2,1)S(1)} %fusion.2), channel_id=1, source_target_pairs={{0,128},{128,0},{1,129},{129,1},{2,130},{130,2},{3,131},{131,3},{4... | collective-permute-start | bytes 1179656 | tf_op jit(solution)/shard_map/ppermute | solution.py:25
  89.7 11.8 %collective-permute-start.6 = (bf16[384,1024]{1,0:T(8,128)(2,1)S(1)}, bf16[384,1024]{1,0:T(8,128)(2,1)S(1)}, u32[]{:S(2)}, u32[]{:S(2)}) collective-permute-start(bf16[384,1024]{1,0:T(8,128)(2,1)S(1)} %pad_maximum_fusion.3), channel_id=1, source_target_pairs={{0,64},{64,0},{1,65},{65,1},{2,66},{66,2},{3,67},{67,3},{4,68},{68... | collective-permute-start | bytes 2359304 | tf_op jit(solution)/shard_map/ppermute | solution.py:25
  99.5 3.6 %collective-permute-start.4 = (bf16[512,384]{1,0:T(8,128)(2,1)S(1)}, bf16[512,384]{1,0:T(8,128)(2,1)S(1)}, u32[]{:S(2)}, u32[]{:S(2)}) collective-permute-start(bf16[512,384]{1,0:T(8,128)(2,1)S(1)} %multiply_convert_fusion.1.hidden), channel_id=1, source_target_pairs={{0,64},{64,0},{1,65},{65,1},{2,66},{66,2},{3,67},{67,3},{4,68},{68... | collective-permute-start | bytes 1179656 | tf_op jit(solution)/shard_map/ppermute | solution.py:25
  106.1 38.0 %all-to-all-start.2 = ((bf16[32,16,1024]{2,1,0:T(8,128)(2,1)}), bf16[32,16,1024]{2,1,0:T(8,128)(2,1)}, u32[]{:S(2)}, u32[]{:S(2)}) async-start(bf16[32,16,1024]{2,1,0:T(8,128)(2,1)} %bitcast.14), calls=%async_computation.2 | async-start | bytes 2097152 | tf_op jit(solution)/shard_map/all_to_all | solution.py:244
  119.4 3.6 %collective-permute-start.7 = (bf16[512,384]{1,0:T(8,128)(2,1)S(1)}, bf16[512,384]{1,0:T(8,128)(2,1)S(1)}, u32[]{:S(2)}, u32[]{:S(2)}) collective-permute-start(bf16[512,384]{1,0:T(8,128)(2,1)S(1)} %get-tuple-element.51), channel_id=1, source_target_pairs={{0,64},{64,0},{1,65},{65,1},{2,66},{66,2},{3,67},{67,3},{4,68},{68... | collective-permute-start | bytes 1179656 | tf_op jit(solution)/shard_map/ppermute | solution.py:25
  123.1 13.1 %collective-permute-start.8 = (bf16[512,384]{1,0:T(8,128)(2,1)S(1)}, bf16[512,384]{1,0:T(8,128)(2,1)S(1)}, u32[]{:S(2)}, u32[]{:S(2)}) collective-permute-start(bf16[512,384]{1,0:T(8,128)(2,1)S(1)} %fusion.3), channel_id=1, source_target_pairs={{0,128},{128,0},{1,129},{129,1},{2,130},{130,2},{3,131},{131,3},{4... | collective-permute-start | bytes 1179656 | tf_op jit(solution)/shard_map/ppermute | solution.py:25
  136.4 3.6 %collective-permute-start.9 = (bf16[512,384]{1,0:T(8,128)(2,1)S(1)}, bf16[512,384]{1,0:T(8,128)(2,1)S(1)}, u32[]{:S(2)}, u32[]{:S(2)}) collective-permute-start(bf16[512,384]{1,0:T(8,128)(2,1)S(1)} %multiply_convert_fusion.hidden), channel_id=1, source_target_pairs={{0,64},{64,0},{1,65},{65,1},{2,66},{66,2},{3,67},{67,3},{4,68},{68... | collective-permute-start | bytes 1179656 | tf_op jit(solution)/shard_map/ppermute | solution.py:25
  142.7 10.0 %copy-start.9 = (bf16[512,64]{1,0:T(8,128)(2,1)S(1)}, bf16[512,64]{1,0:T(8,128)(2,1)}, u32[]{:S(2)}) copy-start(bf16[512,64]{1,0:T(8,128)(2,1)} %copy-done.8) | copy-start | bytes 196612
  144.2 36.9 %all-to-all-start.4 = ((bf16[32,16,1024]{2,1,0:T(8,128)(2,1)}), bf16[32,16,1024]{2,1,0:T(8,128)(2,1)S(1)}, u32[]{:S(2)}, u32[]{:S(2)}) async-start(bf16[32,16,1024]{2,1,0:T(8,128)(2,1)} %bitcast.18), calls=%async_computation.4 | async-start | bytes 2097152 | tf_op jit(solution)/shard_map/all_to_all | solution.py:244
  152.7 28.3 %copy-start.11 = (bf16[512,64]{1,0:T(8,128)(2,1)S(1)}, bf16[512,64]{1,0:T(8,128)(2,1)}, u32[]{:S(2)}) copy-start(bf16[512,64]{1,0:T(8,128)(2,1)} %copy-done.10) | copy-start | bytes 196612
  154.3 27.0 %copy-start.7 = (bf16[512,64]{1,0:T(8,128)(2,1)S(1)}, bf16[512,64]{1,0:T(8,128)(2,1)}, u32[]{:S(2)}) copy-start(bf16[512,64]{1,0:T(8,128)(2,1)} %copy-done.6) | copy-start | bytes 196612

commit v12 on v11

--- a/solution.py
+++ b/solution.py
@@ -170,6 +170,23 @@
     )(came, codes)
 
 
+def pack_kernel(tokens, info, out):
+    count = tokens.shape[0]
+    for i in range(out.shape[0]):
+        out[i, :count] = tokens[...]
+        out[i, count:] = info[...]
+
+
+def pack(tokens, info):
+    vmem = pl.BlockSpec(memory_space=pltpu.VMEM)
+    return pl.pallas_call(
+        pack_kernel,
+        out_shape=jax.ShapeDtypeStruct((4, tokens.shape[0] + info.shape[0], tokens.shape[1]), BF),
+        in_specs=[vmem, vmem],
+        out_specs=vmem,
+    )(tokens, info)
+
+
 def gate_kernel(rows, own, other, send_out, part_out):
     send_out[...] = dot(rows[...], other[...], ((1,), (1,))).astype(BF)
     part_out[...] = dot(rows[...], own[...], ((1,), (1,)))
@@ -182,15 +199,15 @@
 
 def on_rows(kernel, arrays, weights, widths, types):
     count = arrays[0].shape[0]
-    block = count // 4
+    block = count // 2
     by_rows = lambda width: pl.BlockSpec((block, width), lambda i: (i, 0))
-    whole = lambda weight: pl.BlockSpec(weight.shape, lambda i: (0, 0))
+    whole = pl.BlockSpec(memory_space=pltpu.VMEM)
     moved = sum(a.size for a in (*arrays, *weights)) * 2 + 4 * count * sum(widths)
     return pl.pallas_call(
         kernel,
         out_shape=[jax.ShapeDtypeStruct((count, width), held) for width, held in zip(widths, types)],
-        grid=(4,),
-        in_specs=[*(by_rows(a.shape[1]) for a in arrays), *(whole(w) for w in weights)],
+        grid=(2,),
+        in_specs=[*(by_rows(a.shape[1]) for a in arrays), *(whole for _ in weights)],
         out_specs=[by_rows(width) for width in widths],
         compiler_params=pltpu.CompilerParams(vmem_limit_bytes=32 << 20),
         cost_estimate=pl.CostEstimate(
@@ -204,8 +221,7 @@
     peers = lax.axis_size("y") * lax.axis_size("x")
     code = (2 * expert_ids + (replica_pick & 1)).astype(BF)
     info = jnp.stack([code, *halves(route_weight)]).reshape(3, feats)
-    sent = jnp.concatenate([tokens.reshape(-1, feats), jnp.pad(info, ((0, 13), (0, 0)))])
-    sent = jnp.broadcast_to(sent[None], (4, *sent.shape))
+    sent = pack(tokens.reshape(-1, feats), jnp.pad(info, ((0, 13), (0, 0))))
     came = lax.all_to_all(sent, ("p", "zh"), 0, 0, tiled=True)
     plans = [host_codes(old_plan), host_codes(new_plan)]
 

time: 196 us -> 193 us (0.985)
  starting transfers between devices: 71.6 us -> 68.5 us
  waiting for transfers between devices: 71.2 us -> 74.3 us
    all_to_all x2, starting transfers between devices: 18.2 us -> 15 us  [local(): lax.all_to_all(out, ('y', 'x'), 0, 0, tiled=True).reshape(-1, out.shape[2])]
    pallas_call x4, Pallas kernels: 12.7 us -> 9.69 us  [on_rows(): pl.pallas_call(kernel, out_shape=[jax.ShapeDtypeStruct((count, width), he...]
  transfers between devices with their start and end apart: 15 -> 15, of which waited for: 11 -> 11; matrix products, arithmetic and copies ran while one was open for 6% -> 6% of each run, Pallas kernels for 8% -> 7%
where the time goes in v12:
time: 193 us; the launch traced here: 192 us
  waiting for transfers between devices  74.3 us (38%)
  starting transfers between devices  68.5 us (35%)
  Pallas kernels  17.1 us (9%)
  blocking collectives  11.8 us (6%)
  other arithmetic  10.1 us (5%)
  local copies, waits for them, and re-layouts  5.96 us (3%)
  matrix products  3.79 us (2%)
    ppermute x10, waiting for transfers between devices, swap(): return lax.ppermute(array, axes, [(i, last - i) for i in range(last + 1)])  39.3 us
    all_to_all x2, waiting for transfers between devices, local(): lax.all_to_all(out, ('y', 'x'), 0, 0, tiled=True).reshape(-1, out.shape[2])  28 us
    ppermute x10, starting transfers between devices, swap(): return lax.ppermute(array, axes, [(i, last - i) for i in range(last + 1)])  23.1 us
    all_to_all x2, starting transfers between devices, local(): lax.all_to_all(rows, ('y', 'x'), 0, 0, tiled=True)  20 us
    all_to_all x2, starting transfers between devices, local(): lax.all_to_all(out, ('y', 'x'), 0, 0, tiled=True).reshape(-1, out.shape[2])  15 us
    all_to_all x1, blocking collectives, local(): terms = lax.all_to_all(mixed, ('p', 'zh'), 0, 0, tiled=True)  11.8 us
    all_to_all x1, starting transfers between devices, local(): came = lax.all_to_all(sent, ('p', 'zh'), 0, 0, tiled=True)  10.3 us
    pallas_call x4, Pallas kernels, on_rows(): pl.pallas_call(kernel, out_shape=[jax.ShapeDtypeStruct((count, width), he...  9.69 us
  transfers between devices with their start and end apart: 15, of which 11 were waited for; matrix products, arithmetic and copies ran while one was open for 6% of the time, Pallas kernels for 7%

profile of v12, /device:TPU:2, one launch (start us, length us, event | category | flops | bytes accessed | tf_op | source)
XLA Modules:
  0.0 191.8 jit_solution(14756733218742943762)
XLA Ops:
  4.2 10.3 %all-to-all-start = ((bf16[4,80,512]{2,1,0:T(8,128)(2,1)}), bf16[4,80,512]{2,1,0:T(8,128)(2,1)S(1)}, u32[]{:S(2)}, u32[]{:S(2)}) async-start(bf16[4,80,512]{2,1,0:T(8,128)(2,1)} %shard_map.82), calls=%async_computation | async-start | bytes 655360 | tf_op jit(solution)/shard_map/all_to_all | solution.py:225
  21.7 5.3 %all-to-all-done.came = bf16[4,80,512]{2,1,0:T(8,128)(2,1)S(1)} async-done(((bf16[4,80,512]{2,1,0:T(8,128)(2,1)}), bf16[4,80,512]{2,1,0:T(8,128)(2,1)S(1)}, u32[]{:S(2)}, u32[]{:S(2)}) %all-to-all-start) | async-done | bytes 327712 | tf_op jit(solution)/shard_map/all_to_all | solution.py:225
  26.9 2.0 %shard_map.84 = (bf16[512,1024]{1,0:T(8,128)(2,1)}, bf16[512,64]{1,0:T(8,128)(2,1)S(1)}, bf16[512,64]{1,0:T(8,128)(2,1)S(1)}) custom-call(bf16[4,80,512]{2,1,0:T(8,128)(2,1)S(1)} %all-to-all-done.came, f32[64,2]{1,0:T(8,128)S(1)} %copy.50.codes), custom_call_target="tpu_custom_call" | custom-call | flops 67108864 | bytes 2097152 | tf_op jit(solution)/shard_map/pallas_call | solution.py:163
  29.6 10.2 %all-to-all-start.1 = ((bf16[32,16,1024]{2,1,0:T(8,128)(2,1)}), bf16[32,16,1024]{2,1,0:T(8,128)(2,1)S(1)}, u32[]{:S(2)}, u32[]{:S(2)}) async-start(bf16[32,16,1024]{2,1,0:T(8,128)(2,1)} %bitcast.6), calls=%async_computation.1 | async-start | bytes 2097152 | tf_op jit(solution)/shard_map/all_to_all | solution.py:245
  39.9 3.5 %collective-permute-start = (bf16[2,192,1024]{2,1,0:T(8,128)(2,1)S(1)}, bf16[2,192,1024]{2,1,0:T(8,128)(2,1)}, u32[]{:S(2)}, u32[]{:S(2)}) collective-permute-start(bf16[2,192,1024]{2,1,0:T(8,128)(2,1)S(1)} %get-tuple-element.34), channel_id=1, source_target_pairs={{0,128},{128,0},{1,129},{129,1},{2,130},{130,2},{3,131},{131,3},{4... | collective-permute-start | bytes 2359304 | tf_op jit(solution)/shard_map/ppermute | solution.py:25
  43.5 2.1 %shard_map.85 = (bf16[512,1024]{1,0:T(8,128)(2,1)}, bf16[512,64]{1,0:T(8,128)(2,1)S(1)}, bf16[512,64]{1,0:T(8,128)(2,1)S(1)}) custom-call(bf16[4,80,512]{2,1,0:T(8,128)(2,1)S(1)} %all-to-all-done.came, f32[64,2]{1,0:T(8,128)S(1)} %copy.51.codes), custom_call_target="tpu_custom_call" | custom-call | flops 67108864 | bytes 2097152 | tf_op jit(solution)/shard_map/pallas_call | solution.py:163
  45.6 14.1 %collective-permute-done = bf16[2,192,1024]{2,1,0:T(8,128)(2,1)} collective-permute-done((bf16[2,192,1024]{2,1,0:T(8,128)(2,1)S(1)}, bf16[2,192,1024]{2,1,0:T(8,128)(2,1)}, u32[]{:S(2)}, u32[]{:S(2)}) %collective-permute-start) | collective-permute-done | bytes 786464 | tf_op jit(solution)/shard_map/ppermute | solution.py:25
  59.8 2.1 %bitcast_select_fusion.1 = (bf16[192,1024]{1,0:T(8,128)(2,1)S(1)}, bf16[192,1024]{1,0:T(8,128)(2,1)S(1)}, bf16[192,1024]{1,0:T(8,128)(2,1)}, bf16[192,1024]{1,0:T(8,128)(2,1)}) fusion(bf16[192,1024]{1,0:T(8,128)(2,1)S(1)} %get-tuple-element.39, pred[]{:T(512)S(6)} %eq.18, bf16[2,192,1024]{2,1,0:T(8,128)(2,1)} %collective-permute-done, ...), kind=kLoop, calls=%fused_computation.17 | loop fusion | flops 786432 | bytes 3145729 | tf_op jit(solution)/shard_map/jit(_where)/select_n | solution.py:61
  62.9 1.9 collective-permute-start.1
  64.8 3.6 %collective-permute-start.5 = (bf16[2,192,1024]{2,1,0:T(8,128)(2,1)}, bf16[2,192,1024]{2,1,0:T(8,128)(2,1)}, u32[]{:S(2)}, u32[]{:S(2)}) collective-permute-start(bf16[2,192,1024]{2,1,0:T(8,128)(2,1)} %get-tuple-element.44), channel_id=1, source_target_pairs={{0,128},{128,0},{1,129},{129,1},{2,130},{130,2},{3,131},{131,3},{4... | collective-permute-start | bytes 2359304 | tf_op jit(solution)/shard_map/ppermute | solution.py:25
  68.5 9.8 %all-to-all-start.3 = ((bf16[32,16,1024]{2,1,0:T(8,128)(2,1)}), bf16[32,16,1024]{2,1,0:T(8,128)(2,1)S(1)}, u32[]{:S(2)}, u32[]{:S(2)}) async-start(bf16[32,16,1024]{2,1,0:T(8,128)(2,1)} %bitcast.16), calls=%async_computation.3 | async-start | bytes 2097152 | tf_op jit(solution)/shard_map/all_to_all | solution.py:245
  79.5 2.7 %shard_map.86 = (bf16[512,384]{1,0:T(8,128)(2,1)S(1)}, f32[512,384]{1,0:T(8,128)S(1)}) custom-call(bf16[512,1024]{1,0:T(8,128)(2,1)S(1)} %bitcast.48, bf16[384,1024]{1,0:T(8,128)(2,1)S(1)} %pad_maximum_fusion.own, bf16[384,1024]{1,0:T(8,128)(2,1)} %collective-permute-done.1.other), custom_call_target="tpu_custom_call" | custom-call | flops 805306368 | bytes 4194304 | tf_op jit(solution)/shard_map/pallas_call | solution.py:206
  82.1 1.9 %collective-permute-start.2 = (bf16[512,384]{1,0:T(8,128)(2,1)S(1)}, bf16[512,384]{1,0:T(8,128)(2,1)S(1)}, u32[]{:S(2)}, u32[]{:S(2)}) collective-permute-start(bf16[512,384]{1,0:T(8,128)(2,1)S(1)} %get-tuple-element.41), channel_id=1, source_target_pairs={{0,64},{64,0},{1,65},{65,1},{2,66},{66,2},{3,67},{67,3},{4,68},{68... | collective-permute-start | bytes 1179656 | tf_op jit(solution)/shard_map/ppermute | solution.py:25
  84.1 1.7 collective-permute-done.2
  85.8 2.2 %collective-permute-start.3 = (bf16[512,384]{1,0:T(8,128)(2,1)S(1)}, bf16[512,384]{1,0:T(8,128)(2,1)S(1)}, u32[]{:S(2)}, u32[]{:S(2)}) collective-permute-start(bf16[512,384]{1,0:T(8,128)(2,1)S(1)} %fusion.2), channel_id=1, source_target_pairs={{0,128},{128,0},{1,129},{129,1},{2,130},{130,2},{3,131},{131,3},{4... | collective-permute-start | bytes 1179656 | tf_op jit(solution)/shard_map/ppermute | solution.py:25
  89.3 1.9 %collective-permute-start.6 = (bf16[384,1024]{1,0:T(8,128)(2,1)S(1)}, bf16[384,1024]{1,0:T(8,128)(2,1)S(1)}, u32[]{:S(2)}, u32[]{:S(2)}) collective-permute-start(bf16[384,1024]{1,0:T(8,128)(2,1)S(1)} %pad_maximum_fusion.3), channel_id=1, source_target_pairs={{0,64},{64,0},{1,65},{65,1},{2,66},{66,2},{3,67},{67,3},{4,68},{68... | collective-permute-start | bytes 2359304 | tf_op jit(solution)/shard_map/ppermute | solution.py:25
  91.3 7.6 %collective-permute-done.3 = bf16[512,384]{1,0:T(8,128)(2,1)S(1)} collective-permute-done((bf16[512,384]{1,0:T(8,128)(2,1)S(1)}, bf16[512,384]{1,0:T(8,128)(2,1)S(1)}, u32[]{:S(2)}, u32[]{:S(2)}) %collective-permute-start.3) | collective-permute-done | bytes 393248 | tf_op jit(solution)/shard_map/ppermute | solution.py:25
  99.1 1.9 %collective-permute-start.4 = (bf16[512,384]{1,0:T(8,128)(2,1)S(1)}, bf16[512,384]{1,0:T(8,128)(2,1)S(1)}, u32[]{:S(2)}, u32[]{:S(2)}) collective-permute-start(bf16[512,384]{1,0:T(8,128)(2,1)S(1)} %multiply_convert_fusion.1.hidden), channel_id=1, source_target_pairs={{0,64},{64,0},{1,65},{65,1},{2,66},{66,2},{3,67},{67,3},{4,68},{68... | collective-permute-start | bytes 1179656 | tf_op jit(solution)/shard_map/ppermute | solution.py:25
  102.8 2.2 %shard_map.87 = bf16[512,1024]{1,0:T(8,128)(2,1)} custom-call(bf16[512,384]{1,0:T(8,128)(2,1)S(1)} %multiply_convert_fusion.1.hidden, bf16[512,384]{1,0:T(8,128)(2,1)S(1)} %collective-permute-done.4.hidden_other, bf16[384,1024]{1,0:T(8,128)(2,1)S(1)} %pad_maximum_fusion.2.own, bf16[384,1024]{1,0:T(8,128)(2,1)S(1)} %collective-permute-done.6.other), custom_call_target="tpu_custom_call" | custom-call | flops 805306368 | bytes 4456448 | tf_op jit(solution)/shard_map/pallas_call | solution.py:206
  105.0 1.7 all-to-all-done.3
  106.7 8.1 %all-to-all-start.2 = ((bf16[32,16,1024]{2,1,0:T(8,128)(2,1)}), bf16[32,16,1024]{2,1,0:T(8,128)(2,1)}, u32[]{:S(2)}, u32[]{:S(2)}) async-start(bf16[32,16,1024]{2,1,0:T(8,128)(2,1)} %bitcast.14), calls=%async_computation.2 | async-start | bytes 2097152 | tf_op jit(solution)/shard_map/all_to_all | solution.py:260
  114.8 2.6 %shard_map.88 = (bf16[512,384]{1,0:T(8,128)(2,1)S(1)}, f32[512,384]{1,0:T(8,128)S(1)}) custom-call(bf16[512,1024]{1,0:T(8,128)(2,1)S(1)} %bitcast.47, bf16[384,1024]{1,0:T(8,128)(2,1)S(1)} %pad_maximum_fusion.own, bf16[384,1024]{1,0:T(8,128)(2,1)} %collective-permute-done.1.other), custom_call_target="tpu_custom_call" | custom-call | flops 805306368 | bytes 4194304 | tf_op jit(solution)/shard_map/pallas_call | solution.py:206
  117.4 1.9 %collective-permute-start.7 = (bf16[512,384]{1,0:T(8,128)(2,1)S(1)}, bf16[512,384]{1,0:T(8,128)(2,1)S(1)}, u32[]{:S(2)}, u32[]{:S(2)}) collective-permute-start(bf16[512,384]{1,0:T(8,128)(2,1)S(1)} %get-tuple-element.51), channel_id=1, source_target_pairs={{0,64},{64,0},{1,65},{65,1},{2,66},{66,2},{3,67},{67,3},{4,68},{68... | collective-permute-start | bytes 1179656 | tf_op jit(solution)/shard_map/ppermute | solution.py:25
  119.3 1.7 collective-permute-done.7
  121.1 2.2 %collective-permute-start.8 = (bf16[512,384]{1,0:T(8,128)(2,1)S(1)}, bf16[512,384]{1,0:T(8,128)(2,1)S(1)}, u32[]{:S(2)}, u32[]{:S(2)}) collective-permute-start(bf16[512,384]{1,0:T(8,128)(2,1)S(1)} %fusion.3), channel_id=1, source_target_pairs={{0,128},{128,0},{1,129},{129,1},{2,130},{130,2},{3,131},{131,3},{4... | collective-permute-start | bytes 1179656 | tf_op jit(solution)/shard_map/ppermute | solution.py:25
  123.3 10.8 %collective-permute-done.8 = bf16[512,384]{1,0:T(8,128)(2,1)S(1)} collective-permute-done((bf16[512,384]{1,0:T(8,128)(2,1)S(1)}, bf16[512,384]{1,0:T(8,128)(2,1)S(1)}, u32[]{:S(2)}, u32[]{:S(2)}) %collective-permute-start.8) | collective-permute-done | bytes 393248 | tf_op jit(solution)/shard_map/ppermute | solution.py:25
  134.4 1.9 %collective-permute-start.9 = (bf16[512,384]{1,0:T(8,128)(2,1)S(1)}, bf16[512,384]{1,0:T(8,128)(2,1)S(1)}, u32[]{:S(2)}, u32[]{:S(2)}) collective-permute-start(bf16[512,384]{1,0:T(8,128)(2,1)S(1)} %multiply_convert_fusion.hidden), channel_id=1, source_target_pairs={{0,64},{64,0},{1,65},{65,1},{2,66},{66,2},{3,67},{67,3},{4,68},{68... | collective-permute-start | bytes 1179656 | tf_op jit(solution)/shard_map/ppermute | solution.py:25
  138.0 2.2 %shard_map.89 = bf16[512,1024]{1,0:T(8,128)(2,1)} custom-call(bf16[512,384]{1,0:T(8,128)(2,1)S(1)} %multiply_convert_fusion.hidden, bf16[512,384]{1,0:T(8,128)(2,1)S(1)} %collective-permute-done.9.hidden_other, bf16[384,1024]{1,0:T(8,128)(2,1)S(1)} %pad_maximum_fusion.2.own, bf16[384,1024]{1,0:T(8,128)(2,1)S(1)} %collective-permute-done.6.other), custom_call_target="tpu_custom_call" | custom-call | flops 805306368 | bytes 4456448 | tf_op jit(solution)/shard_map/pallas_call | solution.py:206
  140.3 3.0 %all-to-all-done.2 = bf16[32,16,1024]{2,1,0:T(8,128)(2,1)} async-done(((bf16[32,16,1024]{2,1,0:T(8,128)(2,1)}), bf16[32,16,1024]{2,1,0:T(8,128)(2,1)}, u32[]{:S(2)}, u32[]{:S(2)}) %all-to-all-start.2) | async-done | bytes 1048608 | tf_op jit(solution)/shard_map/all_to_all | solution.py:260
  143.2 6.9 %all-to-all-start.4 = ((bf16[32,16,1024]{2,1,0:T(8,128)(2,1)}), bf16[32,16,1024]{2,1,0:T(8,128)(2,1)S(1)}, u32[]{:S(2)}, u32[]{:S(2)}) async-start(bf16[32,16,1024]{2,1,0:T(8,128)(2,1)} %bitcast.18), calls=%async_computation.4 | async-start | bytes 2097152 | tf_op jit(solution)/shard_map/all_to_all | solution.py:260
  153.5 25.0 %all-to-all-done.4 = bf16[32,16,1024]{2,1,0:T(8,128)(2,1)S(1)} async-done(((bf16[32,16,1024]{2,1,0:T(8,128)(2,1)}), bf16[32,16,1024]{2,1,0:T(8,128)(2,1)S(1)}, u32[]{:S(2)}, u32[]{:S(2)}) %all-to-all-start.4) | async-done | bytes 1048608 | tf_op jit(solution)/shard_map/all_to_all | solution.py:260
  179.4 11.8 %all_to_all.30 = bf16[4,64,512]{2,1,0:T(8,128)(2,1)S(1)} all-to-all(bf16[4,64,512]{2,1,0:T(8,128)(2,1)S(1)} %bitcast.51), channel_id=1, replica_groups=mesh['p'=2,'m'=2,'k'=2,'zh'=2,'y'=8,'x'=4] {'p','zh'}, dimensions={0} | all-to-all | bytes 524288 | tf_op jit(solution)/shard_map/all_to_all | solution.py:264
  (68 shorter events, 24.2 us)
Async XLA Ops:
  4.2 22.7 %all-to-all-start = ((bf16[4,80,512]{2,1,0:T(8,128)(2,1)}), bf16[4,80,512]{2,1,0:T(8,128)(2,1)S(1)}, u32[]{:S(2)}, u32[]{:S(2)}) async-start(bf16[4,80,512]{2,1,0:T(8,128)(2,1)} %shard_map.82), calls=%async_computation | async-start | bytes 655360 | tf_op jit(solution)/shard_map/all_to_all | solution.py:225
  15.7 1.4 copy-start
  17.1 1.4 copy-start.1
  20.2 0.7 copy-start.2
  20.9 0.8 copy-start.4
  29.0 0.7 copy-start.8
  29.6 38.8 %all-to-all-start.1 = ((bf16[32,16,1024]{2,1,0:T(8,128)(2,1)}), bf16[32,16,1024]{2,1,0:T(8,128)(2,1)S(1)}, u32[]{:S(2)}, u32[]{:S(2)}) async-start(bf16[32,16,1024]{2,1,0:T(8,128)(2,1)} %bitcast.6), calls=%async_computation.1 | async-start | bytes 2097152 | tf_op jit(solution)/shard_map/all_to_all | solution.py:245
  39.9 19.9 %collective-permute-start = (bf16[2,192,1024]{2,1,0:T(8,128)(2,1)S(1)}, bf16[2,192,1024]{2,1,0:T(8,128)(2,1)}, u32[]{:S(2)}, u32[]{:S(2)}) collective-permute-start(bf16[2,192,1024]{2,1,0:T(8,128)(2,1)S(1)} %get-tuple-element.34), channel_id=1, source_target_pairs={{0,128},{128,0},{1,129},{129,1},{2,130},{130,2},{3,131},{131,3},{4... | collective-permute-start | bytes 2359304 | tf_op jit(solution)/shard_map/ppermute | solution.py:25
  45.6 16.3 %copy-start.6 = (bf16[512,64]{1,0:T(8,128)(2,1)}, bf16[512,64]{1,0:T(8,128)(2,1)S(1)}, u32[]{:S(2)}) copy-start(bf16[512,64]{1,0:T(8,128)(2,1)S(1)} %get-tuple-element.47) | copy-start | bytes 196612
  45.6 16.3 %copy-start.10 = (bf16[512,64]{1,0:T(8,128)(2,1)}, bf16[512,64]{1,0:T(8,128)(2,1)S(1)}, u32[]{:S(2)}) copy-start(bf16[512,64]{1,0:T(8,128)(2,1)S(1)} %get-tuple-element.52) | copy-start | bytes 196612
  62.9 16.5 %collective-permute-start.1 = (bf16[384,1024]{1,0:T(8,128)(2,1)}, bf16[384,1024]{1,0:T(8,128)(2,1)}, u32[]{:S(2)}, u32[]{:S(2)}) collective-permute-start(bf16[384,1024]{1,0:T(8,128)(2,1)} %pad_maximum_fusion.1), channel_id=1, source_target_pairs={{0,64},{64,0},{1,65},{65,1},{2,66},{66,2},{3,67},{67,3},{4,68},{68... | collective-permute-start | bytes 2359304 | tf_op jit(solution)/shard_map/ppermute | solution.py:25
  64.8 23.2 %collective-permute-start.5 = (bf16[2,192,1024]{2,1,0:T(8,128)(2,1)}, bf16[2,192,1024]{2,1,0:T(8,128)(2,1)}, u32[]{:S(2)}, u32[]{:S(2)}) collective-permute-start(bf16[2,192,1024]{2,1,0:T(8,128)(2,1)} %get-tuple-element.44), channel_id=1, source_target_pairs={{0,128},{128,0},{1,129},{129,1},{2,130},{130,2},{3,131},{131,3},{4... | collective-permute-start | bytes 2359304 | tf_op jit(solution)/shard_map/ppermute | solution.py:25
  68.5 38.2 %all-to-all-start.3 = ((bf16[32,16,1024]{2,1,0:T(8,128)(2,1)}), bf16[32,16,1024]{2,1,0:T(8,128)(2,1)S(1)}, u32[]{:S(2)}, u32[]{:S(2)}) async-start(bf16[32,16,1024]{2,1,0:T(8,128)(2,1)} %bitcast.16), calls=%async_computation.3 | async-start | bytes 2097152 | tf_op jit(solution)/shard_map/all_to_all | solution.py:245
  79.4 8.6 %copy-start.3 = (bf16[192,1024]{1,0:T(8,128)(2,1)S(1)}, bf16[192,1024]{1,0:T(8,128)(2,1)}, u32[]{:S(2)}) copy-start(bf16[192,1024]{1,0:T(8,128)(2,1)} %copy-done.2) | copy-start | bytes 1179652
  79.4 8.6 %copy-start.5 = (bf16[192,1024]{1,0:T(8,128)(2,1)S(1)}, bf16[192,1024]{1,0:T(8,128)(2,1)}, u32[]{:S(2)}) copy-start(bf16[192,1024]{1,0:T(8,128)(2,1)} %copy-done.4) | copy-start | bytes 1179652
  82.1 3.6 %collective-permute-start.2 = (bf16[512,384]{1,0:T(8,128)(2,1)S(1)}, bf16[512,384]{1,0:T(8,128)(2,1)S(1)}, u32[]{:S(2)}, u32[]{:S(2)}) collective-permute-start(bf16[512,384]{1,0:T(8,128)(2,1)S(1)} %get-tuple-element.41), channel_id=1, source_target_pairs={{0,64},{64,0},{1,65},{65,1},{2,66},{66,2},{3,67},{67,3},{4,68},{68... | collective-permute-start | bytes 1179656 | tf_op jit(solution)/shard_map/ppermute | solution.py:25
  85.8 13.1 %collective-permute-start.3 = (bf16[512,384]{1,0:T(8,128)(2,1)S(1)}, bf16[512,384]{1,0:T(8,128)(2,1)S(1)}, u32[]{:S(2)}, u32[]{:S(2)}) collective-permute-start(bf16[512,384]{1,0:T(8,128)(2,1)S(1)} %fusion.2), channel_id=1, source_target_pairs={{0,128},{128,0},{1,129},{129,1},{2,130},{130,2},{3,131},{131,3},{4... | collective-permute-start | bytes 1179656 | tf_op jit(solution)/shard_map/ppermute | solution.py:25
  89.3 11.8 %collective-permute-start.6 = (bf16[384,1024]{1,0:T(8,128)(2,1)S(1)}, bf16[384,1024]{1,0:T(8,128)(2,1)S(1)}, u32[]{:S(2)}, u32[]{:S(2)}) collective-permute-start(bf16[384,1024]{1,0:T(8,128)(2,1)S(1)} %pad_maximum_fusion.3), channel_id=1, source_target_pairs={{0,64},{64,0},{1,65},{65,1},{2,66},{66,2},{3,67},{67,3},{4,68},{68... | collective-permute-start | bytes 2359304 | tf_op jit(solution)/shard_map/ppermute | solution.py:25
  99.1 3.6 %collective-permute-start.4 = (bf16[512,384]{1,0:T(8,128)(2,1)S(1)}, bf16[512,384]{1,0:T(8,128)(2,1)S(1)}, u32[]{:S(2)}, u32[]{:S(2)}) collective-permute-start(bf16[512,384]{1,0:T(8,128)(2,1)S(1)} %multiply_convert_fusion.1.hidden), channel_id=1, source_target_pairs={{0,64},{64,0},{1,65},{65,1},{2,66},{66,2},{3,67},{67,3},{4,68},{68... | collective-permute-start | bytes 1179656 | tf_op jit(solution)/shard_map/ppermute | solution.py:25
  106.7 36.5 %all-to-all-start.2 = ((bf16[32,16,1024]{2,1,0:T(8,128)(2,1)}), bf16[32,16,1024]{2,1,0:T(8,128)(2,1)}, u32[]{:S(2)}, u32[]{:S(2)}) async-start(bf16[32,16,1024]{2,1,0:T(8,128)(2,1)} %bitcast.14), calls=%async_computation.2 | async-start | bytes 2097152 | tf_op jit(solution)/shard_map/all_to_all | solution.py:260
  117.4 3.6 %collective-permute-start.7 = (bf16[512,384]{1,0:T(8,128)(2,1)S(1)}, bf16[512,384]{1,0:T(8,128)(2,1)S(1)}, u32[]{:S(2)}, u32[]{:S(2)}) collective-permute-start(bf16[512,384]{1,0:T(8,128)(2,1)S(1)} %get-tuple-element.51), channel_id=1, source_target_pairs={{0,64},{64,0},{1,65},{65,1},{2,66},{66,2},{3,67},{67,3},{4,68},{68... | collective-permute-start | bytes 1179656 | tf_op jit(solution)/shard_map/ppermute | solution.py:25
  121.1 13.1 %collective-permute-start.8 = (bf16[512,384]{1,0:T(8,128)(2,1)S(1)}, bf16[512,384]{1,0:T(8,128)(2,1)S(1)}, u32[]{:S(2)}, u32[]{:S(2)}) collective-permute-start(bf16[512,384]{1,0:T(8,128)(2,1)S(1)} %fusion.3), channel_id=1, source_target_pairs={{0,128},{128,0},{1,129},{129,1},{2,130},{130,2},{3,131},{131,3},{4... | collective-permute-start | bytes 1179656 | tf_op jit(solution)/shard_map/ppermute | solution.py:25
  134.4 3.6 %collective-permute-start.9 = (bf16[512,384]{1,0:T(8,128)(2,1)S(1)}, bf16[512,384]{1,0:T(8,128)(2,1)S(1)}, u32[]{:S(2)}, u32[]{:S(2)}) collective-permute-start(bf16[512,384]{1,0:T(8,128)(2,1)S(1)} %multiply_convert_fusion.hidden), channel_id=1, source_target_pairs={{0,64},{64,0},{1,65},{65,1},{2,66},{66,2},{3,67},{67,3},{4,68},{68... | collective-permute-start | bytes 1179656 | tf_op jit(solution)/shard_map/ppermute | solution.py:25
  140.3 9.9 %copy-start.9 = (bf16[512,64]{1,0:T(8,128)(2,1)S(1)}, bf16[512,64]{1,0:T(8,128)(2,1)}, u32[]{:S(2)}) copy-start(bf16[512,64]{1,0:T(8,128)(2,1)} %copy-done.8) | copy-start | bytes 196612
  143.2 35.3 %all-to-all-start.4 = ((bf16[32,16,1024]{2,1,0:T(8,128)(2,1)}), bf16[32,16,1024]{2,1,0:T(8,128)(2,1)S(1)}, u32[]{:S(2)}, u32[]{:S(2)}) async-start(bf16[32,16,1024]{2,1,0:T(8,128)(2,1)} %bitcast.18), calls=%async_computation.4 | async-start | bytes 2097152 | tf_op jit(solution)/shard_map/all_to_all | solution.py:260
  150.2 28.3 %copy-start.11 = (bf16[512,64]{1,0:T(8,128)(2,1)S(1)}, bf16[512,64]{1,0:T(8,128)(2,1)}, u32[]{:S(2)}) copy-start(bf16[512,64]{1,0:T(8,128)(2,1)} %copy-done.10) | copy-start | bytes 196612
  151.8 27.1 %copy-start.7 = (bf16[512,64]{1,0:T(8,128)(2,1)S(1)}, bf16[512,64]{1,0:T(8,128)(2,1)}, u32[]{:S(2)}) copy-start(bf16[512,64]{1,0:T(8,128)(2,1)} %copy-done.6) | copy-start | bytes 196612

commit v13 on v11

--- a/solution.py
+++ b/solution.py
@@ -170,6 +170,30 @@
     )(came, codes)
 
 
+def order_kernel(place, near, far, out):
+    m, hidden = place[0], near.shape[0]
+    out[pl.ds(pl.multiple_of(m * hidden, 64), hidden)] = near[...]
+    out[pl.ds(pl.multiple_of((1 - m) * hidden, 64), hidden)] = far[0]
+
+
+def ordered(near, far, which):
+    hidden, wide = near.shape
+    place = lax.axis_index("m").astype(jnp.int32).reshape(1)
+    return pl.pallas_call(
+        order_kernel,
+        out_shape=jax.ShapeDtypeStruct((2 * hidden, wide), BF),
+        grid=(1,),
+        in_specs=[
+            pl.BlockSpec(memory_space=pltpu.SMEM),
+            pl.BlockSpec((hidden, wide), lambda i: (0, 0)),
+            pl.BlockSpec((1, hidden, wide), lambda i: (which, 0, 0)),
+        ],
+        out_specs=pl.BlockSpec((2 * hidden, wide), lambda i: (0, 0)),
+        compiler_params=pltpu.CompilerParams(vmem_limit_bytes=32 << 20),
+        cost_estimate=pl.CostEstimate(flops=0, bytes_accessed=8 * near.size, transcendentals=0),
+    )(place, near, far)
+
+
 def gate_kernel(rows, own, other, send_out, part_out):
     send_out[...] = dot(rows[...], other[...], ((1,), (1,))).astype(BF)
     part_out[...] = dot(rows[...], own[...], ((1,), (1,)))
@@ -182,15 +206,15 @@
 
 def on_rows(kernel, arrays, weights, widths, types):
     count = arrays[0].shape[0]
-    block = count // 4
+    block = count // 2
     by_rows = lambda width: pl.BlockSpec((block, width), lambda i: (i, 0))
-    whole = lambda weight: pl.BlockSpec(weight.shape, lambda i: (0, 0))
+    whole = pl.BlockSpec(memory_space=pltpu.VMEM)
     moved = sum(a.size for a in (*arrays, *weights)) * 2 + 4 * count * sum(widths)
     return pl.pallas_call(
         kernel,
         out_shape=[jax.ShapeDtypeStruct((count, width), held) for width, held in zip(widths, types)],
-        grid=(4,),
-        in_specs=[*(by_rows(a.shape[1]) for a in arrays), *(whole(w) for w in weights)],
+        grid=(2,),
+        in_specs=[*(by_rows(a.shape[1]) for a in arrays), *(whole for _ in weights)],
         out_specs=[by_rows(width) for width in widths],
         compiler_params=pltpu.CompilerParams(vmem_limit_bytes=32 << 20),
         cost_estimate=pl.CostEstimate(
@@ -215,7 +239,7 @@
     routed = [route(came, plans[index], index, group) for index in range(batches)]
     gate_far, routed[1] = lax.optimization_barrier((gate_far, routed[1]))
     gate_own = order(gate_parts[0], gate_far[0])
-    gate_other = swap(order(gate_parts[1], gate_far[1]), "k")
+    gate_other = swap(ordered(gate_parts[1], gate_far, 1), "k")
     _, down_sent = lax.optimization_barrier((gate_far, down_parts[2]))
     down_far = swap(down_sent, "m")
     down_own = order(down_parts[0], down_far[0])

time: 196 us -> 193 us (0.985)
  local copies, waits for them, and re-layouts: 6.72 us -> 10.1 us
  starting transfers between devices: 71.6 us -> 68.5 us
  Pallas kernels: 18.5 us -> 15.7 us
  other arithmetic: 10.3 us -> 7.97 us
    unnamed x24 -> x32, local copies, waits for them, and re-layouts: 5 us -> 8.42 us
    all_to_all x2, starting transfers between devices: 18.2 us -> 15 us  [local(): lax.all_to_all(out, ('y', 'x'), 0, 0, tiled=True).reshape(-1, out.shape[2])]
    pallas_call x4, Pallas kernels: 12.7 us -> 9.68 us  [on_rows(): pl.pallas_call(kernel, out_shape=[jax.ShapeDtypeStruct((count, width), he...]
  transfers between devices with their start and end apart: 15 -> 15, of which waited for: 11 -> 11; matrix products, arithmetic and copies ran while one was open for 6% -> 4% of each run, Pallas kernels for 8% -> 7%
where the time goes in v13:
time: 193 us; the launch traced here: 192 us
  waiting for transfers between devices  72.8 us (38%)
  starting transfers between devices  68.5 us (35%)
  Pallas kernels  15.7 us (8%)
  blocking collectives  12.3 us (6%)
  local copies, waits for them, and re-layouts  10.1 us (5%)
  other arithmetic  7.97 us (4%)
  matrix products  3.79 us (2%)
    ppermute x10, waiting for transfers between devices, swap(): return lax.ppermute(array, axes, [(i, last - i) for i in range(last + 1)])  38.8 us
    all_to_all x2, waiting for transfers between devices, local(): lax.all_to_all(out, ('y', 'x'), 0, 0, tiled=True).reshape(-1, out.shape[2])  28 us
    ppermute x10, starting transfers between devices, swap(): return lax.ppermute(array, axes, [(i, last - i) for i in range(last + 1)])  23.1 us
    all_to_all x2, starting transfers between devices, local(): lax.all_to_all(rows, ('y', 'x'), 0, 0, tiled=True)  20.2 us
    all_to_all x2, starting transfers between devices, local(): lax.all_to_all(out, ('y', 'x'), 0, 0, tiled=True).reshape(-1, out.shape[2])  15 us
    all_to_all x1, blocking collectives, local(): terms = lax.all_to_all(mixed, ('p', 'zh'), 0, 0, tiled=True)  12.3 us
    all_to_all x1, starting transfers between devices, local(): came = lax.all_to_all(sent, ('p', 'zh'), 0, 0, tiled=True)  10.3 us
    pallas_call x4, Pallas kernels, on_rows(): pl.pallas_call(kernel, out_shape=[jax.ShapeDtypeStruct((count, width), he...  9.68 us
  transfers between devices with their start and end apart: 15, of which 11 were waited for; matrix products, arithmetic and copies ran while one was open for 4% of the time, Pallas kernels for 7%

profile of v13, /device:TPU:2, one launch (start us, length us, event | category | flops | bytes accessed | tf_op | source)
XLA Modules:
  0.0 191.5 jit_solution(3761208707842612696)
XLA Ops:
  3.6 10.3 %all-to-all-start = ((bf16[4,80,512]{2,1,0:T(8,128)(2,1)}), bf16[4,80,512]{2,1,0:T(8,128)(2,1)S(1)}, u32[]{:S(2)}, u32[]{:S(2)}) async-start(bf16[4,80,512]{2,1,0:T(8,128)(2,1)} %broadcast_in_dim.46), calls=%async_computation | async-start | bytes 655360 | tf_op jit(solution)/shard_map/all_to_all | solution.py:233
  22.2 4.2 %all-to-all-done.came = bf16[4,80,512]{2,1,0:T(8,128)(2,1)S(1)} async-done(((bf16[4,80,512]{2,1,0:T(8,128)(2,1)}), bf16[4,80,512]{2,1,0:T(8,128)(2,1)S(1)}, u32[]{:S(2)}, u32[]{:S(2)}) %all-to-all-start) | async-done | bytes 327712 | tf_op jit(solution)/shard_map/all_to_all | solution.py:233
  26.3 2.1 %shard_map.83 = (bf16[512,1024]{1,0:T(8,128)(2,1)}, bf16[512,64]{1,0:T(8,128)(2,1)S(1)}, bf16[512,64]{1,0:T(8,128)(2,1)S(1)}) custom-call(bf16[4,80,512]{2,1,0:T(8,128)(2,1)S(1)} %all-to-all-done.came, f32[64,2]{1,0:T(8,128)S(1)} %copy.47.codes), custom_call_target="tpu_custom_call" | custom-call | flops 67108864 | bytes 2097152 | tf_op jit(solution)/shard_map/pallas_call | solution.py:163
  29.1 10.3 %all-to-all-start.1 = ((bf16[32,16,1024]{2,1,0:T(8,128)(2,1)}), bf16[32,16,1024]{2,1,0:T(8,128)(2,1)S(1)}, u32[]{:S(2)}, u32[]{:S(2)}) async-start(bf16[32,16,1024]{2,1,0:T(8,128)(2,1)} %bitcast.6), calls=%async_computation.1 | async-start | bytes 2097152 | tf_op jit(solution)/shard_map/all_to_all | solution.py:253
  39.3 3.5 %collective-permute-start = (bf16[2,192,1024]{2,1,0:T(8,128)(2,1)}, bf16[2,192,1024]{2,1,0:T(8,128)(2,1)S(1)}, u32[]{:S(2)}, u32[]{:S(2)}) collective-permute-start(bf16[2,192,1024]{2,1,0:T(8,128)(2,1)} %copy-done.15), channel_id=1, source_target_pairs={{0,128},{128,0},{1,129},{129,1},{2,130},{130,2},{3,131},{131,3},{4... | collective-permute-start | bytes 2359304 | tf_op jit(solution)/shard_map/ppermute | solution.py:25
  43.0 2.1 %shard_map.84 = (bf16[512,1024]{1,0:T(8,128)(2,1)}, bf16[512,64]{1,0:T(8,128)(2,1)S(1)}, bf16[512,64]{1,0:T(8,128)(2,1)S(1)}) custom-call(bf16[4,80,512]{2,1,0:T(8,128)(2,1)S(1)} %all-to-all-done.came, f32[64,2]{1,0:T(8,128)S(1)} %copy.48.codes), custom_call_target="tpu_custom_call" | custom-call | flops 67108864 | bytes 2097152 | tf_op jit(solution)/shard_map/pallas_call | solution.py:163
  45.7 13.6 %collective-permute-done.far = bf16[2,192,1024]{2,1,0:T(8,128)(2,1)S(1)} collective-permute-done((bf16[2,192,1024]{2,1,0:T(8,128)(2,1)}, bf16[2,192,1024]{2,1,0:T(8,128)(2,1)S(1)}, u32[]{:S(2)}, u32[]{:S(2)}) %collective-permute-start) | collective-permute-done | bytes 786464 | tf_op jit(solution)/shard_map/ppermute | solution.py:25
  60.3 1.9 collective-permute-start.1
  62.2 3.6 %collective-permute-start.5 = (bf16[2,192,1024]{2,1,0:T(8,128)(2,1)}, bf16[2,192,1024]{2,1,0:T(8,128)(2,1)}, u32[]{:S(2)}, u32[]{:S(2)}) collective-permute-start(bf16[2,192,1024]{2,1,0:T(8,128)(2,1)} %copy-done.14), channel_id=1, source_target_pairs={{0,128},{128,0},{1,129},{129,1},{2,130},{130,2},{3,131},{131,3},{4... | collective-permute-start | bytes 2359304 | tf_op jit(solution)/shard_map/ppermute | solution.py:25
  67.6 9.9 %all-to-all-start.3 = ((bf16[32,16,1024]{2,1,0:T(8,128)(2,1)}), bf16[32,16,1024]{2,1,0:T(8,128)(2,1)S(1)}, u32[]{:S(2)}, u32[]{:S(2)}) async-start(bf16[32,16,1024]{2,1,0:T(8,128)(2,1)} %bitcast.15), calls=%async_computation.3 | async-start | bytes 2097152 | tf_op jit(solution)/shard_map/all_to_all | solution.py:253
  78.7 2.7 %shard_map.86 = (bf16[512,384]{1,0:T(8,128)(2,1)S(1)}, f32[512,384]{1,0:T(8,128)S(1)}) custom-call(bf16[512,1024]{1,0:T(8,128)(2,1)S(1)} %bitcast.45, bf16[384,1024]{1,0:T(8,128)(2,1)S(1)} %pad_maximum_fusion.own, bf16[384,1024]{1,0:T(8,128)(2,1)} %collective-permute-done.1.other), custom_call_target="tpu_custom_call" | custom-call | flops 805306368 | bytes 4194304 | tf_op jit(solution)/shard_map/pallas_call | solution.py:213
  81.3 1.9 %collective-permute-start.2 = (bf16[512,384]{1,0:T(8,128)(2,1)S(1)}, bf16[512,384]{1,0:T(8,128)(2,1)S(1)}, u32[]{:S(2)}, u32[]{:S(2)}) collective-permute-start(bf16[512,384]{1,0:T(8,128)(2,1)S(1)} %get-tuple-element.41), channel_id=1, source_target_pairs={{0,64},{64,0},{1,65},{65,1},{2,66},{66,2},{3,67},{67,3},{4,68},{68... | collective-permute-start | bytes 1179656 | tf_op jit(solution)/shard_map/ppermute | solution.py:25
  83.3 1.7 collective-permute-done.2
  85.1 2.2 %collective-permute-start.3 = (bf16[512,384]{1,0:T(8,128)(2,1)S(1)}, bf16[512,384]{1,0:T(8,128)(2,1)S(1)}, u32[]{:S(2)}, u32[]{:S(2)}) collective-permute-start(bf16[512,384]{1,0:T(8,128)(2,1)S(1)} %fusion.2), channel_id=1, source_target_pairs={{0,128},{128,0},{1,129},{129,1},{2,130},{130,2},{3,131},{131,3},{4... | collective-permute-start | bytes 1179656 | tf_op jit(solution)/shard_map/ppermute | solution.py:25
  88.6 1.9 %collective-permute-start.6 = (bf16[384,1024]{1,0:T(8,128)(2,1)S(1)}, bf16[384,1024]{1,0:T(8,128)(2,1)S(1)}, u32[]{:S(2)}, u32[]{:S(2)}) collective-permute-start(bf16[384,1024]{1,0:T(8,128)(2,1)S(1)} %pad_maximum_fusion.2), channel_id=1, source_target_pairs={{0,64},{64,0},{1,65},{65,1},{2,66},{66,2},{3,67},{67,3},{4,68},{68... | collective-permute-start | bytes 2359304 | tf_op jit(solution)/shard_map/ppermute | solution.py:25
  90.5 7.6 %collective-permute-done.3 = bf16[512,384]{1,0:T(8,128)(2,1)S(1)} collective-permute-done((bf16[512,384]{1,0:T(8,128)(2,1)S(1)}, bf16[512,384]{1,0:T(8,128)(2,1)S(1)}, u32[]{:S(2)}, u32[]{:S(2)}) %collective-permute-start.3) | collective-permute-done | bytes 393248 | tf_op jit(solution)/shard_map/ppermute | solution.py:25
  98.4 1.9 %collective-permute-start.4 = (bf16[512,384]{1,0:T(8,128)(2,1)S(1)}, bf16[512,384]{1,0:T(8,128)(2,1)S(1)}, u32[]{:S(2)}, u32[]{:S(2)}) collective-permute-start(bf16[512,384]{1,0:T(8,128)(2,1)S(1)} %multiply_convert_fusion.1.hidden), channel_id=1, source_target_pairs={{0,64},{64,0},{1,65},{65,1},{2,66},{66,2},{3,67},{67,3},{4,68},{68... | collective-permute-start | bytes 1179656 | tf_op jit(solution)/shard_map/ppermute | solution.py:25
  102.0 2.2 %shard_map.87 = bf16[512,1024]{1,0:T(8,128)(2,1)} custom-call(bf16[512,384]{1,0:T(8,128)(2,1)S(1)} %multiply_convert_fusion.1.hidden, bf16[512,384]{1,0:T(8,128)(2,1)S(1)} %collective-permute-done.4.hidden_other, bf16[384,1024]{1,0:T(8,128)(2,1)S(1)} %pad_maximum_fusion.1.own, bf16[384,1024]{1,0:T(8,128)(2,1)S(1)} %collective-permute-done.6.other), custom_call_target="tpu_custom_call" | custom-call | flops 805306368 | bytes 4456448 | tf_op jit(solution)/shard_map/pallas_call | solution.py:213
  104.2 1.8 all-to-all-done.3
  106.0 8.0 %all-to-all-start.2 = ((bf16[32,16,1024]{2,1,0:T(8,128)(2,1)}), bf16[32,16,1024]{2,1,0:T(8,128)(2,1)}, u32[]{:S(2)}, u32[]{:S(2)}) async-start(bf16[32,16,1024]{2,1,0:T(8,128)(2,1)} %bitcast.13), calls=%async_computation.2 | async-start | bytes 2097152 | tf_op jit(solution)/shard_map/all_to_all | solution.py:268
  114.1 2.6 %shard_map.88 = (bf16[512,384]{1,0:T(8,128)(2,1)S(1)}, f32[512,384]{1,0:T(8,128)S(1)}) custom-call(bf16[512,1024]{1,0:T(8,128)(2,1)S(1)} %bitcast.44, bf16[384,1024]{1,0:T(8,128)(2,1)S(1)} %pad_maximum_fusion.own, bf16[384,1024]{1,0:T(8,128)(2,1)} %collective-permute-done.1.other), custom_call_target="tpu_custom_call" | custom-call | flops 805306368 | bytes 4194304 | tf_op jit(solution)/shard_map/pallas_call | solution.py:213
  116.7 1.9 %collective-permute-start.7 = (bf16[512,384]{1,0:T(8,128)(2,1)S(1)}, bf16[512,384]{1,0:T(8,128)(2,1)S(1)}, u32[]{:S(2)}, u32[]{:S(2)}) collective-permute-start(bf16[512,384]{1,0:T(8,128)(2,1)S(1)} %get-tuple-element.51), channel_id=1, source_target_pairs={{0,64},{64,0},{1,65},{65,1},{2,66},{66,2},{3,67},{67,3},{4,68},{68... | collective-permute-start | bytes 1179656 | tf_op jit(solution)/shard_map/ppermute | solution.py:25
  118.6 1.7 collective-permute-done.7
  120.3 2.2 %collective-permute-start.8 = (bf16[512,384]{1,0:T(8,128)(2,1)S(1)}, bf16[512,384]{1,0:T(8,128)(2,1)S(1)}, u32[]{:S(2)}, u32[]{:S(2)}) collective-permute-start(bf16[512,384]{1,0:T(8,128)(2,1)S(1)} %fusion.3), channel_id=1, source_target_pairs={{0,128},{128,0},{1,129},{129,1},{2,130},{130,2},{3,131},{131,3},{4... | collective-permute-start | bytes 1179656 | tf_op jit(solution)/shard_map/ppermute | solution.py:25
  122.6 10.8 %collective-permute-done.8 = bf16[512,384]{1,0:T(8,128)(2,1)S(1)} collective-permute-done((bf16[512,384]{1,0:T(8,128)(2,1)S(1)}, bf16[512,384]{1,0:T(8,128)(2,1)S(1)}, u32[]{:S(2)}, u32[]{:S(2)}) %collective-permute-start.8) | collective-permute-done | bytes 393248 | tf_op jit(solution)/shard_map/ppermute | solution.py:25
  133.7 1.9 %collective-permute-start.9 = (bf16[512,384]{1,0:T(8,128)(2,1)S(1)}, bf16[512,384]{1,0:T(8,128)(2,1)S(1)}, u32[]{:S(2)}, u32[]{:S(2)}) collective-permute-start(bf16[512,384]{1,0:T(8,128)(2,1)S(1)} %multiply_convert_fusion.hidden), channel_id=1, source_target_pairs={{0,64},{64,0},{1,65},{65,1},{2,66},{66,2},{3,67},{67,3},{4,68},{68... | collective-permute-start | bytes 1179656 | tf_op jit(solution)/shard_map/ppermute | solution.py:25
  135.6 1.7 collective-permute-done.9.hidden_other
  137.3 2.2 %shard_map.89 = bf16[512,1024]{1,0:T(8,128)(2,1)} custom-call(bf16[512,384]{1,0:T(8,128)(2,1)S(1)} %multiply_convert_fusion.hidden, bf16[512,384]{1,0:T(8,128)(2,1)S(1)} %collective-permute-done.9.hidden_other, bf16[384,1024]{1,0:T(8,128)(2,1)S(1)} %pad_maximum_fusion.1.own, bf16[384,1024]{1,0:T(8,128)(2,1)S(1)} %collective-permute-done.6.other), custom_call_target="tpu_custom_call" | custom-call | flops 805306368 | bytes 4456448 | tf_op jit(solution)/shard_map/pallas_call | solution.py:213
  139.5 3.0 %all-to-all-done.2 = bf16[32,16,1024]{2,1,0:T(8,128)(2,1)} async-done(((bf16[32,16,1024]{2,1,0:T(8,128)(2,1)}), bf16[32,16,1024]{2,1,0:T(8,128)(2,1)}, u32[]{:S(2)}, u32[]{:S(2)}) %all-to-all-start.2) | async-done | bytes 1048608 | tf_op jit(solution)/shard_map/all_to_all | solution.py:268
  142.5 6.9 %all-to-all-start.4 = ((bf16[32,16,1024]{2,1,0:T(8,128)(2,1)}), bf16[32,16,1024]{2,1,0:T(8,128)(2,1)S(1)}, u32[]{:S(2)}, u32[]{:S(2)}) async-start(bf16[32,16,1024]{2,1,0:T(8,128)(2,1)} %bitcast.17), calls=%async_computation.4 | async-start | bytes 2097152 | tf_op jit(solution)/shard_map/all_to_all | solution.py:268
  152.7 25.1 %all-to-all-done.4 = bf16[32,16,1024]{2,1,0:T(8,128)(2,1)S(1)} async-done(((bf16[32,16,1024]{2,1,0:T(8,128)(2,1)}), bf16[32,16,1024]{2,1,0:T(8,128)(2,1)S(1)}, u32[]{:S(2)}, u32[]{:S(2)}) %all-to-all-start.4) | async-done | bytes 1048608 | tf_op jit(solution)/shard_map/all_to_all | solution.py:268
  178.6 12.3 %all_to_all.30 = bf16[4,64,512]{2,1,0:T(8,128)(2,1)S(1)} all-to-all(bf16[4,64,512]{2,1,0:T(8,128)(2,1)S(1)} %bitcast.48), channel_id=1, replica_groups=mesh['p'=2,'m'=2,'k'=2,'zh'=2,'y'=8,'x'=4] {'p','zh'}, dimensions={0} | all-to-all | bytes 524288 | tf_op jit(solution)/shard_map/all_to_all | solution.py:272
  (77 shorter events, 25.4 us)
Async XLA Ops:
  3.6 22.7 %all-to-all-start = ((bf16[4,80,512]{2,1,0:T(8,128)(2,1)}), bf16[4,80,512]{2,1,0:T(8,128)(2,1)S(1)}, u32[]{:S(2)}, u32[]{:S(2)}) async-start(bf16[4,80,512]{2,1,0:T(8,128)(2,1)} %broadcast_in_dim.46), calls=%async_computation | async-start | bytes 655360 | tf_op jit(solution)/shard_map/all_to_all | solution.py:233
  15.1 1.4 copy-start
  16.5 1.4 copy-start.1
  18.9 0.8 copy-start.4
  19.6 0.8 copy-start.6
  20.4 0.9 copy-start.14
  21.3 0.9 copy-start.15
  28.4 0.7 copy-start.10
  29.1 37.6 %all-to-all-start.1 = ((bf16[32,16,1024]{2,1,0:T(8,128)(2,1)}), bf16[32,16,1024]{2,1,0:T(8,128)(2,1)S(1)}, u32[]{:S(2)}, u32[]{:S(2)}) async-start(bf16[32,16,1024]{2,1,0:T(8,128)(2,1)} %bitcast.6), calls=%async_computation.1 | async-start | bytes 2097152 | tf_op jit(solution)/shard_map/all_to_all | solution.py:253
  39.3 20.0 %collective-permute-start = (bf16[2,192,1024]{2,1,0:T(8,128)(2,1)}, bf16[2,192,1024]{2,1,0:T(8,128)(2,1)S(1)}, u32[]{:S(2)}, u32[]{:S(2)}) collective-permute-start(bf16[2,192,1024]{2,1,0:T(8,128)(2,1)} %copy-done.15), channel_id=1, source_target_pairs={{0,128},{128,0},{1,129},{129,1},{2,130},{130,2},{3,131},{131,3},{4... | collective-permute-start | bytes 2359304 | tf_op jit(solution)/shard_map/ppermute | solution.py:25
  45.0 0.7 copy-start.8
  45.7 14.6 %copy-start.12 = (bf16[512,64]{1,0:T(8,128)(2,1)}, bf16[512,64]{1,0:T(8,128)(2,1)S(1)}, u32[]{:S(2)}) copy-start(bf16[512,64]{1,0:T(8,128)(2,1)S(1)} %get-tuple-element.52) | copy-start | bytes 196612
  60.3 18.3 %collective-permute-start.1 = (bf16[384,1024]{1,0:T(8,128)(2,1)}, bf16[384,1024]{1,0:T(8,128)(2,1)}, u32[]{:S(2)}, u32[]{:S(2)}) collective-permute-start(bf16[384,1024]{1,0:T(8,128)(2,1)} %shard_map.85), channel_id=1, source_target_pairs={{0,64},{64,0},{1,65},{65,1},{2,66},{66,2},{3,67},{67,3},{4,68},{68... | collective-permute-start | bytes 2359304 | tf_op jit(solution)/shard_map/ppermute | solution.py:25
  62.2 25.1 %collective-permute-start.5 = (bf16[2,192,1024]{2,1,0:T(8,128)(2,1)}, bf16[2,192,1024]{2,1,0:T(8,128)(2,1)}, u32[]{:S(2)}, u32[]{:S(2)}) collective-permute-start(bf16[2,192,1024]{2,1,0:T(8,128)(2,1)} %copy-done.14), channel_id=1, source_target_pairs={{0,128},{128,0},{1,129},{129,1},{2,130},{130,2},{3,131},{131,3},{4... | collective-permute-start | bytes 2359304 | tf_op jit(solution)/shard_map/ppermute | solution.py:25
  66.7 1.0 copy-start.2
  67.6 11.0 %copy-start.3 = (bf16[32,16,1024]{2,1,0:T(8,128)(2,1)S(1)}, bf16[32,16,1024]{2,1,0:T(8,128)(2,1)}, u32[]{:S(2)}) copy-start(bf16[32,16,1024]{2,1,0:T(8,128)(2,1)} %copy-done.2) | copy-start | bytes 3145732
  67.6 38.4 %all-to-all-start.3 = ((bf16[32,16,1024]{2,1,0:T(8,128)(2,1)}), bf16[32,16,1024]{2,1,0:T(8,128)(2,1)S(1)}, u32[]{:S(2)}, u32[]{:S(2)}) async-start(bf16[32,16,1024]{2,1,0:T(8,128)(2,1)} %bitcast.15), calls=%async_computation.3 | async-start | bytes 2097152 | tf_op jit(solution)/shard_map/all_to_all | solution.py:253
  78.6 8.6 %copy-start.5 = (bf16[192,1024]{1,0:T(8,128)(2,1)S(1)}, bf16[192,1024]{1,0:T(8,128)(2,1)}, u32[]{:S(2)}) copy-start(bf16[192,1024]{1,0:T(8,128)(2,1)} %copy-done.4) | copy-start | bytes 1179652
  78.6 8.6 %copy-start.7 = (bf16[192,1024]{1,0:T(8,128)(2,1)S(1)}, bf16[192,1024]{1,0:T(8,128)(2,1)}, u32[]{:S(2)}) copy-start(bf16[192,1024]{1,0:T(8,128)(2,1)} %copy-done.6) | copy-start | bytes 1179652
  81.3 3.6 %collective-permute-start.2 = (bf16[512,384]{1,0:T(8,128)(2,1)S(1)}, bf16[512,384]{1,0:T(8,128)(2,1)S(1)}, u32[]{:S(2)}, u32[]{:S(2)}) collective-permute-start(bf16[512,384]{1,0:T(8,128)(2,1)S(1)} %get-tuple-element.41), channel_id=1, source_target_pairs={{0,64},{64,0},{1,65},{65,1},{2,66},{66,2},{3,67},{67,3},{4,68},{68... | collective-permute-start | bytes 1179656 | tf_op jit(solution)/shard_map/ppermute | solution.py:25
  85.1 13.1 %collective-permute-start.3 = (bf16[512,384]{1,0:T(8,128)(2,1)S(1)}, bf16[512,384]{1,0:T(8,128)(2,1)S(1)}, u32[]{:S(2)}, u32[]{:S(2)}) collective-permute-start(bf16[512,384]{1,0:T(8,128)(2,1)S(1)} %fusion.2), channel_id=1, source_target_pairs={{0,128},{128,0},{1,129},{129,1},{2,130},{130,2},{3,131},{131,3},{4... | collective-permute-start | bytes 1179656 | tf_op jit(solution)/shard_map/ppermute | solution.py:25
  88.6 11.8 %collective-permute-start.6 = (bf16[384,1024]{1,0:T(8,128)(2,1)S(1)}, bf16[384,1024]{1,0:T(8,128)(2,1)S(1)}, u32[]{:S(2)}, u32[]{:S(2)}) collective-permute-start(bf16[384,1024]{1,0:T(8,128)(2,1)S(1)} %pad_maximum_fusion.2), channel_id=1, source_target_pairs={{0,64},{64,0},{1,65},{65,1},{2,66},{66,2},{3,67},{67,3},{4,68},{68... | collective-permute-start | bytes 2359304 | tf_op jit(solution)/shard_map/ppermute | solution.py:25
  98.4 3.6 %collective-permute-start.4 = (bf16[512,384]{1,0:T(8,128)(2,1)S(1)}, bf16[512,384]{1,0:T(8,128)(2,1)S(1)}, u32[]{:S(2)}, u32[]{:S(2)}) collective-permute-start(bf16[512,384]{1,0:T(8,128)(2,1)S(1)} %multiply_convert_fusion.1.hidden), channel_id=1, source_target_pairs={{0,64},{64,0},{1,65},{65,1},{2,66},{66,2},{3,67},{67,3},{4,68},{68... | collective-permute-start | bytes 1179656 | tf_op jit(solution)/shard_map/ppermute | solution.py:25
  106.0 36.5 %all-to-all-start.2 = ((bf16[32,16,1024]{2,1,0:T(8,128)(2,1)}), bf16[32,16,1024]{2,1,0:T(8,128)(2,1)}, u32[]{:S(2)}, u32[]{:S(2)}) async-start(bf16[32,16,1024]{2,1,0:T(8,128)(2,1)} %bitcast.13), calls=%async_computation.2 | async-start | bytes 2097152 | tf_op jit(solution)/shard_map/all_to_all | solution.py:268
  116.7 3.6 %collective-permute-start.7 = (bf16[512,384]{1,0:T(8,128)(2,1)S(1)}, bf16[512,384]{1,0:T(8,128)(2,1)S(1)}, u32[]{:S(2)}, u32[]{:S(2)}) collective-permute-start(bf16[512,384]{1,0:T(8,128)(2,1)S(1)} %get-tuple-element.51), channel_id=1, source_target_pairs={{0,64},{64,0},{1,65},{65,1},{2,66},{66,2},{3,67},{67,3},{4,68},{68... | collective-permute-start | bytes 1179656 | tf_op jit(solution)/shard_map/ppermute | solution.py:25
  120.3 13.1 %collective-permute-start.8 = (bf16[512,384]{1,0:T(8,128)(2,1)S(1)}, bf16[512,384]{1,0:T(8,128)(2,1)S(1)}, u32[]{:S(2)}, u32[]{:S(2)}) collective-permute-start(bf16[512,384]{1,0:T(8,128)(2,1)S(1)} %fusion.3), channel_id=1, source_target_pairs={{0,128},{128,0},{1,129},{129,1},{2,130},{130,2},{3,131},{131,3},{4... | collective-permute-start | bytes 1179656 | tf_op jit(solution)/shard_map/ppermute | solution.py:25
  133.7 3.6 %collective-permute-start.9 = (bf16[512,384]{1,0:T(8,128)(2,1)S(1)}, bf16[512,384]{1,0:T(8,128)(2,1)S(1)}, u32[]{:S(2)}, u32[]{:S(2)}) collective-permute-start(bf16[512,384]{1,0:T(8,128)(2,1)S(1)} %multiply_convert_fusion.hidden), channel_id=1, source_target_pairs={{0,64},{64,0},{1,65},{65,1},{2,66},{66,2},{3,67},{67,3},{4,68},{68... | collective-permute-start | bytes 1179656 | tf_op jit(solution)/shard_map/ppermute | solution.py:25
  139.5 9.9 %copy-start.11 = (bf16[512,64]{1,0:T(8,128)(2,1)S(1)}, bf16[512,64]{1,0:T(8,128)(2,1)}, u32[]{:S(2)}) copy-start(bf16[512,64]{1,0:T(8,128)(2,1)} %copy-done.10) | copy-start | bytes 196612
  142.5 35.3 %all-to-all-start.4 = ((bf16[32,16,1024]{2,1,0:T(8,128)(2,1)}), bf16[32,16,1024]{2,1,0:T(8,128)(2,1)S(1)}, u32[]{:S(2)}, u32[]{:S(2)}) async-start(bf16[32,16,1024]{2,1,0:T(8,128)(2,1)} %bitcast.17), calls=%async_computation.4 | async-start | bytes 2097152 | tf_op jit(solution)/shard_map/all_to_all | solution.py:268
  149.4 28.4 %copy-start.13 = (bf16[512,64]{1,0:T(8,128)(2,1)S(1)}, bf16[512,64]{1,0:T(8,128)(2,1)}, u32[]{:S(2)}) copy-start(bf16[512,64]{1,0:T(8,128)(2,1)} %copy-done.12) | copy-start | bytes 196612
  151.0 27.1 %copy-start.9 = (bf16[512,64]{1,0:T(8,128)(2,1)S(1)}, bf16[512,64]{1,0:T(8,128)(2,1)}, u32[]{:S(2)}) copy-start(bf16[512,64]{1,0:T(8,128)(2,1)} %copy-done.8) | copy-start | bytes 196612

commit v14 on v13

--- a/solution.py
+++ b/solution.py
@@ -238,8 +238,9 @@
     gate_far = swap(gate_sent, "m")
     routed = [route(came, plans[index], index, group) for index in range(batches)]
     gate_far, routed[1] = lax.optimization_barrier((gate_far, routed[1]))
-    gate_own = order(gate_parts[0], gate_far[0])
     gate_other = swap(ordered(gate_parts[1], gate_far, 1), "k")
+    gate_mine, gate_near, gate_other = lax.optimization_barrier((gate_parts[0], gate_far, gate_other))
+    gate_own = ordered(gate_mine, gate_near, 0)
     _, down_sent = lax.optimization_barrier((gate_far, down_parts[2]))
     down_far = swap(down_sent, "m")
     down_own = order(down_parts[0], down_far[0])

time: 193 us -> 194 us (level)
    unnamed x32 -> x34, local copies, waits for them, and re-layouts: 8.42 us -> 8.88 us
  transfers between devices with their start and end apart: 15 -> 15, of which waited for: 11 -> 10; matrix products, arithmetic and copies ran while one was open for 4% -> 4% of each run, Pallas kernels for 7% -> 7%
where the time goes in v14:
time: 194 us; the launch traced here: 192 us
  waiting for transfers between devices  71.9 us (37%)
  starting transfers between devices  70.2 us (36%)
  Pallas kernels  15.4 us (8%)
  blocking collectives  12.1 us (6%)
  local copies, waits for them, and re-layouts  10.6 us (5%)
  other arithmetic  8.05 us (4%)
  matrix products  3.79 us (2%)
    ppermute x10, waiting for transfers between devices, swap(): return lax.ppermute(array, axes, [(i, last - i) for i in range(last + 1)])  39.5 us
    all_to_all x2, waiting for transfers between devices, local(): lax.all_to_all(out, ('y', 'x'), 0, 0, tiled=True).reshape(-1, out.shape[2])  28 us
    ppermute x10, starting transfers between devices, swap(): return lax.ppermute(array, axes, [(i, last - i) for i in range(last + 1)])  23.1 us
    all_to_all x2, starting transfers between devices, local(): lax.all_to_all(rows, ('y', 'x'), 0, 0, tiled=True)  20 us
    all_to_all x2, starting transfers between devices, local(): lax.all_to_all(out, ('y', 'x'), 0, 0, tiled=True).reshape(-1, out.shape[2])  16.8 us
    all_to_all x1, blocking collectives, local(): terms = lax.all_to_all(mixed, ('p', 'zh'), 0, 0, tiled=True)  12.1 us
    all_to_all x1, starting transfers between devices, local(): came = lax.all_to_all(sent, ('p', 'zh'), 0, 0, tiled=True)  10.3 us
    pallas_call x4, Pallas kernels, on_rows(): pl.pallas_call(kernel, out_shape=[jax.ShapeDtypeStruct((count, width), he...  10.2 us
  transfers between devices with their start and end apart: 15, of which 10 were waited for; matrix products, arithmetic and copies ran while one was open for 4% of the time, Pallas kernels for 7%

profile of v14, /device:TPU:2, one launch (start us, length us, event | category | flops | bytes accessed | tf_op | source)
XLA Modules:
  0.0 192.4 jit_solution(16466083855660551384)
XLA Ops:
  3.6 10.3 %all-to-all-start = ((bf16[4,80,512]{2,1,0:T(8,128)(2,1)}), bf16[4,80,512]{2,1,0:T(8,128)(2,1)S(1)}, u32[]{:S(2)}, u32[]{:S(2)}) async-start(bf16[4,80,512]{2,1,0:T(8,128)(2,1)} %broadcast_in_dim.46), calls=%async_computation | async-start | bytes 655360 | tf_op jit(solution)/shard_map/all_to_all | solution.py:233
  22.0 4.3 %all-to-all-done.came = bf16[4,80,512]{2,1,0:T(8,128)(2,1)S(1)} async-done(((bf16[4,80,512]{2,1,0:T(8,128)(2,1)}), bf16[4,80,512]{2,1,0:T(8,128)(2,1)S(1)}, u32[]{:S(2)}, u32[]{:S(2)}) %all-to-all-start) | async-done | bytes 327712 | tf_op jit(solution)/shard_map/all_to_all | solution.py:233
  26.3 2.1 %shard_map.83 = (bf16[512,1024]{1,0:T(8,128)(2,1)}, bf16[512,64]{1,0:T(8,128)(2,1)S(1)}, bf16[512,64]{1,0:T(8,128)(2,1)S(1)}) custom-call(bf16[4,80,512]{2,1,0:T(8,128)(2,1)S(1)} %all-to-all-done.came, f32[64,2]{1,0:T(8,128)S(1)} %copy.47.codes), custom_call_target="tpu_custom_call" | custom-call | flops 67108864 | bytes 2097152 | tf_op jit(solution)/shard_map/pallas_call | solution.py:163
  29.1 10.3 %all-to-all-start.1 = ((bf16[32,16,1024]{2,1,0:T(8,128)(2,1)}), bf16[32,16,1024]{2,1,0:T(8,128)(2,1)S(1)}, u32[]{:S(2)}, u32[]{:S(2)}) async-start(bf16[32,16,1024]{2,1,0:T(8,128)(2,1)} %bitcast.6), calls=%async_computation.1 | async-start | bytes 2097152 | tf_op jit(solution)/shard_map/all_to_all | solution.py:254
  39.3 3.5 %collective-permute-start = (bf16[2,192,1024]{2,1,0:T(8,128)(2,1)S(1)}, bf16[2,192,1024]{2,1,0:T(8,128)(2,1)S(1)}, u32[]{:S(2)}, u32[]{:S(2)}) collective-permute-start(bf16[2,192,1024]{2,1,0:T(8,128)(2,1)S(1)} %get-tuple-element.37), channel_id=1, source_target_pairs={{0,128},{128,0},{1,129},{129,1},{2,130},{130,2},{3,131},{131,3},{4... | collective-permute-start | bytes 2359304 | tf_op jit(solution)/shard_map/ppermute | solution.py:25
  43.0 2.1 %shard_map.84 = (bf16[512,1024]{1,0:T(8,128)(2,1)}, bf16[512,64]{1,0:T(8,128)(2,1)S(1)}, bf16[512,64]{1,0:T(8,128)(2,1)S(1)}) custom-call(bf16[4,80,512]{2,1,0:T(8,128)(2,1)S(1)} %all-to-all-done.came, f32[64,2]{1,0:T(8,128)S(1)} %copy.48.codes), custom_call_target="tpu_custom_call" | custom-call | flops 67108864 | bytes 2097152 | tf_op jit(solution)/shard_map/pallas_call | solution.py:163
  45.0 14.1 %collective-permute-done.far = bf16[2,192,1024]{2,1,0:T(8,128)(2,1)S(1)} collective-permute-done((bf16[2,192,1024]{2,1,0:T(8,128)(2,1)S(1)}, bf16[2,192,1024]{2,1,0:T(8,128)(2,1)S(1)}, u32[]{:S(2)}, u32[]{:S(2)}) %collective-permute-start) | collective-permute-done | bytes 786464 | tf_op jit(solution)/shard_map/ppermute | solution.py:25
  59.2 1.9 collective-permute-start.1
  61.1 3.6 %collective-permute-start.5 = (bf16[2,192,1024]{2,1,0:T(8,128)(2,1)}, bf16[2,192,1024]{2,1,0:T(8,128)(2,1)}, u32[]{:S(2)}, u32[]{:S(2)}) collective-permute-start(bf16[2,192,1024]{2,1,0:T(8,128)(2,1)} %copy-done.16), channel_id=1, source_target_pairs={{0,128},{128,0},{1,129},{129,1},{2,130},{130,2},{3,131},{131,3},{4... | collective-permute-start | bytes 2359304 | tf_op jit(solution)/shard_map/ppermute | solution.py:25
  65.8 9.8 %all-to-all-start.3 = ((bf16[32,16,1024]{2,1,0:T(8,128)(2,1)}), bf16[32,16,1024]{2,1,0:T(8,128)(2,1)S(1)}, u32[]{:S(2)}, u32[]{:S(2)}) async-start(bf16[32,16,1024]{2,1,0:T(8,128)(2,1)} %bitcast.14), calls=%async_computation.3 | async-start | bytes 2097152 | tf_op jit(solution)/shard_map/all_to_all | solution.py:254
  76.9 3.2 %shard_map.87 = (bf16[512,384]{1,0:T(8,128)(2,1)}, f32[512,384]{1,0:T(8,128)S(1)}) custom-call(bf16[512,1024]{1,0:T(8,128)(2,1)S(1)} %bitcast.42, bf16[384,1024]{1,0:T(8,128)(2,1)S(1)} %shard_map.86.own, bf16[384,1024]{1,0:T(8,128)(2,1)} %collective-permute-done.1.other), custom_call_target="tpu_custom_call" | custom-call | flops 805306368 | bytes 4194304 | tf_op jit(solution)/shard_map/pallas_call | solution.py:213
  80.1 1.9 collective-permute-start.2
  82.0 2.0 %collective-permute-done.2 = bf16[512,384]{1,0:T(8,128)(2,1)} collective-permute-done((bf16[512,384]{1,0:T(8,128)(2,1)}, bf16[512,384]{1,0:T(8,128)(2,1)}, u32[]{:S(2)}, u32[]{:S(2)}) %collective-permute-start.2) | collective-permute-done | bytes 393248 | tf_op jit(solution)/shard_map/ppermute | solution.py:25
  85.1 2.2 %collective-permute-start.3 = (bf16[512,384]{1,0:T(8,128)(2,1)S(1)}, bf16[512,384]{1,0:T(8,128)(2,1)S(1)}, u32[]{:S(2)}, u32[]{:S(2)}) collective-permute-start(bf16[512,384]{1,0:T(8,128)(2,1)S(1)} %fusion.2), channel_id=1, source_target_pairs={{0,128},{128,0},{1,129},{129,1},{2,130},{130,2},{3,131},{131,3},{4... | collective-permute-start | bytes 1179656 | tf_op jit(solution)/shard_map/ppermute | solution.py:25
  88.6 1.9 collective-permute-start.6
  90.5 7.6 %collective-permute-done.3 = bf16[512,384]{1,0:T(8,128)(2,1)S(1)} collective-permute-done((bf16[512,384]{1,0:T(8,128)(2,1)S(1)}, bf16[512,384]{1,0:T(8,128)(2,1)S(1)}, u32[]{:S(2)}, u32[]{:S(2)}) %collective-permute-start.3) | collective-permute-done | bytes 393248 | tf_op jit(solution)/shard_map/ppermute | solution.py:25
  99.4 1.9 collective-permute-start.4
  101.4 1.6 collective-permute-done.4.hidden_other
  103.0 2.2 %shard_map.88 = bf16[512,1024]{1,0:T(8,128)(2,1)} custom-call(bf16[512,384]{1,0:T(8,128)(2,1)S(1)} %multiply_convert_fusion.1.hidden, bf16[512,384]{1,0:T(8,128)(2,1)S(1)} %collective-permute-done.4.hidden_other, bf16[384,1024]{1,0:T(8,128)(2,1)S(1)} %pad_maximum_fusion.own, bf16[384,1024]{1,0:T(8,128)(2,1)S(1)} %collective-permute-done.6.other), custom_call_target="tpu_custom_call" | custom-call | flops 805306368 | bytes 4456448 | tf_op jit(solution)/shard_map/pallas_call | solution.py:213
  105.2 9.8 %all-to-all-start.2 = ((bf16[32,16,1024]{2,1,0:T(8,128)(2,1)}), bf16[32,16,1024]{2,1,0:T(8,128)(2,1)}, u32[]{:S(2)}, u32[]{:S(2)}) async-start(bf16[32,16,1024]{2,1,0:T(8,128)(2,1)} %bitcast.12), calls=%async_computation.2 | async-start | bytes 2097152 | tf_op jit(solution)/shard_map/all_to_all | solution.py:269
  115.1 2.6 %shard_map.89 = (bf16[512,384]{1,0:T(8,128)(2,1)S(1)}, f32[512,384]{1,0:T(8,128)S(1)}) custom-call(bf16[512,1024]{1,0:T(8,128)(2,1)S(1)} %bitcast.41, bf16[384,1024]{1,0:T(8,128)(2,1)S(1)} %shard_map.86.own, bf16[384,1024]{1,0:T(8,128)(2,1)} %collective-permute-done.1.other), custom_call_target="tpu_custom_call" | custom-call | flops 805306368 | bytes 4194304 | tf_op jit(solution)/shard_map/pallas_call | solution.py:213
  117.7 1.9 collective-permute-start.7
  119.6 1.7 collective-permute-done.7
  121.4 2.2 %collective-permute-start.8 = (bf16[512,384]{1,0:T(8,128)(2,1)S(1)}, bf16[512,384]{1,0:T(8,128)(2,1)S(1)}, u32[]{:S(2)}, u32[]{:S(2)}) collective-permute-start(bf16[512,384]{1,0:T(8,128)(2,1)S(1)} %fusion.3), channel_id=1, source_target_pairs={{0,128},{128,0},{1,129},{129,1},{2,130},{130,2},{3,131},{131,3},{4... | collective-permute-start | bytes 1179656 | tf_op jit(solution)/shard_map/ppermute | solution.py:25
  123.6 10.8 %collective-permute-done.8 = bf16[512,384]{1,0:T(8,128)(2,1)S(1)} collective-permute-done((bf16[512,384]{1,0:T(8,128)(2,1)S(1)}, bf16[512,384]{1,0:T(8,128)(2,1)S(1)}, u32[]{:S(2)}, u32[]{:S(2)}) %collective-permute-start.8) | collective-permute-done | bytes 393248 | tf_op jit(solution)/shard_map/ppermute | solution.py:25
  134.7 1.9 collective-permute-start.9
  136.6 1.7 collective-permute-done.9.hidden_other
  138.3 2.2 %shard_map.90 = bf16[512,1024]{1,0:T(8,128)(2,1)} custom-call(bf16[512,384]{1,0:T(8,128)(2,1)S(1)} %multiply_convert_fusion.hidden, bf16[512,384]{1,0:T(8,128)(2,1)S(1)} %collective-permute-done.9.hidden_other, bf16[384,1024]{1,0:T(8,128)(2,1)S(1)} %pad_maximum_fusion.own, bf16[384,1024]{1,0:T(8,128)(2,1)S(1)} %collective-permute-done.6.other), custom_call_target="tpu_custom_call" | custom-call | flops 805306368 | bytes 4456448 | tf_op jit(solution)/shard_map/pallas_call | solution.py:213
  140.5 3.0 %all-to-all-done.2 = bf16[32,16,1024]{2,1,0:T(8,128)(2,1)} async-done(((bf16[32,16,1024]{2,1,0:T(8,128)(2,1)}), bf16[32,16,1024]{2,1,0:T(8,128)(2,1)}, u32[]{:S(2)}, u32[]{:S(2)}) %all-to-all-start.2) | async-done | bytes 1048608 | tf_op jit(solution)/shard_map/all_to_all | solution.py:269
  143.5 6.9 %all-to-all-start.4 = ((bf16[32,16,1024]{2,1,0:T(8,128)(2,1)}), bf16[32,16,1024]{2,1,0:T(8,128)(2,1)S(1)}, u32[]{:S(2)}, u32[]{:S(2)}) async-start(bf16[32,16,1024]{2,1,0:T(8,128)(2,1)} %bitcast.16), calls=%async_computation.4 | async-start | bytes 2097152 | tf_op jit(solution)/shard_map/all_to_all | solution.py:269
  153.7 25.1 %all-to-all-done.4 = bf16[32,16,1024]{2,1,0:T(8,128)(2,1)S(1)} async-done(((bf16[32,16,1024]{2,1,0:T(8,128)(2,1)}), bf16[32,16,1024]{2,1,0:T(8,128)(2,1)S(1)}, u32[]{:S(2)}, u32[]{:S(2)}) %all-to-all-start.4) | async-done | bytes 1048608 | tf_op jit(solution)/shard_map/all_to_all | solution.py:269
  179.6 12.1 %all_to_all.30 = bf16[4,64,512]{2,1,0:T(8,128)(2,1)S(1)} all-to-all(bf16[4,64,512]{2,1,0:T(8,128)(2,1)S(1)} %bitcast.45), channel_id=1, replica_groups=mesh['p'=2,'m'=2,'k'=2,'zh'=2,'y'=8,'x'=4] {'p','zh'}, dimensions={0} | all-to-all | bytes 524288 | tf_op jit(solution)/shard_map/all_to_all | solution.py:273
  (78 shorter events, 23.5 us)
Async XLA Ops:
  3.6 22.7 %all-to-all-start = ((bf16[4,80,512]{2,1,0:T(8,128)(2,1)}), bf16[4,80,512]{2,1,0:T(8,128)(2,1)S(1)}, u32[]{:S(2)}, u32[]{:S(2)}) async-start(bf16[4,80,512]{2,1,0:T(8,128)(2,1)} %broadcast_in_dim.46), calls=%async_computation | async-start | bytes 655360 | tf_op jit(solution)/shard_map/all_to_all | solution.py:233
  15.1 1.4 copy-start
  16.5 1.4 copy-start.1
  18.9 0.8 copy-start.4
  19.6 0.8 copy-start.6
  20.4 0.7 copy-start.8
  21.1 0.9 copy-start.16
  28.4 0.7 copy-start.12
  29.1 35.7 %all-to-all-start.1 = ((bf16[32,16,1024]{2,1,0:T(8,128)(2,1)}), bf16[32,16,1024]{2,1,0:T(8,128)(2,1)S(1)}, u32[]{:S(2)}, u32[]{:S(2)}) async-start(bf16[32,16,1024]{2,1,0:T(8,128)(2,1)} %bitcast.6), calls=%async_computation.1 | async-start | bytes 2097152 | tf_op jit(solution)/shard_map/all_to_all | solution.py:254
  39.3 19.8 %collective-permute-start = (bf16[2,192,1024]{2,1,0:T(8,128)(2,1)S(1)}, bf16[2,192,1024]{2,1,0:T(8,128)(2,1)S(1)}, u32[]{:S(2)}, u32[]{:S(2)}) collective-permute-start(bf16[2,192,1024]{2,1,0:T(8,128)(2,1)S(1)} %get-tuple-element.37), channel_id=1, source_target_pairs={{0,128},{128,0},{1,129},{129,1},{2,130},{130,2},{3,131},{131,3},{4... | collective-permute-start | bytes 2359304 | tf_op jit(solution)/shard_map/ppermute | solution.py:25
  45.0 16.1 %copy-start.10 = (bf16[512,64]{1,0:T(8,128)(2,1)}, bf16[512,64]{1,0:T(8,128)(2,1)S(1)}, u32[]{:S(2)}) copy-start(bf16[512,64]{1,0:T(8,128)(2,1)S(1)} %get-tuple-element.53) | copy-start | bytes 196612
  45.0 16.1 %copy-start.14 = (bf16[512,64]{1,0:T(8,128)(2,1)}, bf16[512,64]{1,0:T(8,128)(2,1)S(1)}, u32[]{:S(2)}) copy-start(bf16[512,64]{1,0:T(8,128)(2,1)S(1)} %get-tuple-element.58) | copy-start | bytes 196612
  59.2 16.4 %collective-permute-start.1 = (bf16[384,1024]{1,0:T(8,128)(2,1)S(1)}, bf16[384,1024]{1,0:T(8,128)(2,1)}, u32[]{:S(2)}, u32[]{:S(2)}) collective-permute-start(bf16[384,1024]{1,0:T(8,128)(2,1)S(1)} %shard_map.85), channel_id=1, source_target_pairs={{0,64},{64,0},{1,65},{65,1},{2,66},{66,2},{3,67},{67,3},{4,68},{68... | collective-permute-start | bytes 2359304 | tf_op jit(solution)/shard_map/ppermute | solution.py:25
  61.1 26.2 %collective-permute-start.5 = (bf16[2,192,1024]{2,1,0:T(8,128)(2,1)}, bf16[2,192,1024]{2,1,0:T(8,128)(2,1)}, u32[]{:S(2)}, u32[]{:S(2)}) collective-permute-start(bf16[2,192,1024]{2,1,0:T(8,128)(2,1)} %copy-done.16), channel_id=1, source_target_pairs={{0,128},{128,0},{1,129},{129,1},{2,130},{130,2},{3,131},{131,3},{4... | collective-permute-start | bytes 2359304 | tf_op jit(solution)/shard_map/ppermute | solution.py:25
  64.8 1.0 copy-start.2
  65.8 39.5 %all-to-all-start.3 = ((bf16[32,16,1024]{2,1,0:T(8,128)(2,1)}), bf16[32,16,1024]{2,1,0:T(8,128)(2,1)S(1)}, u32[]{:S(2)}, u32[]{:S(2)}) async-start(bf16[32,16,1024]{2,1,0:T(8,128)(2,1)} %bitcast.14), calls=%async_computation.3 | async-start | bytes 2097152 | tf_op jit(solution)/shard_map/all_to_all | solution.py:254
  75.5 1.3 copy-start.3
  75.6 1.1 copy-start.5
  76.9 10.4 %copy-start.7 = (bf16[192,1024]{1,0:T(8,128)(2,1)S(1)}, bf16[192,1024]{1,0:T(8,128)(2,1)}, u32[]{:S(2)}) copy-start(bf16[192,1024]{1,0:T(8,128)(2,1)} %copy-done.6) | copy-start | bytes 1179652
  76.9 10.4 %copy-start.9 = (bf16[192,1024]{1,0:T(8,128)(2,1)S(1)}, bf16[192,1024]{1,0:T(8,128)(2,1)}, u32[]{:S(2)}) copy-start(bf16[192,1024]{1,0:T(8,128)(2,1)} %copy-done.8) | copy-start | bytes 1179652
  80.1 3.9 %collective-permute-start.2 = (bf16[512,384]{1,0:T(8,128)(2,1)}, bf16[512,384]{1,0:T(8,128)(2,1)}, u32[]{:S(2)}, u32[]{:S(2)}) collective-permute-start(bf16[512,384]{1,0:T(8,128)(2,1)} %get-tuple-element.47), channel_id=1, source_target_pairs={{0,64},{64,0},{1,65},{65,1},{2,66},{66,2},{3,67},{67,3},{4,68},{68... | collective-permute-start | bytes 1179656 | tf_op jit(solution)/shard_map/ppermute | solution.py:25
  85.1 13.1 %collective-permute-start.3 = (bf16[512,384]{1,0:T(8,128)(2,1)S(1)}, bf16[512,384]{1,0:T(8,128)(2,1)S(1)}, u32[]{:S(2)}, u32[]{:S(2)}) collective-permute-start(bf16[512,384]{1,0:T(8,128)(2,1)S(1)} %fusion.2), channel_id=1, source_target_pairs={{0,128},{128,0},{1,129},{129,1},{2,130},{130,2},{3,131},{131,3},{4... | collective-permute-start | bytes 1179656 | tf_op jit(solution)/shard_map/ppermute | solution.py:25
  88.6 12.8 %collective-permute-start.6 = (bf16[384,1024]{1,0:T(8,128)(2,1)S(1)}, bf16[384,1024]{1,0:T(8,128)(2,1)S(1)}, u32[]{:S(2)}, u32[]{:S(2)}) collective-permute-start(bf16[384,1024]{1,0:T(8,128)(2,1)S(1)} %pad_maximum_fusion.1), channel_id=1, source_target_pairs={{0,64},{64,0},{1,65},{65,1},{2,66},{66,2},{3,67},{67,3},{4,68},{68... | collective-permute-start | bytes 2359304 | tf_op jit(solution)/shard_map/ppermute | solution.py:25
  99.4 3.6 %collective-permute-start.4 = (bf16[512,384]{1,0:T(8,128)(2,1)S(1)}, bf16[512,384]{1,0:T(8,128)(2,1)S(1)}, u32[]{:S(2)}, u32[]{:S(2)}) collective-permute-start(bf16[512,384]{1,0:T(8,128)(2,1)S(1)} %multiply_convert_fusion.1.hidden), channel_id=1, source_target_pairs={{0,64},{64,0},{1,65},{65,1},{2,66},{66,2},{3,67},{67,3},{4,68},{68... | collective-permute-start | bytes 1179656 | tf_op jit(solution)/shard_map/ppermute | solution.py:25
  105.2 38.3 %all-to-all-start.2 = ((bf16[32,16,1024]{2,1,0:T(8,128)(2,1)}), bf16[32,16,1024]{2,1,0:T(8,128)(2,1)}, u32[]{:S(2)}, u32[]{:S(2)}) async-start(bf16[32,16,1024]{2,1,0:T(8,128)(2,1)} %bitcast.12), calls=%async_computation.2 | async-start | bytes 2097152 | tf_op jit(solution)/shard_map/all_to_all | solution.py:269
  117.7 3.6 %collective-permute-start.7 = (bf16[512,384]{1,0:T(8,128)(2,1)S(1)}, bf16[512,384]{1,0:T(8,128)(2,1)S(1)}, u32[]{:S(2)}, u32[]{:S(2)}) collective-permute-start(bf16[512,384]{1,0:T(8,128)(2,1)S(1)} %get-tuple-element.57), channel_id=1, source_target_pairs={{0,64},{64,0},{1,65},{65,1},{2,66},{66,2},{3,67},{67,3},{4,68},{68... | collective-permute-start | bytes 1179656 | tf_op jit(solution)/shard_map/ppermute | solution.py:25
  121.4 13.1 %collective-permute-start.8 = (bf16[512,384]{1,0:T(8,128)(2,1)S(1)}, bf16[512,384]{1,0:T(8,128)(2,1)S(1)}, u32[]{:S(2)}, u32[]{:S(2)}) collective-permute-start(bf16[512,384]{1,0:T(8,128)(2,1)S(1)} %fusion.3), channel_id=1, source_target_pairs={{0,128},{128,0},{1,129},{129,1},{2,130},{130,2},{3,131},{131,3},{4... | collective-permute-start | bytes 1179656 | tf_op jit(solution)/shard_map/ppermute | solution.py:25
  134.7 3.6 %collective-permute-start.9 = (bf16[512,384]{1,0:T(8,128)(2,1)S(1)}, bf16[512,384]{1,0:T(8,128)(2,1)S(1)}, u32[]{:S(2)}, u32[]{:S(2)}) collective-permute-start(bf16[512,384]{1,0:T(8,128)(2,1)S(1)} %multiply_convert_fusion.hidden), channel_id=1, source_target_pairs={{0,64},{64,0},{1,65},{65,1},{2,66},{66,2},{3,67},{67,3},{4,68},{68... | collective-permute-start | bytes 1179656 | tf_op jit(solution)/shard_map/ppermute | solution.py:25
  140.5 9.9 %copy-start.13 = (bf16[512,64]{1,0:T(8,128)(2,1)S(1)}, bf16[512,64]{1,0:T(8,128)(2,1)}, u32[]{:S(2)}) copy-start(bf16[512,64]{1,0:T(8,128)(2,1)} %copy-done.12) | copy-start | bytes 196612
  143.5 35.3 %all-to-all-start.4 = ((bf16[32,16,1024]{2,1,0:T(8,128)(2,1)}), bf16[32,16,1024]{2,1,0:T(8,128)(2,1)S(1)}, u32[]{:S(2)}, u32[]{:S(2)}) async-start(bf16[32,16,1024]{2,1,0:T(8,128)(2,1)} %bitcast.16), calls=%async_computation.4 | async-start | bytes 2097152 | tf_op jit(solution)/shard_map/all_to_all | solution.py:269
  150.4 28.4 %copy-start.15 = (bf16[512,64]{1,0:T(8,128)(2,1)S(1)}, bf16[512,64]{1,0:T(8,128)(2,1)}, u32[]{:S(2)}) copy-start(bf16[512,64]{1,0:T(8,128)(2,1)} %copy-done.14) | copy-start | bytes 196612
  152.0 27.1 %copy-start.11 = (bf16[512,64]{1,0:T(8,128)(2,1)S(1)}, bf16[512,64]{1,0:T(8,128)(2,1)}, u32[]{:S(2)}) copy-start(bf16[512,64]{1,0:T(8,128)(2,1)} %copy-done.10) | copy-start | bytes 196612
